TPU v7x, 32 devices: a whole 2x2x4 slice. The times are simulated.
32 devices in a mesh: row: 4 (over y, x), col: 8 (over z, core).
Axes of the slice: x: 2, y: 2, z: 4, core: 2. Of those that a mesh axis runs over, the one named last changes fastest.
Arguments:
- tokens: bfloat16 [32768, 1024], P(('row', 'col')), may hold values from -6 to 6
- lengths: int32 [32, 4], replicated, may hold values from 1 to 330, 992 in all within a row
- positives: int32 [32], replicated, may hold values from 0 to 127
- w_qkv: bfloat16 [1024, 3072], P(('row', 'col')), may hold values from -0.1875 to 0.1875
- b_qkv: bfloat16 [3072], P(('row', 'col')), may hold values from -1.75 to 1.75
- w_out: bfloat16 [1024, 1024], P(('row', 'col')), may hold values from -0.75 to 0.75
- b_out: bfloat16 [1024], P(('row', 'col')), may hold values from -1.75 to 1.75
- norm1_gain: bfloat16 [1024], P(('row', 'col')), may hold values from 0.25 to 1.75
- norm1_bias: bfloat16 [1024], P(('row', 'col')), may hold values from -1.75 to 1.75
- w_up: bfloat16 [1024, 4096], P(('row', 'col')), may hold values from -0.1875 to 0.1875
- b_up: bfloat16 [4096], P(('row', 'col')), may hold values from -1.75 to 1.75
- w_down: bfloat16 [4096, 1024], P(('row', 'col')), may hold values from -0.09375 to 0.09375
- b_down: bfloat16 [1024], P(('row', 'col')), may hold values from -1.75 to 1.75
- norm2_gain: bfloat16 [1024], P(('row', 'col')), may hold values from 0.25 to 1.75
- norm2_bias: bfloat16 [1024], P(('row', 'col')), may hold values from -1.75 to 1.75
- w_proj: bfloat16 [1024, 288], P(('row', 'col')), may hold values from -0.1875 to 0.1875
Outputs:
- loss_terms: float32 [3, 32], P(None, 'row')
- activations: bfloat16 [32768, 1024], P(('row', 'col'))
- input_grad: float32 [32768, 1024], P(('row', 'col'))
- grad_w_qkv: float32 [1024, 3072], P(('row', 'col'))
- grad_b_qkv: float32 [3072], P(('row', 'col'))
- grad_w_out: float32 [1024, 1024], P(('row', 'col'))
- grad_b_out: float32 [1024], P(('row', 'col'))
- grad_norm1_gain: float32 [1024], P(('row', 'col'))
- grad_norm1_bias: float32 [1024], P(('row', 'col'))
- grad_w_up: float32 [1024, 4096], P(('row', 'col'))
- grad_b_up: float32 [4096], P(('row', 'col'))
- grad_w_down: float32 [4096, 1024], P(('row', 'col'))
- grad_b_down: float32 [1024], P(('row', 'col'))
- grad_norm2_gain: float32 [1024], P(('row', 'col'))
- grad_norm2_bias: float32 [1024], P(('row', 'col'))
- grad_w_proj: float32 [1024, 288], P(('row', 'col'))
Inputs may be any that keep to these rules, and one draw needn't show every extreme that they name: Each row's 4 document lengths sum to 992; in every row the longest is exactly 330.
All inputs are finite; a program needn't handle non-finite values.
Results may differ from a plain program's by a relative error of at most 0.015.
Values may be sent and summed in bfloat16 or wider, within the bound.
No kernel may reach another device: no remote copies, remote signals or barrier semaphores. Data moves between devices by JAX's collectives and lax.ppermute only.
A program may use at most 448 MiB of HBM per device.

v0:
```python
import functools
import math

import jax
import jax.numpy as jnp
from jax import lax
from jax.sharding import PartitionSpec as P

D = 1024
HEADS = 16
HEAD_DIM = 64
PROJ_A = 128
PROJ_B = 96
PROJ_C = 64
QLEN = 32
DPR = 4
QPR = 1


highest = lax.Precision.HIGHEST
eps_norm = 1e-05
eps_vec = 1e-06
score_scale = 16.0


def combined_all(shard, axis, combine):
    everything = jax.tree.map(lambda part: lax.all_gather(part, axis), shard)
    initial = jax.tree.map(lambda part: part[0], everything)

    def lap(k, so_far):
        return combine(so_far, jax.tree.map(lambda part: part[k], everything))

    return lax.fori_loop(1, lax.axis_size(axis), lap, initial)


def head_slices():
    return ((0, PROJ_A), (PROJ_A, PROJ_B), (PROJ_A + PROJ_B, PROJ_C))


def layout(lengths, row_len, q_tokens):
    doc_count = lengths.shape[1]
    places = jnp.arange(row_len, dtype=jnp.int32)
    doc_ends = jnp.cumsum(lengths, axis=1)
    doc_starts = doc_ends - lengths
    offset = places[None, :] - q_tokens
    doc_index = jnp.sum((offset[:, :, None] >= doc_ends[:, None, :]).astype(jnp.int32), axis=2)
    chosen = (
        doc_index[:, :, None] == jnp.arange(doc_count, dtype=jnp.int32)[None, None, :]
    ).astype(jnp.int32)
    doc_start = jnp.sum(chosen * doc_starts[:, None, :], axis=2)
    is_query = places[None, :] < q_tokens
    segment = jnp.where(is_query, places[None, :] // QLEN, q_tokens // QLEN + doc_index)
    position = jnp.where(is_query, places[None, :] % QLEN, offset - doc_start)
    return (segment, position, doc_index)


def rotate(values, position):
    half_dim = values.shape[-1] // 2
    frequency = 10000.0 ** (-jnp.arange(half_dim, dtype=jnp.float32) / half_dim)
    angles = position.astype(jnp.float32)[:, None] * frequency[None, :]
    cosine = jnp.cos(angles)[:, None, :]
    sine_part = jnp.sin(angles)[:, None, :]
    first_half = values[..., :half_dim]
    second = values[..., half_dim:]
    return jnp.concatenate(
        [first_half * cosine - second * sine_part, second * cosine + first_half * sine_part],
        axis=-1,
    )


def layer_norm(resid_in, gain_vec, shift_vec):
    mean_val = jnp.mean(resid_in, axis=-1, keepdims=True)
    centered = resid_in - mean_val
    variance = jnp.mean(centered * centered, axis=-1, keepdims=True)
    return centered * lax.rsqrt(variance + eps_norm) * gain_vec + shift_vec


def normalize_heads(raw_vecs):
    pieces = []
    for head_start, head_width in head_slices():
        head_part = raw_vecs[:, head_start : head_start + head_width]
        pieces.append(
            head_part * lax.rsqrt(jnp.sum(head_part * head_part, axis=1, keepdims=True) + eps_vec)
        )
    return jnp.concatenate(pieces, axis=1)


def merge_scores(first_part, second_part):
    top_value = jnp.maximum(first_part[0], second_part[0])
    combined = first_part[1] * jnp.exp(first_part[0] - top_value) + second_part[1] * jnp.exp(
        second_part[0] - top_value
    )
    return (top_value, combined, first_part[2] + second_part[2])


def on_device(
    tokens,
    lengths,
    positives,
    w_qkv,
    b_qkv,
    w_out,
    b_out,
    norm1_gain,
    norm1_bias,
    w_up,
    b_up,
    w_down,
    b_down,
    norm2_gain,
    norm2_bias,
    w_proj,
):
    row_index = lax.axis_index("row")
    col_index = lax.axis_index("col")
    n_rows = lax.axis_size("row")
    n_cols = lax.axis_size("col")
    shards = (
        w_qkv,
        b_qkv,
        w_out,
        b_out,
        norm1_gain,
        norm1_bias,
        w_up,
        b_up,
        w_down,
        b_down,
        norm2_gain,
        norm2_bias,
        w_proj,
    )
    gathered = (
        lax.all_gather(shards[0], ("row", "col"), axis=0, tiled=True),
        lax.all_gather(shards[1], ("row", "col"), axis=0, tiled=True),
        lax.all_gather(shards[2], ("row", "col"), axis=0, tiled=True),
        lax.all_gather(shards[3], ("row", "col"), axis=0, tiled=True),
        lax.all_gather(shards[4], ("row", "col"), axis=0, tiled=True),
        lax.all_gather(shards[5], ("row", "col"), axis=0, tiled=True),
        lax.all_gather(shards[6], ("row", "col"), axis=0, tiled=True),
        lax.all_gather(shards[7], ("row", "col"), axis=0, tiled=True),
        lax.all_gather(shards[8], ("row", "col"), axis=0, tiled=True),
        lax.all_gather(shards[9], ("row", "col"), axis=0, tiled=True),
        lax.all_gather(shards[10], ("row", "col"), axis=0, tiled=True),
        lax.all_gather(shards[11], ("row", "col"), axis=0, tiled=True),
        lax.all_gather(shards[12], ("row", "col"), axis=0, tiled=True),
    )
    (
        full_qkv,
        full_bqkv,
        full_out,
        full_bout,
        full_gain1,
        full_bias1,
        full_up,
        full_bup,
        full_down,
        full_bdown,
        full_gain2,
        full_bias2,
        full_proj,
    ) = gathered
    gain_one = full_gain1.astype(jnp.float32)
    bias_one = full_bias1.astype(jnp.float32)
    gain_two = full_gain2.astype(jnp.float32)
    bias_two = full_bias2.astype(jnp.float32)
    row_len = tokens.shape[0]
    q_tokens = QPR * QLEN
    own_lengths = lax.dynamic_slice_in_dim(lengths, row_index * n_cols + col_index, 1, 0)
    own_segment, own_position, own_docs = layout(own_lengths, row_len, q_tokens)
    segment = own_segment[0]
    position = own_position[0]
    x_float = tokens.astype(jnp.float32)
    qkv_all = jnp.dot(tokens, full_qkv, preferred_element_type=jnp.float32) + full_bqkv.astype(
        jnp.float32
    )

    def split_heads(part_cols):
        return part_cols.reshape(row_len, HEADS, HEAD_DIM)

    def rope_pair(pair):
        return (rotate(pair[0], position), rotate(pair[1], position))

    rotated_pair, rope_pull = jax.vjp(
        rope_pair, (split_heads(qkv_all[:, :D]), split_heads(qkv_all[:, D : 2 * D]))
    )
    queries = rotated_pair[0].astype(jnp.bfloat16)
    key_vecs = rotated_pair[1].astype(jnp.bfloat16)
    values = split_heads(qkv_all[:, 2 * D :]).astype(jnp.bfloat16)
    attn_scale = HEAD_DIM ** (-0.5)
    allowed = segment[:, None] == segment[None, :]
    rows_block = math.gcd(row_len, 512)
    attended_parts = []
    lse_parts = []
    for start_row in range(0, row_len, rows_block):
        query_block = queries[start_row : start_row + rows_block]
        logits = (
            jnp.einsum("qhd,khd->hqk", query_block, key_vecs, preferred_element_type=jnp.float32)
            * attn_scale
        )
        logits = jnp.where(allowed[None, start_row : start_row + rows_block], logits, -1e30)
        row_peak = jnp.max(logits, axis=-1, keepdims=True)
        exp_vals = jnp.exp(logits - row_peak)
        denominator = jnp.sum(exp_vals, axis=-1, keepdims=True)
        attn_probs = (exp_vals / denominator).astype(jnp.bfloat16)
        attended_parts.append(
            jnp.einsum("hqk,khd->qhd", attn_probs, values, preferred_element_type=jnp.float32)
        )
        lse_parts.append(row_peak + jnp.log(denominator))
    attended = jnp.concatenate(attended_parts, axis=0).reshape(row_len, D).astype(jnp.bfloat16)
    out_proj = jnp.dot(attended, full_out, preferred_element_type=jnp.float32) + full_bout.astype(
        jnp.float32
    )
    resid_one = x_float + out_proj
    hidden_one, first_pull = jax.vjp(layer_norm, resid_one, gain_one, bias_one)
    hidden_low = hidden_one.astype(jnp.bfloat16)
    inner_pre = jnp.dot(hidden_low, full_up, preferred_element_type=jnp.float32) + full_bup.astype(
        jnp.float32
    )
    gelu_out = jax.nn.gelu(inner_pre, approximate=False).astype(jnp.bfloat16)
    branch = jnp.dot(gelu_out, full_down, preferred_element_type=jnp.float32) + full_bdown.astype(
        jnp.float32
    )
    resid_two = hidden_one + branch
    result, second_pull = jax.vjp(layer_norm, resid_two, gain_two, bias_two)
    result_low = result.astype(jnp.bfloat16)
    raw_vecs = jnp.dot(result_low, full_proj, preferred_element_type=jnp.float32)
    normed, norm_pull = jax.vjp(normalize_heads, raw_vecs)
    vectors = normed.astype(jnp.bfloat16)
    query_all = lax.all_gather(vectors[:q_tokens], "col", axis=0, tiled=True)
    doc_all = lax.all_gather(vectors[q_tokens:], "row", axis=0, tiled=True)
    col_lengths = lax.dynamic_slice_in_dim(lengths.reshape(n_rows, n_cols, DPR), col_index, 1, 1)[
        :, 0
    ]
    col_segment, col_position, col_docs = layout(col_lengths, row_len, q_tokens)
    tile_docs = n_rows * DPR
    local_ids = (
        col_docs[:, q_tokens:] + DPR * jnp.arange(n_rows, dtype=jnp.int32)[:, None]
    ).reshape(-1)
    doc_hot = (jnp.arange(tile_docs, dtype=jnp.int32)[:, None] == local_ids[None, :]).astype(
        jnp.float32
    )
    log_count = jnp.log(col_lengths.reshape(-1).astype(jnp.float32))
    global_ids = (
        (jnp.arange(n_rows, dtype=jnp.int32)[:, None] * n_cols + col_index) * DPR
        + jnp.arange(DPR, dtype=jnp.int32)[None, :]
    ).reshape(-1)
    query_count = n_cols * QPR
    own_positives = lax.dynamic_slice_in_dim(positives, row_index * query_count, query_count)
    positive_hot = (own_positives[:, None] == global_ids[None, :]).astype(jnp.float32)
    query_rows = query_all.shape[0]
    tile_block = math.gcd(query_rows, 512)
    kept_peaks = []
    kept_sums = []
    head_scores = []
    for head_start, head_width in head_slices():
        doc_head = doc_all[:, head_start : head_start + head_width]
        peak_list = []
        sum_list = []
        score_list = []
        for start_row in range(0, query_rows, tile_block):
            query_head = query_all[
                start_row : start_row + tile_block, head_start : head_start + head_width
            ]
            tok_scores = (
                jnp.einsum("qe,je->qj", query_head, doc_head, preferred_element_type=jnp.float32)
                * score_scale
            )
            row_peak = jnp.max(tok_scores, axis=1, keepdims=True)
            exp_vals = jnp.exp(tok_scores - row_peak)
            doc_sums = jnp.einsum(
                "qj,dj->qd",
                exp_vals,
                doc_hot,
                precision=highest,
                preferred_element_type=jnp.float32,
            )
            smooth = row_peak + jnp.log(doc_sums) - log_count[None, :]
            score_list.append(jnp.sum(smooth.reshape(tile_block // QLEN, QLEN, tile_docs), axis=1))
            peak_list.append(row_peak)
            sum_list.append(doc_sums)
        kept_peaks.append(peak_list)
        kept_sums.append(sum_list)
        head_scores.append(jnp.concatenate(score_list, axis=0))
    doc_scores = jnp.stack(head_scores)
    local_top = jnp.max(doc_scores, axis=2)
    local_den = jnp.sum(jnp.exp(doc_scores - local_top[..., None]), axis=2)
    local_pos = jnp.sum(doc_scores * positive_hot[None], axis=2)
    top_all, den_all, pos_all = combined_all((local_top, local_den, local_pos), "col", merge_scores)
    losses = top_all + jnp.log(den_all) - pos_all
    score_grad = jnp.exp(doc_scores - top_all[..., None]) / den_all[..., None] - positive_hot[None]
    query_heads = []
    doc_heads = []
    for head_index, (head_start, head_width) in enumerate(head_slices()):
        doc_head = doc_all[:, head_start : head_start + head_width]
        doc_grad = jnp.zeros((doc_all.shape[0], head_width), jnp.float32)
        query_parts = []
        for block_index, start_row in enumerate(range(0, query_rows, tile_block)):
            query_head = query_all[
                start_row : start_row + tile_block, head_start : head_start + head_width
            ]
            tok_scores = (
                jnp.einsum("qe,je->qj", query_head, doc_head, preferred_element_type=jnp.float32)
                * score_scale
            )
            exp_vals = jnp.exp(tok_scores - kept_peaks[head_index][block_index])
            grad_block = score_grad[
                head_index, start_row // QLEN : (start_row + tile_block) // QLEN
            ]
            token_coef = jnp.repeat(grad_block, QLEN, axis=0) / kept_sums[head_index][block_index]
            spread = jnp.einsum(
                "qd,dj->qj",
                token_coef,
                doc_hot,
                precision=highest,
                preferred_element_type=jnp.float32,
            )
            score_back = (exp_vals * spread * score_scale).astype(jnp.bfloat16)
            query_parts.append(
                jnp.einsum("qj,je->qe", score_back, doc_head, preferred_element_type=jnp.float32)
            )
            doc_grad = doc_grad + jnp.einsum(
                "qj,qe->je", score_back, query_head, preferred_element_type=jnp.float32
            )
        query_heads.append(jnp.concatenate(query_parts, axis=0))
        doc_heads.append(doc_grad)
    query_grad_all = jnp.concatenate(query_heads, axis=1)
    doc_grad_all = jnp.concatenate(doc_heads, axis=1)
    query_back = lax.psum_scatter(query_grad_all, "col", scatter_dimension=0, tiled=True)
    doc_back = lax.psum_scatter(doc_grad_all, "row", scatter_dimension=0, tiled=True)
    vector_grad = jnp.concatenate([query_back, doc_back], axis=0)
    raw_grad = norm_pull(vector_grad)[0].astype(jnp.bfloat16)
    grad_proj = jnp.einsum("td,te->de", result_low, raw_grad, preferred_element_type=jnp.float32)
    result_grad = jnp.einsum("te,de->td", raw_grad, full_proj, preferred_element_type=jnp.float32)
    resid_two_grad, grad_gain2, grad_bias2 = second_pull(result_grad)
    branch_grad = resid_two_grad.astype(jnp.bfloat16)
    grad_bdown = jnp.sum(branch_grad.astype(jnp.float32), axis=0)
    grad_down = jnp.einsum("tf,td->fd", gelu_out, branch_grad, preferred_element_type=jnp.float32)
    act_grad = jnp.einsum("td,fd->tf", branch_grad, full_down, preferred_element_type=jnp.float32)
    gelu_value, gelu_pull = jax.vjp(functools.partial(jax.nn.gelu, approximate=False), inner_pre)
    inner_grad = gelu_pull(act_grad)[0].astype(jnp.bfloat16)
    grad_bup = jnp.sum(inner_grad.astype(jnp.float32), axis=0)
    grad_up = jnp.einsum("td,tf->df", hidden_low, inner_grad, preferred_element_type=jnp.float32)
    hidden_grad = resid_two_grad + jnp.einsum(
        "tf,df->td", inner_grad, full_up, preferred_element_type=jnp.float32
    )
    resid_one_grad, grad_gain1, grad_bias1 = first_pull(hidden_grad)
    out_grad = resid_one_grad.astype(jnp.bfloat16)
    grad_bout = jnp.sum(out_grad.astype(jnp.float32), axis=0)
    grad_out = jnp.einsum("td,te->de", attended, out_grad, preferred_element_type=jnp.float32)
    attended_grad = (
        jnp.einsum("te,de->td", out_grad, full_out, preferred_element_type=jnp.float32)
        .astype(jnp.bfloat16)
        .reshape(row_len, HEADS, HEAD_DIM)
    )
    query_grad_parts = []
    key_grad = jnp.zeros((row_len, HEADS, HEAD_DIM), jnp.float32)
    value_grad = jnp.zeros((row_len, HEADS, HEAD_DIM), jnp.float32)
    for block_index, start_row in enumerate(range(0, row_len, rows_block)):
        query_block = queries[start_row : start_row + rows_block]
        logits = (
            jnp.einsum("qhd,khd->hqk", query_block, key_vecs, preferred_element_type=jnp.float32)
            * attn_scale
        )
        logits = jnp.where(allowed[None, start_row : start_row + rows_block], logits, -1e30)
        attn_probs = jnp.exp(logits - lse_parts[block_index])
        probs_low = attn_probs.astype(jnp.bfloat16)
        grad_block = attended_grad[start_row : start_row + rows_block]
        value_grad = value_grad + jnp.einsum(
            "hqk,qhd->khd", probs_low, grad_block, preferred_element_type=jnp.float32
        )
        prob_grad = jnp.einsum(
            "qhd,khd->hqk", grad_block, values, preferred_element_type=jnp.float32
        )
        row_delta = jnp.sum(prob_grad * attn_probs, axis=-1, keepdims=True)
        logit_grad = (attn_probs * (prob_grad - row_delta) * attn_scale).astype(jnp.bfloat16)
        query_grad_parts.append(
            jnp.einsum("hqk,khd->qhd", logit_grad, key_vecs, preferred_element_type=jnp.float32)
        )
        key_grad = key_grad + jnp.einsum(
            "hqk,qhd->khd", logit_grad, query_block, preferred_element_type=jnp.float32
        )
    query_grad = jnp.concatenate(query_grad_parts, axis=0)
    pair_grad = rope_pull((query_grad, key_grad))[0]
    qkv_grad = jnp.concatenate(
        [
            pair_grad[0].reshape(row_len, D),
            pair_grad[1].reshape(row_len, D),
            value_grad.reshape(row_len, D),
        ],
        axis=1,
    ).astype(jnp.bfloat16)
    grad_bqkv = jnp.sum(qkv_grad.astype(jnp.float32), axis=0)
    grad_qkv = jnp.einsum("td,te->de", tokens, qkv_grad, preferred_element_type=jnp.float32)
    input_grad = resid_one_grad + jnp.einsum(
        "te,de->td", qkv_grad, full_qkv, preferred_element_type=jnp.float32
    )
    summed = (
        lax.psum_scatter(grad_qkv, ("row", "col"), scatter_dimension=0, tiled=True),
        lax.psum_scatter(grad_bqkv, ("row", "col"), scatter_dimension=0, tiled=True),
        lax.psum_scatter(grad_out, ("row", "col"), scatter_dimension=0, tiled=True),
        lax.psum_scatter(grad_bout, ("row", "col"), scatter_dimension=0, tiled=True),
        lax.psum_scatter(grad_gain1, ("row", "col"), scatter_dimension=0, tiled=True),
        lax.psum_scatter(grad_bias1, ("row", "col"), scatter_dimension=0, tiled=True),
        lax.psum_scatter(grad_up, ("row", "col"), scatter_dimension=0, tiled=True),
        lax.psum_scatter(grad_bup, ("row", "col"), scatter_dimension=0, tiled=True),
        lax.psum_scatter(grad_down, ("row", "col"), scatter_dimension=0, tiled=True),
        lax.psum_scatter(grad_bdown, ("row", "col"), scatter_dimension=0, tiled=True),
        lax.psum_scatter(grad_gain2, ("row", "col"), scatter_dimension=0, tiled=True),
        lax.psum_scatter(grad_bias2, ("row", "col"), scatter_dimension=0, tiled=True),
        lax.psum_scatter(grad_proj, ("row", "col"), scatter_dimension=0, tiled=True),
    )
    return (
        losses,
        result_low,
        input_grad,
        summed[0],
        summed[1],
        summed[2],
        summed[3],
        summed[4],
        summed[5],
        summed[6],
        summed[7],
        summed[8],
        summed[9],
        summed[10],
        summed[11],
        summed[12],
    )


def solution(mesh):
    in_specs = (
        P(("row", "col"), None),
        P(),
        P(),
        P(("row", "col"), None),
        P(("row", "col")),
        P(("row", "col"), None),
        P(("row", "col")),
        P(("row", "col")),
        P(("row", "col")),
        P(("row", "col"), None),
        P(("row", "col")),
        P(("row", "col"), None),
        P(("row", "col")),
        P(("row", "col")),
        P(("row", "col")),
        P(("row", "col"), None),
    )
    out_specs = (
        P(None, "row"),
        P(("row", "col"), None),
        P(("row", "col"), None),
        P(("row", "col"), None),
        P(("row", "col")),
        P(("row", "col"), None),
        P(("row", "col")),
        P(("row", "col")),
        P(("row", "col")),
        P(("row", "col"), None),
        P(("row", "col")),
        P(("row", "col"), None),
        P(("row", "col")),
        P(("row", "col")),
        P(("row", "col")),
        P(("row", "col"), None),
    )
    return jax.shard_map(
        on_device, mesh=mesh, in_specs=in_specs, out_specs=out_specs, check_vma=False
    )
```

profile of v0, /device:TPU:0, one launch (start us, length us, event | category | flops | bytes accessed | tf_op | source)
XLA Modules:
  0.0 1544.7 jit_solution(12872043645270139226)
XLA Ops:
  17.9 42.7 %all-reduce.23 = (bf16[1024]{0:T(1024)(128)(2,1)S(1)}, bf16[3072]{0:T(1024)(128)(2,1)S(1)}, bf16[1024]{0:T(1024)(128)(2,1)S(1)}, bf16[1024]{0:T(1024)(128)(2,1)S...) all-reduce(bf16[1024]{0:T(1024)(128)(2,1)S(1)} %dynamic-update-slic, ...), channel_id=1, replica_groups=mesh['row'=4,'col'=8] {'row','col'}, use_global_device_ids=true, to_apply=%add.8 | all-reduce | flops 9216 | bytes 36864
  62.0 2.6 copy.112
  65.8 39.9 %all-gather.3 = bf16[32,1,128]{2,1,0:T(2,128)(2,1)S(1)} all-gather(bf16[1,1,128]{2,1,0:T(2,128)(2,1)S(1)} %bitcast.159), channel_id=1, replica_groups=mesh['row'=4,'col'=8] {'row','col'}, dimensions={0}, use_global_device_ids=true | all-gather | bytes 8448 | tf_op jit(solution)/shard_map/all_gather | solution.py:141
  108.1 44.9 %all_gather.75 = bf16[1024,288]{1,0:T(8,128)(2,1)} all-gather(bf16[32,288]{1,0:T(8,128)(2,1)S(1)} %copy-done.96), channel_id=1, replica_groups=mesh['row'=4,'col'=8] {'row','col'}, dimensions={0}, use_global_device_ids=true | all-gather | bytes 608256 | tf_op jit(solution)/shard_map/all_gather | solution.py:146
  153.6 9.3 broadcast_add_fusion
  162.8 4.3 fusion.188
  168.8 5.3 copy.114
  174.1 5.4 copy.115
  179.5 4.9 subtract_convert_fusion
  184.5 14.9 fusion.8
  199.4 14.1 fusion.9
  213.4 2.9 copy.113
  216.3 26.2 %fusion.6 = (f32[16,512]{1,0:T(8,128)S(1)}, f32[16,512]{1,0:T(8,128)S(1)}) fusion(f32[16,512,1024]{2,1,0:T(8,128)} %get-tuple-element.363, f32[16,512]{1,0:T(8,128)S(1)} %get-tuple-element.362, pred[512,1024]{1,0:T(8,128)(4,1)S(1)} %get-tuple-element.346, f32[16,512]{1,0:T(8,128)S(1)} %get-tuple-element.360, f32[16,512,1024]{2,1,0:T(8,128)} %get-tuple-element.361, ...), kind=kLoop, calls=%fused_computation.22 | loop fusion | flops 67092480 | bytes 68288512 | tf_op jit(solution)/shard_map/reduce_sum | solution.py:204
  242.6 14.4 fusion.100
  257.0 14.2 fusion.101
  272.0 5.2 fusion.191
  279.9 48.3 %multiply_convert_fusion.2 = (bf16[1024,4096]{1,0:T(8,128)(2,1)}, f32[1024,4096]{1,0:T(8,128)}, f32[1024,4096]{1,0:T(8,128)}) fusion(f32[4096]{0:T(1024)S(1)} %bitcast.155, bf16[1024,4096]{1,0:T(8,128)(2,1)} %all-gather.18.cloned.1.call-done, bf16[1024,1024]{0,1:T(8,128)(2,1)S(1)} %fusion.183.clone.4), kind=kOutput, calls=%fused_computation.40 | convolution fusion | flops 8866758656 | bytes 52445184 | tf_op jit(solution)/shard_map/dot_general | solution.py:217
  328.2 14.9 fusion.192
  351.1 14.1 all_gather.76
  365.2 20.1 %all-gather.22.cloned.1.call-done = bf16[4,992,288]{1,2,0:T(8,128)(2,1)} async-done(((bf16[1,992,288]{1,2,0:T(8,128)(2,1)}), bf16[4,992,288]{1,2,0:T(8,128)(2,1)}) %all-gather.22.cloned.1.call-update) | async-done | bytes 2285584 | tf_op jit(solution)/shard_map/all_gather | solution.py:231
  385.3 4.9 copy.117
  390.2 5.0 reshape.594
  397.9 2.4 fusion.82
  400.3 2.4 fusion.81
  402.7 2.4 add_subtract_fusion.2
  406.2 12.8 all-gather.7
  418.9 12.7 all-gather.6
  431.6 12.7 all-gather.5
  445.8 4.5 fusion.77
  453.9 4.5 fusion.78
  462.0 4.5 fusion.79
  472.7 2.4 pad_maximum_fusion.1
  475.0 6.1 copy.136
  481.9 17.4 %reduce-scatter.22.cloned.1.call-done = f32[32,288]{1,0:T(8,128)} async-done(((f32[256,288]{1,0:T(8,128)}), f32[32,288]{1,0:T(8,128)}) %reduce-scatter.22.cloned.1.call-update) | async-done | bytes 36880
  500.3 69.1 %reduce-scatter.24.cloned.1.call-done = f32[992,288]{1,0:T(8,128)} async-done(((f32[3968,288]{1,0:T(8,128)}), f32[992,288]{1,0:T(8,128)}) %reduce-scatter.24.cloned.1.call-update) | async-done | bytes 1142800
  573.0 2.4 fusion.175
  575.4 3.9 fusion.196
  579.8 5.4 copy.125
  585.2 5.5 multiply_reduce_fusion.2
  594.4 24.5 %convert_reduce_fusion = (f32[4096]{0:T(1024)}, bf16[1024,4096]{1,0:T(8,128)(2,1)}) fusion(f32[1024,4096]{1,0:T(8,128)} %get-tuple-element.332, f32[1024,4096]{1,0:T(8,128)} %get-tuple-element.366, f32[4096]{0:T(1024)S(1)} %bitcast.156, bf16[1024,1024]{0,1:T(8,128)(2,1)S(1)} %get-tuple-element.318, bf16[4096,1024]{1,0:T(8,128)(2,1)} %all-gather.20.cloned.1.call-done), kind=kOutput, calls=%fused_computation.34 | convolution fusion | flops 8661233664 | bytes 52461568 | tf_op jit(solution)/shard_map/td,fd->tf/dot_general | solution.py:339
  618.9 16.5 %multiply_reduce_fusion.3 = (f32[1024]{0:T(1024)}, f32[1024]{0:T(1024)S(1)}, f32[1024]{0:T(1024)}, f32[1024,1024]{0,1:T(8,128)S(1)}) fusion(f32[1024,1024]{0,1:T(8,128)S(1)} %copy-done.5, f32[1024]{0:T(1024)S(1)} %copy-done.76, f32[1024]{0:T(1024)S(1)} %copy-done.70, f32[1024]{0:T(1024)S(1)} %copy-done.73, bf16[1024,4096]{1,0:T(8,128)(2,1)} %get-tuple-element.320, ...), kind=kOutput, calls=%fused_computation.96 | convolution fusion | flops 8600417280 | bytes 29388800 | tf_op jit(solution)/shard_map/tf,df->td/dot_general | solution.py:344
  639.6 2.3 convolution_convert_fusion
  643.9 13.2 fusion.198
  657.1 4.5 fusion.200
  661.6 14.5 fusion.199
  677.7 67.7 %fusion.95 = f32[512,16,64]{0,2,1:T(8,128)} fusion(f32[16,512,1024]{2,1,0:T(8,128)} %fusion.198, f32[16,512,1024]{2,1,0:T(8,128)} %get-tuple-element.363, f32[16,512]{1,0:T(8,128)S(1)} %log_add_fusion.1, pred[512,1024]{1,0:T(8,128)(4,1)} %copy-done.34, bf16[1024,16,32]{0,2,1:T(8,128)(2,1)S(1)} %copy-done.31, bf16[1024,16,32]{0,2,1:T(8,128)(2,1)S(1)} %copy-done.29), kind=kOutput, calls=%fused_computation.141 | convolution fusion | flops 1170220032 | bytes 71860224 | tf_op jit(solution)/shard_map/hqk,khd->qhd/dot_general | solution.py:378
  745.4 68.1 %fusion.92 = f32[512,16,64]{0,2,1:T(8,128)} fusion(f32[16,512,1024]{2,1,0:T(8,128)} %fusion.199, f32[16,512,1024]{2,1,0:T(8,128)} %get-tuple-element.361, f32[16,512]{1,0:T(8,128)S(1)} %log_add_fusion, pred[512,1024]{1,0:T(8,128)(4,1)} %copy-done.22, bf16[1024,16,32]{0,2,1:T(8,128)(2,1)} %copy-done.30, bf16[1024,16,32]{0,2,1:T(8,128)(2,1)} %copy-done.28), kind=kOutput, calls=%fused_computation.140 | convolution fusion | flops 1170220032 | bytes 71860224 | tf_op jit(solution)/shard_map/hqk,khd->qhd/dot_general | solution.py:378
  813.5 60.4 %fusion.16 = f32[16,64,1024]{2,1,0:T(8,128)} fusion(f32[16,512,1024]{2,1,0:T(8,128)} %fusion.198, f32[16,512,1024]{2,1,0:T(8,128)} %get-tuple-element.363, f32[16,512]{1,0:T(8,128)S(1)} %log_add_fusion.1, pred[512,1024]{1,0:T(8,128)(4,1)} %copy-done.34, bf16[1024,16,32]{0,2,1:T(8,128)(2,1)S(1)} %copy-done.27, bf16[1024,16,32]{0,2,1:T(8,128)(2,1)S(1)} %copy-done.25), kind=kOutput, calls=%fused_computation.28 | convolution fusion | flops 1168122880 | bytes 141623296 | tf_op jit(solution)/shard_map/hqk,qhd->khd/dot_general | solution.py:380
  873.9 64.1 %add_bitcast_fusion = f32[1024,16,64]{0,2,1:T(8,128)} fusion(f32[16,64,1024]{2,1,0:T(8,128)} %fusion.16, f32[16,512,1024]{2,1,0:T(8,128)} %fusion.199, f32[16,512,1024]{2,1,0:T(8,128)} %get-tuple-element.361, f32[16,512]{1,0:T(8,128)S(1)} %log_add_fusion, pred[512,1024]{1,0:T(8,128)(4,1)} %copy-done.22, bf16[1024,16,32]{0,2,1:T(8,128)(2,1)S(1)} %copy-done.25, ...), kind=kOutput, calls=%fused_computation.100 | convolution fusion | flops 1169171456 | bytes 78151680 | tf_op jit(solution)/shard_map/hqk,qhd->khd/dot_general | solution.py:380
  938.0 4.8 multiply_add_fusion.4
  945.6 16.3 %fusion.58 = f32[16,64,1024]{2,1,0:T(8,128)} fusion(bf16[512,16,64]{0,2,1:T(8,128)(2,1)S(1)} %bitcast.138, f32[16,512,1024]{2,1,0:T(8,128)} %get-tuple-element.361, f32[16,512]{1,0:T(8,128)S(1)} %log_add_fusion, pred[512,1024]{1,0:T(8,128)(4,1)S(1)} %copy-done.23), kind=kOutput, calls=%fused_computation.61 | convolution fusion | flops 1107296256 | bytes 39354368 | tf_op jit(solution)/shard_map/hqk,qhd->khd/dot_general | solution.py:369
  962.0 17.2 %add_convert_fusion.1 = bf16[16,64,1024]{2,1,0:T(8,128)(2,1)} fusion(f32[16,64,1024]{2,1,0:T(8,128)} %fusion.58, bf16[512,16,64]{0,2,1:T(8,128)(2,1)S(1)} %bitcast.136, f32[16,512,1024]{2,1,0:T(8,128)} %get-tuple-element.363, f32[16,512]{1,0:T(8,128)S(1)} %log_add_fusion.1, pred[512,1024]{1,0:T(8,128)(4,1)} %copy-done.34), kind=kOutput, calls=%fused_computation.98 | convolution fusion | flops 1109393408 | bytes 41451520 | tf_op jit(solution)/shard_map/hqk,qhd->khd/dot_general | solution.py:369
  979.2 13.3 convolution_bitcast_fusion
  992.5 12.6 copy.138
  1006.7 14.7 fusion.201
  1022.1 17.5 %fusion.180 = f32[1024,4096]{1,0:T(8,128)} fusion(bf16[1024,4096]{1,0:T(8,128)(2,1)} %get-tuple-element.320, f32[1024,1024]{0,1:T(8,128)} %copy-done.4, f32[1024]{0:T(1024)S(1)} %copy-done.100, f32[1024]{0:T(1024)S(1)} %copy-done.74, f32[1024]{0:T(1024)S(1)} %copy-done.77, f32[1024]{0:T(1024)S(1)} %copy-done.71), kind=kOutput, calls=%fused_computation.288 | convolution fusion | flops 8595177472 | bytes 29376512 | tf_op jit(solution)/shard_map/td,tf->df/dot_general | solution.py:343
  1041.3 2.5 copy.129
  1044.5 4.7 convert_reduce_fusion.1
  1049.3 43.9 %all-reduce.22 = (f32[3072]{0:T(1024)S(1)}, f32[1024]{0:T(1024)S(1)}, f32[1024]{0:T(1024)S(1)}, f32[1024]{0:T(1024)S(1)}, f32[4096]{0:T(1024)S(1)}, /*index=5*/f...) all-reduce(f32[3072]{0:T(1024)S(1)} %convert_reduce_fusion.1, ...), channel_id=8, replica_groups=mesh['row'=4,'col'=8] {'row','col'}, use_global_device_ids=true, to_apply=%region_40.41.clone | all-reduce | flops 13312 | bytes 106496
  1096.7 12.7 add_add_fusion.4
  1109.3 5.3 copy.130
  1115.8 46.0 %reduce-scatter.26.cloned.1.call-done = f32[32,3072]{1,0:T(8,128)} async-done(((f32[1024,3072]{1,0:T(8,128)}), f32[32,3072]{1,0:T(8,128)}) %reduce-scatter.26.cloned.1.call-update) | async-done | bytes 393232
  1161.8 188.7 %reduce-scatter.18.cloned.1.call-done = f32[128,1024]{1,0:T(8,128)} async-done(((f32[4096,1024]{1,0:T(8,128)}), f32[128,1024]{1,0:T(8,128)}) %reduce-scatter.18.cloned.1.call-update) | async-done | bytes 524304 | tf_op jit(solution)/shard_map/reduce_scatter | solution.py:407
  1350.5 187.1 %reduce-scatter.16.cloned.1.call-done = f32[32,4096]{1,0:T(8,128)} async-done(((f32[1024,4096]{1,0:T(8,128)}), f32[32,4096]{1,0:T(8,128)}) %reduce-scatter.16.cloned.1.call-update) | async-done | bytes 524304 | tf_op jit(solution)/shard_map/reduce_scatter | solution.py:405
  (417 shorter events, 76.4 us)
Async XLA Ops:
  7.2 54.8 %copy-start.35 = (bf16[1024,1024]{1,0:T(8,128)(2,1)S(1)}, bf16[1024,1024]{1,0:T(8,128)(2,1)}, u32[]{:S(2)}) copy-start(bf16[1024,1024]{1,0:T(8,128)(2,1)} %param.18) | copy-start | bytes 6291460
  7.2 58.6 %copy-start.116 = (bf16[128]{0:T(256)(128)(2,1)S(1)}, bf16[128]{0:T(256)(128)(2,1)}, u32[]{:S(2)}) copy-start(bf16[128]{0:T(256)(128)(2,1)} %param.28) | copy-start | bytes 772
  7.2 100.9 %copy-start.96 = (bf16[32,288]{1,0:T(8,128)(2,1)S(1)}, bf16[32,288]{1,0:T(8,128)(2,1)}, u32[]{:S(2)}) copy-start(bf16[32,288]{1,0:T(8,128)(2,1)} %param.33) | copy-start | bytes 55300
  7.2 146.3 %all-gather.14.cloned.1.call-start = ((), (), s32[]{:S(2)}) async-start(), calls=%async_computation.7 | async-start | bytes 6488064 | tf_op jit(solution)/shard_map/all_gather | solution.py:134
  7.9 263.6 %all-gather.16.cloned.1.call-start = ((), (), s32[]{:S(2)}) async-start(), calls=%async_computation.8 | async-start | bytes 2162688 | tf_op jit(solution)/shard_map/all_gather | solution.py:136
  8.7 271.2 %all-gather.18.cloned.1.call-start = ((), (), s32[]{:S(2)}) async-start(), calls=%async_computation.9 | async-start | bytes 8650752 | tf_op jit(solution)/shard_map/all_gather | solution.py:140
  9.4 318.8 %all-gather.20.cloned.1.call-start = ((), (), s32[]{:S(2)}) async-start(), calls=%async_computation.10 | async-start | bytes 8650752 | tf_op jit(solution)/shard_map/all_gather | solution.py:142
  10.0 375.3 %all-gather.22.cloned.1.call-start = ((), (), s32[]{:S(2)}) async-start(), calls=%async_computation.15 | async-start | bytes 2949120 | tf_op jit(solution)/shard_map/all_gather | solution.py:231
  61.3 181.2 %copy-start.34 = (pred[512,1024]{1,0:T(8,128)(4,1)}, pred[512,1024]{1,0:T(8,128)(4,1)S(1)}, u32[]{:S(2)}) copy-start(pred[512,1024]{1,0:T(8,128)(4,1)S(1)} %get-tuple-element.346) | copy-start | bytes 1572868
  61.3 195.7 %copy-start.22 = (pred[512,1024]{1,0:T(8,128)(4,1)}, pred[512,1024]{1,0:T(8,128)(4,1)S(1)}, u32[]{:S(2)}) copy-start(pred[512,1024]{1,0:T(8,128)(4,1)S(1)} %get-tuple-element.347) | copy-start | bytes 1572868
  153.5 26.0 %copy-start.41 = (f32[1024,32]{0,1:T(8,128)}, f32[1024,32]{0,1:T(8,128)S(1)}, u32[]{:S(2)}) copy-start(f32[1024,32]{0,1:T(8,128)S(1)} %get-tuple-element.355) | copy-start | bytes 393220
  153.5 26.0 %copy-start.43 = (f32[1024,32]{0,1:T(8,128)}, f32[1024,32]{0,1:T(8,128)S(1)}, u32[]{:S(2)}) copy-start(f32[1024,32]{0,1:T(8,128)S(1)} %get-tuple-element.356) | copy-start | bytes 393220
  184.4 14.9 copy-start.24
  184.5 14.9 copy-start.26
  184.5 14.9 copy-start.28
  184.5 14.9 copy-start.30
  199.3 43.2 %copy-start.50 = (f32[16,512]{1,0:T(8,128)}, f32[16,512]{1,0:T(8,128)S(1)}, u32[]{:S(2)}) copy-start(f32[16,512]{1,0:T(8,128)S(1)} %get-tuple-element.362) | copy-start | bytes 98308
  213.4 43.6 %copy-start.47 = (f32[16,512]{1,0:T(8,128)}, f32[16,512]{1,0:T(8,128)S(1)}, u32[]{:S(2)}) copy-start(f32[16,512]{1,0:T(8,128)S(1)} %get-tuple-element.360) | copy-start | bytes 98308
  216.3 40.7 %copy-start.2 = (bf16[1024,1024]{0,1:T(8,128)(2,1)}, bf16[1024,1024]{0,1:T(8,128)(2,1)S(1)}, u32[]{:S(2)}) copy-start(bf16[1024,1024]{0,1:T(8,128)(2,1)S(1)} %copy.113) | copy-start | bytes 6291460
  242.5 14.5 copy-start.54
  242.5 14.5 copy-start.52
  271.6 5.6 copy-start.36
  277.2 51.0 %copy-start.69 = (f32[1024]{0:T(1024)}, f32[1024]{0:T(1024)S(1)}, u32[]{:S(2)}) copy-start(f32[1024]{0:T(1024)S(1)} %broadcast_multiply_fusion.1) | copy-start | bytes 12292
  279.2 49.0 %copy-start.75 = (f32[1024]{0:T(1024)}, f32[1024]{0:T(1024)S(1)}, u32[]{:S(2)}) copy-start(f32[1024]{0:T(1024)S(1)} %fusion.142) | copy-start | bytes 12292
  279.9 48.3 %copy-start.112 = (f32[1024]{0:T(1024)S(1)}, f32[1024]{0:T(1024)}, u32[]{:S(2)}) copy-start(f32[1024]{0:T(1024)} %convert_element_type.155) | copy-start | bytes 12292
  349.8 149.6 %reduce-scatter.22.cloned.1.call-start = ((), (), s32[]{:S(2)}) async-start(), calls=%async_computation.16 | async-start | bytes 442368
  350.6 103.3 %copy-start.45 = (s32[3968]{0:T(1024)}, s32[3968]{0:T(1024)S(1)}, u32[]{:S(2)}) copy-start(s32[3968]{0:T(1024)S(1)} %eq.75) | copy-start | bytes 47620
  365.2 86.6 %copy-start.40 = (bf16[256,288]{1,0:T(8,128)(2,1)}, bf16[256,288]{1,0:T(8,128)(2,1)S(1)}, u32[]{:S(2)}) copy-start(bf16[256,288]{1,0:T(8,128)(2,1)S(1)} %all_gather.76) | copy-start | bytes 442372
  395.1 63.2 %copy-start.15 = (bf16[3968,288]{0,1:T(8,128)(2,1)}, bf16[3968,288]{0,1:T(8,128)(2,1)S(1)}, u32[]{:S(2)}) copy-start(bf16[3968,288]{0,1:T(8,128)(2,1)S(1)} %reshape.594) | copy-start | bytes 6856708
  396.0 6.7 copy-start.98
  397.5 7.6 copy-start.9
  462.0 6.3 copy-start.46
  462.0 6.3 copy-start.60
  470.9 98.5 %reduce-scatter.24.cloned.1.call-start = ((), (), s32[]{:S(2)}) async-start(), calls=%async_computation.17 | async-start | bytes 7618560
  481.1 90.1 %copy-start.11 = (f32[1024,288]{0,1:T(8,128)S(1)}, f32[1024,288]{0,1:T(8,128)}, u32[]{:S(2)}) copy-start(f32[1024,288]{0,1:T(8,128)} %copy-done.10) | copy-start | bytes 3538948
  481.2 634.7 %reduce-scatter.20.cloned.1.call-start = ((), (), s32[]{:S(2)}) async-start(), calls=%async_computation.14 | async-start | bytes 1622016 | tf_op jit(solution)/shard_map/reduce_scatter | solution.py:411
  500.3 71.6 %copy-start.89 = (f32[1024]{0:T(1024)S(1)}, f32[1024]{0:T(1024)}, u32[]{:S(2)}) copy-start(f32[1024]{0:T(1024)} %copy-done.88) | copy-start | bytes 12292
  500.3 71.6 %copy-start.87 = (f32[1024]{0:T(1024)S(1)}, f32[1024]{0:T(1024)}, u32[]{:S(2)}) copy-start(f32[1024]{0:T(1024)} %copy-done.86) | copy-start | bytes 12292
  500.3 71.6 %copy-start.85 = (f32[1024]{0:T(1024)S(1)}, f32[1024]{0:T(1024)}, u32[]{:S(2)}) copy-start(f32[1024]{0:T(1024)} %copy-done.84) | copy-start | bytes 12292
  500.3 71.6 %copy-start.83 = (f32[1024]{0:T(1024)S(1)}, f32[1024]{0:T(1024)}, u32[]{:S(2)}) copy-start(f32[1024]{0:T(1024)} %copy-done.82) | copy-start | bytes 12292
  579.3 536.5 %reduce-scatter.14.cloned.1.call-start = ((), (), s32[]{:S(2)}) async-start(), calls=%async_computation.11 | async-start | bytes 4325376 | tf_op jit(solution)/shard_map/reduce_scatter | solution.py:401
  585.2 5.5 copy-start.95
  585.2 5.5 copy-start.1
  585.2 6.1 copy-start.6
  593.7 25.1 %copy-start.38 = (bf16[1024,1024]{0,1:T(8,128)(2,1)}, bf16[1024,1024]{0,1:T(8,128)(2,1)S(1)}, u32[]{:S(2)}) copy-start(bf16[1024,1024]{0,1:T(8,128)(2,1)S(1)} %get-tuple-element.318) | copy-start | bytes 6291460
  594.4 24.5 %copy-start.5 = (f32[1024,1024]{0,1:T(8,128)S(1)}, f32[1024,1024]{0,1:T(8,128)}, u32[]{:S(2)}) copy-start(f32[1024,1024]{0,1:T(8,128)} %copy-done.4) | copy-start | bytes 12582916
  594.4 24.5 %copy-start.70 = (f32[1024]{0:T(1024)S(1)}, f32[1024]{0:T(1024)}, u32[]{:S(2)}) copy-start(f32[1024]{0:T(1024)} %copy-done.69) | copy-start | bytes 12292
  594.4 24.5 %copy-start.73 = (f32[1024]{0:T(1024)S(1)}, f32[1024]{0:T(1024)}, u32[]{:S(2)}) copy-start(f32[1024]{0:T(1024)} %convert_element_type.150) | copy-start | bytes 12292
  594.4 24.5 %copy-start.76 = (f32[1024]{0:T(1024)S(1)}, f32[1024]{0:T(1024)}, u32[]{:S(2)}) copy-start(f32[1024]{0:T(1024)} %copy-done.75) | copy-start | bytes 12292
  618.9 16.5 %copy-start.93 = (f32[1024]{0:T(1024)S(1)}, f32[1024]{0:T(1024)}, u32[]{:S(2)}) copy-start(f32[1024]{0:T(1024)} %copy-done.92) | copy-start | bytes 12292
  636.4 5.5 copy-start.13
  643.9 13.2 copy-start.37
  676.1 485.7 %reduce-scatter.26.cloned.1.call-start = ((), (), s32[]{:S(2)}) async-start(), calls=%async_computation.18 | async-start | bytes 12976128
  745.4 68.1 %copy-start.25 = (bf16[1024,16,32]{0,2,1:T(8,128)(2,1)S(1)}, bf16[1024,16,32]{0,2,1:T(8,128)(2,1)}, u32[]{:S(2)}) copy-start(bf16[1024,16,32]{0,2,1:T(8,128)(2,1)} %copy-done.24) | copy-start | bytes 3145732
  745.4 68.1 %copy-start.27 = (bf16[1024,16,32]{0,2,1:T(8,128)(2,1)S(1)}, bf16[1024,16,32]{0,2,1:T(8,128)(2,1)}, u32[]{:S(2)}) copy-start(bf16[1024,16,32]{0,2,1:T(8,128)(2,1)} %copy-done.26) | copy-start | bytes 3145732
  873.8 64.1 %copy-start.42 = (f32[1024,32]{0,1:T(8,128)S(1)}, f32[1024,32]{0,1:T(8,128)}, u32[]{:S(2)}) copy-start(f32[1024,32]{0,1:T(8,128)} %copy-done.41) | copy-start | bytes 393220
  873.8 64.1 %copy-start.44 = (f32[1024,32]{0,1:T(8,128)S(1)}, f32[1024,32]{0,1:T(8,128)}, u32[]{:S(2)}) copy-start(f32[1024,32]{0,1:T(8,128)} %copy-done.43) | copy-start | bytes 393220
  943.1 36.1 %copy-start.19 = (bf16[1024,16,64]{0,2,1:T(8,128)(2,1)}, bf16[1024,16,64]{0,2,1:T(8,128)(2,1)S(1)}, u32[]{:S(2)}) copy-start(bf16[1024,16,64]{0,2,1:T(8,128)(2,1)S(1)} %add_convert_fusion.3) | copy-start | bytes 6291460
  1005.1 345.4 %reduce-scatter.18.cloned.1.call-start = ((), (), s32[]{:S(2)}) async-start(), calls=%async_computation.13 | async-start | bytes 17301504 | tf_op jit(solution)/shard_map/reduce_scatter | solution.py:407
  1021.4 516.2 %reduce-scatter.16.cloned.1.call-start = ((), (), s32[]{:S(2)}) async-start(), calls=%async_computation.12 | async-start | bytes 17301504 | tf_op jit(solution)/shard_map/reduce_scatter | solution.py:405
  1043.8 5.5 copy-start.111
  1043.8 5.5 copy-start.114
  1043.8 52.8 %copy-start.20 = (bf16[1024,16,64]{0,2,1:T(8,128)(2,1)S(1)}, bf16[1024,16,64]{0,2,1:T(8,128)(2,1)}, u32[]{:S(2)}) copy-start(bf16[1024,16,64]{0,2,1:T(8,128)(2,1)} %copy-done.19) | copy-start | bytes 6291460
  1043.9 52.8 %copy-start.102 = (f32[1024]{0:T(1024)S(1)}, f32[1024]{0:T(1024)}, u32[]{:S(2)}) copy-start(f32[1024]{0:T(1024)} %copy-done.101) | copy-start | bytes 12292
  (67 other events, 154.4 us)
Sparse Core Ops, SparseCore 0:
  11.1 72.3 all-gather.13
  86.5 55.6 all-gather.15
  145.1 76.5 all-gather.17
  224.6 75.9 all-gather.19
  349.9 35.3 all-gather.21
  471.1 28.2 reduce-scatter.21
  502.7 66.6 reduce-scatter.23
  579.5 97.0 reduce-scatter.19
  679.5 141.6 reduce-scatter.13
  1005.2 156.5 reduce-scatter.25
  1164.7 185.7 reduce-scatter.17
  1353.2 184.3 reduce-scatter.15
where the time goes:
time: 1550 us; the launch traced here: 1540 us
  matrix products  602 us (39%)
  waiting for transfers between devices  531 us (34%)
  blocking collectives  224 us (14%)
  local copies, waits for them, and re-layouts  101 us (7%)
  other arithmetic  68.9 us (4%)
  between operations  16.1 us (1%)
    reduce_scatter x1, waiting for transfers between devices, on_device(): lax.psum_scatter(grad_down, ('row', 'col'), scatter_dimension=0, tiled=True)  189 us
    reduce_scatter x1, waiting for transfers between devices, on_device(): lax.psum_scatter(grad_up, ('row', 'col'), scatter_dimension=0, tiled=True)  187 us
    dot_general x2, matrix products, on_device(): jnp.einsum('hqk,khd->qhd', logit_grad, key_vecs, preferred_element_type=j...  136 us
    unnamed x15, waiting for transfers between devices  135 us
    dot_general x2, matrix products, on_device(): jnp.einsum('hqk,qhd->khd', logit_grad, query_block, preferred_element_typ...  124 us
    unnamed x2, blocking collectives  86.5 us
    unnamed x270, local copies, waits for them, and re-layouts  66.6 us
    dot_general x1, matrix products, on_device(): jnp.dot(hidden_low, full_up, preferred_element_type=jnp.float32)  48.3 us
  transfers between devices with their start and end apart: 12, of which 6 were waited for; matrix products, arithmetic and copies ran while one was open for 44% of the time, Pallas kernels for 0%

commit v1 on v0

v1 whole, which is shorter than its diff:
```python
import functools

import jax
import jax.numpy as jnp
from jax import lax
from jax.experimental import pallas as pl
from jax.experimental.pallas import tpu as pltpu
from jax.sharding import PartitionSpec as P

D = 1024
HEADS = 16
HEAD_DIM = 64
PROJ_A = 128
PROJ_B = 96
PROJ_C = 64
QLEN = 32
DPR = 4
QPR = 1
DMOST = 330

AXES = ("row", "col")
highest = lax.Precision.HIGHEST
eps_norm = 1e-05
eps_vec = 1e-06
score_scale = 16.0
f32 = jnp.float32
bf16 = jnp.bfloat16


def sizes():
    n_rows = lax.axis_size("row")
    n_z = lax.axis_size("col") // 2
    return n_rows, n_z, n_rows.bit_length() - 1, n_z.bit_length() - 1


def place():
    col = lax.axis_index("col")
    return lax.axis_index("row"), col // 2, col % 2


def exchange(value, row_masks=(0, 0), z_mask=0, swap_core=False):
    n_rows, n_z, _, _ = sizes()
    pairs = []
    for r in range(n_rows):
        for z in range(n_z):
            for c in range(2):
                here = (r * n_z + z) * 2 + c
                there = ((r ^ row_masks[c]) * n_z + (z ^ z_mask)) * 2 + (
                    1 - c if swap_core else c
                )
                pairs.append((here, there))
    return lax.ppermute(value, AXES, pairs)


def stage_bit(core, stage, row_bits):
    return (stage + core) % row_bits


def stage_masks(stage):
    _, _, row_bits, _ = sizes()
    return tuple(1 << stage_bit(c, stage, row_bits) for c in range(2))


def piece_mask(core, piece):
    _, _, row_bits, _ = sizes()
    return sum(
        1 << stage_bit(core, j, row_bits) for j in range(row_bits) if piece >> j & 1
    )


def ordered(bit, own, other, axis):
    return jnp.stack([jnp.where(bit == 0, own, other), jnp.where(bit == 0, other, own)], axis)


def gather_pieces(shard):
    n_rows, n_z, row_bits, z_bits = sizes()
    _, z, _ = place()
    held = shard
    for count, bit in enumerate(reversed(range(z_bits))):
        other = exchange(held, z_mask=1 << bit)
        held = ordered(z >> bit & 1, held, other, count)
    pieces = [held.reshape((n_z,) + shard.shape)]
    for stage in range(row_bits):
        pieces = pieces + [exchange(p, row_masks=stage_masks(stage)) for p in pieces]
    return pieces, [exchange(p, swap_core=True) for p in pieces]


def piece_table():
    n_rows, _, _, _ = sizes()
    row, _, core = place()
    tables = [
        jnp.array([piece_mask(c, k) for k in range(n_rows)], jnp.int32) for c in range(2)
    ]
    own = row ^ jnp.where(core == 0, tables[0], tables[1])
    sib = row ^ jnp.where(core == 0, tables[1], tables[0])
    return jnp.concatenate([own, sib, core[None]]).astype(jnp.int32)


def assemble_kernel(n_rows, table, *refs):
    pieces, out, sems = refs[: 2 * n_rows], refs[2 * n_rows], refs[2 * n_rows + 1]
    core = table[2 * n_rows]
    copies = []
    for k in range(n_rows):
        for half in range(2):
            index = half * n_rows + k
            side = core if half == 0 else 1 - core
            copies.append(
                pltpu.make_async_copy(
                    pieces[index], out.at[table[index], :, side], sems.at[index]
                )
            )
    for c in copies:
        c.start()
    for c in copies:
        c.wait()


def assemble(table, pieces, sibs):
    n_rows, n_z, _, _ = sizes()
    _, r, n = pieces[0].shape
    out = pl.pallas_call(
        functools.partial(assemble_kernel, n_rows),
        grid_spec=pltpu.PrefetchScalarGridSpec(
            num_scalar_prefetch=1,
            grid=(1,),
            in_specs=[pl.BlockSpec(memory_space=pl.ANY)] * (2 * n_rows),
            out_specs=pl.BlockSpec(memory_space=pltpu.VMEM),
            scratch_shapes=[pltpu.SemaphoreType.DMA((2 * n_rows,))],
        ),
        compiler_params=pltpu.CompilerParams(vmem_limit_bytes=32 << 20),
        out_shape=jax.ShapeDtypeStruct((n_rows, n_z, 2, r, n), pieces[0].dtype),
        cost_estimate=pl.CostEstimate(
            flops=0, bytes_accessed=n_rows * n_z * 8 * r * n, transcendentals=0
        ),
        name="assemble",
    )(table, *pieces, *sibs)
    return out.reshape(n_rows * n_z * 2 * r, n)


def gather_small(shard):
    n_rows, n_z, row_bits, z_bits = sizes()
    row, z, core = place()
    held = shard
    for count, bit in enumerate(reversed(range(z_bits))):
        held = ordered(z >> bit & 1, held, exchange(held, z_mask=1 << bit), count)
    for count, bit in enumerate(reversed(range(row_bits))):
        other = exchange(held, row_masks=(1 << bit, 1 << bit))
        held = ordered(row >> bit & 1, held, other, count)
    held = ordered(core, held, exchange(held, swap_core=True), row_bits + z_bits)
    return held.reshape((n_rows * n_z * 2,) + shard.shape)


def scatter_small(blocks, dtype):
    n_rows, n_z, row_bits, z_bits = sizes()
    row, z, core = place()
    held = blocks.reshape((2,) * (row_bits + z_bits + 1) + blocks.shape[1:])

    def halve(held, axis, bit, **move):
        send = lax.dynamic_index_in_dim(held, 1 - bit, axis, keepdims=False)
        keep = lax.dynamic_index_in_dim(held, bit, axis, keepdims=False)
        return keep.astype(f32) + exchange(send.astype(dtype), **move).astype(f32)

    held = halve(held, row_bits + z_bits, core, swap_core=True)
    for bit in range(row_bits):
        held = halve(held, row_bits - 1 - bit, row >> bit & 1, row_masks=(1 << bit, 1 << bit))
    for bit in range(z_bits):
        held = halve(held, z_bits - 1 - bit, z >> bit & 1, z_mask=1 << bit)
    return held


def scatter_pieces(own, sib):
    n_rows, n_z, row_bits, z_bits = sizes()
    _, z, _ = place()
    terms = [own, exchange(sib, swap_core=True)]

    def total(parts):
        out = parts[0].astype(f32)
        for part in parts[1:]:
            out = out + part.astype(f32)
        return out

    for stage in reversed(range(row_bits)):
        half = 1 << stage
        send = total([t[half : 2 * half] for t in terms]).astype(bf16)
        terms = [t[:half] for t in terms] + [exchange(send, row_masks=stage_masks(stage))]
    terms = [t.reshape((2,) * z_bits + t.shape[2:]) for t in terms]
    for bit in range(z_bits):
        axis = z_bits - 1 - bit
        take = lambda t, b: lax.dynamic_index_in_dim(t, b, axis, keepdims=False)
        mine = z >> bit & 1
        send = total([take(t, 1 - mine) for t in terms]).astype(bf16)
        terms = [take(t, mine) for t in terms] + [exchange(send, z_mask=1 << bit)]
    return total(terms)


def scatter_matrix(table, grad):
    n_rows, n_z, _, _ = sizes()
    _, _, core = place()
    rows, n = grad.shape
    grad = grad.reshape(n_rows, n_z, 2, rows // (n_rows * n_z * 2), n)

    def picked(offset, side):
        return jnp.stack(
            [
                lax.dynamic_slice(
                    grad,
                    (table[offset + k], 0, side, 0, 0),
                    (1, n_z, 1, grad.shape[3], n),
                )[0, :, 0]
                for k in range(n_rows)
            ]
        )

    return scatter_pieces(picked(0, core), picked(n_rows, 1 - core))


WIN = -(-(DMOST + 15) // 32) * 32
NEG = -1e30


def contract(a, b, ca, cb):
    return lax.dot_general(a, b, (((ca,), (cb,)), ((), ())), preferred_element_type=f32)


def spans(len_ref, row_len):
    found = []
    start = jnp.int32(QPR * QLEN)
    for d in range(DPR):
        size = len_ref[d]
        base = pl.multiple_of(jnp.minimum((start // 16) * 16, row_len - WIN), 16)
        found.append((base, start - base, start - base + size))
        start = start + size
    return found


def head_pair(x):
    lane = lax.broadcasted_iota(jnp.int32, x.shape, 1)
    zero = jnp.zeros_like(x)
    return jnp.concatenate(
        [jnp.where(lane < HEAD_DIM, x, zero), jnp.where(lane < HEAD_DIM, zero, x)], axis=0
    )


def pair_heads(x):
    n = x.shape[0] // 2
    lane = lax.broadcasted_iota(jnp.int32, (n, x.shape[1]), 1)
    return jnp.where(lane < HEAD_DIM, x[:n], x[n:])


def inside(n, low, high, axis):
    shape = (n, 1) if axis == 0 else (1, n)
    at = lax.broadcasted_iota(jnp.int32, shape, axis)
    return (at >= low) & (at < high)


def attend(q, k, v, low, high):
    s = contract(head_pair(q), k, 1, 1)
    s = s + jnp.where(inside(k.shape[0], low, high, 1), 0.0, NEG)
    p = jnp.exp(s - jnp.max(s, axis=1, keepdims=True))
    total = jnp.sum(p, axis=1, keepdims=True)
    return pair_heads(contract(p.astype(bf16), v, 1, 0) / total)


def attention_kernel(len_ref, q_ref, k_ref, v_ref, o_ref):
    row_len = q_ref.shape[0]
    for base, low, high in spans(len_ref, row_len):
        w = pl.ds(base, WIN)
        o = attend(q_ref[w, :], k_ref[w, :], v_ref[w, :], low, high)
        keep = inside(WIN, low, high, 0)
        o_ref[w, :] = jnp.where(keep, o, o_ref[w, :].astype(f32)).astype(bf16)
    o_ref[:QLEN, :] = attend(q_ref[:QLEN, :], k_ref[:128, :], v_ref[:128, :], 0, QLEN).astype(bf16)


def attention(lengths, q, k, v):
    t = q.shape[0]
    spec = pl.BlockSpec((t, 128), lambda i, _: (0, i))
    return pl.pallas_call(
        attention_kernel,
        grid_spec=pltpu.PrefetchScalarGridSpec(
            num_scalar_prefetch=1, grid=(HEADS // 2,), in_specs=[spec] * 3, out_specs=spec
        ),
        out_shape=jax.ShapeDtypeStruct(q.shape, bf16),
        compiler_params=pltpu.CompilerParams(vmem_limit_bytes=48 << 20),
        cost_estimate=pl.CostEstimate(
            flops=2 * 10**10, bytes_accessed=8 << 20, transcendentals=10**7
        ),
        name="attention",
    )(lengths, q, k, v)


def attend_back(q, k, v, g, low, high):
    n = q.shape[0]
    g = jnp.where(inside(n, low, high, 0), g, jnp.zeros_like(g))
    qq = head_pair(q)
    gg = head_pair(g)
    st = contract(k, qq, 1, 1)
    st = st + jnp.where(inside(k.shape[0], low, high, 0), 0.0, NEG)
    p = jnp.exp(st - jnp.max(st, axis=0, keepdims=True))
    p = p * (1.0 / jnp.sum(p, axis=0, keepdims=True))
    dp = contract(v, gg, 1, 1)
    delta = jnp.sum(p * dp, axis=0, keepdims=True)
    ds = (p * (dp - delta)).astype(bf16)
    dv = contract(p.astype(bf16), gg, 1, 0)
    dk = contract(ds, qq, 1, 0)
    dq = contract(ds, k, 0, 0) * (HEAD_DIM**-0.5)
    return pair_heads(dq), dk, dv


def attention_back_kernel(len_ref, q_ref, k_ref, v_ref, g_ref, dq_ref, dk_ref, dv_ref):
    row_len = q_ref.shape[0]
    outs = (dq_ref, dk_ref, dv_ref)
    for ref in outs:
        ref[...] = jnp.zeros_like(ref)
    parts = attend_back(
        q_ref[:QLEN, :], k_ref[:128, :], v_ref[:128, :], g_ref[:QLEN, :], 0, QLEN
    )
    dq_ref[:QLEN, :] = parts[0].astype(bf16)
    dk_ref[:128, :] = parts[1].astype(bf16)
    dv_ref[:128, :] = parts[2].astype(bf16)
    for base, low, high in spans(len_ref, row_len):
        w = pl.ds(base, WIN)
        parts = attend_back(q_ref[w, :], k_ref[w, :], v_ref[w, :], g_ref[w, :], low, high)
        for ref, x in zip(outs, parts):
            ref[w, :] = (ref[w, :].astype(f32) + x).astype(bf16)


def attention_back(lengths, q, k, v, g):
    t = q.shape[0]
    spec = pl.BlockSpec((t, 128), lambda i, _: (0, i))
    out = jax.ShapeDtypeStruct(q.shape, bf16)
    return pl.pallas_call(
        attention_back_kernel,
        grid_spec=pltpu.PrefetchScalarGridSpec(
            num_scalar_prefetch=1, grid=(HEADS // 2,), in_specs=[spec] * 4, out_specs=[spec] * 3
        ),
        out_shape=[out] * 3,
        compiler_params=pltpu.CompilerParams(vmem_limit_bytes=48 << 20),
        cost_estimate=pl.CostEstimate(
            flops=5 * 10**10, bytes_accessed=16 << 20, transcendentals=10**7
        ),
        name="attention_back",
    )(lengths, q, k, v, g)


def head_slices():
    return ((0, PROJ_A), (PROJ_A, PROJ_B), (PROJ_A + PROJ_B, PROJ_C))


def layout(lengths, row_len, q_tokens):
    count = lengths.shape[0]
    before = jnp.arange(count)[:, None] <= jnp.arange(count)[None, :]
    ends = jnp.sum(jnp.where(before, lengths[:, None], 0), axis=0)
    offset = jnp.arange(row_len, dtype=jnp.int32) - q_tokens
    doc = jnp.sum((offset[:, None] >= ends[None, :]).astype(jnp.int32), axis=1)
    chosen = (doc[:, None] == jnp.arange(count, dtype=jnp.int32)[None, :]).astype(
        jnp.int32
    )
    begin = jnp.sum(chosen * (ends - lengths)[None, :], axis=1)
    is_query = offset < 0
    position = jnp.where(is_query, (offset + q_tokens) % QLEN, offset - begin)
    return position, doc


def turn(values, cosine, sine):
    x = values.reshape(values.shape[0], -1, HEAD_DIM)
    half = HEAD_DIM // 2
    a, b = x[..., :half], x[..., half:]
    c, s = cosine[:, None, :], sine[:, None, :]
    return jnp.concatenate([a * c - b * s, b * c + a * s], axis=-1).reshape(values.shape)


def layer_norm(resid_in, gain_vec, shift_vec):
    mean_val = jnp.mean(resid_in, axis=-1, keepdims=True)
    centered = resid_in - mean_val
    variance = jnp.mean(centered * centered, axis=-1, keepdims=True)
    return centered * lax.rsqrt(variance + eps_norm) * gain_vec + shift_vec


def normalize_heads(raw_vecs):
    pieces = []
    for head_start, head_width in head_slices():
        part = raw_vecs[:, head_start : head_start + head_width]
        pieces.append(part * lax.rsqrt(jnp.sum(part * part, axis=1, keepdims=True) + eps_vec))
    return jnp.concatenate(pieces, axis=1)


def matmul(a, b):
    return jnp.dot(a, b, preferred_element_type=f32)


def matmul_tn(a, b):
    return jnp.einsum("td,te->de", a, b, preferred_element_type=f32)


def matmul_nt(a, b):
    return jnp.einsum("te,de->td", a, b, preferred_element_type=f32)


def combine_stats(one, two):
    top = jnp.maximum(one[0], two[0])
    den = one[1] * jnp.exp(one[0] - top) + two[1] * jnp.exp(two[0] - top)
    return jnp.stack([top, den, one[2] + two[2]])


def reduce_stats(stats):
    _, _, row_bits, z_bits = sizes()
    stats = combine_stats(stats, exchange(stats, swap_core=True))
    for bit in range(row_bits):
        stats = combine_stats(stats, exchange(stats, row_masks=(1 << bit, 1 << bit)))
    for bit in range(z_bits):
        stats = combine_stats(stats, exchange(stats, z_mask=1 << bit))
    return stats


def on_device(
    tokens,
    lengths,
    positives,
    w_qkv,
    b_qkv,
    w_out,
    b_out,
    norm1_gain,
    norm1_bias,
    w_up,
    b_up,
    w_down,
    b_down,
    norm2_gain,
    norm2_bias,
    w_proj,
):
    n_rows, n_z, _, _ = sizes()
    n_devices = n_rows * n_z * 2
    row, z, core = place()
    device = (row * n_z + z) * 2 + core
    table = piece_table()
    row_len = tokens.shape[0]
    q_tokens = QPR * QLEN

    vectors = (b_qkv, b_out, norm1_gain, norm1_bias, b_up, b_down, norm2_gain, norm2_bias)
    widths = [v.shape[0] for v in vectors]
    packed = jnp.concatenate(vectors)
    pad = -packed.shape[0] % 128
    packed = jnp.pad(packed, (0, pad)).reshape(-1, 128)
    packed = gather_small(packed).reshape(n_devices, -1)
    whole = []
    at = 0
    for width in widths:
        whole.append(packed[:, at : at + width].reshape(-1).astype(f32))
        at += width
    full_bqkv, full_bout, gain_one, bias_one, full_bup, full_bdown, gain_two, bias_two = whole
    full_qkv = assemble(table, *gather_pieces(w_qkv))
    full_out = assemble(table, *gather_pieces(w_out))
    full_up = assemble(table, *gather_pieces(w_up))
    full_down = assemble(table, *gather_pieces(w_down))
    full_proj = gather_small(w_proj).reshape(-1, w_proj.shape[1])

    own_lengths = lax.dynamic_index_in_dim(lengths, device, 0, keepdims=False)
    position, doc_index = layout(own_lengths, row_len, q_tokens)
    frequency = 10000.0 ** (-jnp.arange(HEAD_DIM // 2, dtype=f32) / (HEAD_DIM // 2))
    angles = position.astype(f32)[:, None] * frequency[None, :]
    cosine, sine = jnp.cos(angles), jnp.sin(angles)
    qkv = matmul(tokens, full_qkv) + full_bqkv
    attn_scale = HEAD_DIM**-0.5
    queries = (turn(qkv[:, :D], cosine, sine) * attn_scale).astype(bf16)
    keys = turn(qkv[:, D : 2 * D], cosine, sine).astype(bf16)
    values = qkv[:, 2 * D :].astype(bf16)
    attended = attention(own_lengths, queries, keys, values)
    resid_one = tokens.astype(f32) + matmul(attended, full_out) + full_bout
    hidden_one, first_pull = jax.vjp(layer_norm, resid_one, gain_one, bias_one)

    hidden_low = hidden_one.astype(bf16)
    inner_pre = matmul(hidden_low, full_up) + full_bup
    gelu_out = jax.nn.gelu(inner_pre, approximate=False).astype(bf16)
    resid_two = hidden_one + matmul(gelu_out, full_down) + full_bdown
    result, second_pull = jax.vjp(layer_norm, resid_two, gain_two, bias_two)
    result_low = result.astype(bf16)

    normed, norm_pull = jax.vjp(normalize_heads, matmul(result_low, full_proj))
    vecs = normed.astype(bf16)
    query_all = gather_small(vecs[:q_tokens]).reshape(n_devices * q_tokens, -1)
    docs = vecs[q_tokens:]
    n_queries = n_devices * QPR
    doc_hot = (
        doc_index[q_tokens:][:, None] == jnp.arange(DPR, dtype=jnp.int32)[None, :]
    ).astype(f32)
    log_count = jnp.log(own_lengths.astype(f32))
    exps, sums, scores = [], [], []
    for start, width in head_slices():
        t = matmul_nt(query_all[:, start : start + width], docs[:, start : start + width])
        e = jnp.exp(t * score_scale)
        total = jnp.dot(e, doc_hot, precision=highest)
        smooth = jnp.log(total) - log_count
        exps.append(e)
        sums.append(total)
        scores.append(jnp.sum(smooth.reshape(n_queries, QLEN, DPR), axis=1))
    doc_scores = jnp.stack(scores)
    doc_ids = device * DPR + jnp.arange(DPR, dtype=jnp.int32)
    positive_hot = (positives[:, None] == doc_ids[None, :]).astype(f32)
    local_top = jnp.max(doc_scores, axis=2)
    local_den = jnp.sum(jnp.exp(doc_scores - local_top[..., None]), axis=2)
    local_pos = jnp.sum(doc_scores * positive_hot, axis=2)
    top, den, pos = reduce_stats(jnp.stack([local_top, local_den, local_pos]))
    query_count = n_z * 2 * QPR
    losses = lax.dynamic_slice_in_dim(
        top + jnp.log(den) - pos, row * query_count, query_count, 1
    )
    score_grad = jnp.exp(doc_scores - top[..., None]) / den[..., None] - positive_hot
    query_parts, doc_parts = [], []
    for head, (start, width) in enumerate(head_slices()):
        coef = score_scale * jnp.repeat(score_grad[head], QLEN, axis=0) / sums[head]
        spread = jnp.dot(coef, doc_hot.T, precision=highest)
        back = (exps[head] * spread).astype(bf16)
        query_parts.append(matmul(back, docs[:, start : start + width]))
        doc_parts.append(matmul_tn(back, query_all[:, start : start + width]))
    query_grads = jnp.concatenate(query_parts, axis=1)
    query_grad = scatter_small(query_grads.reshape(n_devices, q_tokens, -1), bf16)
    vector_grad = jnp.concatenate([query_grad, jnp.concatenate(doc_parts, axis=1)], axis=0)
    raw_grad = norm_pull(vector_grad)[0].astype(bf16)

    grad_proj = matmul_tn(result_low, raw_grad)
    result_grad = matmul_nt(raw_grad, full_proj)
    resid_two_grad, grad_gain2, grad_bias2 = second_pull(result_grad)
    branch_grad = resid_two_grad.astype(bf16)
    grad_bdown = jnp.sum(branch_grad.astype(f32), axis=0)
    sum_down = scatter_matrix(table, matmul_tn(gelu_out, branch_grad).astype(bf16))
    act_grad = matmul_nt(branch_grad, full_down)
    _, gelu_pull = jax.vjp(functools.partial(jax.nn.gelu, approximate=False), inner_pre)
    inner_grad = gelu_pull(act_grad)[0].astype(bf16)
    grad_bup = jnp.sum(inner_grad.astype(f32), axis=0)
    sum_up = scatter_matrix(table, matmul_tn(hidden_low, inner_grad).astype(bf16))
    hidden_grad = resid_two_grad + matmul_nt(inner_grad, full_up)
    resid_one_grad, grad_gain1, grad_bias1 = first_pull(hidden_grad)
    out_grad = resid_one_grad.astype(bf16)
    grad_bout = jnp.sum(out_grad.astype(f32), axis=0)
    sum_out = scatter_matrix(table, matmul_tn(attended, out_grad).astype(bf16))
    attended_grad = matmul_nt(out_grad, full_out).astype(bf16)
    dq, dk, dv = attention_back(own_lengths, queries, keys, values, attended_grad)
    qkv_grad = jnp.concatenate(
        [
            turn(dq.astype(f32), cosine, -sine).astype(bf16),
            turn(dk.astype(f32), cosine, -sine).astype(bf16),
            dv,
        ],
        axis=1,
    )
    grad_bqkv = jnp.sum(qkv_grad.astype(f32), axis=0)
    sum_qkv = scatter_matrix(table, matmul_tn(tokens, qkv_grad).astype(bf16))
    input_grad = resid_one_grad + matmul_nt(qkv_grad, full_qkv)
    sum_proj = scatter_small(grad_proj.reshape(n_devices, -1, grad_proj.shape[1]), bf16)
    small = [
        g.reshape(n_devices, -1)
        for g in (
            grad_bqkv,
            grad_bout,
            grad_gain1,
            grad_bias1,
            grad_bup,
            grad_bdown,
            grad_gain2,
            grad_bias2,
        )
    ]
    small = jnp.pad(jnp.concatenate(small, axis=1), ((0, 0), (0, pad)))
    small = scatter_small(small.reshape(n_devices, -1, 128), f32).reshape(-1)
    sums_small = []
    at = 0
    for width in widths:
        sums_small.append(small[at : at + width])
        at += width
    s_bqkv, s_bout, s_gain1, s_bias1, s_bup, s_bdown, s_gain2, s_bias2 = sums_small
    return (
        losses,
        result_low,
        input_grad,
        sum_qkv,
        s_bqkv,
        sum_out,
        s_bout,
        s_gain1,
        s_bias1,
        sum_up,
        s_bup,
        sum_down,
        s_bdown,
        s_gain2,
        s_bias2,
        sum_proj,
    )


def solution(mesh):
    shard = P(AXES, None)
    vec = P(AXES)
    in_specs = (
        shard,
        P(),
        P(),
        shard,
        vec,
        shard,
        vec,
        vec,
        vec,
        shard,
        vec,
        shard,
        vec,
        vec,
        vec,
        shard,
    )
    out_specs = (P(None, "row"), shard) + (shard,) + in_specs[3:]
    return jax.shard_map(
        on_device, mesh=mesh, in_specs=in_specs, out_specs=out_specs, check_vma=False
    )
```

time: 1550 us -> 845 us (0.55)
  matrix products: 602 us -> 207 us
  waiting for transfers between devices: 531 us -> 222 us
  blocking collectives: 224 us -> 0 us
  starting transfers between devices: 0.89 us -> 87 us
  Pallas kernels: 0 us -> 70 us
  local copies, waits for them, and re-layouts: 101 us -> 145 us
    dot_general x42 -> x30, matrix products: 602 us -> 207 us  [the longest x8 75.1 us: matmul(): return jnp.dot(a, b, preferred_element_type=f32)]
    reduce_scatter x4 -> x0, waiting for transfers between devices: 376 us -> none  [the longest x1 189 us: on_device(): lax.psum_scatter(grad_down, ('row', 'col'), scatter_dimension=0, tiled=True)]
    ppermute x0 -> x91, waiting for transfers between devices: none -> 222 us  [exchange(): return lax.ppermute(value, AXES, pairs)]
    all_gather x6 -> x0, blocking collectives: 137 us -> none  [the longest x1 44.9 us: on_device(): lax.all_gather(shards[12], ('row', 'col'), axis=0, tiled=True)]
    unnamed x15 -> x0, waiting for transfers between devices: 135 us -> none
    ppermute x0 -> x91, starting transfers between devices: none -> 87 us  [exchange(): return lax.ppermute(value, AXES, pairs)]
    unnamed x2 -> x0, blocking collectives: 86.5 us -> none
    pallas_call x0 -> x6, Pallas kernels: none -> 70 us  [the longest x1 41 us: attention_back(): pl.pallas_call(attention_back_kernel, grid_spec=pltpu.PrefetchScalarGridS...]
  transfers between devices with their start and end apart: 12 -> 91, of which waited for: 6 -> 40; matrix products, arithmetic and copies ran while one was open for 44% -> 25% of each run, Pallas kernels for 0% -> 3%
where the time goes in v1:
time: 845 us; the launch traced here: 833 us
  waiting for transfers between devices  222 us (26%)
  matrix products  207 us (24%)
  local copies, waits for them, and re-layouts  145 us (17%)
  starting transfers between devices  87 us (10%)
  other arithmetic  82.6 us (10%)
  Pallas kernels  70 us (8%)
  between operations  18.9 us (2%)
    ppermute x91, waiting for transfers between devices, exchange(): return lax.ppermute(value, AXES, pairs)  222 us
    ppermute x91, starting transfers between devices, exchange(): return lax.ppermute(value, AXES, pairs)  87 us
    dot_general x8, matrix products, matmul(): return jnp.dot(a, b, preferred_element_type=f32)  75.1 us
    dot_general x8, matrix products, matmul_nt(): return jnp.einsum('te,de->td', a, b, preferred_element_type=f32)  59.8 us
    dot_general x8, matrix products, matmul_tn(): return jnp.einsum('td,te->de', a, b, preferred_element_type=f32)  53.4 us
    pallas_call x1, Pallas kernels, attention_back(): pl.pallas_call(attention_back_kernel, grid_spec=pltpu.PrefetchScalarGridS...  41 us
    unnamed x214, local copies, waits for them, and re-layouts  38.7 us
    pallas_call x1, Pallas kernels, attention(): pl.pallas_call(attention_kernel, grid_spec=pltpu.PrefetchScalarGridSpec(n...  19.7 us
  transfers between devices with their start and end apart: 91, of which 40 were waited for; matrix products, arithmetic and copies ran while one was open for 25% of the time, Pallas kernels for 3%

profile of v1, /device:TPU:0, one launch (start us, length us, event | category | flops | bytes accessed | tf_op | source)
XLA Modules:
  0.0 832.8 jit_solution(12005216397302285078)
XLA Ops:
  1.6 4.1 collective-permute-start.41
  5.8 5.4 concatenate.49
  11.2 2.9 collective-permute-start.9
  14.2 2.8 collective-permute-start.23
  17.5 8.1 collective-permute-done.9
  35.0 4.0 copy.141
  62.1 5.4 collective-permute-done.1
  68.3 10.1 %collective-permute-done.24 = bf16[2,32,4096]{2,1,0:T(8,128)(2,1)S(1)} collective-permute-done((bf16[2,32,4096]{2,1,0:T(8,128)(2,1)S(1)}, bf16[2,32,4096]{2,1,0:T(8,128)(2,1)S(1)}, u32[]{:S(2)}, u32[]{:S(2)}) %collective-permute-start.24) | collective-permute-done | bytes 524320 | tf_op jit(solution)/shard_map/ppermute | solution.py:52
  82.6 14.4 %collective-permute-done.2.refs_1_ = bf16[4,32,3072]{2,1,0:T(8,128)(2,1)} collective-permute-done((bf16[4,32,3072]{2,1,0:T(8,128)(2,1)S(1)}, bf16[4,32,3072]{2,1,0:T(8,128)(2,1)}, u32[]{:S(2)}, u32[]{:S(2)}) %collective-permute-start.2) | collective-permute-done | bytes 786464 | tf_op jit(solution)/shard_map/ppermute | solution.py:52
  111.2 5.9 collective-permute-done.4.refs_3_
  135.4 6.7 add_bitcast_fusion
  142.1 4.3 fusion.139
  148.1 5.4 copy.148
  153.4 5.8 copy.149
  159.2 7.1 subtract_convert_fusion.2
  168.0 4.0 copy.151.k_ref
  172.0 4.2 fusion.6
  176.2 3.9 copy.150.q_ref
  181.8 19.7 %attention.1 = bf16[1024,1024]{1,0:T(8,128)(2,1)S(1)} custom-call(s32[4]{0:T(128)S(1)} %bitcast.614, bf16[1024,1024]{1,0:T(8,128)(2,1)S(1)} %copy-done.9, bf16[1024,1024]{1,0:T(8,128)(2,1)} %copy.151.k_ref, bf16[1024,1024]{1,0:T(8,128)(2,1)} %slice.618.v_ref), custom_call_target="tpu_custom_call" | custom-call | flops 20000000000 | bytes 8388608 | tf_op jit(solution)/shard_map/attention/pallas_call | solution.py:277
  201.5 2.8 fusion.143
  208.9 11.0 %collective-permute-done.36.refs_3_ = bf16[4,128,1024]{2,1,0:T(8,128)(2,1)S(1)} collective-permute-done((bf16[4,128,1024]{2,1,0:T(8,128)(2,1)}, bf16[4,128,1024]{2,1,0:T(8,128)(2,1)S(1)}, u32[]{:S(2)}, u32[]{:S(2)}) %collective-permute-start.36) | collective-permute-done | bytes 1048608 | tf_op jit(solution)/shard_map/ppermute | solution.py:52
  220.0 2.9 assemble.6
  222.9 46.5 %multiply_convert_fusion = (bf16[1024,4096]{1,0:T(8,128)(2,1)}, f32[1024,4096]{1,0:T(8,128)}, f32[1024,4096]{1,0:T(8,128)}) fusion(f32[4096]{0:T(1024)S(1)} %copy-done.91, bf16[1024,4096]{1,0:T(8,128)(2,1)S(1)} %bitcast.585, bf16[1024,1024]{0,1:T(8,128)(2,1)S(1)} %fusion.133.clone.4), kind=kOutput, calls=%fused_computation.4 | convolution fusion | flops 8866758656 | bytes 52445184 | tf_op jit(solution)/shard_map/dot_general | solution.py:388
  271.8 3.3 copy-done.3
  275.1 15.1 %fusion.144 = (f32[1024]{0:T(1024)S(1)}, f32[1024,1024]{0,1:T(8,128)S(1)}) fusion(f32[1024]{0:T(1024)S(1)} %copy-done.93, bf16[1024,4096]{1,0:T(8,128)(2,1)} %get-tuple-element.116, bf16[4096,1024]{1,0:T(8,128)(2,1)} %bitcast.589, f32[1024]{0:T(1024)S(1)} %reshape.924, f32[1024]{0:T(1024)S(1)} %reshape.923, f32[1024]{0:T(1024)S(1)} %fusion.90, ...), kind=kOutput, calls=%fused_computation.460 | convolution fusion | flops 8597273600 | bytes 25190400 | tf_op jit(solution)/shard_map/dot_general | solution.py:388
  295.5 3.9 collective-permute-done.46
  306.0 3.0 collective-permute-done.48
  310.7 4.1 collective-permute-done.49
  343.1 4.7 multiply_convert_fusion.3
  350.6 4.2 multiply_convert_fusion.2
  357.6 4.3 multiply_convert_fusion.1
  363.5 2.9 copy.174
  384.6 4.1 copy.189
  391.8 3.1 fusion.52
  405.1 5.8 collective-permute-done.58
  423.2 3.9 fusion.145
  427.1 5.4 copy.178
  432.5 5.4 multiply_reduce_fusion
  442.9 11.3 %convolution_convert_fusion = bf16[4096,1024]{1,0:T(8,128)(2,1)} fusion(bf16[1024,4096]{1,0:T(8,128)(2,1)S(1)} %bitcast.712, bf16[1024,1024]{0,1:T(8,128)(2,1)S(1)} %get-tuple-element.94), kind=kOutput, calls=%fused_computation.20 | convolution fusion | flops 8594128896 | bytes 18874368 | tf_op jit(solution)/shard_map/td,te->de/dot_general | solution.py:392
  454.2 24.5 %convert_reduce_fusion = (f32[4096]{0:T(1024)}, bf16[1024,4096]{1,0:T(8,128)(2,1)}) fusion(f32[1024,4096]{1,0:T(8,128)} %get-tuple-element.117, f32[1024,4096]{1,0:T(8,128)} %get-tuple-element.245, f32[4096]{0:T(1024)S(1)} %copy-done.91, bf16[1024,1024]{0,1:T(8,128)(2,1)S(1)} %get-tuple-element.94, bf16[4096,1024]{1,0:T(8,128)(2,1)} %bitcast.590), kind=kOutput, calls=%fused_computation.2 | convolution fusion | flops 8661233664 | bytes 52461568 | tf_op jit(solution)/shard_map/te,de->td/dot_general | solution.py:396
  478.7 15.6 %convolution_convert_fusion.1 = bf16[1024,4096]{1,0:T(8,128)(2,1)} fusion(bf16[1024,4096]{1,0:T(8,128)(2,1)} %get-tuple-element.96, f32[1024,1024]{0,1:T(8,128)} %copy-done.24, f32[1024]{0:T(1024)S(1)} %reshape.924, f32[1024]{0:T(1024)S(1)} %reshape.923, f32[1024]{0:T(1024)S(1)} %fusion.90, f32[1024]{0:T(1024)S(1)} %broadcast_multiply_fusion.1), kind=kOutput, calls=%fused_computation.21 | convolution fusion | flops 8599371776 | bytes 20987904 | tf_op jit(solution)/shard_map/td,te->de/dot_general | solution.py:392
  494.4 14.8 %multiply_reduce_fusion.1 = (f32[1024]{0:T(1024)}, f32[1024]{0:T(1024)S(1)}, f32[1024]{0:T(1024)}, f32[1024,1024]{0,1:T(8,128)}) fusion(f32[1024,1024]{0,1:T(8,128)S(1)} %copy-done.25, f32[1024]{0:T(1024)S(1)} %fusion.90, f32[1024]{0:T(1024)S(1)} %broadcast_multiply_fusion.1, f32[1024]{0:T(1024)S(1)} %reshape.923, ...), kind=kOutput, calls=%fused_computation.35 | convolution fusion | flops 8600417280 | bytes 29388800 | tf_op jit(solution)/shard_map/te,de->td/dot_general | solution.py:396
  509.2 3.3 fusion.134
  515.6 3.7 convolution_convert_fusion.3
  519.3 3.7 convolution_convert_fusion.4.g_ref
  523.1 41.0 %attention_back.1 = (bf16[1024,1024]{1,0:T(8,128)(2,1)S(1)}, bf16[1024,1024]{1,0:T(8,128)(2,1)S(1)}, bf16[1024,1024]{1,0:T(8,128)(2,1)}) custom-call(s32[4]{0:T(128)S(1)} %bitcast.615, bf16[1024,1024]{1,0:T(8,128)(2,1)} %copy.150.q_ref, bf16[1024,1024]{1,0:T(8,128)(2,1)} %copy.151.k_ref, bf16[1024,1024]{1,0:T(8,128)(2,1)} %slice.618.v_ref, ...), custom_call_target="tpu_custom_call" | custom-call | flops 49999998976 | bytes 16777216 | tf_op jit(solution)/shard_map/attention_back/pallas_call | solution.py:331
  565.3 4.1 copy.182
  569.5 3.1 copy.183
  572.6 4.9 subtract_convert_fusion.1
  580.1 4.1 copy.184
  584.2 4.0 copy.185
  588.1 13.0 %convolution_convert_fusion.2 = bf16[3072,1024]{0,1:T(8,128)(2,1)} fusion(bf16[1024,1024]{1,0:T(8,128)(2,1)} %param.18, bf16[1024,1024]{1,0:T(8,128)(2,1)} %get-tuple-element.21, bf16[1024,1024]{1,0:T(8,128)(2,1)} %copy.185, bf16[1024,1024]{1,0:T(8,128)(2,1)} %copy.184), kind=kOutput, calls=%fused_computation.25 | convolution fusion | flops 6464471040 | bytes 14680064 | tf_op jit(solution)/shard_map/td,te->de/dot_general | solution.py:392
  601.1 10.4 %add_add_fusion.4 = f32[1024,1024]{0,1:T(8,128)} fusion(f32[1024,1024]{0,1:T(8,128)S(1)} %copy-done.33, f32[1024]{0:T(1024)S(1)} %negate_multiply_fusion.1, bf16[1024,3072]{1,0:T(8,128)(2,1)S(1)} %bitcast.594, bf16[1024,1024]{1,0:T(8,128)(2,1)} %get-tuple-element.21, bf16[1024,1024]{1,0:T(8,128)(2,1)} %copy.185, bf16[1024,1024]{1,0:T(8,128)(2,1)} %copy.184), kind=kOutput, calls=%fused_computation.51 | convolution fusion | flops 6463422464 | bytes 20975616 | tf_op jit(solution)/shard_map/te,de->td/dot_general | solution.py:396
  611.5 5.7 constant_dynamic-slice_fusion.1
  619.6 5.5 constant_dynamic-slice_fusion
  661.4 5.7 copy.190
  667.2 3.2 collective-permute-start.70
  672.3 6.5 collective-permute-done.87
  692.7 59.6 %collective-permute-done.72 = bf16[2,4,32,1024]{3,2,1,0:T(8,128)(2,1)S(1)} collective-permute-done((bf16[2,4,32,1024]{3,2,1,0:T(8,128)(2,1)S(1)}, bf16[2,4,32,1024]{3,2,1,0:T(8,128)(2,1)S(1)}, u32[]{:S(2)}, u32[]{:S(2)}) %collective-permute-start.72) | collective-permute-done | bytes 524320 | tf_op jit(solution)/shard_map/ppermute | solution.py:52
  777.3 2.8 collective-permute-done.83
  780.6 10.8 %collective-permute-done.78 = bf16[1,4,32,4096]{3,2,1,0:T(8,128)(2,1)S(1)} collective-permute-done((bf16[1,4,32,4096]{3,2,1,0:T(8,128)(2,1)S(1)}, bf16[1,4,32,4096]{3,2,1,0:T(8,128)(2,1)S(1)}, u32[]{:S(2)}, u32[]{:S(2)}) %collective-permute-start.78) | collective-permute-done | bytes 1048608 | tf_op jit(solution)/shard_map/ppermute | solution.py:52
  794.9 11.9 %collective-permute-done.84 = bf16[2,128,1024]{2,1,0:T(8,128)(2,1)S(1)} collective-permute-done((bf16[2,128,1024]{2,1,0:T(8,128)(2,1)S(1)}, bf16[2,128,1024]{2,1,0:T(8,128)(2,1)S(1)}, u32[]{:S(2)}, u32[]{:S(2)}) %collective-permute-start.84) | collective-permute-done | bytes 524320 | tf_op jit(solution)/shard_map/ppermute | solution.py:52
  807.1 7.0 collective-permute-done.79
  815.3 13.0 %collective-permute-done.85 = bf16[128,1024]{1,0:T(8,128)(2,1)S(1)} collective-permute-done((bf16[128,1024]{1,0:T(8,128)(2,1)S(1)}, bf16[128,1024]{1,0:T(8,128)(2,1)S(1)}, u32[]{:S(2)}, u32[]{:S(2)}) %collective-permute-start.85) | collective-permute-done | bytes 262176 | tf_op jit(solution)/shard_map/ppermute | solution.py:52
  (618 shorter events, 259.9 us)
Async XLA Ops:
  1.6 38.7 %collective-permute-start.41 = (bf16[32,288]{0,1:T(8,128)(2,1)S(1)}, bf16[32,288]{0,1:T(8,128)(2,1)S(1)}, u32[]{:S(2)}, u32[]{:S(2)}) collective-permute-start(bf16[32,288]{0,1:T(8,128)(2,1)S(1)} %copy.156), channel_id=1, source_target_pairs={{0,4},{1,5},{2,6},{3,7},{4,0},{5,1},{6,2},{7,3},{8,12},{9,13},{10,... | collective-permute-start | bytes 55304 | tf_op jit(solution)/shard_map/ppermute | solution.py:52
  5.7 48.0 %collective-permute-start = (bf16[32,3072]{1,0:T(8,128)(2,1)}, bf16[32,3072]{1,0:T(8,128)(2,1)S(1)}, u32[]{:S(2)}, u32[]{:S(2)}) collective-permute-start(bf16[32,3072]{1,0:T(8,128)(2,1)} %param.21), channel_id=1, source_target_pairs={{0,4},{1,5},{2,6},{3,7},{4,0},{5,1},{6,2},{7,3},{8,12},{9,13},{10,... | collective-permute-start | bytes 589832 | tf_op jit(solution)/shard_map/ppermute | solution.py:52
  11.2 14.4 %collective-permute-start.9 = (bf16[4,128]{1,0:T(4,128)(2,1)S(1)}, bf16[4,128]{1,0:T(4,128)(2,1)S(1)}, u32[]{:S(2)}, u32[]{:S(2)}) collective-permute-start(bf16[4,128]{1,0:T(4,128)(2,1)S(1)} %pad_bitcast_fusion), channel_id=1, source_target_pairs={{0,4},{1,5},{2,6},{3,7},{4,0},{5,1},{6,2},{7,3},{8,12},{9,13},{10,... | collective-permute-start | bytes 3080 | tf_op jit(solution)/shard_map/ppermute | solution.py:52
  14.1 33.6 %collective-permute-start.14 = (bf16[32,1024]{1,0:T(8,128)(2,1)}, bf16[32,1024]{1,0:T(8,128)(2,1)S(1)}, u32[]{:S(2)}, u32[]{:S(2)}) collective-permute-start(bf16[32,1024]{1,0:T(8,128)(2,1)} %param.23), channel_id=1, source_target_pairs={{0,4},{1,5},{2,6},{3,7},{4,0},{5,1},{6,2},{7,3},{8,12},{9,13},{10,... | collective-permute-start | bytes 196616 | tf_op jit(solution)/shard_map/ppermute | solution.py:52
  14.2 41.2 %collective-permute-start.23 = (bf16[32,4096]{1,0:T(8,128)(2,1)}, bf16[32,4096]{1,0:T(8,128)(2,1)S(1)}, u32[]{:S(2)}, u32[]{:S(2)}) collective-permute-start(bf16[32,4096]{1,0:T(8,128)(2,1)} %param.27), channel_id=1, source_target_pairs={{0,4},{1,5},{2,6},{3,7},{4,0},{5,1},{6,2},{7,3},{8,12},{9,13},{10,... | collective-permute-start | bytes 786440 | tf_op jit(solution)/shard_map/ppermute | solution.py:52
  39.0 16.6 %collective-permute-start.32 = (bf16[128,1024]{1,0:T(8,128)(2,1)S(1)}, bf16[128,1024]{1,0:T(8,128)(2,1)}, u32[]{:S(2)}, u32[]{:S(2)}) collective-permute-start(bf16[128,1024]{1,0:T(8,128)(2,1)S(1)} %copy-done.77), channel_id=1, source_target_pairs={{0,4},{1,5},{2,6},{3,7},{4,0},{5,1},{6,2},{7,3},{8,12},{9,13},{10,... | collective-permute-start | bytes 786440 | tf_op jit(solution)/shard_map/ppermute | solution.py:52
  50.9 7.9 collective-permute-start.44
  53.1 9.0 %collective-permute-start.16 = (bf16[4,32,1024]{2,1,0:T(8,128)(2,1)S(1)}, bf16[4,32,1024]{2,1,0:T(8,128)(2,1)S(1)}, u32[]{:S(2)}, u32[]{:S(2)}) collective-permute-start(bf16[4,32,1024]{2,1,0:T(8,128)(2,1)S(1)} %bitcast.609), channel_id=1, source_target_pairs={{0,8},{1,17},{2,10},{3,19},{4,12},{5,21},{6,14},{7,23},{8,0},{9,25... | collective-permute-start | bytes 786440 | tf_op jit(solution)/shard_map/ppermute | solution.py:52
  53.7 26.2 %collective-permute-start.17 = (bf16[4,32,1024]{2,1,0:T(8,128)(2,1)S(1)}, bf16[4,32,1024]{2,1,0:T(8,128)(2,1)S(1)}, u32[]{:S(2)}, u32[]{:S(2)}) collective-permute-start(bf16[4,32,1024]{2,1,0:T(8,128)(2,1)S(1)} %bitcast.610), channel_id=1, source_target_pairs={{0,16},{1,9},{2,18},{3,11},{4,20},{5,13},{6,22},{7,15},{8,24},{9,1... | collective-permute-start | bytes 786440 | tf_op jit(solution)/shard_map/ppermute | solution.py:52
  55.3 25.2 %collective-permute-start.19 = (bf16[4,32,1024]{2,1,0:T(8,128)(2,1)S(1)}, bf16[4,32,1024]{2,1,0:T(8,128)(2,1)S(1)}, u32[]{:S(2)}, u32[]{:S(2)}) collective-permute-start(bf16[4,32,1024]{2,1,0:T(8,128)(2,1)S(1)} %bitcast.611), channel_id=1, source_target_pairs={{0,1},{1,0},{2,3},{3,2},{4,5},{5,4},{6,7},{7,6},{8,9},{9,8},{10,11... | collective-permute-start | bytes 786440 | tf_op jit(solution)/shard_map/ppermute | solution.py:52
  55.6 12.0 %collective-permute-start.1 = (bf16[2,32,3072]{2,1,0:T(8,128)(2,1)S(1)}, bf16[2,32,3072]{2,1,0:T(8,128)(2,1)S(1)}, u32[]{:S(2)}, u32[]{:S(2)}) collective-permute-start(bf16[2,32,3072]{2,1,0:T(8,128)(2,1)S(1)} %pad_maximum_fusion.20), channel_id=1, source_target_pairs={{0,2},{1,3},{2,0},{3,1},{4,6},{5,7},{6,4},{7,5},{8,10},{9,11},{10,... | collective-permute-start | bytes 1179656 | tf_op jit(solution)/shard_map/ppermute | solution.py:52
  58.8 19.6 %collective-permute-start.24 = (bf16[2,32,4096]{2,1,0:T(8,128)(2,1)S(1)}, bf16[2,32,4096]{2,1,0:T(8,128)(2,1)S(1)}, u32[]{:S(2)}, u32[]{:S(2)}) collective-permute-start(bf16[2,32,4096]{2,1,0:T(8,128)(2,1)S(1)} %pad_maximum_fusion.17), channel_id=1, source_target_pairs={{0,2},{1,3},{2,0},{3,1},{4,6},{5,7},{6,4},{7,5},{8,10},{9,11},{10,... | collective-permute-start | bytes 1572872 | tf_op jit(solution)/shard_map/ppermute | solution.py:52
  62.1 18.4 %collective-permute-start.45 = (bf16[2,2,2,2,32,288]{5,4,3,2,1,0:T(8,128)(2,1)S(1)}, bf16[2,2,2,2,32,288]{5,4,3,2,1,0:T(8,128)(2,1)S(1)}, u32[]{:S(2)}, u32[]{:S(2)}) collective-permute-start(bf16[2,2,2,2,32,288]{5,4,3,2,1,0:T(8,128)(2,1)S(1)} %pad_maximum_fusion.21), channel_id=1, source_target_pairs={{0,1},{1,0},{2,3},{3,2},{4,5},{5,4},{6,7},{7,6},{8,9},{9,8},{10,11... | collective-permute-start | bytes 884744 | tf_op jit(solution)/shard_map/ppermute | solution.py:52
  67.5 13.5 %collective-permute-start.18 = (bf16[4,32,1024]{2,1,0:T(8,128)(2,1)S(1)}, bf16[4,32,1024]{2,1,0:T(8,128)(2,1)S(1)}, u32[]{:S(2)}, u32[]{:S(2)}) collective-permute-start(bf16[4,32,1024]{2,1,0:T(8,128)(2,1)S(1)} %collective-permute-done.16.refs_1_), channel_id=1, source_target_pairs={{0,16},{1,9},{2,18},{3,11},{4,20},{5,13},{6,22},{7,15},{8,24},{9,1... | collective-permute-start | bytes 786440 | tf_op jit(solution)/shard_map/ppermute | solution.py:52
  78.4 18.6 %collective-permute-start.2 = (bf16[4,32,3072]{2,1,0:T(8,128)(2,1)S(1)}, bf16[4,32,3072]{2,1,0:T(8,128)(2,1)}, u32[]{:S(2)}, u32[]{:S(2)}) collective-permute-start(bf16[4,32,3072]{2,1,0:T(8,128)(2,1)S(1)} %bitcast.603), channel_id=1, source_target_pairs={{0,8},{1,17},{2,10},{3,19},{4,12},{5,21},{6,14},{7,23},{8,0},{9,25... | collective-permute-start | bytes 2359304 | tf_op jit(solution)/shard_map/ppermute | solution.py:52
  79.9 30.5 %collective-permute-start.33 = (bf16[2,128,1024]{2,1,0:T(8,128)(2,1)}, bf16[2,128,1024]{2,1,0:T(8,128)(2,1)}, u32[]{:S(2)}, u32[]{:S(2)}) collective-permute-start(bf16[2,128,1024]{2,1,0:T(8,128)(2,1)} %pad_maximum_fusion.18), channel_id=1, source_target_pairs={{0,2},{1,3},{2,0},{3,1},{4,6},{5,7},{6,4},{7,5},{8,10},{9,11},{10,... | collective-permute-start | bytes 1572872 | tf_op jit(solution)/shard_map/ppermute | solution.py:52
  80.5 16.6 %collective-permute-start.20 = (bf16[4,32,1024]{2,1,0:T(8,128)(2,1)S(1)}, bf16[4,32,1024]{2,1,0:T(8,128)(2,1)S(1)}, u32[]{:S(2)}, u32[]{:S(2)}) collective-permute-start(bf16[4,32,1024]{2,1,0:T(8,128)(2,1)S(1)} %collective-permute-done.16.refs_1_), channel_id=1, source_target_pairs={{0,1},{1,0},{2,3},{3,2},{4,5},{5,4},{6,7},{7,6},{8,9},{9,8},{10,11... | collective-permute-start | bytes 786440 | tf_op jit(solution)/shard_map/ppermute | solution.py:52
  80.6 16.7 %collective-permute-start.21 = (bf16[4,32,1024]{2,1,0:T(8,128)(2,1)S(1)}, bf16[4,32,1024]{2,1,0:T(8,128)(2,1)S(1)}, u32[]{:S(2)}, u32[]{:S(2)}) collective-permute-start(bf16[4,32,1024]{2,1,0:T(8,128)(2,1)S(1)} %collective-permute-done.17.refs_2_), channel_id=1, source_target_pairs={{0,1},{1,0},{2,3},{3,2},{4,5},{5,4},{6,7},{7,6},{8,9},{9,8},{10,11... | collective-permute-start | bytes 786440 | tf_op jit(solution)/shard_map/ppermute | solution.py:52
  81.1 29.9 %collective-permute-start.3 = (bf16[4,32,3072]{2,1,0:T(8,128)(2,1)S(1)}, bf16[4,32,3072]{2,1,0:T(8,128)(2,1)}, u32[]{:S(2)}, u32[]{:S(2)}) collective-permute-start(bf16[4,32,3072]{2,1,0:T(8,128)(2,1)S(1)} %bitcast.604), channel_id=1, source_target_pairs={{0,16},{1,9},{2,18},{3,11},{4,20},{5,13},{6,22},{7,15},{8,24},{9,1... | collective-permute-start | bytes 2359304 | tf_op jit(solution)/shard_map/ppermute | solution.py:52
  97.0 20.2 %collective-permute-start.4 = (bf16[4,32,3072]{2,1,0:T(8,128)(2,1)}, bf16[4,32,3072]{2,1,0:T(8,128)(2,1)}, u32[]{:S(2)}, u32[]{:S(2)}) collective-permute-start(bf16[4,32,3072]{2,1,0:T(8,128)(2,1)} %collective-permute-done.2.refs_1_), channel_id=1, source_target_pairs={{0,16},{1,9},{2,18},{3,11},{4,20},{5,13},{6,22},{7,15},{8,24},{9,1... | collective-permute-start | bytes 2359304 | tf_op jit(solution)/shard_map/ppermute | solution.py:52
  97.2 13.5 %collective-permute-start.22 = (bf16[4,32,1024]{2,1,0:T(8,128)(2,1)S(1)}, bf16[4,32,1024]{2,1,0:T(8,128)(2,1)}, u32[]{:S(2)}, u32[]{:S(2)}) collective-permute-start(bf16[4,32,1024]{2,1,0:T(8,128)(2,1)S(1)} %collective-permute-done.18.refs_3_), channel_id=1, source_target_pairs={{0,1},{1,0},{2,3},{3,2},{4,5},{5,4},{6,7},{7,6},{8,9},{9,8},{10,11... | collective-permute-start | bytes 786440 | tf_op jit(solution)/shard_map/ppermute | solution.py:52
  98.0 27.9 %collective-permute-start.25 = (bf16[4,32,4096]{2,1,0:T(8,128)(2,1)S(1)}, bf16[4,32,4096]{2,1,0:T(8,128)(2,1)}, u32[]{:S(2)}, u32[]{:S(2)}) collective-permute-start(bf16[4,32,4096]{2,1,0:T(8,128)(2,1)S(1)} %bitcast.595), channel_id=1, source_target_pairs={{0,8},{1,17},{2,10},{3,19},{4,12},{5,21},{6,14},{7,23},{8,0},{9,25... | collective-permute-start | bytes 3145736 | tf_op jit(solution)/shard_map/ppermute | solution.py:52
  110.4 15.5 %collective-permute-start.5 = (bf16[4,32,3072]{2,1,0:T(8,128)(2,1)S(1)}, bf16[4,32,3072]{2,1,0:T(8,128)(2,1)S(1)}, u32[]{:S(2)}, u32[]{:S(2)}) collective-permute-start(bf16[4,32,3072]{2,1,0:T(8,128)(2,1)S(1)} %bitcast.605), channel_id=1, source_target_pairs={{0,1},{1,0},{2,3},{3,2},{4,5},{5,4},{6,7},{7,6},{8,9},{9,8},{10,11... | collective-permute-start | bytes 2359304 | tf_op jit(solution)/shard_map/ppermute | solution.py:52
  110.7 17.2 %collective-permute-start.6 = (bf16[4,32,3072]{2,1,0:T(8,128)(2,1)}, bf16[4,32,3072]{2,1,0:T(8,128)(2,1)S(1)}, u32[]{:S(2)}, u32[]{:S(2)}) collective-permute-start(bf16[4,32,3072]{2,1,0:T(8,128)(2,1)} %collective-permute-done.2.refs_1_), channel_id=1, source_target_pairs={{0,1},{1,0},{2,3},{3,2},{4,5},{5,4},{6,7},{7,6},{8,9},{9,8},{10,11... | collective-permute-start | bytes 2359304 | tf_op jit(solution)/shard_map/ppermute | solution.py:52
  110.9 17.4 %collective-permute-start.7 = (bf16[4,32,3072]{2,1,0:T(8,128)(2,1)}, bf16[4,32,3072]{2,1,0:T(8,128)(2,1)S(1)}, u32[]{:S(2)}, u32[]{:S(2)}) collective-permute-start(bf16[4,32,3072]{2,1,0:T(8,128)(2,1)} %collective-permute-done.3.refs_2_), channel_id=1, source_target_pairs={{0,1},{1,0},{2,3},{3,2},{4,5},{5,4},{6,7},{7,6},{8,9},{9,8},{10,11... | collective-permute-start | bytes 2359304 | tf_op jit(solution)/shard_map/ppermute | solution.py:52
  117.2 12.7 %collective-permute-start.8 = (bf16[4,32,3072]{2,1,0:T(8,128)(2,1)}, bf16[4,32,3072]{2,1,0:T(8,128)(2,1)S(1)}, u32[]{:S(2)}, u32[]{:S(2)}) collective-permute-start(bf16[4,32,3072]{2,1,0:T(8,128)(2,1)} %collective-permute-done.4.refs_3_), channel_id=1, source_target_pairs={{0,1},{1,0},{2,3},{3,2},{4,5},{5,4},{6,7},{7,6},{8,9},{9,8},{10,11... | collective-permute-start | bytes 2359304 | tf_op jit(solution)/shard_map/ppermute | solution.py:52
  125.9 78.4 %collective-permute-start.26 = (bf16[4,32,4096]{2,1,0:T(8,128)(2,1)S(1)}, bf16[4,32,4096]{2,1,0:T(8,128)(2,1)}, u32[]{:S(2)}, u32[]{:S(2)}) collective-permute-start(bf16[4,32,4096]{2,1,0:T(8,128)(2,1)S(1)} %bitcast.596), channel_id=1, source_target_pairs={{0,16},{1,9},{2,18},{3,11},{4,20},{5,13},{6,22},{7,15},{8,24},{9,1... | collective-permute-start | bytes 3145736 | tf_op jit(solution)/shard_map/ppermute | solution.py:52
  126.0 78.5 %collective-permute-start.28 = (bf16[4,32,4096]{2,1,0:T(8,128)(2,1)S(1)}, bf16[4,32,4096]{2,1,0:T(8,128)(2,1)}, u32[]{:S(2)}, u32[]{:S(2)}) collective-permute-start(bf16[4,32,4096]{2,1,0:T(8,128)(2,1)S(1)} %bitcast.597), channel_id=1, source_target_pairs={{0,1},{1,0},{2,3},{3,2},{4,5},{5,4},{6,7},{7,6},{8,9},{9,8},{10,11... | collective-permute-start | bytes 3145736 | tf_op jit(solution)/shard_map/ppermute | solution.py:52
  128.0 77.0 %collective-permute-start.34 = (bf16[4,128,1024]{2,1,0:T(8,128)(2,1)S(1)}, bf16[4,128,1024]{2,1,0:T(8,128)(2,1)}, u32[]{:S(2)}, u32[]{:S(2)}) collective-permute-start(bf16[4,128,1024]{2,1,0:T(8,128)(2,1)S(1)} %bitcast.599), channel_id=1, source_target_pairs={{0,8},{1,17},{2,10},{3,19},{4,12},{5,21},{6,14},{7,23},{8,0},{9,25... | collective-permute-start | bytes 3145736 | tf_op jit(solution)/shard_map/ppermute | solution.py:52
  128.3 79.4 %collective-permute-start.35 = (bf16[4,128,1024]{2,1,0:T(8,128)(2,1)S(1)}, bf16[4,128,1024]{2,1,0:T(8,128)(2,1)}, u32[]{:S(2)}, u32[]{:S(2)}) collective-permute-start(bf16[4,128,1024]{2,1,0:T(8,128)(2,1)S(1)} %bitcast.600), channel_id=1, source_target_pairs={{0,16},{1,9},{2,18},{3,11},{4,20},{5,13},{6,22},{7,15},{8,24},{9,1... | collective-permute-start | bytes 3145736 | tf_op jit(solution)/shard_map/ppermute | solution.py:52
  129.9 76.7 %collective-permute-start.27 = (bf16[4,32,4096]{2,1,0:T(8,128)(2,1)}, bf16[4,32,4096]{2,1,0:T(8,128)(2,1)}, u32[]{:S(2)}, u32[]{:S(2)}) collective-permute-start(bf16[4,32,4096]{2,1,0:T(8,128)(2,1)} %collective-permute-done.25.refs_1_), channel_id=1, source_target_pairs={{0,16},{1,9},{2,18},{3,11},{4,20},{5,13},{6,22},{7,15},{8,24},{9,1... | collective-permute-start | bytes 3145736 | tf_op jit(solution)/shard_map/ppermute | solution.py:52
  204.9 15.0 %collective-permute-start.36 = (bf16[4,128,1024]{2,1,0:T(8,128)(2,1)}, bf16[4,128,1024]{2,1,0:T(8,128)(2,1)S(1)}, u32[]{:S(2)}, u32[]{:S(2)}) collective-permute-start(bf16[4,128,1024]{2,1,0:T(8,128)(2,1)} %collective-permute-done.34.refs_1_), channel_id=1, source_target_pairs={{0,16},{1,9},{2,18},{3,11},{4,20},{5,13},{6,22},{7,15},{8,24},{9,1... | collective-permute-start | bytes 3145736 | tf_op jit(solution)/shard_map/ppermute | solution.py:52
  206.5 13.4 %collective-permute-start.31 = (bf16[4,32,4096]{2,1,0:T(8,128)(2,1)}, bf16[4,32,4096]{2,1,0:T(8,128)(2,1)S(1)}, u32[]{:S(2)}, u32[]{:S(2)}) collective-permute-start(bf16[4,32,4096]{2,1,0:T(8,128)(2,1)} %collective-permute-done.27.refs_3_), channel_id=1, source_target_pairs={{0,1},{1,0},{2,3},{3,2},{4,5},{5,4},{6,7},{7,6},{8,9},{9,8},{10,11... | collective-permute-start | bytes 3145736 | tf_op jit(solution)/shard_map/ppermute | solution.py:52
  207.7 61.7 %collective-permute-start.37 = (bf16[4,128,1024]{2,1,0:T(8,128)(2,1)S(1)}, bf16[4,128,1024]{2,1,0:T(8,128)(2,1)S(1)}, u32[]{:S(2)}, u32[]{:S(2)}) collective-permute-start(bf16[4,128,1024]{2,1,0:T(8,128)(2,1)S(1)} %bitcast.601), channel_id=1, source_target_pairs={{0,1},{1,0},{2,3},{3,2},{4,5},{5,4},{6,7},{7,6},{8,9},{9,8},{10,11... | collective-permute-start | bytes 3145736 | tf_op jit(solution)/shard_map/ppermute | solution.py:52
  208.3 61.2 %collective-permute-start.38 = (bf16[4,128,1024]{2,1,0:T(8,128)(2,1)}, bf16[4,128,1024]{2,1,0:T(8,128)(2,1)S(1)}, u32[]{:S(2)}, u32[]{:S(2)}) collective-permute-start(bf16[4,128,1024]{2,1,0:T(8,128)(2,1)} %collective-permute-done.34.refs_1_), channel_id=1, source_target_pairs={{0,1},{1,0},{2,3},{3,2},{4,5},{5,4},{6,7},{7,6},{8,9},{9,8},{10,11... | collective-permute-start | bytes 3145736 | tf_op jit(solution)/shard_map/ppermute | solution.py:52
  208.8 60.7 %collective-permute-start.39 = (bf16[4,128,1024]{2,1,0:T(8,128)(2,1)}, bf16[4,128,1024]{2,1,0:T(8,128)(2,1)S(1)}, u32[]{:S(2)}, u32[]{:S(2)}) collective-permute-start(bf16[4,128,1024]{2,1,0:T(8,128)(2,1)} %collective-permute-done.35.refs_2_), channel_id=1, source_target_pairs={{0,1},{1,0},{2,3},{3,2},{4,5},{5,4},{6,7},{7,6},{8,9},{9,8},{10,11... | collective-permute-start | bytes 3145736 | tf_op jit(solution)/shard_map/ppermute | solution.py:52
  220.0 49.5 %collective-permute-start.40 = (bf16[4,128,1024]{2,1,0:T(8,128)(2,1)S(1)}, bf16[4,128,1024]{2,1,0:T(8,128)(2,1)S(1)}, u32[]{:S(2)}, u32[]{:S(2)}) collective-permute-start(bf16[4,128,1024]{2,1,0:T(8,128)(2,1)S(1)} %collective-permute-done.36.refs_3_), channel_id=1, source_target_pairs={{0,1},{1,0},{2,3},{3,2},{4,5},{5,4},{6,7},{7,6},{8,9},{9,8},{10,11... | collective-permute-start | bytes 3145736 | tf_op jit(solution)/shard_map/ppermute | solution.py:52
  368.4 20.3 %collective-permute-start.56 = (bf16[2,2,2,2,32,288]{5,4,3,2,1,0:T(8,128)(2,1)}, bf16[2,2,2,2,32,288]{5,4,3,2,1,0:T(8,128)(2,1)}, u32[]{:S(2)}, u32[]{:S(2)}) collective-permute-start(bf16[2,2,2,2,32,288]{5,4,3,2,1,0:T(8,128)(2,1)} %fusion.28), channel_id=1, source_target_pairs={{0,1},{1,0},{2,3},{3,2},{4,5},{5,4},{6,7},{7,6},{8,9},{9,8},{10,11... | collective-permute-start | bytes 884744 | tf_op jit(solution)/shard_map/ppermute | solution.py:52
  390.1 8.0 collective-permute-start.57
  401.7 9.2 %collective-permute-start.58 = (bf16[2,2,32,288]{2,3,0,1:T(8,128)(2,1)S(1)}, bf16[2,2,32,288]{2,3,0,1:T(8,128)(2,1)S(1)}, u32[]{:S(2)}, u32[]{:S(2)}) collective-permute-start(bf16[2,2,32,288]{2,3,0,1:T(8,128)(2,1)S(1)} %fusion.33), channel_id=1, source_target_pairs={{0,16},{1,17},{2,18},{3,19},{4,20},{5,21},{6,22},{7,23},{8,24},{9,... | collective-permute-start | bytes 221192 | tf_op jit(solution)/shard_map/ppermute | solution.py:52
  619.6 63.4 %collective-permute-start.81 = (bf16[4,4,128,1024]{3,2,1,0:T(8,128)(2,1)}, bf16[4,4,128,1024]{3,2,1,0:T(8,128)(2,1)}, u32[]{:S(2)}, u32[]{:S(2)}) collective-permute-start(bf16[4,4,128,1024]{3,2,1,0:T(8,128)(2,1)} %pad_maximum_fusion.2), channel_id=1, source_target_pairs={{0,1},{1,0},{2,3},{3,2},{4,5},{5,4},{6,7},{7,6},{8,9},{9,8},{10,11... | collective-permute-start | bytes 12582920 | tf_op jit(solution)/shard_map/ppermute | solution.py:52
  628.5 50.6 %collective-permute-start.61 = (bf16[4,4,32,3072]{3,2,1,0:T(8,128)(2,1)}, bf16[4,4,32,3072]{3,2,1,0:T(8,128)(2,1)}, u32[]{:S(2)}, u32[]{:S(2)}) collective-permute-start(bf16[4,4,32,3072]{3,2,1,0:T(8,128)(2,1)} %pad_maximum_fusion.3), channel_id=1, source_target_pairs={{0,1},{1,0},{2,3},{3,2},{4,5},{5,4},{6,7},{7,6},{8,9},{9,8},{10,11... | collective-permute-start | bytes 9437192 | tf_op jit(solution)/shard_map/ppermute | solution.py:52
  634.4 51.7 %collective-permute-start.76 = (bf16[4,4,32,4096]{3,2,1,0:T(8,128)(2,1)}, bf16[4,4,32,4096]{3,2,1,0:T(8,128)(2,1)}, u32[]{:S(2)}, u32[]{:S(2)}) collective-permute-start(bf16[4,4,32,4096]{3,2,1,0:T(8,128)(2,1)} %pad_maximum_fusion.1), channel_id=1, source_target_pairs={{0,1},{1,0},{2,3},{3,2},{4,5},{5,4},{6,7},{7,6},{8,9},{9,8},{10,11... | collective-permute-start | bytes 12582920 | tf_op jit(solution)/shard_map/ppermute | solution.py:52
  652.1 15.1 %collective-permute-start.86 = (bf16[2,2,2,2,32,288]{5,4,3,2,1,0:T(8,128)(2,1)}, bf16[2,2,2,2,32,288]{5,4,3,2,1,0:T(8,128)(2,1)S(1)}, u32[]{:S(2)}, u32[]{:S(2)}) collective-permute-start(bf16[2,2,2,2,32,288]{5,4,3,2,1,0:T(8,128)(2,1)} %fusion.30), channel_id=1, source_target_pairs={{0,1},{1,0},{2,3},{3,2},{4,5},{5,4},{6,7},{7,6},{8,9},{9,8},{10,11... | collective-permute-start | bytes 884744 | tf_op jit(solution)/shard_map/ppermute | solution.py:52
  658.4 8.6 %collective-permute-start.69 = (f32[2,4,128]{2,1,0:T(4,128)S(1)}, f32[2,4,128]{2,1,0:T(4,128)S(1)}, u32[]{:S(2)}, u32[]{:S(2)}) collective-permute-start(f32[2,4,128]{2,1,0:T(4,128)S(1)} %fusion.86), channel_id=1, source_target_pairs={{0,2},{1,3},{2,0},{3,1},{4,6},{5,7},{6,4},{7,5},{8,10},{9,11},{10,... | collective-permute-start | bytes 12296 | tf_op jit(solution)/shard_map/ppermute | solution.py:52
  667.1 23.1 %collective-permute-start.71 = (bf16[4,4,32,1024]{3,2,1,0:T(8,128)(2,1)}, bf16[4,4,32,1024]{3,2,1,0:T(8,128)(2,1)S(1)}, u32[]{:S(2)}, u32[]{:S(2)}) collective-permute-start(bf16[4,4,32,1024]{3,2,1,0:T(8,128)(2,1)} %pad_maximum_fusion.10), channel_id=1, source_target_pairs={{0,1},{1,0},{2,3},{3,2},{4,5},{5,4},{6,7},{7,6},{8,9},{9,8},{10,11... | collective-permute-start | bytes 3145736 | tf_op jit(solution)/shard_map/ppermute | solution.py:52
  672.0 6.8 collective-permute-start.87
  678.9 13.6 %collective-permute-start.88 = (bf16[2,2,32,288]{3,2,1,0:T(8,128)(2,1)S(1)}, bf16[2,2,32,288]{3,2,1,0:T(8,128)(2,1)S(1)}, u32[]{:S(2)}, u32[]{:S(2)}) collective-permute-start(bf16[2,2,32,288]{3,2,1,0:T(8,128)(2,1)S(1)} %fusion.67), channel_id=1, source_target_pairs={{0,16},{1,17},{2,18},{3,19},{4,20},{5,21},{6,22},{7,23},{8,24},{9,... | collective-permute-start | bytes 221192 | tf_op jit(solution)/shard_map/ppermute | solution.py:52
  681.2 73.9 %collective-permute-start.62 = (bf16[2,4,32,3072]{3,2,1,0:T(8,128)(2,1)S(1)}, bf16[2,4,32,3072]{3,2,1,0:T(8,128)(2,1)S(1)}, u32[]{:S(2)}, u32[]{:S(2)}) collective-permute-start(bf16[2,4,32,3072]{3,2,1,0:T(8,128)(2,1)S(1)} %add_convert_fusion.6), channel_id=1, source_target_pairs={{0,16},{1,9},{2,18},{3,11},{4,20},{5,13},{6,22},{7,15},{8,24},{9,1... | collective-permute-start | bytes 4718600 | tf_op jit(solution)/shard_map/ppermute | solution.py:52
  685.6 71.6 %collective-permute-start.82 = (bf16[2,4,128,1024]{3,2,1,0:T(8,128)(2,1)S(1)}, bf16[2,4,128,1024]{3,2,1,0:T(8,128)(2,1)S(1)}, u32[]{:S(2)}, u32[]{:S(2)}) collective-permute-start(bf16[2,4,128,1024]{3,2,1,0:T(8,128)(2,1)S(1)} %add_convert_fusion.1), channel_id=1, source_target_pairs={{0,16},{1,9},{2,18},{3,11},{4,20},{5,13},{6,22},{7,15},{8,24},{9,1... | collective-permute-start | bytes 6291464 | tf_op jit(solution)/shard_map/ppermute | solution.py:52
  688.5 72.7 %collective-permute-start.77 = (bf16[2,4,32,4096]{3,2,1,0:T(8,128)(2,1)S(1)}, bf16[2,4,32,4096]{3,2,1,0:T(8,128)(2,1)S(1)}, u32[]{:S(2)}, u32[]{:S(2)}) collective-permute-start(bf16[2,4,32,4096]{3,2,1,0:T(8,128)(2,1)S(1)} %add_convert_fusion.2), channel_id=1, source_target_pairs={{0,16},{1,9},{2,18},{3,11},{4,20},{5,13},{6,22},{7,15},{8,24},{9,1... | collective-permute-start | bytes 6291464 | tf_op jit(solution)/shard_map/ppermute | solution.py:52
  690.4 61.8 %collective-permute-start.72 = (bf16[2,4,32,1024]{3,2,1,0:T(8,128)(2,1)S(1)}, bf16[2,4,32,1024]{3,2,1,0:T(8,128)(2,1)S(1)}, u32[]{:S(2)}, u32[]{:S(2)}) collective-permute-start(bf16[2,4,32,1024]{3,2,1,0:T(8,128)(2,1)S(1)} %add_convert_fusion.13), channel_id=1, source_target_pairs={{0,16},{1,9},{2,18},{3,11},{4,20},{5,13},{6,22},{7,15},{8,24},{9,1... | collective-permute-start | bytes 1572872 | tf_op jit(solution)/shard_map/ppermute | solution.py:52
  692.6 71.1 %collective-permute-start.89 = (bf16[2,32,288]{2,1,0:T(8,128)(2,1)S(1)}, bf16[2,32,288]{2,1,0:T(8,128)(2,1)S(1)}, u32[]{:S(2)}, u32[]{:S(2)}) collective-permute-start(bf16[2,32,288]{2,1,0:T(8,128)(2,1)S(1)} %fusion.69), channel_id=1, source_target_pairs={{0,2},{1,3},{2,0},{3,1},{4,6},{5,7},{6,4},{7,5},{8,10},{9,11},{10,... | collective-permute-start | bytes 110600 | tf_op jit(solution)/shard_map/ppermute | solution.py:52
  753.3 12.8 %collective-permute-start.73 = (bf16[1,4,32,1024]{3,2,1,0:T(8,128)(2,1)S(1)}, bf16[1,4,32,1024]{3,2,1,0:T(8,128)(2,1)S(1)}, u32[]{:S(2)}, u32[]{:S(2)}) collective-permute-start(bf16[1,4,32,1024]{3,2,1,0:T(8,128)(2,1)S(1)} %fusion.27), channel_id=1, source_target_pairs={{0,8},{1,17},{2,10},{3,19},{4,12},{5,21},{6,14},{7,23},{8,0},{9,25... | collective-permute-start | bytes 786440 | tf_op jit(solution)/shard_map/ppermute | solution.py:52
  756.8 19.5 %collective-permute-start.63 = (bf16[1,4,32,3072]{3,2,1,0:T(8,128)(2,1)S(1)}, bf16[1,4,32,3072]{3,2,1,0:T(8,128)(2,1)S(1)}, u32[]{:S(2)}, u32[]{:S(2)}) collective-permute-start(bf16[1,4,32,3072]{3,2,1,0:T(8,128)(2,1)S(1)} %fusion.19), channel_id=1, source_target_pairs={{0,8},{1,17},{2,10},{3,19},{4,12},{5,21},{6,14},{7,23},{8,0},{9,25... | collective-permute-start | bytes 2359304 | tf_op jit(solution)/shard_map/ppermute | solution.py:52
  759.4 20.7 %collective-permute-start.83 = (bf16[1,4,128,1024]{3,2,1,0:T(8,128)(2,1)S(1)}, bf16[1,4,128,1024]{3,2,1,0:T(8,128)(2,1)S(1)}, u32[]{:S(2)}, u32[]{:S(2)}) collective-permute-start(bf16[1,4,128,1024]{3,2,1,0:T(8,128)(2,1)S(1)} %fusion.12), channel_id=1, source_target_pairs={{0,8},{1,17},{2,10},{3,19},{4,12},{5,21},{6,14},{7,23},{8,0},{9,25... | collective-permute-start | bytes 3145736 | tf_op jit(solution)/shard_map/ppermute | solution.py:52
  763.2 28.1 %collective-permute-start.78 = (bf16[1,4,32,4096]{3,2,1,0:T(8,128)(2,1)S(1)}, bf16[1,4,32,4096]{3,2,1,0:T(8,128)(2,1)S(1)}, u32[]{:S(2)}, u32[]{:S(2)}) collective-permute-start(bf16[1,4,32,4096]{3,2,1,0:T(8,128)(2,1)S(1)} %fusion.14), channel_id=1, source_target_pairs={{0,8},{1,17},{2,10},{3,19},{4,12},{5,21},{6,14},{7,23},{8,0},{9,25... | collective-permute-start | bytes 3145736 | tf_op jit(solution)/shard_map/ppermute | solution.py:52
  771.9 19.7 %collective-permute-start.75 = (bf16[32,1024]{1,0:T(8,128)(2,1)S(1)}, bf16[32,1024]{1,0:T(8,128)(2,1)S(1)}, u32[]{:S(2)}, u32[]{:S(2)}) collective-permute-start(bf16[32,1024]{1,0:T(8,128)(2,1)S(1)} %fusion.62), channel_id=1, source_target_pairs={{0,4},{1,5},{2,6},{3,7},{4,0},{5,1},{6,2},{7,3},{8,12},{9,13},{10,... | collective-permute-start | bytes 196616 | tf_op jit(solution)/shard_map/ppermute | solution.py:52
  776.5 15.9 %collective-permute-start.64 = (bf16[2,32,3072]{2,1,0:T(8,128)(2,1)S(1)}, bf16[2,32,3072]{2,1,0:T(8,128)(2,1)S(1)}, u32[]{:S(2)}, u32[]{:S(2)}) collective-permute-start(bf16[2,32,3072]{2,1,0:T(8,128)(2,1)S(1)} %fusion.29), channel_id=1, source_target_pairs={{0,2},{1,3},{2,0},{3,1},{4,6},{5,7},{6,4},{7,5},{8,10},{9,11},{10,... | collective-permute-start | bytes 1179656 | tf_op jit(solution)/shard_map/ppermute | solution.py:52
  780.5 26.3 %collective-permute-start.84 = (bf16[2,128,1024]{2,1,0:T(8,128)(2,1)S(1)}, bf16[2,128,1024]{2,1,0:T(8,128)(2,1)S(1)}, u32[]{:S(2)}, u32[]{:S(2)}) collective-permute-start(bf16[2,128,1024]{2,1,0:T(8,128)(2,1)S(1)} %fusion.21), channel_id=1, source_target_pairs={{0,2},{1,3},{2,0},{3,1},{4,6},{5,7},{6,4},{7,5},{8,10},{9,11},{10,... | collective-permute-start | bytes 1572872 | tf_op jit(solution)/shard_map/ppermute | solution.py:52
  791.6 22.5 %collective-permute-start.79 = (bf16[2,32,4096]{2,1,0:T(8,128)(2,1)S(1)}, bf16[2,32,4096]{2,1,0:T(8,128)(2,1)S(1)}, u32[]{:S(2)}, u32[]{:S(2)}) collective-permute-start(bf16[2,32,4096]{2,1,0:T(8,128)(2,1)S(1)} %fusion.20), channel_id=1, source_target_pairs={{0,2},{1,3},{2,0},{3,1},{4,6},{5,7},{6,4},{7,5},{8,10},{9,11},{10,... | collective-permute-start | bytes 1572872 | tf_op jit(solution)/shard_map/ppermute | solution.py:52
  792.5 21.8 %collective-permute-start.65 = (bf16[32,3072]{1,0:T(8,128)(2,1)S(1)}, bf16[32,3072]{1,0:T(8,128)(2,1)S(1)}, u32[]{:S(2)}, u32[]{:S(2)}) collective-permute-start(bf16[32,3072]{1,0:T(8,128)(2,1)S(1)} %fusion.31), channel_id=1, source_target_pairs={{0,4},{1,5},{2,6},{3,7},{4,0},{5,1},{6,2},{7,3},{8,12},{9,13},{10,... | collective-permute-start | bytes 589832 | tf_op jit(solution)/shard_map/ppermute | solution.py:52
  807.0 21.2 %collective-permute-start.85 = (bf16[128,1024]{1,0:T(8,128)(2,1)S(1)}, bf16[128,1024]{1,0:T(8,128)(2,1)S(1)}, u32[]{:S(2)}, u32[]{:S(2)}) collective-permute-start(bf16[128,1024]{1,0:T(8,128)(2,1)S(1)} %fusion.22), channel_id=1, source_target_pairs={{0,4},{1,5},{2,6},{3,7},{4,0},{5,1},{6,2},{7,3},{8,12},{9,13},{10,... | collective-permute-start | bytes 786440 | tf_op jit(solution)/shard_map/ppermute | solution.py:52
  814.3 17.1 %collective-permute-start.80 = (bf16[32,4096]{1,0:T(8,128)(2,1)S(1)}, bf16[32,4096]{1,0:T(8,128)(2,1)S(1)}, u32[]{:S(2)}, u32[]{:S(2)}) collective-permute-start(bf16[32,4096]{1,0:T(8,128)(2,1)S(1)} %fusion.24), channel_id=1, source_target_pairs={{0,4},{1,5},{2,6},{3,7},{4,0},{5,1},{6,2},{7,3},{8,12},{9,13},{10,... | collective-permute-start | bytes 786440 | tf_op jit(solution)/shard_map/ppermute | solution.py:52
  (131 other events, 1413.9 us)

commit v2 on v1

v2 whole, which is shorter than its diff:
```python
import functools

import jax
import jax.numpy as jnp
from jax import lax
from jax.experimental import pallas as pl
from jax.experimental.pallas import tpu as pltpu
from jax.sharding import PartitionSpec as P

D = 1024
HEADS = 16
HEAD_DIM = 64
PROJ_A = 128
PROJ_B = 96
PROJ_C = 64
QLEN = 32
DPR = 4
QPR = 1
DMOST = 330

AXES = ("row", "col")
highest = lax.Precision.HIGHEST
eps_norm = 1e-05
eps_vec = 1e-06
score_scale = 16.0
f32 = jnp.float32
bf16 = jnp.bfloat16


def sizes():
    n_rows = lax.axis_size("row")
    n_z = lax.axis_size("col") // 2
    return n_rows, n_z, n_rows.bit_length() - 1, n_z.bit_length() - 1


def after(value, *before):
    return lax.optimization_barrier((value,) + before)[0] if before else value


def place():
    col = lax.axis_index("col")
    return lax.axis_index("row"), col // 2, col % 2


def exchange(value, row_masks=(0, 0), z_mask=0, swap_core=False):
    n_rows, n_z, _, _ = sizes()
    pairs = []
    for r in range(n_rows):
        for z in range(n_z):
            for c in range(2):
                here = (r * n_z + z) * 2 + c
                there = ((r ^ row_masks[c]) * n_z + (z ^ z_mask)) * 2 + (
                    1 - c if swap_core else c
                )
                pairs.append((here, there))
    return lax.ppermute(value, AXES, pairs)


def stage_bit(core, stage, row_bits):
    return (stage + core) % row_bits


def stage_masks(stage):
    _, _, row_bits, _ = sizes()
    return tuple(1 << stage_bit(c, stage, row_bits) for c in range(2))


def piece_mask(core, piece):
    _, _, row_bits, _ = sizes()
    return sum(
        1 << stage_bit(core, j, row_bits) for j in range(row_bits) if piece >> j & 1
    )


def ordered(bit, own, other, axis):
    return jnp.stack([jnp.where(bit == 0, own, other), jnp.where(bit == 0, other, own)], axis)


def transfer(value, start=(), use=(), **move):
    return after(exchange(after(value, *start), **move), *use)


class Gather:
    def __init__(self, shard):
        self.held, self.count, self.shard = shard, 0, shard

    def along_z(self, start=(), use=()):
        _, n_z, _, z_bits = sizes()
        _, z, _ = place()
        bit = z_bits - 1 - self.count
        other = transfer(self.held, start, use, z_mask=1 << bit)
        self.held = ordered(z >> bit & 1, self.held, other, self.count)
        self.count += 1
        if self.count == z_bits:
            self.pieces = [self.held.reshape((n_z,) + self.shard.shape)]

    def all_z(self, *bounds):
        _, _, _, z_bits = sizes()
        for i in range(z_bits):
            self.along_z(*bounds[min(i, len(bounds) - 1)])

    def all_rows(self, first, rest):
        _, _, row_bits, _ = sizes()
        for stage in range(row_bits):
            self.pieces = self.pieces + [
                transfer(p, *(rest if i else first), row_masks=stage_masks(stage))
                for i, p in enumerate(self.pieces)
            ]

    def whole(self, table, early=(), late=()):
        last = len(self.pieces) - 1
        sibs = [
            transfer(p, *(late if i == last else early), swap_core=True)
            for i, p in enumerate(self.pieces)
        ]
        return Weight(table, self.pieces + sibs)


def piece_table():
    n_rows, _, _, _ = sizes()
    row, _, core = place()
    tables = [
        jnp.array([piece_mask(c, k) for k in range(n_rows)], jnp.int32) for c in range(2)
    ]
    own = row ^ jnp.where(core == 0, tables[0], tables[1])
    sib = row ^ jnp.where(core == 0, tables[1], tables[0])
    steps = jnp.arange(n_rows)

    def piece_of(rows):
        return jnp.sum(jnp.where(rows[None, :] == steps[:, None], steps[None, :], 0), axis=1)

    return jnp.concatenate([own, sib, core[None], piece_of(own), piece_of(sib)]).astype(jnp.int32)


class Weight:
    def __init__(self, table, pieces):
        n_rows, n_z, _, _ = sizes()
        self.table, self.pieces = table, pieces
        r, n = pieces[0].shape[1:]
        self.shape = (n_rows, n_z, 2, r, n)
        self.rows = n_rows * n_z * 2 * r

    def specs(self):
        return [pl.BlockSpec(memory_space=pl.ANY)] * len(self.pieces)

    def scratch(self):
        return [
            pltpu.VMEM(self.shape, self.pieces[0].dtype),
            pltpu.SemaphoreType.DMA((len(self.pieces) + 1,)),
        ]

    def out_shape(self):
        return jax.ShapeDtypeStruct(self.shape, self.pieces[0].dtype)


def load_weight(table, pieces, out_ref, w_ref, sems):
    n_rows = len(pieces) // 2
    core = table[2 * n_rows]
    out = pltpu.make_async_copy(w_ref, out_ref, sems.at[2 * n_rows])

    @pl.when(pl.program_id(0) == 0)
    def _():
        copies = [
            pltpu.make_async_copy(
                piece,
                w_ref.at[table[i], :, core if i < n_rows else 1 - core],
                sems.at[i],
            )
            for i, piece in enumerate(pieces)
        ]
        for c in copies:
            c.start()
        for c in copies:
            c.wait()
        out.start()

    @pl.when(pl.program_id(0) == pl.num_programs(0) - 1)
    def _():
        out.wait()


def gather_small(shard):
    n_rows, n_z, row_bits, z_bits = sizes()
    row, z, core = place()
    held = shard
    for count, bit in enumerate(reversed(range(z_bits))):
        held = ordered(z >> bit & 1, held, exchange(held, z_mask=1 << bit), count)
    for count, bit in enumerate(reversed(range(row_bits))):
        other = exchange(held, row_masks=(1 << bit, 1 << bit))
        held = ordered(row >> bit & 1, held, other, count)
    held = ordered(core, held, exchange(held, swap_core=True), row_bits + z_bits)
    return held.reshape((n_rows * n_z * 2,) + shard.shape)


def scatter_small(blocks, dtype):
    n_rows, n_z, row_bits, z_bits = sizes()
    row, z, core = place()
    held = blocks.reshape((2,) * (row_bits + z_bits + 1) + blocks.shape[1:])

    def halve(held, axis, bit, **move):
        send = lax.dynamic_index_in_dim(held, 1 - bit, axis, keepdims=False)
        keep = lax.dynamic_index_in_dim(held, bit, axis, keepdims=False)
        return keep.astype(f32) + exchange(send.astype(dtype), **move).astype(f32)

    held = halve(held, row_bits + z_bits, core, swap_core=True)
    for bit in range(row_bits):
        held = halve(held, row_bits - 1 - bit, row >> bit & 1, row_masks=(1 << bit, 1 << bit))
    for bit in range(z_bits):
        held = halve(held, z_bits - 1 - bit, z >> bit & 1, z_mask=1 << bit)
    return held


def gather_relative(block):
    n_rows, n_z, _, _ = sizes()
    held = jnp.stack([block] + [exchange(block, z_mask=m) for m in range(1, n_z)])
    held = jnp.stack([held] + [exchange(held, row_masks=(m, m)) for m in range(1, n_rows)])
    return jnp.stack([held, exchange(held, swap_core=True)])


def scatter_relative(blocks, dtype):
    n_rows, n_z, _, _ = sizes()

    def step(held, count, move):
        parts = [exchange(held[m].astype(dtype), **move(m)) for m in range(1, count)]
        total = held[0]
        for part in parts:
            total = total + part.astype(f32)
        return total

    held = step(blocks, 2, lambda m: dict(swap_core=True))
    held = step(held, n_rows, lambda m: dict(row_masks=(m, m)))
    return step(held, n_z, lambda m: dict(z_mask=m))


def relative_order():
    n_rows, n_z, _, _ = sizes()
    row, z, core = place()
    at = jnp.arange(n_rows * n_z * 2)
    there_core = core ^ at // (n_rows * n_z)
    there_row = row ^ at // n_z % n_rows
    return ((there_row * n_z + (z ^ at % n_z)) * 2 + there_core).astype(jnp.int32)


class Scatter:
    def __init__(self, send, keep, wide=False):
        _, _, row_bits, z_bits = sizes()
        self.send, self.keep = send, keep
        self.wide = ("z", z_bits - 1) if wide else None
        self.stages = [("row", j) for j in reversed(range(row_bits))]
        self.stages += [("z", b) for b in range(sizes()[3])]

    def step(self, *use):
        _, _, _, z_bits = sizes()
        _, z, _ = place()
        kind, at = self.stages.pop(0)
        move = dict(row_masks=stage_masks(at)) if kind == "row" else dict(z_mask=1 << at)
        parts = (self.keep, after(exchange(self.send, **move), *use))
        if not self.stages:
            return parts[0] + parts[1].astype(f32)
        kind, at = self.stages[0]
        if kind == "row":
            half = 1 << at
            pick = lambda x, other: x[half:] if other else x[:half]
        else:
            if at == 0:
                parts = tuple(x.reshape((2,) * z_bits + x.shape[2:]) for x in parts)
            mine = z >> at & 1
            pick = lambda x, other: lax.dynamic_index_in_dim(
                x, 1 - mine if other else mine, z_bits - 1 - at, keepdims=False
            )
        total = lambda other: pick(parts[0], other) + pick(parts[1], other).astype(f32)
        self.send, self.keep = total(True), total(False)
        if self.stages[0] != self.wide:
            self.send = self.send.astype(bf16)
        return self.send

    def finish(self, *use):
        while self.stages:
            out = self.step(*use)
        return out


def head_slices():
    return ((0, PROJ_A), (PROJ_A, PROJ_B), (PROJ_A + PROJ_B, PROJ_C))


LANES = 128


def whole_spec(shape):
    return pl.BlockSpec(
        shape, lambda *_: (0,) * len(shape), pipeline_mode=pl.Buffered(buffer_count=1)
    )


def row_spec(rows, width):
    return pl.BlockSpec((rows, width), lambda i, *_: (i, 0))


def col_spec(rows, width):
    return pl.BlockSpec((rows, width), lambda i, *_: (0, i))


def like(shape, dtype):
    return jax.ShapeDtypeStruct(shape, dtype)


def call(
    kernel, name, grid, in_specs, out_specs, out_shape, flops, moved, scratch=(), table=None, wait=(), aliases=None
):
    first = len(in_specs) + (0 if table is None else 1)
    in_specs = list(in_specs) + [pl.BlockSpec(memory_space=pl.ANY)] * len(wait)

    def body(*refs):
        kernel(*refs[:first], *refs[first + len(wait) :])

    run = pl.pallas_call(
        body,
        grid_spec=pltpu.PrefetchScalarGridSpec(
            num_scalar_prefetch=0 if table is None else 1,
            grid=grid,
            in_specs=in_specs,
            out_specs=out_specs,
            scratch_shapes=list(scratch),
        ),
        out_shape=out_shape,
        input_output_aliases=aliases or {},
        compiler_params=pltpu.CompilerParams(vmem_limit_bytes=56 << 20),
        cost_estimate=pl.CostEstimate(
            flops=int(flops), bytes_accessed=int(moved), transcendentals=0
        ),
        name=name,
    )
    return lambda *operands: run(*operands, *wait)


def swap_halves(x):
    lane = lax.broadcasted_iota(jnp.int32, x.shape, 1)
    half = HEAD_DIM // 2
    return jnp.where(
        lane % HEAD_DIM < half, pltpu.roll(x, LANES - half, 1), pltpu.roll(x, half, 1)
    )


QKV_TILE = 1024


def qkv_kernel(n_pieces, table, x_ref, b_ref, cos_ref, sin_ref, *refs):
    pieces, (o_ref, w_out, acc_ref, w_ref, sems) = refs[:n_pieces], refs[n_pieces:]
    load_weight(table, pieces, w_out, w_ref, sems)
    tile = pl.program_id(0)
    per_part = D // QKV_TILE
    cols = pl.ds(pl.multiple_of(tile * QKV_TILE, LANES), QKV_TILE)
    w = w_ref[:, :, :, :, cols].reshape(x_ref.shape[1], QKV_TILE)
    acc_ref[...] = contract(x_ref[...], w, 1, 0) + b_ref[...]

    @pl.when(tile < 2 * per_part)
    def _():
        scale = jnp.where(tile < per_part, HEAD_DIM**-0.5, 1.0)
        cosine = cos_ref[...] * scale
        sine = sin_ref[...] * scale
        for j in range(QKV_TILE // LANES):
            at = slice(j * LANES, (j + 1) * LANES)
            a = acc_ref[:, at]
            o_ref[:, at] = (a * cosine + swap_halves(a) * sine).astype(bf16)

    @pl.when(tile >= 2 * per_part)
    def _():
        o_ref[...] = acc_ref[...].astype(bf16)


def project_qkv(x, w, b, cosine, sine, wait=()):
    t = x.shape[0]
    any_out = pl.BlockSpec(memory_space=pl.ANY)
    return call(
        functools.partial(qkv_kernel, len(w.pieces)),
        "project_qkv",
        (3 * D // QKV_TILE,),
        [
            whole_spec((t, D)),
            pl.BlockSpec((1, QKV_TILE), lambda i, _: (0, i)),
            whole_spec((t, LANES)),
            whole_spec((t, LANES)),
        ]
        + w.specs(),
        [col_spec(t, QKV_TILE), any_out],
        [like((t, 3 * D), bf16), w.out_shape()],
        6 * t * D * D,
        20 * t * D,
        [pltpu.VMEM((t, QKV_TILE), f32)] + w.scratch(),
        table=w.table,
        wait=wait,
    )(w.table, x, b, cosine, sine, *w.pieces)


TILE = 256


def normalized(v):
    mean = jnp.mean(v, axis=1, keepdims=True)
    centered = v - mean
    rstd = lax.rsqrt(jnp.mean(centered * centered, axis=1, keepdims=True) + eps_norm)
    return centered * rstd, rstd


def norm_back(g, hat, rstd, gain):
    y = g * gain
    return rstd * (
        y - jnp.mean(y, axis=1, keepdims=True) - hat * jnp.mean(y * hat, axis=1, keepdims=True)
    )


def add_up(ref, value):
    @pl.when(pl.program_id(0) == 0)
    def _():
        ref[...] = jnp.zeros_like(ref)

    ref[...] += value


def column_sum(x):
    return jnp.sum(x, axis=0, keepdims=True)


def out_norm_kernel(n_pieces, table, a_ref, b_ref, x_ref, gain_ref, bias_ref, *refs):
    pieces = refs[:n_pieces]
    hat_ref, rstd_ref, low_ref, w_out, w_ref, sems = refs[n_pieces:]
    load_weight(table, pieces, w_out, w_ref, sems)
    w = w_ref[...].reshape(a_ref.shape[1], -1)
    v = x_ref[...].astype(f32) + contract(a_ref[...], w, 1, 0) + b_ref[...]
    hat, rstd = normalized(v)
    hat_ref[...] = hat
    rstd_ref[...] = jnp.broadcast_to(rstd, rstd_ref.shape)
    low_ref[...] = (hat * gain_ref[...] + bias_ref[...]).astype(bf16)


def out_norm(attended, w, b, x, gain, bias, wait=()):
    t = x.shape[0]
    vec = whole_spec((1, D))
    return call(
        functools.partial(out_norm_kernel, len(w.pieces)),
        "out_norm",
        (t // TILE,),
        [row_spec(TILE, D), vec, row_spec(TILE, D), vec, vec] + w.specs(),
        [row_spec(TILE, D), row_spec(TILE, LANES), row_spec(TILE, D), pl.BlockSpec(memory_space=pl.ANY)],
        [like((t, D), f32), like((t, LANES), f32), like((t, D), bf16), w.out_shape()],
        2 * t * D * D,
        12 * t * D,
        w.scratch(),
        table=w.table,
        wait=wait,
    )(w.table, attended, b, x, gain, bias, *w.pieces)


UP_TILE = 1024
CHUNK = 16


def gelu_pair(x):
    u = jnp.abs(x)
    e = jnp.exp(x * x * -0.5)
    t = 1.0 / (1.0 + (0.3275911 * 0.5**0.5) * u)
    poly = t * (
        0.254829592 * 0.5
        + t
        * (
            -0.284496736 * 0.5
            + t * (1.421413741 * 0.5 + t * (-1.453152027 * 0.5 + t * (1.061405429 * 0.5)))
        )
    )
    tail = poly * e
    phi = jnp.where(x < 0, tail, 1.0 - tail)
    return x * phi, phi + x * e * (2.0 * jnp.pi) ** -0.5


def up_kernel(n_pieces, first, table, h_ref, b_ref, *refs):
    pieces = refs[:n_pieces]
    act_ref, slope_ref, w_out, acc_ref, w_ref, sems = refs[-6:]
    n = w_ref.shape[-1]
    if first:
        pieces = [p.at[:, :, pl.ds(n, n)] for p in pieces]
        w_out = w_out.at[:, :, :, :, pl.ds(n, n)]
    else:
        pieces = [p.at[:, :, pl.ds(0, n)] for p in pieces]
        w_out = w_out.at[:, :, :, :, pl.ds(0, n)]
    load_weight(table, pieces, w_out, w_ref, sems)
    cols = pl.ds(pl.multiple_of(pl.program_id(0) * UP_TILE, LANES), UP_TILE)
    acc_ref[...] = contract(h_ref[...], w_ref[:, :, :, :, cols].reshape(-1, UP_TILE), 1, 0)
    bias = b_ref[...]

    def step(i, _):
        rows = pl.ds(pl.multiple_of(i * CHUNK, CHUNK), CHUNK)
        act, slope = gelu_pair(acc_ref[rows, :] + bias)
        act_ref[rows, :] = act.astype(bf16)
        slope_ref[rows, :] = slope.astype(bf16)
        return 0

    lax.fori_loop(0, h_ref.shape[0] // CHUNK, step, 0)


def up_gelu(hidden, w, b, before=None, wait=()):
    t, ff = hidden.shape[0], w.shape[-1]
    any_space = pl.BlockSpec(memory_space=pl.ANY)
    steps = ff // UP_TILE // 2
    first = 0 if before is None else steps
    before = [] if before is None else list(before)
    n_in = 3 + len(w.pieces)
    w_ref, sems = w.scratch()
    half = pltpu.VMEM(w.shape[:-1] + (ff // 2,), bf16)
    return call(
        functools.partial(up_kernel, len(w.pieces), first),
        "up_gelu",
        (steps,),
        [whole_spec((t, D)), pl.BlockSpec((1, UP_TILE), lambda i, _: (0, first + i))]
        + w.specs()
        + [any_space] * len(before),
        [pl.BlockSpec((t, UP_TILE), lambda i, _: (0, first + i))] * 2 + [any_space],
        [like((t, ff), bf16)] * 2 + [w.out_shape()],
        t * D * ff,
        2 * t * ff + D * ff,
        [pltpu.VMEM((t, UP_TILE), f32), half, sems],
        table=w.table,
        wait=wait,
        aliases={n_in + i: i for i in range(len(before))},
    )(w.table, hidden, b, *w.pieces, *before)


def head_masks(width):
    lane = lax.broadcasted_iota(jnp.int32, (1, width), 1)
    return [(lane >= start) & (lane < start + size) for start, size in head_slices()]


def head_sums(x):
    out = jnp.zeros_like(x)
    for mask in head_masks(x.shape[1]):
        total = jnp.sum(jnp.where(mask, x, 0.0), axis=1, keepdims=True)
        out = jnp.where(mask, total, out)
    return out


def down_norm_kernel(
    n_pieces, table, a_ref, b_ref, hat1_ref, gain1_ref, bias1_ref, gain_ref, bias_ref, proj_ref, *refs
):
    pieces = refs[:n_pieces]
    hat_ref, rstd_ref, low_ref, raw_ref, vec_ref, w_out, w_ref, sems = refs[n_pieces:]
    load_weight(table, pieces, w_out, w_ref, sems)
    hidden = hat1_ref[...] * gain1_ref[...] + bias1_ref[...]
    w = w_ref[...].reshape(a_ref.shape[1], -1)
    hat, rstd = normalized(hidden + contract(a_ref[...], w, 1, 0) + b_ref[...])
    hat_ref[...] = hat
    rstd_ref[...] = jnp.broadcast_to(rstd, rstd_ref.shape)
    low = (hat * gain_ref[...] + bias_ref[...]).astype(bf16)
    low_ref[...] = low
    raw = contract(low, proj_ref[...], 1, 0)
    raw_ref[...] = raw
    vec_ref[...] = (raw * lax.rsqrt(head_sums(raw * raw) + eps_vec)).astype(bf16)


def down_norm(act, w, b, hat1, gain1, bias1, gain, bias, proj, wait=()):
    t, ff = act.shape
    e = proj.shape[1]
    vec = whole_spec((1, D))
    return call(
        functools.partial(down_norm_kernel, len(w.pieces)),
        "down_norm",
        (t // TILE,),
        [row_spec(TILE, ff), vec, row_spec(TILE, D), vec, vec, vec, vec, whole_spec((D, e))]
        + w.specs(),
        [
            row_spec(TILE, D),
            row_spec(TILE, LANES),
            row_spec(TILE, D),
            row_spec(TILE, e),
            row_spec(TILE, e),
            pl.BlockSpec(memory_space=pl.ANY),
        ],
        [
            like((t, D), f32),
            like((t, LANES), f32),
            like((t, D), bf16),
            like((t, e), f32),
            like((t, e), bf16),
            w.out_shape(),
        ],
        2 * t * D * ff,
        20 * t * D,
        w.scratch(),
        table=w.table,
        wait=wait,
    )(w.table, act, b, hat1, gain1, bias1, gain, bias, proj, *w.pieces)


def head_back_kernel(
    g_ref, raw_ref, low_ref, proj_ref, hat_ref, rstd_ref, gain_ref,
    grad_ref, branch_ref, dproj_ref, sums_ref,
):
    g, raw = g_ref[...], raw_ref[...]
    scale = lax.rsqrt(head_sums(raw * raw) + eps_vec)
    y = raw * scale
    raw_grad = (scale * (g - y * head_sums(y * g))).astype(bf16)
    result_grad = contract(raw_grad, proj_ref[...], 1, 1)
    hat = hat_ref[...]
    grad = norm_back(result_grad, hat, rstd_ref[:, :1], gain_ref[...])
    branch = grad.astype(bf16)
    grad_ref[...] = grad
    branch_ref[...] = branch
    add_up(dproj_ref, contract(low_ref[...], raw_grad, 0, 0))
    add_up(
        sums_ref,
        jnp.concatenate(
            [
                column_sum(result_grad * hat),
                column_sum(result_grad),
                column_sum(branch.astype(f32)),
            ],
            axis=0,
        ),
    )


def head_back(g, raw, low, proj, hat, rstd, gain, wait=()):
    t, e = raw.shape
    return call(
        head_back_kernel,
        "head_back",
        (t // TILE,),
        [
            row_spec(TILE, e),
            row_spec(TILE, e),
            row_spec(TILE, D),
            whole_spec((D, e)),
            row_spec(TILE, D),
            row_spec(TILE, LANES),
            whole_spec((1, D)),
        ],
        [row_spec(TILE, D), row_spec(TILE, D), whole_spec((D, e)), whole_spec((3, D))],
        [like((t, D), f32), like((t, D), bf16), like((D, e), f32), like((3, D), f32)],
        4 * t * D * e,
        16 * t * D,
        wait=wait,
    )(g, raw, low, proj, hat, rstd, gain)


def act_back_kernel(g_ref, w_ref, slope_ref, o_ref, sum_ref):
    back = (contract(g_ref[...], w_ref[...], 1, 1) * slope_ref[...].astype(f32)).astype(bf16)
    o_ref[...] = back
    sum_ref[...] = column_sum(back.astype(f32))


def act_back(branch, w, slope, wait=()):
    t, ff = slope.shape
    return call(
        act_back_kernel,
        "act_back",
        (ff // UP_TILE,),
        [whole_spec((t, D)), row_spec(UP_TILE, D), col_spec(t, UP_TILE)],
        [col_spec(t, UP_TILE), col_spec(1, UP_TILE)],
        [like((t, ff), bf16), like((1, ff), f32)],
        2 * t * D * ff,
        4 * t * ff + 2 * D * ff,
        wait=wait,
    )(branch, w, slope)


def hidden_back_kernel(
    g_ref, w_ref, resid_ref, hat_ref, rstd_ref, gain_ref, wout_ref,
    grad_ref, out_ref, att_ref, sums_ref,
):
    hidden_grad = resid_ref[...] + contract(g_ref[...], w_ref[...], 1, 1)
    hat = hat_ref[...]
    grad = norm_back(hidden_grad, hat, rstd_ref[:, :1], gain_ref[...])
    low = grad.astype(bf16)
    grad_ref[...] = grad
    out_ref[...] = low
    att_ref[...] = contract(low, wout_ref[...], 1, 1).astype(bf16)
    add_up(
        sums_ref,
        jnp.concatenate(
            [column_sum(hidden_grad * hat), column_sum(hidden_grad), column_sum(low.astype(f32))],
            axis=0,
        ),
    )


def hidden_back(inner, w, resid, hat, rstd, gain, w_out, wait=()):
    t, ff = inner.shape
    return call(
        hidden_back_kernel,
        "hidden_back",
        (t // TILE,),
        [
            row_spec(TILE, ff),
            whole_spec((D, ff)),
            row_spec(TILE, D),
            row_spec(TILE, D),
            row_spec(TILE, LANES),
            whole_spec((1, D)),
            whole_spec((D, D)),
        ],
        [row_spec(TILE, D)] * 3 + [whole_spec((3, D))],
        [like((t, D), f32), like((t, D), bf16), like((t, D), bf16), like((3, D), f32)],
        2 * t * D * ff + 2 * t * D * D,
        2 * t * ff + 24 * t * D,
        wait=wait,
    )(inner, w, resid, hat, rstd, gain, w_out)


def input_back_kernel(groups, *refs):
    g_refs, (w_ref, resid_ref, o_ref) = refs[:groups], refs[groups:]
    total = resid_ref[...]
    for part in range(3):
        for i, g_ref in enumerate(g_refs):
            width = g_ref.shape[2]
            at = part * D + i * width
            total = total + contract(g_ref[part], w_ref[:, at : at + width], 1, 1)
    o_ref[...] = total


def input_back(grads, w, resid, wait=()):
    t = resid.shape[0]
    return call(
        functools.partial(input_back_kernel, len(grads)),
        "input_back",
        (t // TILE,),
        [pl.BlockSpec((3, TILE, g.shape[2]), lambda i: (0, i, 0)) for g in grads]
        + [whole_spec((D, 3 * D)), row_spec(TILE, D)],
        row_spec(TILE, D),
        like((t, D), f32),
        6 * t * D * D,
        20 * t * D,
        wait=wait,
    )(*grads, w, resid)


def unpack_kernel(n_devices, widths, p_ref, *o_refs):
    at = 0
    for width, o_ref in zip(widths, o_refs):
        n = width * n_devices
        x = p_ref[:, at : at + width]
        copies = (
            lax.broadcasted_iota(jnp.int32, (width, n), 1) % width
            == lax.broadcasted_iota(jnp.int32, (width, n), 0)
        ).astype(bf16)
        mine = (
            lax.broadcasted_iota(jnp.int32, (n_devices, n), 1) // width
            == lax.broadcasted_iota(jnp.int32, (n_devices, n), 0)
        )
        o_ref[...] = column_sum(jnp.where(mine, contract(x, copies, 1, 0), 0.0))
        at += width


def unpack(packed, widths, wait=()):
    n_devices = packed.shape[0]
    return call(
        functools.partial(unpack_kernel, n_devices, widths),
        "unpack",
        (1,),
        [whole_spec(packed.shape)],
        [whole_spec((1, w * n_devices)) for w in widths],
        [like((1, w * n_devices), f32) for w in widths],
        10**8,
        10**5,
        wait=wait,
    )(packed)


def pack_kernel(n_devices, widths, *refs):
    o_ref = refs[-1]
    o_ref[...] = jnp.zeros_like(o_ref)
    at = 0
    for width, ref in zip(widths, refs):
        n = width * n_devices
        mine = (
            lax.broadcasted_iota(jnp.int32, (n_devices, n), 1) // width
            == lax.broadcasted_iota(jnp.int32, (n_devices, n), 0)
        )
        copies = (
            lax.broadcasted_iota(jnp.int32, (n, width), 0) % width
            == lax.broadcasted_iota(jnp.int32, (n, width), 1)
        ).astype(f32)
        o_ref[:, at : at + width] = lax.dot_general(
            jnp.where(mine, ref[...], 0.0),
            copies,
            (((1,), (0,)), ((), ())),
            precision=highest,
            preferred_element_type=f32,
        )
        at += width


def pack(vectors, n_devices, wait=()):
    widths = [v.shape[1] // n_devices for v in vectors]
    total = sum(widths)
    total += -total % LANES
    return call(
        functools.partial(pack_kernel, n_devices, widths),
        "pack",
        (1,),
        [whole_spec(v.shape) for v in vectors],
        whole_spec((n_devices, total)),
        like((n_devices, total), f32),
        10**8,
        10**5,
        wait=wait,
    )(*vectors)


def weight_kernel(n_rows, n_z, offset, table, a_ref, b_ref, *refs):
    t, k = a_ref.shape
    block = k // n_rows
    r = block // (2 * n_z)
    turned = refs[-1]

    @pl.when(pl.program_id(0) == 0)
    def _():
        core = table[2 * n_rows]
        side = core if offset == 0 else 1 - core
        for piece in range(n_rows):
            mesh_row = table[offset + piece]
            cols = pl.ds(pl.multiple_of(mesh_row * block, block), block)
            x = a_ref[:, cols].T.reshape(n_z, 2, r, t)
            half = jnp.where(side == 0, x[:, 0], x[:, 1]).reshape(n_z * r, t)
            turned[piece * n_z * r : (piece + 1) * n_z * r, :] = half

    total = contract(turned[...], b_ref[...].reshape(b_ref.shape[-2:]), 1, 0)
    total = total.reshape(n_rows, n_z, r, total.shape[1])
    if offset:
        refs[0][...] = total.astype(refs[0].dtype)
    else:
        other, send_ref, keep_ref = refs[:3]
        total += other[...].astype(f32)
        send_ref[...] = total[n_rows // 2 :].astype(send_ref.dtype)
        keep_ref[...] = total[: n_rows // 2]


def weight_half(
    name, table, a, b, n_rows, n_z, tile, other=None, other_type=bf16, wait=()
):
    t, k = a.shape
    per_part = b.shape[-1] // tile
    n = b.shape[-1] * (b.shape[0] if b.ndim == 3 else 1)
    r = k // (n_rows * n_z * 2)
    if b.ndim == 3:
        b_spec = pl.BlockSpec((1, t, tile), lambda i, _: (i // per_part, 0, i % per_part))
    else:
        b_spec = col_spec(t, tile)

    def block(rows):
        return pl.BlockSpec((rows, n_z, r, tile), lambda i, _: (0, 0, 0, i))

    def shape(rows, dtype):
        return like((rows, n_z, r, n), dtype)

    own = other is not None
    return call(
        functools.partial(weight_kernel, n_rows, n_z, 0 if own else n_rows),
        name,
        (n // tile,),
        [whole_spec((t, k)), b_spec] + ([block(n_rows)] if own else []),
        [block(n_rows // 2)] * 2 if own else block(n_rows),
        [shape(n_rows // 2, bf16), shape(n_rows // 2, f32)] if own else shape(n_rows, other_type),
        t * k * n,
        2 * t * (k + n) + 3 * k * n,
        [pltpu.VMEM((k // 2, t), bf16)],
        table=table,
        wait=wait,
    )(table, a, b, *([other] if own else []))


WIN = -(-(DMOST + 15) // 32) * 32
NEG = -1e30


def contract(a, b, ca, cb):
    return lax.dot_general(a, b, (((ca,), (cb,)), ((), ())), preferred_element_type=f32)


def spans(len_ref, row_len):
    found = []
    start = jnp.int32(QPR * QLEN)
    for d in range(DPR):
        size = len_ref[d]
        base = pl.multiple_of(jnp.minimum((start // 16) * 16, row_len - WIN), 16)
        found.append((base, start - base, start - base + size))
        start = start + size
    return found


def head_pair(x):
    lane = lax.broadcasted_iota(jnp.int32, x.shape, 1)
    zero = jnp.zeros_like(x)
    return jnp.concatenate(
        [jnp.where(lane < HEAD_DIM, x, zero), jnp.where(lane < HEAD_DIM, zero, x)], axis=0
    )


def pair_heads(x):
    n = x.shape[0] // 2
    lane = lax.broadcasted_iota(jnp.int32, (n, x.shape[1]), 1)
    return jnp.where(lane < HEAD_DIM, x[:n], x[n:])


def inside(n, low, high, axis):
    shape = (n, 1) if axis == 0 else (1, n)
    at = lax.broadcasted_iota(jnp.int32, shape, axis)
    return (at >= low) & (at < high)


def attend(q, k, v, low, high):
    s = contract(head_pair(q), k, 1, 1)
    s = s + jnp.where(inside(k.shape[0], low, high, 1), 0.0, NEG)
    p = jnp.exp(s - jnp.max(s, axis=1, keepdims=True))
    total = jnp.sum(p, axis=1, keepdims=True)
    return pair_heads(contract(p.astype(bf16), v, 1, 0) / total)


def attention_kernel(len_ref, q_ref, k_ref, v_ref, o_ref):
    row_len = q_ref.shape[0]
    for base, low, high in spans(len_ref, row_len):
        w = pl.ds(base, WIN)
        o = attend(q_ref[w, :], k_ref[w, :], v_ref[w, :], low, high)
        keep = inside(WIN, low, high, 0)
        o_ref[w, :] = jnp.where(keep, o, o_ref[w, :].astype(f32)).astype(bf16)
    o_ref[:QLEN, :] = attend(q_ref[:QLEN, :], k_ref[:128, :], v_ref[:128, :], 0, QLEN).astype(bf16)


def qkv_specs(t):
    per_part = D // LANES
    return [
        pl.BlockSpec((t, LANES), lambda i, _, p=p: (0, p * per_part + i)) for p in range(3)
    ]


def attention(lengths, qkv, wait=()):
    t = qkv.shape[0]
    return call(
        attention_kernel,
        "attention",
        (HEADS // 2,),
        qkv_specs(t),
        col_spec(t, LANES),
        like((t, D), bf16),
        2 * 10**10,
        8 * t * D,
        table=lengths,
        wait=wait,
    )(lengths, qkv, qkv, qkv)


def attend_back(q, k, v, g, low, high):
    n = q.shape[0]
    g = jnp.where(inside(n, low, high, 0), g, jnp.zeros_like(g))
    qq = head_pair(q)
    gg = head_pair(g)
    st = contract(k, qq, 1, 1)
    st = st + jnp.where(inside(k.shape[0], low, high, 0), 0.0, NEG)
    p = jnp.exp(st - jnp.max(st, axis=0, keepdims=True))
    p = p * (1.0 / jnp.sum(p, axis=0, keepdims=True))
    dp = contract(v, gg, 1, 1)
    delta = jnp.sum(p * dp, axis=0, keepdims=True)
    ds = (p * (dp - delta)).astype(bf16)
    dv = contract(p.astype(bf16), gg, 1, 0)
    dk = contract(ds, qq, 1, 0)
    dq = contract(ds, k, 0, 0) * (HEAD_DIM**-0.5)
    return pair_heads(dq), dk, dv


def attention_back_kernel(len_ref, q_ref, k_ref, v_ref, g_ref, cos_ref, sin_ref, o_ref, sum_ref, *sums):
    row_len = q_ref.shape[0]
    for ref in sums:
        ref[...] = jnp.zeros_like(ref)
    parts = attend_back(
        q_ref[:QLEN, :], k_ref[:128, :], v_ref[:128, :], g_ref[:QLEN, :], 0, QLEN
    )
    for ref, x in zip(sums, parts):
        ref[: x.shape[0], :] = x
    for base, low, high in spans(len_ref, row_len):
        w = pl.ds(base, WIN)
        parts = attend_back(q_ref[w, :], k_ref[w, :], v_ref[w, :], g_ref[w, :], low, high)
        for ref, x in zip(sums, parts):
            ref[w, :] += x
    cosine, sine = cos_ref[...], sin_ref[...]
    for part in range(3):
        x = sums[part][...]
        if part < 2:
            x = x * cosine - swap_halves(x) * sine
        x = x.astype(bf16)
        o_ref[part] = x
        sum_ref[part] = column_sum(x.astype(f32))


def attention_back(lengths, qkv, g, cosine, sine, group, groups, wait=()):
    t = qkv.shape[0]
    table = whole_spec((t, LANES))
    pairs = HEADS // 2 // groups
    first = group * pairs
    per_part = D // LANES
    specs = [
        pl.BlockSpec((t, LANES), lambda i, _, p=p: (0, p * per_part + first + i)) for p in range(3)
    ]
    return call(
        attention_back_kernel,
        "attention_back",
        (pairs,),
        specs + [pl.BlockSpec((t, LANES), lambda i, _: (0, first + i)), table, table],
        [
            pl.BlockSpec((3, t, LANES), lambda i, _: (0, 0, i)),
            pl.BlockSpec((3, 1, LANES), lambda i, _: (0, 0, i)),
        ],
        [like((3, t, D // groups), bf16), like((3, 1, D // groups), f32)],
        5 * 10**10 // groups,
        14 * t * D // groups,
        [pltpu.VMEM((t, LANES), f32)] * 3,
        table=lengths,
        wait=wait,
    )(lengths, qkv, qkv, qkv, g, cosine, sine)


SCORE_TILE = 256


def doc_inside(doc_ref, d):
    return doc_ref[...] == d


def score_exps(docs, queries, mask):
    picked = jnp.where(mask, docs, jnp.zeros_like(docs))
    return picked, jnp.exp(contract(picked, queries, 1, 1) * score_scale)


def split_dot(hot, x):
    high = x.astype(bf16)
    rest = (x - high.astype(f32)).astype(bf16)
    return contract(hot, high, 1, 0) + contract(hot, rest, 1, 0)


def score_kernel(
    doc_ref, query_ref, id_ref, hot_ref, count_ref, pos_ref, sum_ref, score_ref, stat_ref
):
    docs = doc_ref[...]
    n_queries = score_ref.shape[2]
    live = lax.broadcasted_iota(jnp.int32, (8, n_queries), 0) < DPR
    for head, mask in enumerate(head_masks(docs.shape[1])):
        scores = jnp.zeros((8, n_queries), f32)
        for at in range(0, query_ref.shape[0], SCORE_TILE):
            _, e = score_exps(docs, query_ref[at : at + SCORE_TILE, :], mask)
            total = split_dot(hot_ref[...], e)
            sum_ref[head, :, at : at + SCORE_TILE] = total
            smooth = jnp.log(total) - count_ref[:, :1]
            query = lax.broadcasted_iota(jnp.int32, (SCORE_TILE, n_queries), 1)
            hot = (id_ref[at : at + SCORE_TILE, :] == query).astype(f32)
            scores += lax.dot_general(
                jnp.where(lax.broadcasted_iota(jnp.int32, smooth.shape, 0) < DPR, smooth, 0.0),
                hot,
                (((1,), (0,)), ((), ())),
                precision=highest,
                preferred_element_type=f32,
            )
        score_ref[head] = scores
        top = jnp.max(jnp.where(live, scores, NEG), axis=0, keepdims=True)
        den = column_sum(jnp.where(live, jnp.exp(scores - top), 0.0))
        pos = column_sum(jnp.where(live, scores * pos_ref[...], 0.0))
        stat_ref[head] = jnp.concatenate([top, den, pos], axis=0)


def score_grad_kernel(
    doc_ref, query_ref, id_ref, index_ref, sum_ref, score_ref, stat_ref, pos_ref, dq_ref, dd_ref
):
    docs = doc_ref[...]
    n_queries = score_ref.shape[2]
    dd_ref[...] = jnp.zeros_like(dd_ref)
    dq_ref[...] = jnp.zeros_like(dq_ref)
    index = index_ref[...]
    for head, mask in enumerate(head_masks(docs.shape[1])):
        stats = stat_ref[head]
        grad = jnp.exp(score_ref[head] - stats[0:1]) / stats[1:2] - pos_ref[...]
        for at in range(0, query_ref.shape[0], SCORE_TILE):
            queries = query_ref[at : at + SCORE_TILE, :]
            picked, e = score_exps(docs, queries, mask)
            query = lax.broadcasted_iota(jnp.int32, (n_queries, SCORE_TILE), 0)
            hot = (id_ref[:, at : at + SCORE_TILE] == query).astype(f32)
            spread = lax.dot_general(
                grad, hot, (((1,), (0,)), ((), ())), precision=highest, preferred_element_type=f32
            )
            coef = score_scale * spread / sum_ref[head, :, at : at + SCORE_TILE]
            wide = coef[0:1]
            for d in range(1, DPR):
                wide = jnp.where(index == d, coef[d : d + 1], wide)
            back = (e * wide).astype(bf16)
            dd_ref[...] += jnp.where(mask, contract(back, queries, 1, 0), 0.0)
            dq_ref[at : at + SCORE_TILE, :] += contract(back, picked, 0, 0)


def score_stats(docs, queries, ids, hot, counts, positive, wait=()):
    n, e = docs.shape
    n_tokens = queries.shape[0]
    n_queries = n_tokens // QLEN
    return call(
        score_kernel,
        "scores",
        (1,),
        [
            whole_spec((n, e)),
            whole_spec((n_tokens, e)),
            whole_spec((n_tokens, 1)),
            whole_spec((8, n)),
            whole_spec((8, LANES)),
            whole_spec((8, n_queries)),
        ],
        [
            whole_spec((3, 8, n_tokens)),
            whole_spec((3, 8, n_queries)),
            whole_spec((3, 3, n_queries)),
        ],
        [
            like((3, 8, n_tokens), f32),
            like((3, 8, n_queries), f32),
            like((3, 3, n_queries), f32),
        ],
        12 * n * n_tokens * e,
        10**6,
        wait=wait,
    )(docs, queries, ids[:, None], hot, counts, positive)


def score_grads(docs, queries, ids, index, sums, scores, stats, positive, wait=()):
    n, e = docs.shape
    n_tokens = queries.shape[0]
    n_queries = n_tokens // QLEN
    return call(
        score_grad_kernel,
        "score_grads",
        (1,),
        [
            whole_spec((n, e)),
            whole_spec((n_tokens, e)),
            whole_spec((1, n_tokens)),
            whole_spec((n, 1)),
            whole_spec((3, 8, n_tokens)),
            whole_spec((3, 8, n_queries)),
            whole_spec((3, 3, n_queries)),
            whole_spec((8, n_queries)),
        ],
        [whole_spec((n_tokens, e)), whole_spec((n, e))],
        [like((n_tokens, e), f32), like((n, e), f32)],
        24 * n * n_tokens * e,
        10**6,
        wait=wait,
    )(docs, queries, ids[None], index, sums, scores, stats, positive)


def layout(lengths, row_len, q_tokens):
    count = lengths.shape[0]
    before = jnp.arange(count)[:, None] <= jnp.arange(count)[None, :]
    ends = jnp.sum(jnp.where(before, lengths[:, None], 0), axis=0)
    offset = jnp.arange(row_len, dtype=jnp.int32) - q_tokens
    doc = jnp.sum((offset[:, None] >= ends[None, :]).astype(jnp.int32), axis=1)
    chosen = (doc[:, None] == jnp.arange(count, dtype=jnp.int32)[None, :]).astype(
        jnp.int32
    )
    begin = jnp.sum(chosen * (ends - lengths)[None, :], axis=1)
    is_query = offset < 0
    position = jnp.where(is_query, (offset + q_tokens) % QLEN, offset - begin)
    return position, doc


def combine_stats(one, two):
    top = jnp.maximum(one[:, 0], two[:, 0])
    den = one[:, 1] * jnp.exp(one[:, 0] - top) + two[:, 1] * jnp.exp(two[:, 0] - top)
    return jnp.stack([top, den, one[:, 2] + two[:, 2]], axis=1)


def reduce_stats(stats):
    n_rows, n_z, _, _ = sizes()
    moves = [[dict(swap_core=True)]]
    moves.append([dict(row_masks=(m, m)) for m in range(1, n_rows)])
    moves.append([dict(z_mask=m) for m in range(1, n_z)])
    for level in moves:
        parts = [exchange(stats, **move) for move in level]
        for part in parts:
            stats = combine_stats(stats, part)
    return stats


def on_device(
    tokens,
    lengths,
    positives,
    w_qkv,
    b_qkv,
    w_out,
    b_out,
    norm1_gain,
    norm1_bias,
    w_up,
    b_up,
    w_down,
    b_down,
    norm2_gain,
    norm2_bias,
    w_proj,
):
    n_rows, n_z, _, _ = sizes()
    n_devices = n_rows * n_z * 2
    row, z, core = place()
    device = (row * n_z + z) * 2 + core
    table = piece_table()
    row_len = tokens.shape[0]
    q_tokens = QPR * QLEN

    g_qkv, g_out, g_up, g_down = (Gather(w) for w in (w_qkv, w_out, w_up, w_down))
    g_qkv.all_z(())
    g_out.all_z([[g_qkv.held]])
    g_qkv.all_rows((), ())
    first, last = g_qkv.pieces[1:-1], g_qkv.pieces[-1]
    vectors = (b_qkv, b_out, norm1_gain, norm1_bias, b_up, b_down, norm2_gain, norm2_bias)
    widths = [v.shape[0] for v in vectors]
    packed = jnp.concatenate([after(v, g_qkv.held) for v in vectors])
    packed = jnp.pad(packed, (0, -packed.shape[0] % LANES)).reshape(-1, LANES)
    packed = gather_small(packed).reshape(n_devices, -1)
    full_bqkv, full_bout, gain_one, bias_one, full_bup, full_bdown, gain_two, bias_two = unpack(
        packed, widths
    )
    full_proj = gather_small(after(w_proj, *first)).reshape(-1, w_proj.shape[1])
    g_up.all_z([[g_out.held, *first]], [[last]])
    g_out.all_rows([first], [[last]])
    w_qkv_all = g_qkv.whole(table)

    own_lengths = lax.dynamic_index_in_dim(lengths, device, 0, keepdims=False)
    position, doc_index = layout(own_lengths, row_len, q_tokens)
    half = HEAD_DIM // 2
    frequency = 10000.0 ** (-jnp.arange(half, dtype=f32) / half)
    angles = position.astype(f32)[:, None] * frequency[None, :]
    cosine, sine = jnp.cos(angles), jnp.sin(angles)
    cosine = jnp.concatenate([cosine] * 4, axis=1)
    sine = jnp.concatenate([-sine, sine] * 2, axis=1)
    qkv, full_qkv = project_qkv(
        tokens, w_qkv_all, full_bqkv, cosine, sine, wait=[g_up.held, full_proj]
    )
    g_up.all_rows([[g_out.pieces[1], last], [qkv]], [[qkv]])
    w_out_all = g_out.whole(table, [[qkv]], [[qkv]])
    g_up_first = g_up.pieces[1:-1]
    attended = attention(own_lengths, qkv, wait=g_up_first)
    g_down.all_z([[g_up.held], [qkv]], [[qkv], [attended]])
    hat1, rstd1, hidden_low, full_out = out_norm(
        attended, w_out_all, full_bout, tokens, gain_one, bias_one, wait=[g_down.held]
    )

    w_up_all = g_up.whole(table, [[qkv], [attended]], [[attended]])
    part = up_gelu(hidden_low, w_up_all, full_bup)
    g_down.all_rows([[attended], [part[0]]], [[part[0]]])
    act, slope, full_up = up_gelu(hidden_low, w_up_all, full_bup, part, wait=g_down.pieces[1:-1])
    w_down_all = g_down.whole(table, [[part[0]], [act]], [[act]])
    hat2, rstd2, result_low, raw, vecs, full_down = down_norm(
        act, w_down_all, full_bdown, hat1, gain_one, bias_one, gain_two, bias_two, full_proj
    )
    full_qkv, full_out, full_up, full_down = (
        w.reshape(-1, w.shape[-1]) for w in (full_qkv, full_out, full_up, full_down)
    )

    query_all = gather_relative(vecs[:q_tokens]).reshape(n_devices * q_tokens, -1)
    query_ids = relative_order()[:, None] * QPR + jnp.arange(q_tokens, dtype=jnp.int32)[None, :] // QLEN
    query_ids = query_ids.reshape(-1)
    docs = vecs[q_tokens:]
    doc_index = doc_index[q_tokens:]
    slots = jnp.arange(8, dtype=jnp.int32)
    hot = (slots[:, None] == doc_index[None, :]).astype(bf16)
    counts = jnp.broadcast_to(
        jnp.log(jnp.pad(own_lengths, (0, 8 - DPR), constant_values=1).astype(f32))[:, None],
        (8, LANES),
    )
    positive = ((positives[None, :] == device * DPR + slots[:, None]) & (slots < DPR)[:, None]).astype(f32)
    sums, doc_scores, stats = score_stats(docs, query_all, query_ids, hot, counts, positive)
    stats = reduce_stats(stats)
    query_count = n_z * 2 * QPR
    losses = lax.dynamic_slice_in_dim(
        stats[:, 0] + jnp.log(stats[:, 1]) - stats[:, 2], row * query_count, query_count, 1
    )
    query_grads, doc_grads = score_grads(
        docs, query_all, query_ids, doc_index[:, None], sums, doc_scores, stats, positive
    )
    query_grad = scatter_relative(query_grads.reshape(2, n_rows, n_z, q_tokens, -1), bf16)
    vector_grad = jnp.concatenate([query_grad, doc_grads], axis=0)

    resid_two_grad, branch_grad, grad_proj, sums2 = head_back(
        vector_grad, raw, result_low, full_proj, hat2, rstd2, gain_two
    )
    def sib_half(name, a, b, tile, dtype=bf16, wait=()):
        return weight_half(
            name + "_sib", table, a, b, n_rows, n_z, tile, other_type=dtype, wait=wait
        )

    def own_half(name, a, b, tile, sib, wide=False, wait=()):
        other = exchange(sib, swap_core=True)
        return Scatter(*weight_half(name, table, a, b, n_rows, n_z, tile, other, wait=wait), wide)

    def attention_part(i, wait):
        return attention_back(own_lengths, qkv, attended_grad, cosine, sine, i, 2, wait=wait)

    down_sib = sib_half("grad_down", act, branch_grad, 512)
    inner_grad, grad_bup = act_back(branch_grad, full_down, slope, wait=[down_sib])
    down = own_half("grad_down", act, branch_grad, 512, down_sib, True, wait=[grad_bup])
    up_sib = sib_half("grad_up", hidden_low, inner_grad, 1024, f32, wait=[down.send])
    resid_one_grad, out_grad, attended_grad, sums1 = hidden_back(
        inner_grad, full_up, resid_two_grad, hat1, rstd1, gain_one, full_out, wait=[up_sib]
    )
    d2 = down.step(sums1)
    up = own_half("grad_up", hidden_low, inner_grad, 1024, up_sib, wait=[sums1, d2])
    d3 = down.step(up.send)
    grad_a, sums_a = attention_part(0, [up.send, d3])
    sib_a = sib_half("grad_qkv", tokens, grad_a, 512)
    d4 = down.step(sums_a)
    u2 = up.step(sums_a)
    out_sib = sib_half("grad_out", attended, out_grad, 1024, wait=[sib_a])
    grad_b, sums_b = attention_part(1, [out_sib, d4, u2])
    qkv_a = own_half("grad_qkv", tokens, grad_a, 512, sib_a, wait=[sums_b])
    sum_down = down.finish(sums_b)
    u3 = up.step(sums_b)
    out = own_half("grad_out", attended, out_grad, 1024, out_sib, True, wait=[qkv_a.send, u3])
    sib_b = sib_half("grad_qkv", tokens, grad_b, 512, wait=[out.send])
    u4 = up.step(sib_b)
    a2 = qkv_a.step(sib_b)
    qkv_b = own_half("grad_qkv", tokens, grad_b, 512, sib_b, wait=[u4, a2])
    a3 = qkv_a.step(qkv_b.send)
    o2 = out.step(qkv_b.send)
    input_grad = input_back([grad_a, grad_b], full_qkv, resid_one_grad, wait=[qkv_b.send, a3, o2])
    sum_up = up.finish(input_grad)
    grads = [sums_a[i] if j == 0 else sums_b[i] for i in range(3) for j in range(2)]
    grad_bqkv = jnp.concatenate(grads, axis=1)
    small = pack(
        [grad_bqkv, sums1[2:3], sums1[0:1], sums1[1:2], grad_bup, sums2[2:3], sums2[0:1], sums2[1:2]],
        n_devices,
        wait=[input_grad],
    )
    small = scatter_small(small.reshape(n_devices, -1, LANES), f32).reshape(-1)
    sum_proj = scatter_small(
        after(grad_proj, input_grad).reshape(n_devices, -1, grad_proj.shape[1]), bf16
    )
    sum_out = out.finish()
    sum_a, sum_b = qkv_a.finish(), qkv_b.finish()
    width = sum_a.shape[1] // 3
    sum_qkv = jnp.concatenate(
        [x[:, i * width : (i + 1) * width] for i in range(3) for x in (sum_a, sum_b)], axis=1
    )
    pieces = []
    at = 0
    for width in widths:
        pieces.append(small[at : at + width])
        at += width
    s_bqkv, s_bout, s_gain1, s_bias1, s_bup, s_bdown, s_gain2, s_bias2 = pieces
    return (
        losses,
        result_low,
        input_grad,
        sum_qkv,
        s_bqkv,
        sum_out,
        s_bout,
        s_gain1,
        s_bias1,
        sum_up,
        s_bup,
        sum_down,
        s_bdown,
        s_gain2,
        s_bias2,
        sum_proj,
    )


def solution(mesh):
    shard = P(AXES, None)
    vec = P(AXES)
    in_specs = (
        shard,
        P(),
        P(),
        shard,
        vec,
        shard,
        vec,
        vec,
        vec,
        shard,
        vec,
        shard,
        vec,
        vec,
        vec,
        shard,
    )
    out_specs = (P(None, "row"), shard) + (shard,) + in_specs[3:]
    return jax.shard_map(
        on_device, mesh=mesh, in_specs=in_specs, out_specs=out_specs, check_vma=False
    )
```

time: 845 us -> 649 us (0.77)
  Pallas kernels: 70 us -> 345 us
  matrix products: 207 us -> 0 us
  local copies, waits for them, and re-layouts: 145 us -> 22.6 us
  waiting for transfers between devices: 222 us -> 134 us
  other arithmetic: 82.6 us -> 32.7 us
  starting transfers between devices: 87 us -> 105 us
  between operations: 18.9 us -> 2.29 us
    pallas_call x6 -> x26, Pallas kernels: 70 us -> 345 us  [call(): return lambda *operands: run(*operands, *wait)]
    dot_general x30 -> x0, matrix products: 207 us -> none  [the longest x8 75.1 us: matmul(): return jnp.dot(a, b, preferred_element_type=f32)]
    ppermute x91 -> x102, waiting for transfers between devices: 222 us -> 134 us  [exchange(): return lax.ppermute(value, AXES, pairs)]
    unnamed x214 -> x148, local copies, waits for them, and re-layouts: 38.7 us -> 8.16 us
    convert_element_type x11 -> x2, local copies, waits for them, and re-layouts: 24.5 us -> 0.04 us  [step(): held[m].astype(dtype)]
    convert_element_type x19 -> x11, other arithmetic: 23 us -> 4.19 us  [the longest x9 2.92 us: step(): self.send = self.send.astype(bf16)]
    another operation x14 -> x8, other arithmetic: 19.9 us -> 1.97 us  [the longest x2 1.13 us: gather_relative(): return jnp.stack([held, exchange(held, swap_core=True)])]
    ppermute x91 -> x102, starting transfers between devices: 87 us -> 105 us  [exchange(): return lax.ppermute(value, AXES, pairs)]
  transfers between devices with their start and end apart: 91 -> 102, of which waited for: 40 -> 42; matrix products, arithmetic and copies ran while one was open for 25% -> 6% of each run, Pallas kernels for 3% -> 38%
where the time goes in v2:
time: 649 us; the launch traced here: 641 us
  Pallas kernels  345 us (53%)
  waiting for transfers between devices  134 us (21%)
  starting transfers between devices  105 us (16%)
  other arithmetic  32.7 us (5%)
  local copies, waits for them, and re-layouts  22.6 us (3%)
    pallas_call x26, Pallas kernels, call(): return lambda *operands: run(*operands, *wait)  345 us
    ppermute x102, waiting for transfers between devices, exchange(): return lax.ppermute(value, AXES, pairs)  134 us
    ppermute x102, starting transfers between devices, exchange(): return lax.ppermute(value, AXES, pairs)  105 us
  transfers between devices with their start and end apart: 102, of which 42 were waited for; matrix products, arithmetic and copies ran while one was open for 6% of the time, Pallas kernels for 38%

profile of v2, /device:TPU:0, one launch (start us, length us, event | category | flops | bytes accessed | tf_op | source)
XLA Modules:
  0.0 641.2 jit_solution(1373848330613932573)
XLA Ops:
  0.7 4.1 collective-permute-start
  5.1 9.0 %collective-permute-done = bf16[32,3072]{1,0:T(8,128)(2,1)S(1)} collective-permute-done((bf16[32,3072]{1,0:T(8,128)(2,1)}, bf16[32,3072]{1,0:T(8,128)(2,1)S(1)}, u32[]{:S(2)}, u32[]{:S(2)}) %collective-permute-start) | collective-permute-done | bytes 196640 | tf_op jit(solution)/shard_map/ppermute | solution.py:56
  16.2 9.4 %collective-permute-done.1 = bf16[2,32,3072]{2,1,0:T(8,128)(2,1)S(1)} collective-permute-done((bf16[2,32,3072]{2,1,0:T(8,128)(2,1)S(1)}, bf16[2,32,3072]{2,1,0:T(8,128)(2,1)S(1)}, u32[]{:S(2)}, u32[]{:S(2)}) %collective-permute-start.1) | collective-permute-done | bytes 393248 | tf_op jit(solution)/shard_map/ppermute | solution.py:56
  25.9 3.1 collective-permute-start.2
  41.6 2.5 collective-permute-start.14
  44.2 11.7 %collective-permute-done.5 = bf16[2,2,2,4,128]{4,3,2,1,0:T(4,128)(2,1)S(1)} collective-permute-done((bf16[2,2,2,4,128]{4,3,2,1,0:T(4,128)(2,1)S(1)}, bf16[2,2,2,4,128]{4,3,2,1,0:T(4,128)(2,1)S(1)}, u32[]{:S(2)}, u32[]{:S(2)}) %collective-permute-start.5) | collective-permute-done | bytes 8224 | tf_op jit(solution)/shard_map/ppermute | solution.py:56
  71.5 9.0 %collective-permute-done.16 = bf16[32,4096]{1,0:T(8,128)(2,1)S(1)} collective-permute-done((bf16[32,4096]{1,0:T(8,128)(2,1)S(1)}, bf16[32,4096]{1,0:T(8,128)(2,1)S(1)}, u32[]{:S(2)}, u32[]{:S(2)}) %collective-permute-start.16) | collective-permute-done | bytes 262176 | tf_op jit(solution)/shard_map/ppermute | solution.py:56
  84.3 2.2 unpack.1
  88.8 7.1 %collective-permute-done.17 = bf16[2,32,4096]{2,1,0:T(8,128)(2,1)S(1)} collective-permute-done((bf16[2,32,4096]{2,1,0:T(8,128)(2,1)S(1)}, bf16[2,32,4096]{2,1,0:T(8,128)(2,1)S(1)}, u32[]{:S(2)}, u32[]{:S(2)}) %collective-permute-start.17) | collective-permute-done | bytes 524320 | tf_op jit(solution)/shard_map/ppermute | solution.py:56
  104.4 19.2 %project_qkv.1 = (bf16[1024,3072]{1,0:T(8,128)(2,1)}, bf16[4,4,2,32,3072]{4,3,2,1,0:T(8,128)(2,1)}) custom-call(s32[17]{0:T(128)} %concatenate.21.refs_0_, bf16[1024,1024]{1,0:T(8,128)(2,1)} %refs_1_.9, f32[1,3072]{1,0:T(1,128)} %get-tuple-element.134.refs_2_, f32[1024,128]{1,0:T(8,128)} %get-tuple-element.344.refs_3_.refs_5_, ...), custom_call_target="tpu_custom_call" | custom-call | flops 6442450944 | bytes 20971520 | tf_op jit(solution)/shard_map/project_qkv/pallas_call | solution.py:334
  123.5 4.9 collective-permute-done.27.refs_9_
  132.0 19.4 %attention.1.refs_1_ = bf16[1024,1024]{1,0:T(8,128)(2,1)} custom-call(s32[4]{0:T(128)} %bitcast.565, bf16[1024,3072]{1,0:T(8,128)(2,1)} %get-tuple-element.140.refs_1_.refs_2_.refs_3_, bf16[1024,3072]{1,0:T(8,128)(2,1)} %get-tuple-element.140.refs_1_.refs_2_.refs_3_, bf16[1024,3072]{1,0:T(8,128)(2,1)} %get-tuple-element.140.refs_1_.refs_2_.refs_3_, ...), custom_call_target="tpu_custom_call" | custom-call | flops 20000000000 | bytes 8388608 | tf_op jit(solution)/shard_map/attention/pallas_call | solution.py:334
  156.9 9.7 %out_norm.1 = (f32[1024,1024]{1,0:T(8,128)}, f32[1024,128]{1,0:T(8,128)}, bf16[1024,1024]{1,0:T(8,128)(2,1)}, bf16[4,4,2,32,1024]{4,3,2,1,0:T(8,128)(2,1)}) custom-call(s32[17]{0:T(128)} %concatenate.21.refs_0_, bf16[1024,1024]{1,0:T(8,128)(2,1)} %attention.1.refs_1_, f32[1,1024]{1,0:T(1,128)} %get-tuple-element.145.refs_2_, bf16[1024,1024]{1,0:T(8,128)(2,1)} %refs_1_.9, ...), custom_call_target="tpu_custom_call" | custom-call | flops 2147483648 | bytes 12582912 | tf_op jit(solution)/shard_map/out_norm/pallas_call | solution.py:334
  169.1 19.8 %up_gelu.2 = (bf16[1024,4096]{1,0:T(8,128)(2,1)}, bf16[1024,4096]{1,0:T(8,128)(2,1)}, bf16[4,4,2,32,4096]{4,3,2,1,0:T(8,128)(2,1)}) custom-call(s32[17]{0:T(128)} %concatenate.21.refs_0_, bf16[1024,1024]{1,0:T(8,128)(2,1)} %get-tuple-element.157.refs_1_, f32[1,4096]{1,0:T(1,128)} %get-tuple-element.158.refs_2_, bf16[4,32,4096]{2,1,0:T(8,128)(2,1)} %bitcast.43.refs_3_, ...), custom_call_target="tpu_custom_call" | custom-call | flops 4294967296 | bytes 12582912 | tf_op jit(solution)/shard_map/up_gelu/pallas_call | solution.py:334
  191.2 19.6 %up_gelu.3 = (bf16[1024,4096]{1,0:T(8,128)(2,1)}, bf16[1024,4096]{1,0:T(8,128)(2,1)}, bf16[4,4,2,32,4096]{4,3,2,1,0:T(8,128)(2,1)}) custom-call(s32[17]{0:T(128)} %concatenate.21.refs_0_, bf16[1024,1024]{1,0:T(8,128)(2,1)} %get-tuple-element.157.refs_1_, ...), custom_call_target="tpu_custom_call", output_to_operand_aliasing={{0}: (11, {}), {1}: (12, {}), {2}: (13, {})} | custom-call | flops 4294967296 | bytes 12582912 | tf_op jit(solution)/shard_map/up_gelu/pallas_call | solution.py:334
  211.5 2.5 collective-permute-done.45.refs_16_
  214.0 20.6 %down_norm.1 = (f32[1024,1024]{1,0:T(8,128)}, f32[1024,128]{1,0:T(8,128)}, bf16[1024,1024]{1,0:T(8,128)(2,1)}, f32[1024,288]{1,0:T(8,128)}, bf16[1024,288]{1,0:T...) custom-call(s32[17]{0:T(128)} %concatenate.21.refs_0_, bf16[1024,4096]{1,0:T(8,128)(2,1)} %get-tuple-element.172.refs_1_, ...), custom_call_target="tpu_custom_call" | custom-call | flops 8589934592 | bytes 20971520 | tf_op jit(solution)/shard_map/down_norm/pallas_call | solution.py:334
  237.5 2.3 collective-permute-start.48
  240.5 2.6 collective-permute-done.48
  244.5 2.2 collective-permute-start.51
  253.6 13.4 %scores.1 = (f32[3,8,1024]{2,1,0:T(8,128)}, f32[3,8,32]{2,1,0:T(8,128)}, f32[3,3,32]{2,1,0:T(4,128)}) custom-call(bf16[992,288]{1,0:T(8,128)(2,1)} %slice.266.refs_0_, bf16[1024,288]{1,0:T(8,128)(2,1)} %bitcast.541, s32[1024,1]{1,0:T(8,128)} %add.655.refs_2_, bf16[8,992]{1,0:T(8,128)(2,1)} %fusion.29.refs_3_, f32[8,128]{1,0:T(8,128)} %broadcast_in_dim.42.refs_4_, ...), custom_call_target="tpu_custom_call" | custom-call | flops 3510632448 | bytes 1000000 | tf_op jit(solution)/shard_map/scores/pallas_call | solution.py:334
  274.4 2.3 collective-permute-done.56
  276.8 2.9 collective-permute-start.58
  282.9 2.3 collective-permute-done.59
  285.8 17.7 %score_grads.1 = (f32[1024,288]{1,0:T(8,128)}, f32[992,288]{1,0:T(8,128)}) custom-call(bf16[992,288]{1,0:T(8,128)(2,1)} %slice.266.refs_0_, bf16[1024,288]{1,0:T(8,128)(2,1)} %bitcast.542, s32[1,1024]{1,0:T(1,128)} %add.576.refs_2_, s32[992,1]{1,0:T(8,128)} %copy.107.refs_3_, f32[3,8,1024]{2,1,0:T(8,128)} %get-tuple-element.187.refs_4_, ...), custom_call_target="tpu_custom_call" | custom-call | flops 7021264896 | bytes 1000000 | tf_op jit(solution)/shard_map/score_grads/pallas_call | solution.py:334
  308.0 2.2 collective-permute-start.63
  310.2 2.0 collective-permute-done.61
  314.1 2.0 collective-permute-start.65
  316.1 2.4 collective-permute-start.66
  318.9 2.8 collective-permute-done.66
  323.1 11.2 %head_back.1 = (f32[1024,1024]{1,0:T(8,128)}, bf16[1024,1024]{1,0:T(8,128)(2,1)}, f32[1024,288]{1,0:T(8,128)}, f32[3,1024]{1,0:T(4,128)}) custom-call(f32[1024,288]{1,0:T(8,128)} %pad_maximum_fusion.refs_0_, f32[1024,288]{1,0:T(8,128)} %get-tuple-element.191.refs_1_, bf16[1024,1024]{1,0:T(8,128)(2,1)} %get-tuple-element.111.refs_2_, ...), custom_call_target="tpu_custom_call" | custom-call | flops 1207959552 | bytes 16777216 | tf_op jit(solution)/shard_map/head_back/pallas_call | solution.py:334
  334.3 12.7 %grad_down_sib.1.refs_3_ = bf16[4,4,128,1024]{3,2,1,0:T(8,128)(2,1)} custom-call(s32[17]{0:T(128)} %concatenate.21.refs_0_, bf16[1024,4096]{1,0:T(8,128)(2,1)} %get-tuple-element.172.refs_1_, bf16[1024,1024]{1,0:T(8,128)(2,1)} %get-tuple-element.194.refs_2_.refs_0_), custom_call_target="tpu_custom_call" | custom-call | flops 4294967296 | bytes 23068672 | tf_op jit(solution)/shard_map/grad_down_sib/pallas_call | solution.py:334
  347.0 14.9 %act_back.1 = (bf16[1024,4096]{1,0:T(8,128)(2,1)}, f32[1,4096]{1,0:T(1,128)}) custom-call(bf16[1024,1024]{1,0:T(8,128)(2,1)} %get-tuple-element.194.refs_2_.refs_0_, bf16[4096,1024]{1,0:T(8,128)(2,1)} %bitcast.569, bf16[1024,4096]{1,0:T(8,128)(2,1)} %get-tuple-element.196.refs_2_, bf16[4,4,128,1024]{3,2,1,0:T(8,128)(2,1)} %grad_down_sib.1.refs_3_), custom_call_target="tpu_custom_call" | custom-call | flops 8589934592 | bytes 25165824 | tf_op jit(solution)/shard_map/act_back/pallas_call | solution.py:334
  363.9 13.4 %grad_down.1 = (bf16[2,4,128,1024]{3,2,1,0:T(8,128)(2,1)}, f32[2,4,128,1024]{3,2,1,0:T(8,128)}) custom-call(s32[17]{0:T(128)} %concatenate.21.refs_0_, bf16[1024,4096]{1,0:T(8,128)(2,1)} %get-tuple-element.172.refs_1_, bf16[1024,1024]{1,0:T(8,128)(2,1)} %get-tuple-element.194.refs_2_.refs_0_, bf16[4,4,128,1024]{3,2,1,0:T(8,128)(2,1)} %copy-done.56, ...), custom_call_target="tpu_custom_call" | custom-call | flops 4294967296 | bytes 23068672 | tf_op jit(solution)/shard_map/grad_down/pallas_call | solution.py:334
  377.3 11.7 %grad_up_sib.1.refs_7_ = f32[4,4,32,4096]{3,2,1,0:T(8,128)} custom-call(s32[17]{0:T(128)} %concatenate.21.refs_0_, bf16[1024,1024]{1,0:T(8,128)(2,1)} %get-tuple-element.157.refs_1_, bf16[1024,4096]{1,0:T(8,128)(2,1)} %get-tuple-element.197.refs_2_.refs_0_, bf16[2,4,128,1024]{3,2,1,0:T(8,128)(2,1)} %get-tuple-element.203.refs_3_), custom_call_target="tpu_custom_call" | custom-call | flops 4294967296 | bytes 23068672 | tf_op jit(solution)/shard_map/grad_up_sib/pallas_call | solution.py:334
  390.6 20.6 %hidden_back.1 = (f32[1024,1024]{1,0:T(8,128)}, bf16[1024,1024]{1,0:T(8,128)(2,1)}, bf16[1024,1024]{1,0:T(8,128)(2,1)}, f32[3,1024]{1,0:T(4,128)}) custom-call(bf16[1024,4096]{1,0:T(8,128)(2,1)} %get-tuple-element.197.refs_2_.refs_0_, bf16[1024,4096]{1,0:T(8,128)(2,1)} %bitcast.520, f32[1024,1024]{1,0:T(8,128)} %get-tuple-element.199.refs_2_, ...), custom_call_target="tpu_custom_call" | custom-call | flops 10737418240 | bytes 33554432 | tf_op jit(solution)/shard_map/hidden_back/pallas_call | solution.py:334
  411.2 4.7 collective-permute-done.69
  415.9 2.5 convert_add_fusion.1
  421.2 13.1 %grad_up.1 = (bf16[2,4,32,4096]{3,2,1,0:T(8,128)(2,1)}, f32[2,4,32,4096]{3,2,1,0:T(8,128)}) custom-call(s32[17]{0:T(128)} %concatenate.21.refs_0_, bf16[1024,1024]{1,0:T(8,128)(2,1)} %get-tuple-element.157.refs_1_, bf16[1024,4096]{1,0:T(8,128)(2,1)} %get-tuple-element.197.refs_2_.refs_0_, f32[4,4,32,4096]{3,2,1,0:T(8,128)} %collective-permute-done.68.refs_3_, ...), custom_call_target="tpu_custom_call" | custom-call | flops 4294967296 | bytes 23068672 | tf_op jit(solution)/shard_map/grad_up/pallas_call | solution.py:334
  436.2 23.8 %attention_back.2 = (bf16[3,1024,512]{2,1,0:T(8,128)(2,1)}, f32[3,1,512]{2,1,0:T(1,128)}) custom-call(s32[4]{0:T(128)} %bitcast.566, bf16[1024,3072]{1,0:T(8,128)(2,1)} %get-tuple-element.140.refs_1_.refs_2_.refs_3_, bf16[1024,3072]{1,0:T(8,128)(2,1)} %get-tuple-element.140.refs_1_.refs_2_.refs_3_, ...), custom_call_target="tpu_custom_call" | custom-call | flops 24999999488 | bytes 7340032 | tf_op jit(solution)/shard_map/attention_back/pallas_call | solution.py:334
  460.1 7.1 %grad_qkv_sib.2.refs_3_ = bf16[4,4,32,1536]{3,2,1,0:T(8,128)(2,1)} custom-call(s32[17]{0:T(128)} %concatenate.21.refs_0_, bf16[1024,1024]{1,0:T(8,128)(2,1)} %refs_1_.9, bf16[3,1024,512]{2,1,0:T(8,128)(2,1)} %get-tuple-element.210.refs_2_.refs_0_), custom_call_target="tpu_custom_call" | custom-call | flops 1610612736 | bytes 9961472 | tf_op jit(solution)/shard_map/grad_qkv_sib/pallas_call | solution.py:334
  467.1 5.7 grad_out_sib.1.refs_7_
  476.5 2.0 collective-permute-start.96
  478.5 3.1 convert_add_fusion
  482.4 23.8 %attention_back.3 = (bf16[3,1024,512]{2,1,0:T(8,128)(2,1)}, f32[3,1,512]{2,1,0:T(1,128)}) custom-call(s32[4]{0:T(128)} %bitcast.567, bf16[1024,3072]{1,0:T(8,128)(2,1)} %get-tuple-element.140.refs_1_.refs_2_.refs_3_, bf16[1024,3072]{1,0:T(8,128)(2,1)} %get-tuple-element.140.refs_1_.refs_2_.refs_3_, ...), custom_call_target="tpu_custom_call" | custom-call | flops 24999999488 | bytes 7340032 | tf_op jit(solution)/shard_map/attention_back/pallas_call | solution.py:334
  506.2 7.4 %grad_qkv.2 = (bf16[2,4,32,1536]{3,2,1,0:T(8,128)(2,1)}, f32[2,4,32,1536]{3,2,1,0:T(8,128)}) custom-call(s32[17]{0:T(128)} %concatenate.21.refs_0_, bf16[1024,1024]{1,0:T(8,128)(2,1)} %refs_1_.9, bf16[3,1024,512]{2,1,0:T(8,128)(2,1)} %get-tuple-element.210.refs_2_.refs_0_, bf16[4,4,32,1536]{3,2,1,0:T(8,128)(2,1)} %collective-permute-done.74.refs_3_, ...), custom_call_target="tpu_custom_call" | custom-call | flops 1610612736 | bytes 9961472 | tf_op jit(solution)/shard_map/grad_qkv/pallas_call | solution.py:334
  515.5 5.5 grad_out.1
  521.1 7.2 %grad_qkv_sib.3 = bf16[4,4,32,1536]{3,2,1,0:T(8,128)(2,1)} custom-call(s32[17]{0:T(128)} %concatenate.21.refs_0_, bf16[1024,1024]{1,0:T(8,128)(2,1)} %refs_1_.9, bf16[3,1024,512]{2,1,0:T(8,128)(2,1)} %get-tuple-element.216.refs_2_.refs_1_, bf16[2,4,32,1024]{3,2,1,0:T(8,128)(2,1)} %get-tuple-element.222.refs_3_), custom_call_target="tpu_custom_call" | custom-call | flops 1610612736 | bytes 9961472 | tf_op jit(solution)/shard_map/grad_qkv_sib/pallas_call | solution.py:334
  532.1 10.6 %collective-permute-done.77 = bf16[2,32,4096]{2,1,0:T(8,128)(2,1)S(1)} collective-permute-done((bf16[2,32,4096]{2,1,0:T(8,128)(2,1)S(1)}, bf16[2,32,4096]{2,1,0:T(8,128)(2,1)S(1)}, u32[]{:S(2)}, u32[]{:S(2)}) %collective-permute-start.77) | collective-permute-done | bytes 524320 | tf_op jit(solution)/shard_map/ppermute | solution.py:56
  544.3 7.4 %grad_qkv.3 = (bf16[2,4,32,1536]{3,2,1,0:T(8,128)(2,1)}, f32[2,4,32,1536]{3,2,1,0:T(8,128)}) custom-call(s32[17]{0:T(128)} %concatenate.21.refs_0_, bf16[1024,1024]{1,0:T(8,128)(2,1)} %refs_1_.9, bf16[3,1024,512]{2,1,0:T(8,128)(2,1)} %get-tuple-element.216.refs_2_.refs_1_, bf16[4,4,32,1536]{3,2,1,0:T(8,128)(2,1)} %collective-permute-done.76.refs_3_, ...), custom_call_target="tpu_custom_call" | custom-call | flops 1610612736 | bytes 9961472 | tf_op jit(solution)/shard_map/grad_qkv/pallas_call | solution.py:334
  551.8 2.2 convert_add_fusion.7
  554.7 12.2 %input_back.1.refs_8_ = f32[1024,1024]{1,0:T(8,128)} custom-call(bf16[3,1024,512]{2,1,0:T(8,128)(2,1)} %get-tuple-element.210.refs_2_.refs_0_, bf16[3,1024,512]{2,1,0:T(8,128)(2,1)} %get-tuple-element.216.refs_2_.refs_1_, bf16[1024,3072]{1,0:T(8,128)(2,1)} %bitcast.570, f32[1024,1024]{1,0:T(8,128)} %get-tuple-element.218.refs_3_, ...), custom_call_target="tpu_custom_call" | custom-call | flops 6442450944 | bytes 20971520 | tf_op jit(solution)/shard_map/input_back/pallas_call | solution.py:334
  567.0 5.2 pack.1
  575.9 2.0 bitcast_add_fusion.3
  581.7 11.1 %collective-permute-done.95 = bf16[32,4096]{1,0:T(8,128)(2,1)S(1)} collective-permute-done((bf16[32,4096]{1,0:T(8,128)(2,1)}, bf16[32,4096]{1,0:T(8,128)(2,1)S(1)}, u32[]{:S(2)}, u32[]{:S(2)}) %collective-permute-start.95) | collective-permute-done | bytes 262176 | tf_op jit(solution)/shard_map/ppermute | solution.py:56
  602.7 2.5 collective-permute-done.81
  607.2 4.0 collective-permute-done.82
  613.2 2.1 collective-permute-start.94
  615.3 2.7 collective-permute-done.99
  622.3 2.4 collective-permute-start.101
  624.7 2.7 collective-permute-done.84
  628.4 5.1 collective-permute-done.85
  633.5 2.6 collective-permute-start.86
  636.8 3.3 collective-permute-done.86
  (455 shorter events, 139.2 us)
Async XLA Ops:
  0.7 13.4 %collective-permute-start = (bf16[32,3072]{1,0:T(8,128)(2,1)}, bf16[32,3072]{1,0:T(8,128)(2,1)S(1)}, u32[]{:S(2)}, u32[]{:S(2)}) collective-permute-start(bf16[32,3072]{1,0:T(8,128)(2,1)} %param.21), channel_id=1, source_target_pairs={{0,4},{1,5},{2,6},{3,7},{4,0},{5,1},{6,2},{7,3},{8,12},{9,13},{10,... | collective-permute-start | bytes 589832 | tf_op jit(solution)/shard_map/ppermute | solution.py:56
  15.2 10.4 %collective-permute-start.1 = (bf16[2,32,3072]{2,1,0:T(8,128)(2,1)S(1)}, bf16[2,32,3072]{2,1,0:T(8,128)(2,1)S(1)}, u32[]{:S(2)}, u32[]{:S(2)}) collective-permute-start(bf16[2,32,3072]{2,1,0:T(8,128)(2,1)S(1)} %pad_maximum_fusion.10), channel_id=1, source_target_pairs={{0,2},{1,3},{2,0},{3,1},{4,6},{5,7},{6,4},{7,5},{8,10},{9,11},{10,... | collective-permute-start | bytes 1179656 | tf_op jit(solution)/shard_map/ppermute | solution.py:56
  38.2 17.9 %collective-permute-start.7 = (bf16[4,32,3072]{2,1,0:T(8,128)(2,1)S(1)}, bf16[4,32,3072]{2,1,0:T(8,128)(2,1)S(1)}, u32[]{:S(2)}, u32[]{:S(2)}) collective-permute-start(bf16[4,32,3072]{2,1,0:T(8,128)(2,1)S(1)} %bitcast.537), channel_id=1, source_target_pairs={{0,8},{1,17},{2,10},{3,19},{4,12},{5,21},{6,14},{7,23},{8,0},{9,25... | collective-permute-start | bytes 2359304 | tf_op jit(solution)/shard_map/ppermute | solution.py:56
  39.7 16.3 %collective-permute-start.8 = (bf16[4,32,3072]{2,1,0:T(8,128)(2,1)S(1)}, bf16[4,32,3072]{2,1,0:T(8,128)(2,1)}, u32[]{:S(2)}, u32[]{:S(2)}) collective-permute-start(bf16[4,32,3072]{2,1,0:T(8,128)(2,1)S(1)} %bitcast.538), channel_id=1, source_target_pairs={{0,16},{1,9},{2,18},{3,11},{4,20},{5,13},{6,22},{7,15},{8,24},{9,1... | collective-permute-start | bytes 2359304 | tf_op jit(solution)/shard_map/ppermute | solution.py:56
  40.3 15.6 %collective-permute-start.5 = (bf16[2,2,2,4,128]{4,3,2,1,0:T(4,128)(2,1)S(1)}, bf16[2,2,2,4,128]{4,3,2,1,0:T(4,128)(2,1)S(1)}, u32[]{:S(2)}, u32[]{:S(2)}) collective-permute-start(bf16[2,2,2,4,128]{4,3,2,1,0:T(4,128)(2,1)S(1)} %pad_maximum_fusion.21), channel_id=1, source_target_pairs={{0,8},{1,9},{2,10},{3,11},{4,12},{5,13},{6,14},{7,15},{8,0},{9,1},... | collective-permute-start | bytes 24584 | tf_op jit(solution)/shard_map/ppermute | solution.py:56
  41.6 56.9 %collective-permute-start.10 = (bf16[4,32,3072]{2,1,0:T(8,128)(2,1)S(1)}, bf16[4,32,3072]{2,1,0:T(8,128)(2,1)S(1)}, u32[]{:S(2)}, u32[]{:S(2)}) collective-permute-start(bf16[4,32,3072]{2,1,0:T(8,128)(2,1)S(1)} %bitcast.539), channel_id=1, source_target_pairs={{0,1},{1,0},{2,3},{3,2},{4,5},{5,4},{6,7},{7,6},{8,9},{9,8},{10,11... | collective-permute-start | bytes 2359304 | tf_op jit(solution)/shard_map/ppermute | solution.py:56
  41.6 14.4 %collective-permute-start.14 = (bf16[32,1024]{1,0:T(8,128)(2,1)S(1)}, bf16[32,1024]{1,0:T(8,128)(2,1)S(1)}, u32[]{:S(2)}, u32[]{:S(2)}) collective-permute-start(bf16[32,1024]{1,0:T(8,128)(2,1)S(1)} %copy-done.36), channel_id=1, source_target_pairs={{0,4},{1,5},{2,6},{3,7},{4,0},{5,1},{6,2},{7,3},{8,12},{9,13},{10,... | collective-permute-start | bytes 196616 | tf_op jit(solution)/shard_map/ppermute | solution.py:56
  55.9 27.7 %collective-permute-start.6 = (bf16[2,2,2,2,4,128]{5,4,3,2,1,0:T(4,128)(2,1)S(1)}, bf16[2,2,2,2,4,128]{5,4,3,2,1,0:T(4,128)(2,1)S(1)}, u32[]{:S(2)}, u32[]{:S(2)}) collective-permute-start(bf16[2,2,2,2,4,128]{5,4,3,2,1,0:T(4,128)(2,1)S(1)} %pad_maximum_fusion.20), channel_id=1, source_target_pairs={{0,1},{1,0},{2,3},{3,2},{4,5},{5,4},{6,7},{7,6},{8,9},{9,8},{10,11... | collective-permute-start | bytes 49160 | tf_op jit(solution)/shard_map/ppermute | solution.py:56
  66.8 13.7 %collective-permute-start.16 = (bf16[32,4096]{1,0:T(8,128)(2,1)S(1)}, bf16[32,4096]{1,0:T(8,128)(2,1)S(1)}, u32[]{:S(2)}, u32[]{:S(2)}) collective-permute-start(bf16[32,4096]{1,0:T(8,128)(2,1)S(1)} %copy-done.33), channel_id=1, source_target_pairs={{0,4},{1,5},{2,6},{3,7},{4,0},{5,1},{6,2},{7,3},{8,12},{9,13},{10,... | collective-permute-start | bytes 786440 | tf_op jit(solution)/shard_map/ppermute | solution.py:56
  68.5 13.4 %collective-permute-start.9 = (bf16[4,32,3072]{2,1,0:T(8,128)(2,1)S(1)}, bf16[4,32,3072]{2,1,0:T(8,128)(2,1)S(1)}, u32[]{:S(2)}, u32[]{:S(2)}) collective-permute-start(bf16[4,32,3072]{2,1,0:T(8,128)(2,1)S(1)} %collective-permute-done.7.refs_6_), channel_id=1, source_target_pairs={{0,16},{1,9},{2,18},{3,11},{4,20},{5,13},{6,22},{7,15},{8,24},{9,1... | collective-permute-start | bytes 2359304 | tf_op jit(solution)/shard_map/ppermute | solution.py:56
  69.9 10.7 %collective-permute-start.21 = (bf16[2,2,2,32,288]{4,3,1,2,0:T(8,128)(2,1)S(1)}, bf16[2,2,2,32,288]{4,3,1,2,0:T(8,128)(2,1)S(1)}, u32[]{:S(2)}, u32[]{:S(2)}) collective-permute-start(bf16[2,2,2,32,288]{4,3,1,2,0:T(8,128)(2,1)S(1)} %pad_maximum_fusion.14), channel_id=1, source_target_pairs={{0,8},{1,9},{2,10},{3,11},{4,12},{5,13},{6,14},{7,15},{8,0},{9,1},... | collective-permute-start | bytes 442376 | tf_op jit(solution)/shard_map/ppermute | solution.py:56
  80.7 7.4 %collective-permute-start.22 = (bf16[2,2,2,2,32,288]{5,4,2,3,0,1:T(8,128)(2,1)S(1)}, bf16[2,2,2,2,32,288]{5,4,2,3,0,1:T(8,128)(2,1)S(1)}, u32[]{:S(2)}, u32[]{:S(2)}) collective-permute-start(bf16[2,2,2,2,32,288]{5,4,2,3,0,1:T(8,128)(2,1)S(1)} %pad_maximum_fusion.11), channel_id=1, source_target_pairs={{0,1},{1,0},{2,3},{3,2},{4,5},{5,4},{6,7},{7,6},{8,9},{9,8},{10,11... | collective-permute-start | bytes 884744 | tf_op jit(solution)/shard_map/ppermute | solution.py:56
  81.9 13.9 %collective-permute-start.17 = (bf16[2,32,4096]{2,1,0:T(8,128)(2,1)S(1)}, bf16[2,32,4096]{2,1,0:T(8,128)(2,1)S(1)}, u32[]{:S(2)}, u32[]{:S(2)}) collective-permute-start(bf16[2,32,4096]{2,1,0:T(8,128)(2,1)S(1)} %pad_maximum_fusion.8), channel_id=1, source_target_pairs={{0,2},{1,3},{2,0},{3,1},{4,6},{5,7},{6,4},{7,5},{8,10},{9,11},{10,... | collective-permute-start | bytes 1572872 | tf_op jit(solution)/shard_map/ppermute | solution.py:56
  86.6 10.4 %collective-permute-start.23 = (bf16[4,32,1024]{2,1,0:T(8,128)(2,1)S(1)}, bf16[4,32,1024]{2,1,0:T(8,128)(2,1)S(1)}, u32[]{:S(2)}, u32[]{:S(2)}) collective-permute-start(bf16[4,32,1024]{2,1,0:T(8,128)(2,1)S(1)} %bitcast.549), channel_id=1, source_target_pairs={{0,8},{1,17},{2,10},{3,19},{4,12},{5,21},{6,14},{7,23},{8,0},{9,25... | collective-permute-start | bytes 786440 | tf_op jit(solution)/shard_map/ppermute | solution.py:56
  88.1 12.1 %collective-permute-start.11 = (bf16[4,32,3072]{2,1,0:T(8,128)(2,1)S(1)}, bf16[4,32,3072]{2,1,0:T(8,128)(2,1)S(1)}, u32[]{:S(2)}, u32[]{:S(2)}) collective-permute-start(bf16[4,32,3072]{2,1,0:T(8,128)(2,1)S(1)} %collective-permute-done.7.refs_6_), channel_id=1, source_target_pairs={{0,1},{1,0},{2,3},{3,2},{4,5},{5,4},{6,7},{7,6},{8,9},{9,8},{10,11... | collective-permute-start | bytes 2359304 | tf_op jit(solution)/shard_map/ppermute | solution.py:56
  88.1 13.6 %collective-permute-start.12 = (bf16[4,32,3072]{2,1,0:T(8,128)(2,1)}, bf16[4,32,3072]{2,1,0:T(8,128)(2,1)S(1)}, u32[]{:S(2)}, u32[]{:S(2)}) collective-permute-start(bf16[4,32,3072]{2,1,0:T(8,128)(2,1)} %collective-permute-done.8.refs_7_), channel_id=1, source_target_pairs={{0,1},{1,0},{2,3},{3,2},{4,5},{5,4},{6,7},{7,6},{8,9},{9,8},{10,11... | collective-permute-start | bytes 2359304 | tf_op jit(solution)/shard_map/ppermute | solution.py:56
  95.8 6.4 collective-permute-start.13
  97.0 32.1 %collective-permute-start.24 = (bf16[4,32,4096]{2,1,0:T(8,128)(2,1)}, bf16[4,32,4096]{2,1,0:T(8,128)(2,1)S(1)}, u32[]{:S(2)}, u32[]{:S(2)}) collective-permute-start(bf16[4,32,4096]{2,1,0:T(8,128)(2,1)} %bitcast.43.refs_3_), channel_id=1, source_target_pairs={{0,8},{1,17},{2,10},{3,19},{4,12},{5,21},{6,14},{7,23},{8,0},{9,25... | collective-permute-start | bytes 3145736 | tf_op jit(solution)/shard_map/ppermute | solution.py:56
  98.5 32.5 %collective-permute-start.25 = (bf16[4,32,4096]{2,1,0:T(8,128)(2,1)}, bf16[4,32,4096]{2,1,0:T(8,128)(2,1)S(1)}, u32[]{:S(2)}, u32[]{:S(2)}) collective-permute-start(bf16[4,32,4096]{2,1,0:T(8,128)(2,1)} %bitcast.43.refs_3_), channel_id=1, source_target_pairs={{0,16},{1,9},{2,18},{3,11},{4,20},{5,13},{6,22},{7,15},{8,24},{9,1... | collective-permute-start | bytes 3145736 | tf_op jit(solution)/shard_map/ppermute | solution.py:56
  100.2 28.3 %collective-permute-start.26 = (bf16[4,32,1024]{2,1,0:T(8,128)(2,1)S(1)}, bf16[4,32,1024]{2,1,0:T(8,128)(2,1)S(1)}, u32[]{:S(2)}, u32[]{:S(2)}) collective-permute-start(bf16[4,32,1024]{2,1,0:T(8,128)(2,1)S(1)} %bitcast.550), channel_id=1, source_target_pairs={{0,16},{1,9},{2,18},{3,11},{4,20},{5,13},{6,22},{7,15},{8,24},{9,1... | collective-permute-start | bytes 786440 | tf_op jit(solution)/shard_map/ppermute | solution.py:56
  101.7 26.7 %collective-permute-start.27 = (bf16[4,32,1024]{2,1,0:T(8,128)(2,1)S(1)}, bf16[4,32,1024]{2,1,0:T(8,128)(2,1)S(1)}, u32[]{:S(2)}, u32[]{:S(2)}) collective-permute-start(bf16[4,32,1024]{2,1,0:T(8,128)(2,1)S(1)} %collective-permute-done.23.refs_7_), channel_id=1, source_target_pairs={{0,16},{1,9},{2,18},{3,11},{4,20},{5,13},{6,22},{7,15},{8,24},{9,1... | collective-permute-start | bytes 786440 | tf_op jit(solution)/shard_map/ppermute | solution.py:56
  102.6 26.3 %collective-permute-start.32 = (bf16[128,1024]{1,0:T(8,128)(2,1)S(1)}, bf16[128,1024]{1,0:T(8,128)(2,1)S(1)}, u32[]{:S(2)}, u32[]{:S(2)}) collective-permute-start(bf16[128,1024]{1,0:T(8,128)(2,1)S(1)} %copy-done.34), channel_id=1, source_target_pairs={{0,4},{1,5},{2,6},{3,7},{4,0},{5,1},{6,2},{7,3},{8,12},{9,13},{10,... | collective-permute-start | bytes 786440 | tf_op jit(solution)/shard_map/ppermute | solution.py:56
  128.4 23.7 %collective-permute-start.31 = (bf16[4,32,1024]{2,1,0:T(8,128)(2,1)S(1)}, bf16[4,32,1024]{2,1,0:T(8,128)(2,1)S(1)}, u32[]{:S(2)}, u32[]{:S(2)}) collective-permute-start(bf16[4,32,1024]{2,1,0:T(8,128)(2,1)S(1)} %collective-permute-done.27.refs_9_), channel_id=1, source_target_pairs={{0,1},{1,0},{2,3},{3,2},{4,5},{5,4},{6,7},{7,6},{8,9},{9,8},{10,11... | collective-permute-start | bytes 786440 | tf_op jit(solution)/shard_map/ppermute | solution.py:56
  128.5 23.8 %collective-permute-start.30 = (bf16[4,32,1024]{2,1,0:T(8,128)(2,1)S(1)}, bf16[4,32,1024]{2,1,0:T(8,128)(2,1)}, u32[]{:S(2)}, u32[]{:S(2)}) collective-permute-start(bf16[4,32,1024]{2,1,0:T(8,128)(2,1)S(1)} %collective-permute-done.26.refs_8_), channel_id=1, source_target_pairs={{0,1},{1,0},{2,3},{3,2},{4,5},{5,4},{6,7},{7,6},{8,9},{9,8},{10,11... | collective-permute-start | bytes 786440 | tf_op jit(solution)/shard_map/ppermute | solution.py:56
  128.9 23.7 %collective-permute-start.29 = (bf16[4,32,1024]{2,1,0:T(8,128)(2,1)S(1)}, bf16[4,32,1024]{2,1,0:T(8,128)(2,1)S(1)}, u32[]{:S(2)}, u32[]{:S(2)}) collective-permute-start(bf16[4,32,1024]{2,1,0:T(8,128)(2,1)S(1)} %collective-permute-done.23.refs_7_), channel_id=1, source_target_pairs={{0,1},{1,0},{2,3},{3,2},{4,5},{5,4},{6,7},{7,6},{8,9},{9,8},{10,11... | collective-permute-start | bytes 786440 | tf_op jit(solution)/shard_map/ppermute | solution.py:56
  129.2 22.3 %collective-permute-start.33 = (bf16[2,128,1024]{2,1,0:T(8,128)(2,1)S(1)}, bf16[2,128,1024]{2,1,0:T(8,128)(2,1)S(1)}, u32[]{:S(2)}, u32[]{:S(2)}) collective-permute-start(bf16[2,128,1024]{2,1,0:T(8,128)(2,1)S(1)} %pad_maximum_fusion.9), channel_id=1, source_target_pairs={{0,2},{1,3},{2,0},{3,1},{4,6},{5,7},{6,4},{7,5},{8,10},{9,11},{10,... | collective-permute-start | bytes 1572872 | tf_op jit(solution)/shard_map/ppermute | solution.py:56
  131.0 20.8 %collective-permute-start.34 = (bf16[4,32,4096]{2,1,0:T(8,128)(2,1)S(1)}, bf16[4,32,4096]{2,1,0:T(8,128)(2,1)S(1)}, u32[]{:S(2)}, u32[]{:S(2)}) collective-permute-start(bf16[4,32,4096]{2,1,0:T(8,128)(2,1)S(1)} %collective-permute-done.24.refs_4_), channel_id=1, source_target_pairs={{0,16},{1,9},{2,18},{3,11},{4,20},{5,13},{6,22},{7,15},{8,24},{9,1... | collective-permute-start | bytes 3145736 | tf_op jit(solution)/shard_map/ppermute | solution.py:56
  151.4 15.2 %collective-permute-start.35 = (bf16[4,32,4096]{2,1,0:T(8,128)(2,1)}, bf16[4,32,4096]{2,1,0:T(8,128)(2,1)S(1)}, u32[]{:S(2)}, u32[]{:S(2)}) collective-permute-start(bf16[4,32,4096]{2,1,0:T(8,128)(2,1)} %bitcast.43.refs_3_), channel_id=1, source_target_pairs={{0,1},{1,0},{2,3},{3,2},{4,5},{5,4},{6,7},{7,6},{8,9},{9,8},{10,11... | collective-permute-start | bytes 3145736 | tf_op jit(solution)/shard_map/ppermute | solution.py:56
  152.1 15.3 %collective-permute-start.37 = (bf16[4,32,4096]{2,1,0:T(8,128)(2,1)}, bf16[4,32,4096]{2,1,0:T(8,128)(2,1)S(1)}, u32[]{:S(2)}, u32[]{:S(2)}) collective-permute-start(bf16[4,32,4096]{2,1,0:T(8,128)(2,1)} %copy-done.12), channel_id=1, source_target_pairs={{0,1},{1,0},{2,3},{3,2},{4,5},{5,4},{6,7},{7,6},{8,9},{9,8},{10,11... | collective-permute-start | bytes 3145736 | tf_op jit(solution)/shard_map/ppermute | solution.py:56
  152.4 15.1 %collective-permute-start.36 = (bf16[4,32,4096]{2,1,0:T(8,128)(2,1)}, bf16[4,32,4096]{2,1,0:T(8,128)(2,1)S(1)}, u32[]{:S(2)}, u32[]{:S(2)}) collective-permute-start(bf16[4,32,4096]{2,1,0:T(8,128)(2,1)} %copy-done.11), channel_id=1, source_target_pairs={{0,1},{1,0},{2,3},{3,2},{4,5},{5,4},{6,7},{7,6},{8,9},{9,8},{10,11... | collective-permute-start | bytes 3145736 | tf_op jit(solution)/shard_map/ppermute | solution.py:56
  152.6 14.8 %collective-permute-start.38 = (bf16[4,32,4096]{2,1,0:T(8,128)(2,1)S(1)}, bf16[4,32,4096]{2,1,0:T(8,128)(2,1)S(1)}, u32[]{:S(2)}, u32[]{:S(2)}) collective-permute-start(bf16[4,32,4096]{2,1,0:T(8,128)(2,1)S(1)} %collective-permute-done.34.refs_6_), channel_id=1, source_target_pairs={{0,1},{1,0},{2,3},{3,2},{4,5},{5,4},{6,7},{7,6},{8,9},{9,8},{10,11... | collective-permute-start | bytes 3145736 | tf_op jit(solution)/shard_map/ppermute | solution.py:56
  155.4 33.4 %collective-permute-start.39 = (bf16[4,128,1024]{2,1,0:T(8,128)(2,1)}, bf16[4,128,1024]{2,1,0:T(8,128)(2,1)S(1)}, u32[]{:S(2)}, u32[]{:S(2)}) collective-permute-start(bf16[4,128,1024]{2,1,0:T(8,128)(2,1)} %bitcast.50.refs_9_), channel_id=1, source_target_pairs={{0,8},{1,17},{2,10},{3,19},{4,12},{5,21},{6,14},{7,23},{8,0},{9,25... | collective-permute-start | bytes 3145736 | tf_op jit(solution)/shard_map/ppermute | solution.py:56
  166.6 23.6 %collective-permute-start.40 = (bf16[4,128,1024]{2,1,0:T(8,128)(2,1)}, bf16[4,128,1024]{2,1,0:T(8,128)(2,1)S(1)}, u32[]{:S(2)}, u32[]{:S(2)}) collective-permute-start(bf16[4,128,1024]{2,1,0:T(8,128)(2,1)} %bitcast.50.refs_9_), channel_id=1, source_target_pairs={{0,16},{1,9},{2,18},{3,11},{4,20},{5,13},{6,22},{7,15},{8,24},{9,1... | collective-permute-start | bytes 3145736 | tf_op jit(solution)/shard_map/ppermute | solution.py:56
  188.8 22.0 %collective-permute-start.41 = (bf16[4,128,1024]{2,1,0:T(8,128)(2,1)S(1)}, bf16[4,128,1024]{2,1,0:T(8,128)(2,1)}, u32[]{:S(2)}, u32[]{:S(2)}) collective-permute-start(bf16[4,128,1024]{2,1,0:T(8,128)(2,1)S(1)} %collective-permute-done.39.refs_14_.refs_10_), channel_id=1, source_target_pairs={{0,16},{1,9},{2,18},{3,11},{4,20},{5,13},{6,22},{7,15},{8,24},{9,1... | collective-permute-start | bytes 3145736 | tf_op jit(solution)/shard_map/ppermute | solution.py:56
  190.2 21.3 %collective-permute-start.43 = (bf16[4,128,1024]{2,1,0:T(8,128)(2,1)S(1)}, bf16[4,128,1024]{2,1,0:T(8,128)(2,1)}, u32[]{:S(2)}, u32[]{:S(2)}) collective-permute-start(bf16[4,128,1024]{2,1,0:T(8,128)(2,1)S(1)} %collective-permute-done.39.refs_14_.refs_10_), channel_id=1, source_target_pairs={{0,1},{1,0},{2,3},{3,2},{4,5},{5,4},{6,7},{7,6},{8,9},{9,8},{10,11... | collective-permute-start | bytes 3145736 | tf_op jit(solution)/shard_map/ppermute | solution.py:56
  190.2 21.3 %collective-permute-start.44 = (bf16[4,128,1024]{2,1,0:T(8,128)(2,1)S(1)}, bf16[4,128,1024]{2,1,0:T(8,128)(2,1)}, u32[]{:S(2)}, u32[]{:S(2)}) collective-permute-start(bf16[4,128,1024]{2,1,0:T(8,128)(2,1)S(1)} %collective-permute-done.40.refs_15_.refs_11_), channel_id=1, source_target_pairs={{0,1},{1,0},{2,3},{3,2},{4,5},{5,4},{6,7},{7,6},{8,9},{9,8},{10,11... | collective-permute-start | bytes 3145736 | tf_op jit(solution)/shard_map/ppermute | solution.py:56
  190.7 20.8 %collective-permute-start.42 = (bf16[4,128,1024]{2,1,0:T(8,128)(2,1)}, bf16[4,128,1024]{2,1,0:T(8,128)(2,1)}, u32[]{:S(2)}, u32[]{:S(2)}) collective-permute-start(bf16[4,128,1024]{2,1,0:T(8,128)(2,1)} %bitcast.50.refs_9_), channel_id=1, source_target_pairs={{0,1},{1,0},{2,3},{3,2},{4,5},{5,4},{6,7},{7,6},{8,9},{9,8},{10,11... | collective-permute-start | bytes 3145736 | tf_op jit(solution)/shard_map/ppermute | solution.py:56
  307.3 6.7 %collective-permute-start.62 = (bf16[4,32,288]{2,1,0:T(8,128)(2,1)S(1)}, bf16[4,32,288]{2,1,0:T(8,128)(2,1)S(1)}, u32[]{:S(2)}, u32[]{:S(2)}) collective-permute-start(bf16[4,32,288]{2,1,0:T(8,128)(2,1)S(1)} %get-tuple-element.270), channel_id=1, source_target_pairs={{0,16},{1,17},{2,18},{3,19},{4,20},{5,21},{6,22},{7,23},{8,24},{9,... | collective-permute-start | bytes 221192 | tf_op jit(solution)/shard_map/ppermute | solution.py:56
  347.0 14.9 %collective-permute-start.67 = (bf16[4,4,128,1024]{3,2,1,0:T(8,128)(2,1)}, bf16[4,4,128,1024]{3,2,1,0:T(8,128)(2,1)S(1)}, u32[]{:S(2)}, u32[]{:S(2)}) collective-permute-start(bf16[4,4,128,1024]{3,2,1,0:T(8,128)(2,1)} %grad_down_sib.1.refs_3_), channel_id=1, source_target_pairs={{0,1},{1,0},{2,3},{3,2},{4,5},{5,4},{6,7},{7,6},{8,9},{9,8},{10,11... | collective-permute-start | bytes 12582920 | tf_op jit(solution)/shard_map/ppermute | solution.py:56
  389.0 32.1 %collective-permute-start.68 = (f32[4,4,32,4096]{3,2,1,0:T(8,128)}, f32[4,4,32,4096]{3,2,1,0:T(8,128)}, u32[]{:S(2)}, u32[]{:S(2)}) collective-permute-start(f32[4,4,32,4096]{3,2,1,0:T(8,128)} %grad_up_sib.1.refs_7_), channel_id=1, source_target_pairs={{0,1},{1,0},{2,3},{3,2},{4,5},{5,4},{6,7},{7,6},{8,9},{9,8},{10,11... | collective-permute-start | bytes 25165832 | tf_op jit(solution)/shard_map/ppermute | solution.py:56
  389.5 26.4 %collective-permute-start.69 = (bf16[2,4,128,1024]{3,2,1,0:T(8,128)(2,1)}, bf16[2,4,128,1024]{3,2,1,0:T(8,128)(2,1)}, u32[]{:S(2)}, u32[]{:S(2)}) collective-permute-start(bf16[2,4,128,1024]{3,2,1,0:T(8,128)(2,1)} %get-tuple-element.203.refs_3_), channel_id=1, source_target_pairs={{0,16},{1,9},{2,18},{3,11},{4,20},{5,13},{6,22},{7,15},{8,24},{9,1... | collective-permute-start | bytes 6291464 | tf_op jit(solution)/shard_map/ppermute | solution.py:56
  418.4 16.7 %collective-permute-start.70 = (bf16[1,4,128,1024]{3,2,1,0:T(8,128)(2,1)S(1)}, bf16[1,4,128,1024]{3,2,1,0:T(8,128)(2,1)S(1)}, u32[]{:S(2)}, u32[]{:S(2)}) collective-permute-start(bf16[1,4,128,1024]{3,2,1,0:T(8,128)(2,1)S(1)} %get-tuple-element.247.refs_5_), channel_id=1, source_target_pairs={{0,8},{1,17},{2,10},{3,19},{4,12},{5,21},{6,14},{7,23},{8,0},{9,25... | collective-permute-start | bytes 3145736 | tf_op jit(solution)/shard_map/ppermute | solution.py:56
  434.3 44.2 %collective-permute-start.72 = (bf16[2,4,32,4096]{3,2,1,0:T(8,128)(2,1)}, bf16[2,4,32,4096]{3,2,1,0:T(8,128)(2,1)}, u32[]{:S(2)}, u32[]{:S(2)}) collective-permute-start(bf16[2,4,32,4096]{3,2,1,0:T(8,128)(2,1)} %get-tuple-element.208.refs_7_), channel_id=1, source_target_pairs={{0,16},{1,9},{2,18},{3,11},{4,20},{5,13},{6,22},{7,15},{8,24},{9,1... | collective-permute-start | bytes 6291464 | tf_op jit(solution)/shard_map/ppermute | solution.py:56
  435.3 39.3 %collective-permute-start.71 = (bf16[2,128,1024]{2,1,0:T(8,128)(2,1)S(1)}, bf16[2,128,1024]{2,1,0:T(8,128)(2,1)}, u32[]{:S(2)}, u32[]{:S(2)}) collective-permute-start(bf16[2,128,1024]{2,1,0:T(8,128)(2,1)S(1)} %fusion.2.refs_8_), channel_id=1, source_target_pairs={{0,2},{1,3},{2,0},{3,1},{4,6},{5,7},{6,4},{7,5},{8,10},{9,11},{10,... | collective-permute-start | bytes 1572872 | tf_op jit(solution)/shard_map/ppermute | solution.py:56
  467.1 39.1 %collective-permute-start.74 = (bf16[4,4,32,1536]{3,2,1,0:T(8,128)(2,1)}, bf16[4,4,32,1536]{3,2,1,0:T(8,128)(2,1)}, u32[]{:S(2)}, u32[]{:S(2)}) collective-permute-start(bf16[4,4,32,1536]{3,2,1,0:T(8,128)(2,1)} %grad_qkv_sib.2.refs_3_), channel_id=1, source_target_pairs={{0,1},{1,0},{2,3},{3,2},{4,5},{5,4},{6,7},{7,6},{8,9},{9,8},{10,11... | collective-permute-start | bytes 4718600 | tf_op jit(solution)/shard_map/ppermute | solution.py:56
  472.9 42.7 %collective-permute-start.73 = (bf16[4,4,32,1024]{3,2,1,0:T(8,128)(2,1)}, bf16[4,4,32,1024]{3,2,1,0:T(8,128)(2,1)}, u32[]{:S(2)}, u32[]{:S(2)}) collective-permute-start(bf16[4,4,32,1024]{3,2,1,0:T(8,128)(2,1)} %grad_out_sib.1.refs_7_), channel_id=1, source_target_pairs={{0,1},{1,0},{2,3},{3,2},{4,5},{5,4},{6,7},{7,6},{8,9},{9,8},{10,11... | collective-permute-start | bytes 3145736 | tf_op jit(solution)/shard_map/ppermute | solution.py:56
  476.5 97.3 %collective-permute-start.96 = (f32[128,1024]{1,0:T(8,128)}, f32[128,1024]{1,0:T(8,128)}, u32[]{:S(2)}, u32[]{:S(2)}) collective-permute-start(f32[128,1024]{1,0:T(8,128)} %fusion.5.refs_8_), channel_id=1, source_target_pairs={{0,4},{1,5},{2,6},{3,7},{4,0},{5,1},{6,2},{7,3},{8,12},{9,13},{10,... | collective-permute-start | bytes 1572872 | tf_op jit(solution)/shard_map/ppermute | solution.py:56
  481.6 32.9 %collective-permute-start.75 = (bf16[1,4,32,4096]{3,2,1,0:T(8,128)(2,1)}, bf16[1,4,32,4096]{3,2,1,0:T(8,128)(2,1)S(1)}, u32[]{:S(2)}, u32[]{:S(2)}) collective-permute-start(bf16[1,4,32,4096]{3,2,1,0:T(8,128)(2,1)} %get-tuple-element.245.refs_9_), channel_id=1, source_target_pairs={{0,8},{1,17},{2,10},{3,19},{4,12},{5,21},{6,14},{7,23},{8,0},{9,25... | collective-permute-start | bytes 3145736 | tf_op jit(solution)/shard_map/ppermute | solution.py:56
  513.6 16.8 %collective-permute-start.78 = (bf16[2,4,32,1536]{3,2,1,0:T(8,128)(2,1)}, bf16[2,4,32,1536]{3,2,1,0:T(8,128)(2,1)S(1)}, u32[]{:S(2)}, u32[]{:S(2)}) collective-permute-start(bf16[2,4,32,1536]{3,2,1,0:T(8,128)(2,1)} %get-tuple-element.220.refs_4_), channel_id=1, source_target_pairs={{0,16},{1,9},{2,18},{3,11},{4,20},{5,13},{6,22},{7,15},{8,24},{9,1... | collective-permute-start | bytes 2359304 | tf_op jit(solution)/shard_map/ppermute | solution.py:56
  528.3 16.0 %collective-permute-start.76 = (bf16[4,4,32,1536]{3,2,1,0:T(8,128)(2,1)}, bf16[4,4,32,1536]{3,2,1,0:T(8,128)(2,1)}, u32[]{:S(2)}, u32[]{:S(2)}) collective-permute-start(bf16[4,4,32,1536]{3,2,1,0:T(8,128)(2,1)} %grad_qkv_sib.3), channel_id=1, source_target_pairs={{0,1},{1,0},{2,3},{3,2},{4,5},{5,4},{6,7},{7,6},{8,9},{9,8},{10,11... | collective-permute-start | bytes 4718600 | tf_op jit(solution)/shard_map/ppermute | solution.py:56
  528.4 14.4 %collective-permute-start.77 = (bf16[2,32,4096]{2,1,0:T(8,128)(2,1)S(1)}, bf16[2,32,4096]{2,1,0:T(8,128)(2,1)S(1)}, u32[]{:S(2)}, u32[]{:S(2)}) collective-permute-start(bf16[2,32,4096]{2,1,0:T(8,128)(2,1)S(1)} %copy-done.6), channel_id=1, source_target_pairs={{0,2},{1,3},{2,0},{3,1},{4,6},{5,7},{6,4},{7,5},{8,10},{9,11},{10,... | collective-permute-start | bytes 1572872 | tf_op jit(solution)/shard_map/ppermute | solution.py:56
  529.3 22.4 %collective-permute-start.80 = (bf16[2,4,32,1024]{3,2,1,0:T(8,128)(2,1)}, bf16[2,4,32,1024]{3,2,1,0:T(8,128)(2,1)}, u32[]{:S(2)}, u32[]{:S(2)}) collective-permute-start(bf16[2,4,32,1024]{3,2,1,0:T(8,128)(2,1)} %get-tuple-element.222.refs_3_), channel_id=1, source_target_pairs={{0,16},{1,9},{2,18},{3,11},{4,20},{5,13},{6,22},{7,15},{8,24},{9,1... | collective-permute-start | bytes 1572872 | tf_op jit(solution)/shard_map/ppermute | solution.py:56
  530.6 21.1 %collective-permute-start.79 = (bf16[1,4,32,1536]{3,2,1,0:T(8,128)(2,1)S(1)}, bf16[1,4,32,1536]{3,2,1,0:T(8,128)(2,1)S(1)}, u32[]{:S(2)}, u32[]{:S(2)}) collective-permute-start(bf16[1,4,32,1536]{3,2,1,0:T(8,128)(2,1)S(1)} %get-tuple-element.251.refs_5_), channel_id=1, source_target_pairs={{0,8},{1,17},{2,10},{3,19},{4,12},{5,21},{6,14},{7,23},{8,0},{9,25... | collective-permute-start | bytes 1179656 | tf_op jit(solution)/shard_map/ppermute | solution.py:56
  578.0 14.8 %collective-permute-start.95 = (bf16[32,4096]{1,0:T(8,128)(2,1)}, bf16[32,4096]{1,0:T(8,128)(2,1)S(1)}, u32[]{:S(2)}, u32[]{:S(2)}) collective-permute-start(bf16[32,4096]{1,0:T(8,128)(2,1)} %fusion.9.refs_4_), channel_id=1, source_target_pairs={{0,4},{1,5},{2,6},{3,7},{4,0},{5,1},{6,2},{7,3},{8,12},{9,13},{10,... | collective-permute-start | bytes 786440 | tf_op jit(solution)/shard_map/ppermute | solution.py:56
  578.8 26.5 %collective-permute-start.92 = (bf16[1,4,32,1024]{3,2,1,0:T(8,128)(2,1)}, bf16[1,4,32,1024]{3,2,1,0:T(8,128)(2,1)S(1)}, u32[]{:S(2)}, u32[]{:S(2)}) collective-permute-start(bf16[1,4,32,1024]{3,2,1,0:T(8,128)(2,1)} %get-tuple-element.253.refs_6_), channel_id=1, source_target_pairs={{0,8},{1,17},{2,10},{3,19},{4,12},{5,21},{6,14},{7,23},{8,0},{9,25... | collective-permute-start | bytes 786440 | tf_op jit(solution)/shard_map/ppermute | solution.py:56
  579.4 39.9 %collective-permute-start.83 = (bf16[2,4,32,1536]{3,2,1,0:T(8,128)(2,1)}, bf16[2,4,32,1536]{3,2,1,0:T(8,128)(2,1)S(1)}, u32[]{:S(2)}, u32[]{:S(2)}) collective-permute-start(bf16[2,4,32,1536]{3,2,1,0:T(8,128)(2,1)} %get-tuple-element.226.refs_4_), channel_id=1, source_target_pairs={{0,16},{1,9},{2,18},{3,11},{4,20},{5,13},{6,22},{7,15},{8,24},{9,1... | collective-permute-start | bytes 2359304 | tf_op jit(solution)/shard_map/ppermute | solution.py:56
  580.6 12.2 %collective-permute-start.89 = (f32[2,2,4,128]{3,2,1,0:T(4,128)S(1)}, f32[2,2,4,128]{3,2,1,0:T(4,128)S(1)}, u32[]{:S(2)}, u32[]{:S(2)}) collective-permute-start(f32[2,2,4,128]{3,2,1,0:T(4,128)S(1)} %fusion.33), channel_id=1, source_target_pairs={{0,16},{1,17},{2,18},{3,19},{4,20},{5,21},{6,22},{7,23},{8,24},{9,... | collective-permute-start | bytes 24584 | tf_op jit(solution)/shard_map/ppermute | solution.py:56
  581.6 24.7 %collective-permute-start.97 = (bf16[2,2,2,2,32,288]{5,4,2,3,0,1:T(8,128)(2,1)S(1)}, bf16[2,2,2,2,32,288]{5,4,2,3,0,1:T(8,128)(2,1)S(1)}, u32[]{:S(2)}, u32[]{:S(2)}) collective-permute-start(bf16[2,2,2,2,32,288]{5,4,2,3,0,1:T(8,128)(2,1)S(1)} %fusion.6), channel_id=1, source_target_pairs={{0,1},{1,0},{2,3},{3,2},{4,5},{5,4},{6,7},{7,6},{8,9},{9,8},{10,11... | collective-permute-start | bytes 884744 | tf_op jit(solution)/shard_map/ppermute | solution.py:56
  598.4 6.8 %collective-permute-start.81 = (bf16[2,32,1536]{2,1,0:T(8,128)(2,1)S(1)}, bf16[2,32,1536]{2,1,0:T(8,128)(2,1)S(1)}, u32[]{:S(2)}, u32[]{:S(2)}) collective-permute-start(bf16[2,32,1536]{2,1,0:T(8,128)(2,1)S(1)} %copy-done.35), channel_id=1, source_target_pairs={{0,2},{1,3},{2,0},{3,1},{4,6},{5,7},{6,4},{7,5},{8,10},{9,11},{10,... | collective-permute-start | bytes 589832 | tf_op jit(solution)/shard_map/ppermute | solution.py:56
  605.3 7.9 %collective-permute-start.93 = (bf16[2,32,1024]{2,1,0:T(8,128)(2,1)S(1)}, bf16[2,32,1024]{2,1,0:T(8,128)(2,1)S(1)}, u32[]{:S(2)}, u32[]{:S(2)}) collective-permute-start(bf16[2,32,1024]{2,1,0:T(8,128)(2,1)S(1)} %fusion.20), channel_id=1, source_target_pairs={{0,2},{1,3},{2,0},{3,1},{4,6},{5,7},{6,4},{7,5},{8,10},{9,11},{10,... | collective-permute-start | bytes 393224 | tf_op jit(solution)/shard_map/ppermute | solution.py:56
  613.2 7.9 %collective-permute-start.94 = (f32[32,1024]{1,0:T(8,128)S(1)}, f32[32,1024]{1,0:T(8,128)S(1)}, u32[]{:S(2)}, u32[]{:S(2)}) collective-permute-start(f32[32,1024]{1,0:T(8,128)S(1)} %fusion.21), channel_id=1, source_target_pairs={{0,4},{1,5},{2,6},{3,7},{4,0},{5,1},{6,2},{7,3},{8,12},{9,13},{10,... | collective-permute-start | bytes 393224 | tf_op jit(solution)/shard_map/ppermute | solution.py:56
  619.5 7.8 %collective-permute-start.84 = (bf16[1,4,32,1536]{3,2,1,0:T(8,128)(2,1)S(1)}, bf16[1,4,32,1536]{3,2,1,0:T(8,128)(2,1)S(1)}, u32[]{:S(2)}, u32[]{:S(2)}) collective-permute-start(bf16[1,4,32,1536]{3,2,1,0:T(8,128)(2,1)S(1)} %get-tuple-element.248), channel_id=1, source_target_pairs={{0,8},{1,17},{2,10},{3,19},{4,12},{5,21},{6,14},{7,23},{8,0},{9,25... | collective-permute-start | bytes 1179656 | tf_op jit(solution)/shard_map/ppermute | solution.py:56
  622.3 13.9 %collective-permute-start.101 = (bf16[32,288]{1,0:T(8,128)(2,1)S(1)}, bf16[32,288]{1,0:T(8,128)(2,1)S(1)}, u32[]{:S(2)}, u32[]{:S(2)}) collective-permute-start(bf16[32,288]{1,0:T(8,128)(2,1)S(1)} %fusion.30), channel_id=1, source_target_pairs={{0,4},{1,5},{2,6},{3,7},{4,0},{5,1},{6,2},{7,3},{8,12},{9,13},{10,... | collective-permute-start | bytes 55304 | tf_op jit(solution)/shard_map/ppermute | solution.py:56
  633.5 6.6 %collective-permute-start.86 = (bf16[32,1536]{1,0:T(8,128)(2,1)S(1)}, bf16[32,1536]{1,0:T(8,128)(2,1)S(1)}, u32[]{:S(2)}, u32[]{:S(2)}) collective-permute-start(bf16[32,1536]{1,0:T(8,128)(2,1)S(1)} %fusion.24), channel_id=1, source_target_pairs={{0,4},{1,5},{2,6},{3,7},{4,0},{5,1},{6,2},{7,3},{8,12},{9,13},{10,... | collective-permute-start | bytes 294920 | tf_op jit(solution)/shard_map/ppermute | solution.py:56
  (106 other events, 994.2 us)

commit v3 on v2

--- a/solution.py
+++ b/solution.py
@@ -82,13 +82,14 @@
 
 class Gather:
     def __init__(self, shard):
-        self.held, self.count, self.shard = shard, 0, shard
+        self.held, self.count, self.shard, self.received = shard, 0, shard, []
 
     def along_z(self, start=(), use=()):
         _, n_z, _, z_bits = sizes()
         _, z, _ = place()
         bit = z_bits - 1 - self.count
         other = transfer(self.held, start, use, z_mask=1 << bit)
+        self.received.append(other)
         self.held = ordered(z >> bit & 1, self.held, other, self.count)
         self.count += 1
         if self.count == z_bits:
@@ -99,13 +100,26 @@
         for i in range(z_bits):
             self.along_z(*bounds[min(i, len(bounds) - 1)])
 
-    def all_rows(self, first, rest):
+    def own_rows(self, start=(), use=()):
         _, _, row_bits, _ = sizes()
-        for stage in range(row_bits):
-            self.pieces = self.pieces + [
-                transfer(p, *(rest if i else first), row_masks=stage_masks(stage))
-                for i, p in enumerate(self.pieces)
+        self.own = [
+            transfer(self.pieces[0], start, use, row_masks=stage_masks(stage))
+            for stage in range(row_bits)
+        ]
+        self.pieces = self.pieces + self.own
+
+    def other_rows(self, start=(), use=()):
+        _, _, row_bits, _ = sizes()
+        pieces = [self.pieces[0], self.own[0]]
+        for stage in range(1, row_bits):
+            pieces = pieces + [self.own[stage]] + [
+                transfer(p, start, use, row_masks=stage_masks(stage)) for p in pieces[1:]
             ]
+        self.pieces = pieces
+
+    def all_rows(self, own, other):
+        self.own_rows(*own)
+        self.other_rows(*other)
 
     def whole(self, table, early=(), late=()):
         last = len(self.pieces) - 1
@@ -133,12 +147,17 @@
 
 
 class Weight:
-    def __init__(self, table, pieces):
+    def __init__(self, table, pieces, start=0, size=None):
+        self.table, self.pieces = table, pieces
+        self.start, self.size = start, size or pieces[0].shape[2]
+
+    def columns(self, start, size):
+        return Weight(self.table, self.pieces, self.start + start, size)
+
+    @property
+    def shape(self):
         n_rows, n_z, _, _ = sizes()
-        self.table, self.pieces = table, pieces
-        r, n = pieces[0].shape[1:]
-        self.shape = (n_rows, n_z, 2, r, n)
-        self.rows = n_rows * n_z * 2 * r
+        return (n_rows, n_z, 2, self.pieces[0].shape[1], self.size)
 
     def specs(self):
         return [pl.BlockSpec(memory_space=pl.ANY)] * len(self.pieces)
@@ -152,43 +171,49 @@
     def out_shape(self):
         return jax.ShapeDtypeStruct(self.shape, self.pieces[0].dtype)
 
-
-def load_weight(table, pieces, out_ref, w_ref, sems):
-    n_rows = len(pieces) // 2
-    core = table[2 * n_rows]
-    out = pltpu.make_async_copy(w_ref, out_ref, sems.at[2 * n_rows])
-
-    @pl.when(pl.program_id(0) == 0)
-    def _():
-        copies = [
-            pltpu.make_async_copy(
-                piece,
-                w_ref.at[table[i], :, core if i < n_rows else 1 - core],
-                sems.at[i],
-            )
-            for i, piece in enumerate(pieces)
-        ]
-        for c in copies:
-            c.start()
-        for c in copies:
-            c.wait()
-        out.start()
-
-    @pl.when(pl.program_id(0) == pl.num_programs(0) - 1)
-    def _():
-        out.wait()
-
-
-def gather_small(shard):
+    def load(self, table, pieces, out_ref, w_ref, sems):
+        n_rows = len(pieces) // 2
+        core = table[2 * n_rows]
+        out = pltpu.make_async_copy(w_ref, out_ref, sems.at[2 * n_rows])
+        if self.size != pieces[0].shape[2]:
+            pieces = [p.at[:, :, pl.ds(self.start, self.size)] for p in pieces]
+
+        @pl.when(pl.program_id(0) == 0)
+        def _():
+            copies = [
+                pltpu.make_async_copy(
+                    piece,
+                    w_ref.at[table[i], :, core if i < n_rows else 1 - core],
+                    sems.at[i],
+                )
+                for i, piece in enumerate(pieces)
+            ]
+            for c in copies:
+                c.start()
+            for c in copies:
+                c.wait()
+            out.start()
+
+        @pl.when(pl.program_id(0) == pl.num_programs(0) - 1)
+        def _():
+            out.wait()
+
+
+def gather_small(shard, uses=()):
     n_rows, n_z, row_bits, z_bits = sizes()
     row, z, core = place()
+    uses = list(uses)
+
+    def arrive(**move):
+        other = exchange(held, **move)
+        return after(other, uses.pop(0)) if uses else other
+
     held = shard
     for count, bit in enumerate(reversed(range(z_bits))):
-        held = ordered(z >> bit & 1, held, exchange(held, z_mask=1 << bit), count)
+        held = ordered(z >> bit & 1, held, arrive(z_mask=1 << bit), count)
     for count, bit in enumerate(reversed(range(row_bits))):
-        other = exchange(held, row_masks=(1 << bit, 1 << bit))
-        held = ordered(row >> bit & 1, held, other, count)
-    held = ordered(core, held, exchange(held, swap_core=True), row_bits + z_bits)
+        held = ordered(row >> bit & 1, held, arrive(row_masks=(1 << bit, 1 << bit)), count)
+    held = ordered(core, held, arrive(swap_core=True), row_bits + z_bits)
     return held.reshape((n_rows * n_z * 2,) + shard.shape)
 
 
@@ -217,17 +242,17 @@
     return jnp.stack([held, exchange(held, swap_core=True)])
 
 
-def scatter_relative(blocks, dtype):
+def scatter_relative(blocks, dtype, use=()):
     n_rows, n_z, _, _ = sizes()
 
-    def step(held, count, move):
-        parts = [exchange(held[m].astype(dtype), **move(m)) for m in range(1, count)]
+    def step(held, count, move, use=()):
+        parts = [after(exchange(held[m].astype(dtype), **move(m)), *use) for m in range(1, count)]
         total = held[0]
         for part in parts:
             total = total + part.astype(f32)
         return total
 
-    held = step(blocks, 2, lambda m: dict(swap_core=True))
+    held = step(blocks, 2, lambda m: dict(swap_core=True), use)
     held = step(held, n_rows, lambda m: dict(row_masks=(m, m)))
     return step(held, n_z, lambda m: dict(z_mask=m))
 
@@ -244,35 +269,42 @@
 class Scatter:
     def __init__(self, send, keep, wide=False):
         _, _, row_bits, z_bits = sizes()
-        self.send, self.keep = send, keep
-        self.wide = ("z", z_bits - 1) if wide else None
+        flat = lambda x: x.reshape((-1,) + x.shape[-2:])
+        self.send, self.keep = flat(send), flat(keep)
         self.stages = [("row", j) for j in reversed(range(row_bits))]
-        self.stages += [("z", b) for b in range(sizes()[3])]
-
-    def step(self, *use):
-        _, _, _, z_bits = sizes()
-        _, z, _ = place()
+        self.stages += [("z", b) for b in range(z_bits)]
+        self.wide = self.stages[-1] if wide else None
+
+    def receive(self):
         kind, at = self.stages.pop(0)
         move = dict(row_masks=stage_masks(at)) if kind == "row" else dict(z_mask=1 << at)
-        parts = (self.keep, after(exchange(self.send, **move), *use))
+        return exchange(self.send, **move)
+
+    def step(self, *use):
+        _, z, _ = place()
+        parts = (self.keep, after(self.receive(), *use))
         if not self.stages:
-            return parts[0] + parts[1].astype(f32)
+            return (parts[0] + parts[1].astype(f32))[0]
         kind, at = self.stages[0]
+        half = self.keep.shape[0] // 2
         if kind == "row":
-            half = 1 << at
             pick = lambda x, other: x[half:] if other else x[:half]
         else:
-            if at == 0:
-                parts = tuple(x.reshape((2,) * z_bits + x.shape[2:]) for x in parts)
             mine = z >> at & 1
+            parts = tuple(x.reshape((half, 2) + x.shape[1:]) for x in parts)
             pick = lambda x, other: lax.dynamic_index_in_dim(
-                x, 1 - mine if other else mine, z_bits - 1 - at, keepdims=False
+                x, 1 - mine if other else mine, 1, keepdims=False
             )
         total = lambda other: pick(parts[0], other) + pick(parts[1], other).astype(f32)
         self.send, self.keep = total(True), total(False)
         if self.stages[0] != self.wide:
             self.send = self.send.astype(bf16)
         return self.send
+
+    def merge(self, other):
+        self.send = jnp.concatenate([self.send, other.send], axis=-1)
+        self.keep = jnp.concatenate([self.keep, other.keep], axis=-1)
+        return self
 
     def finish(self, *use):
         while self.stages:
@@ -345,35 +377,40 @@
 QKV_TILE = 1024
 
 
-def qkv_kernel(n_pieces, table, x_ref, b_ref, cos_ref, sin_ref, *refs):
-    pieces, (o_ref, w_out, acc_ref, w_ref, sems) = refs[:n_pieces], refs[n_pieces:]
-    load_weight(table, pieces, w_out, w_ref, sems)
+def qkv_kernel(weight, table, x_ref, b_ref, cos_ref, sin_ref, *refs):
+    pieces, (o_ref, w_out, w_ref, sems) = refs[:-4], refs[-4:]
+    weight.load(table, pieces, w_out, w_ref, sems)
     tile = pl.program_id(0)
     per_part = D // QKV_TILE
     cols = pl.ds(pl.multiple_of(tile * QKV_TILE, LANES), QKV_TILE)
     w = w_ref[:, :, :, :, cols].reshape(x_ref.shape[1], QKV_TILE)
-    acc_ref[...] = contract(x_ref[...], w, 1, 0) + b_ref[...]
+    bias = b_ref[...]
 
     @pl.when(tile < 2 * per_part)
     def _():
         scale = jnp.where(tile < per_part, HEAD_DIM**-0.5, 1.0)
-        cosine = cos_ref[...] * scale
-        sine = sin_ref[...] * scale
-        for j in range(QKV_TILE // LANES):
-            at = slice(j * LANES, (j + 1) * LANES)
-            a = acc_ref[:, at]
-            o_ref[:, at] = (a * cosine + swap_halves(a) * sine).astype(bf16)
+        for row in range(0, x_ref.shape[0], TILE):
+            rows = slice(row, row + TILE)
+            acc = contract(x_ref[rows, :], w, 1, 0) + bias
+            cosine = cos_ref[rows, :] * scale
+            sine = sin_ref[rows, :] * scale
+            for j in range(QKV_TILE // LANES):
+                at = slice(j * LANES, (j + 1) * LANES)
+                a = acc[:, at]
+                o_ref[rows, at] = (a * cosine + swap_halves(a) * sine).astype(bf16)
 
     @pl.when(tile >= 2 * per_part)
     def _():
-        o_ref[...] = acc_ref[...].astype(bf16)
+        for row in range(0, x_ref.shape[0], TILE):
+            rows = slice(row, row + TILE)
+            o_ref[rows, :] = (contract(x_ref[rows, :], w, 1, 0) + bias).astype(bf16)
 
 
 def project_qkv(x, w, b, cosine, sine, wait=()):
     t = x.shape[0]
     any_out = pl.BlockSpec(memory_space=pl.ANY)
     return call(
-        functools.partial(qkv_kernel, len(w.pieces)),
+        functools.partial(qkv_kernel, w),
         "project_qkv",
         (3 * D // QKV_TILE,),
         [
@@ -387,7 +424,7 @@
         [like((t, 3 * D), bf16), w.out_shape()],
         6 * t * D * D,
         20 * t * D,
-        [pltpu.VMEM((t, QKV_TILE), f32)] + w.scratch(),
+        w.scratch(),
         table=w.table,
         wait=wait,
     )(w.table, x, b, cosine, sine, *w.pieces)
@@ -422,10 +459,9 @@
     return jnp.sum(x, axis=0, keepdims=True)
 
 
-def out_norm_kernel(n_pieces, table, a_ref, b_ref, x_ref, gain_ref, bias_ref, *refs):
-    pieces = refs[:n_pieces]
-    hat_ref, rstd_ref, low_ref, w_out, w_ref, sems = refs[n_pieces:]
-    load_weight(table, pieces, w_out, w_ref, sems)
+def out_norm_kernel(weight, table, a_ref, b_ref, x_ref, gain_ref, bias_ref, *refs):
+    hat_ref, rstd_ref, low_ref, w_out, w_ref, sems = refs[-6:]
+    weight.load(table, refs[:-6], w_out, w_ref, sems)
     w = w_ref[...].reshape(a_ref.shape[1], -1)
     v = x_ref[...].astype(f32) + contract(a_ref[...], w, 1, 0) + b_ref[...]
     hat, rstd = normalized(v)
@@ -438,7 +474,7 @@
     t = x.shape[0]
     vec = whole_spec((1, D))
     return call(
-        functools.partial(out_norm_kernel, len(w.pieces)),
+        functools.partial(out_norm_kernel, w),
         "out_norm",
         (t // TILE,),
         [row_spec(TILE, D), vec, row_spec(TILE, D), vec, vec] + w.specs(),
@@ -453,37 +489,18 @@
 
 
 UP_TILE = 1024
-CHUNK = 16
+CHUNK = 32
 
 
 def gelu_pair(x):
-    u = jnp.abs(x)
-    e = jnp.exp(x * x * -0.5)
-    t = 1.0 / (1.0 + (0.3275911 * 0.5**0.5) * u)
-    poly = t * (
-        0.254829592 * 0.5
-        + t
-        * (
-            -0.284496736 * 0.5
-            + t * (1.421413741 * 0.5 + t * (-1.453152027 * 0.5 + t * (1.061405429 * 0.5)))
-        )
-    )
-    tail = poly * e
-    phi = jnp.where(x < 0, tail, 1.0 - tail)
-    return x * phi, phi + x * e * (2.0 * jnp.pi) ** -0.5
-
-
-def up_kernel(n_pieces, first, table, h_ref, b_ref, *refs):
-    pieces = refs[:n_pieces]
+    phi = 0.5 + 0.5 * lax.erf(x * 0.5**0.5)
+    return x * phi, phi + x * jnp.exp(x * x * -0.5) * (2.0 * jnp.pi) ** -0.5
+
+
+def up_kernel(weight, table, h_ref, b_ref, *refs):
     act_ref, slope_ref, w_out, acc_ref, w_ref, sems = refs[-6:]
-    n = w_ref.shape[-1]
-    if first:
-        pieces = [p.at[:, :, pl.ds(n, n)] for p in pieces]
-        w_out = w_out.at[:, :, :, :, pl.ds(n, n)]
-    else:
-        pieces = [p.at[:, :, pl.ds(0, n)] for p in pieces]
-        w_out = w_out.at[:, :, :, :, pl.ds(0, n)]
-    load_weight(table, pieces, w_out, w_ref, sems)
+    out = w_out.at[:, :, :, :, pl.ds(weight.start, weight.size)]
+    weight.load(table, refs[: len(weight.pieces)], out, w_ref, sems)
     cols = pl.ds(pl.multiple_of(pl.program_id(0) * UP_TILE, LANES), UP_TILE)
     acc_ref[...] = contract(h_ref[...], w_ref[:, :, :, :, cols].reshape(-1, UP_TILE), 1, 0)
     bias = b_ref[...]
@@ -499,16 +516,15 @@
 
 
 def up_gelu(hidden, w, b, before=None, wait=()):
-    t, ff = hidden.shape[0], w.shape[-1]
+    t, ff = hidden.shape[0], w.size
     any_space = pl.BlockSpec(memory_space=pl.ANY)
     steps = ff // UP_TILE // 2
     first = 0 if before is None else steps
     before = [] if before is None else list(before)
     n_in = 3 + len(w.pieces)
-    w_ref, sems = w.scratch()
-    half = pltpu.VMEM(w.shape[:-1] + (ff // 2,), bf16)
+    half = w.columns(first * UP_TILE, ff // 2)
     return call(
-        functools.partial(up_kernel, len(w.pieces), first),
+        functools.partial(up_kernel, half),
         "up_gelu",
         (steps,),
         [whole_spec((t, D)), pl.BlockSpec((1, UP_TILE), lambda i, _: (0, first + i))]
@@ -518,7 +534,7 @@
         [like((t, ff), bf16)] * 2 + [w.out_shape()],
         t * D * ff,
         2 * t * ff + D * ff,
-        [pltpu.VMEM((t, UP_TILE), f32), half, sems],
+        [pltpu.VMEM((t, UP_TILE), f32)] + half.scratch(),
         table=w.table,
         wait=wait,
         aliases={n_in + i: i for i in range(len(before))},
@@ -528,6 +544,14 @@
 def head_masks(width):
     lane = lax.broadcasted_iota(jnp.int32, (1, width), 1)
     return [(lane >= start) & (lane < start + size) for start, size in head_slices()]
+
+
+def head_lanes():
+    for start, size in head_slices():
+        low = start // LANES * LANES
+        high = -(-(start + size) // LANES) * LANES
+        lane = lax.broadcasted_iota(jnp.int32, (1, high - low), 1) + low
+        yield slice(low, high), (lane >= start) & (lane < start + size)
 
 
 def head_sums(x):
@@ -539,40 +563,46 @@
 
 
 def down_norm_kernel(
-    n_pieces, table, a_ref, b_ref, hat1_ref, gain1_ref, bias1_ref, gain_ref, bias_ref, proj_ref, *refs
+    weight, proj, table, a_ref, b_ref, hat1_ref, gain1_ref, bias1_ref, gain_ref, bias_ref, *refs
 ):
-    pieces = refs[:n_pieces]
-    hat_ref, rstd_ref, low_ref, raw_ref, vec_ref, w_out, w_ref, sems = refs[n_pieces:]
-    load_weight(table, pieces, w_out, w_ref, sems)
-    hidden = hat1_ref[...] * gain1_ref[...] + bias1_ref[...]
+    n = len(weight.pieces)
+    hat_ref, rstd_ref, low_ref, raw_ref, vec_ref = refs[-11:-6]
+    w_out, p_out, w_ref, w_sems, p_ref, p_sems = refs[-6:]
+    proj.load(table, refs[n : 2 * n], p_out, p_ref, p_sems)
+    weight.load(table, refs[:n], w_out, w_ref, w_sems)
     w = w_ref[...].reshape(a_ref.shape[1], -1)
-    hat, rstd = normalized(hidden + contract(a_ref[...], w, 1, 0) + b_ref[...])
-    hat_ref[...] = hat
-    rstd_ref[...] = jnp.broadcast_to(rstd, rstd_ref.shape)
-    low = (hat * gain_ref[...] + bias_ref[...]).astype(bf16)
-    low_ref[...] = low
-    raw = contract(low, proj_ref[...], 1, 0)
-    raw_ref[...] = raw
-    vec_ref[...] = (raw * lax.rsqrt(head_sums(raw * raw) + eps_vec)).astype(bf16)
+    p = p_ref[...].reshape(w.shape[1], -1)
+    for row in range(0, a_ref.shape[0], TILE):
+        rows = slice(row, row + TILE)
+        hidden = hat1_ref[rows, :] * gain1_ref[...] + bias1_ref[...]
+        hat, rstd = normalized(hidden + contract(a_ref[rows, :], w, 1, 0) + b_ref[...])
+        hat_ref[rows, :] = hat
+        rstd_ref[rows, :] = jnp.broadcast_to(rstd, (TILE, LANES))
+        low = (hat * gain_ref[...] + bias_ref[...]).astype(bf16)
+        low_ref[rows, :] = low
+        raw = contract(low, p, 1, 0)
+        raw_ref[rows, :] = raw
+        vec_ref[rows, :] = (raw * lax.rsqrt(head_sums(raw * raw) + eps_vec)).astype(bf16)
 
 
 def down_norm(act, w, b, hat1, gain1, bias1, gain, bias, proj, wait=()):
     t, ff = act.shape
-    e = proj.shape[1]
+    e = proj.size
     vec = whole_spec((1, D))
+    any_space = pl.BlockSpec(memory_space=pl.ANY)
     return call(
-        functools.partial(down_norm_kernel, len(w.pieces)),
+        functools.partial(down_norm_kernel, w, proj),
         "down_norm",
         (t // TILE,),
-        [row_spec(TILE, ff), vec, row_spec(TILE, D), vec, vec, vec, vec, whole_spec((D, e))]
-        + w.specs(),
+        [row_spec(TILE, ff), vec, row_spec(TILE, D), vec, vec, vec, vec] + w.specs() + proj.specs(),
         [
             row_spec(TILE, D),
             row_spec(TILE, LANES),
             row_spec(TILE, D),
             row_spec(TILE, e),
             row_spec(TILE, e),
-            pl.BlockSpec(memory_space=pl.ANY),
+            any_space,
+            any_space,
         ],
         [
             like((t, D), f32),
@@ -581,20 +611,24 @@
             like((t, e), f32),
             like((t, e), bf16),
             w.out_shape(),
+            proj.out_shape(),
         ],
         2 * t * D * ff,
         20 * t * D,
-        w.scratch(),
+        w.scratch() + proj.scratch(),
         table=w.table,
         wait=wait,
-    )(w.table, act, b, hat1, gain1, bias1, gain, bias, proj, *w.pieces)
+    )(w.table, act, b, hat1, gain1, bias1, gain, bias, *w.pieces, *proj.pieces)
 
 
 def head_back_kernel(
-    g_ref, raw_ref, low_ref, proj_ref, hat_ref, rstd_ref, gain_ref,
-    grad_ref, branch_ref, dproj_ref, sums_ref,
+    has_query, g_ref, raw_ref, proj_ref, hat_ref, rstd_ref, gain_ref, *refs
 ):
+    grad_ref, branch_ref, raw_out, sums_ref = refs[-4:]
     g, raw = g_ref[...], raw_ref[...]
+    if has_query:
+        q = refs[0][...]
+        g = g + jnp.concatenate([q, jnp.zeros((g.shape[0] - q.shape[0], q.shape[1]), f32)], axis=0)
     scale = lax.rsqrt(head_sums(raw * raw) + eps_vec)
     y = raw * scale
     raw_grad = (scale * (g - y * head_sums(y * g))).astype(bf16)
@@ -604,7 +638,7 @@
     branch = grad.astype(bf16)
     grad_ref[...] = grad
     branch_ref[...] = branch
-    add_up(dproj_ref, contract(low_ref[...], raw_grad, 0, 0))
+    raw_out[...] = raw_grad
     add_up(
         sums_ref,
         jnp.concatenate(
@@ -618,33 +652,43 @@
     )
 
 
-def head_back(g, raw, low, proj, hat, rstd, gain, wait=()):
+def head_back(g, raw, proj, hat, rstd, gain, query=None, before=(), wait=()):
     t, e = raw.shape
+    first, steps = (1, t // TILE - 1) if query is None else (0, 1)
+    extra = [] if query is None else [query]
+    rows = lambda width: pl.BlockSpec((TILE, width), lambda i, *_: (first + i, 0))
     return call(
-        head_back_kernel,
+        functools.partial(head_back_kernel, query is not None),
         "head_back",
-        (t // TILE,),
+        (steps,),
         [
-            row_spec(TILE, e),
-            row_spec(TILE, e),
-            row_spec(TILE, D),
+            rows(e),
+            rows(e),
             whole_spec((D, e)),
-            row_spec(TILE, D),
-            row_spec(TILE, LANES),
+            rows(D),
+            rows(LANES),
             whole_spec((1, D)),
-        ],
-        [row_spec(TILE, D), row_spec(TILE, D), whole_spec((D, e)), whole_spec((3, D))],
-        [like((t, D), f32), like((t, D), bf16), like((D, e), f32), like((3, D), f32)],
-        4 * t * D * e,
-        16 * t * D,
+        ]
+        + [whole_spec(x.shape) for x in extra]
+        + [pl.BlockSpec(memory_space=pl.ANY)] * len(before),
+        [rows(D), rows(D), rows(e), whole_spec((3, D))],
+        [like((t, D), f32), like((t, D), bf16), like((t, e), bf16), like((3, D), f32)],
+        2 * steps * TILE * D * e,
+        16 * steps * TILE * D,
         wait=wait,
-    )(g, raw, low, proj, hat, rstd, gain)
+        aliases={6 + len(extra) + i: i for i in range(len(before))},
+    )(g, raw, proj, hat, rstd, gain, *extra, *before)
 
 
 def act_back_kernel(g_ref, w_ref, slope_ref, o_ref, sum_ref):
-    back = (contract(g_ref[...], w_ref[...], 1, 1) * slope_ref[...].astype(f32)).astype(bf16)
-    o_ref[...] = back
-    sum_ref[...] = column_sum(back.astype(f32))
+    total = jnp.zeros(sum_ref.shape, f32)
+    for row in range(0, g_ref.shape[0], TILE):
+        rows = slice(row, row + TILE)
+        back = contract(g_ref[rows, :], w_ref[...], 1, 1) * slope_ref[rows, :].astype(f32)
+        back = back.astype(bf16)
+        o_ref[rows, :] = back
+        total = total + column_sum(back.astype(f32))
+    sum_ref[...] = total
 
 
 def act_back(branch, w, slope, wait=()):
@@ -666,20 +710,20 @@
     g_ref, w_ref, resid_ref, hat_ref, rstd_ref, gain_ref, wout_ref,
     grad_ref, out_ref, att_ref, sums_ref,
 ):
-    hidden_grad = resid_ref[...] + contract(g_ref[...], w_ref[...], 1, 1)
-    hat = hat_ref[...]
-    grad = norm_back(hidden_grad, hat, rstd_ref[:, :1], gain_ref[...])
-    low = grad.astype(bf16)
-    grad_ref[...] = grad
-    out_ref[...] = low
-    att_ref[...] = contract(low, wout_ref[...], 1, 1).astype(bf16)
-    add_up(
-        sums_ref,
-        jnp.concatenate(
-            [column_sum(hidden_grad * hat), column_sum(hidden_grad), column_sum(low.astype(f32))],
-            axis=0,
-        ),
-    )
+    for row in range(0, g_ref.shape[0], TILE):
+        rows = slice(row, row + TILE)
+        hidden_grad = resid_ref[rows, :] + contract(g_ref[rows, :], w_ref[...], 1, 1)
+        hat = hat_ref[rows, :]
+        grad = norm_back(hidden_grad, hat, rstd_ref[rows, :1], gain_ref[...])
+        low = grad.astype(bf16)
+        grad_ref[rows, :] = grad
+        out_ref[rows, :] = low
+        att_ref[rows, :] = contract(low, wout_ref[...], 1, 1).astype(bf16)
+        sums = [column_sum(hidden_grad * hat), column_sum(hidden_grad), column_sum(low.astype(f32))]
+        if row == 0:
+            add_up(sums_ref, jnp.concatenate(sums, axis=0))
+        else:
+            sums_ref[...] += jnp.concatenate(sums, axis=0)
 
 
 def hidden_back(inner, w, resid, hat, rstd, gain, w_out, wait=()):
@@ -732,21 +776,23 @@
     )(*grads, w, resid)
 
 
+def block_masks(n_devices, width):
+    n = width * n_devices
+    column = lax.broadcasted_iota(jnp.int32, (n_devices, n), 1)
+    first = lax.broadcasted_iota(jnp.int32, (n_devices, n), 0) * width
+    mine = (column >= first) & (column < first + width)
+    at = lax.broadcasted_iota(jnp.int32, (1, n), 1) % width
+    return mine, at
+
+
 def unpack_kernel(n_devices, widths, p_ref, *o_refs):
-    at = 0
+    start = 0
     for width, o_ref in zip(widths, o_refs):
-        n = width * n_devices
-        x = p_ref[:, at : at + width]
-        copies = (
-            lax.broadcasted_iota(jnp.int32, (width, n), 1) % width
-            == lax.broadcasted_iota(jnp.int32, (width, n), 0)
-        ).astype(bf16)
-        mine = (
-            lax.broadcasted_iota(jnp.int32, (n_devices, n), 1) // width
-            == lax.broadcasted_iota(jnp.int32, (n_devices, n), 0)
-        )
-        o_ref[...] = column_sum(jnp.where(mine, contract(x, copies, 1, 0), 0.0))
-        at += width
+        mine, at = block_masks(n_devices, width)
+        copies = (at == lax.broadcasted_iota(jnp.int32, (width, at.shape[1]), 0)).astype(bf16)
+        spread = contract(p_ref[:, start : start + width], copies, 1, 0)
+        o_ref[...] = column_sum(jnp.where(mine, spread, 0.0))
+        start += width
 
 
 def unpack(packed, widths, wait=()):
@@ -767,25 +813,18 @@
 def pack_kernel(n_devices, widths, *refs):
     o_ref = refs[-1]
     o_ref[...] = jnp.zeros_like(o_ref)
-    at = 0
+    start = 0
     for width, ref in zip(widths, refs):
-        n = width * n_devices
-        mine = (
-            lax.broadcasted_iota(jnp.int32, (n_devices, n), 1) // width
-            == lax.broadcasted_iota(jnp.int32, (n_devices, n), 0)
-        )
-        copies = (
-            lax.broadcasted_iota(jnp.int32, (n, width), 0) % width
-            == lax.broadcasted_iota(jnp.int32, (n, width), 1)
-        ).astype(f32)
-        o_ref[:, at : at + width] = lax.dot_general(
-            jnp.where(mine, ref[...], 0.0),
-            copies,
-            (((1,), (0,)), ((), ())),
-            precision=highest,
-            preferred_element_type=f32,
-        )
-        at += width
+        mine, at = block_masks(n_devices, width)
+        copies = (at == lax.broadcasted_iota(jnp.int32, (width, at.shape[1]), 0)).astype(bf16)
+        rest = jnp.where(mine, ref[...], 0.0)
+        total = jnp.zeros((n_devices, width), f32)
+        for _ in range(3):
+            term = rest.astype(bf16)
+            total = total + contract(term, copies, 1, 1)
+            rest = rest - term.astype(f32)
+        o_ref[:, start : start + width] = total
+        start += width
 
 
 def pack(vectors, n_devices, wait=()):
@@ -805,45 +844,71 @@
     )(*vectors)
 
 
-def weight_kernel(n_rows, n_z, offset, table, a_ref, b_ref, *refs):
+def pick_columns(table, offset, n_rows, n_z, a_ref, picked):
     t, k = a_ref.shape
     block = k // n_rows
-    r = block // (2 * n_z)
-    turned = refs[-1]
+    half = block // 2
+    r = half // n_z
+    core = table[2 * n_rows]
+    side = core if offset == 0 else 1 - core
+    if r % LANES:
+        m = lax.broadcasted_iota(jnp.int32, (block, half), 1)
+        source = (m // r) * (2 * r) + side * r + m % r
+        choose = (lax.broadcasted_iota(jnp.int32, (block, half), 0) == source).astype(bf16)
+    for piece in range(n_rows):
+        first = table[offset + piece] * block
+        if r % LANES:
+            x = a_ref[:, pl.ds(pl.multiple_of(first, LANES), block)]
+            picked[:, piece * half : (piece + 1) * half] = contract(x, choose, 1, 0).astype(bf16)
+        else:
+            for z in range(n_z):
+                x = a_ref[:, pl.ds(pl.multiple_of(first + (2 * z + side) * r, LANES), r)]
+                at = piece * half + z * r
+                picked[:, at : at + r] = x
+
+
+def weight_kernel(pairs, offset, n_rows, n_z, table, *refs):
+    ins, refs = refs[: 2 * pairs], refs[2 * pairs :]
+    refs, picked = refs[:-pairs], refs[-pairs:]
 
     @pl.when(pl.program_id(0) == 0)
     def _():
-        core = table[2 * n_rows]
-        side = core if offset == 0 else 1 - core
-        for piece in range(n_rows):
-            mesh_row = table[offset + piece]
-            cols = pl.ds(pl.multiple_of(mesh_row * block, block), block)
-            x = a_ref[:, cols].T.reshape(n_z, 2, r, t)
-            half = jnp.where(side == 0, x[:, 0], x[:, 1]).reshape(n_z * r, t)
-            turned[piece * n_z * r : (piece + 1) * n_z * r, :] = half
-
-    total = contract(turned[...], b_ref[...].reshape(b_ref.shape[-2:]), 1, 0)
-    total = total.reshape(n_rows, n_z, r, total.shape[1])
-    if offset:
-        refs[0][...] = total.astype(refs[0].dtype)
+        for a_ref, p_ref in zip(ins[::2], picked):
+            pick_columns(table, offset, n_rows, n_z, a_ref, p_ref)
+
+    totals = []
+    for p_ref, b_ref in zip(picked, ins[1::2]):
+        b = b_ref[...]
+        totals.append(contract(p_ref[...], b.reshape(b.shape[-2:]), 0, 0))
+    total = totals[0] if pairs == 1 else jnp.concatenate(totals, axis=1)
+    if len(refs) == 1:
+        refs[0][...] = total.reshape(refs[0].shape).astype(refs[0].dtype)
     else:
-        other, send_ref, keep_ref = refs[:3]
-        total += other[...].astype(f32)
-        send_ref[...] = total[n_rows // 2 :].astype(send_ref.dtype)
-        keep_ref[...] = total[: n_rows // 2]
-
-
-def weight_half(
-    name, table, a, b, n_rows, n_z, tile, other=None, other_type=bf16, wait=()
-):
-    t, k = a.shape
-    per_part = b.shape[-1] // tile
-    n = b.shape[-1] * (b.shape[0] if b.ndim == 3 else 1)
+        other, send_ref, keep_ref = refs
+        total = total.reshape(other.shape) + other[...].astype(f32)
+        half = keep_ref.shape[0]
+        send_ref[...] = total[half:].astype(send_ref.dtype)
+        keep_ref[...] = total[:half]
+
+
+def weight_half(name, table, operands, n_rows, n_z, tile, other=None, other_type=bf16, wait=()):
+    t, k = operands[0][0].shape
     r = k // (n_rows * n_z * 2)
-    if b.ndim == 3:
-        b_spec = pl.BlockSpec((1, t, tile), lambda i, _: (i // per_part, 0, i % per_part))
+    specs, arrays = [], []
+    if len(operands) == 1:
+        a, b = operands[0]
+        per_part = b.shape[-1] // tile
+        n = b.shape[-1] * (b.shape[0] if b.ndim == 3 else 1)
+        if b.ndim == 3:
+            b_spec = pl.BlockSpec((1, t, tile), lambda i, _: (i // per_part, 0, i % per_part))
+        else:
+            b_spec = col_spec(t, tile)
+        specs, arrays = [whole_spec((t, k)), b_spec], [a, b]
     else:
-        b_spec = col_spec(t, tile)
+        n = tile = sum(b.shape[1] for _, b in operands)
+        for a, b in operands:
+            specs += [whole_spec((t, k)), whole_spec(b.shape)]
+            arrays += [a, b]
 
     def block(rows):
         return pl.BlockSpec((rows, n_z, r, tile), lambda i, _: (0, 0, 0, i))
@@ -853,21 +918,21 @@
 
     own = other is not None
     return call(
-        functools.partial(weight_kernel, n_rows, n_z, 0 if own else n_rows),
+        functools.partial(weight_kernel, len(operands), 0 if own else n_rows, n_rows, n_z),
         name,
         (n // tile,),
-        [whole_spec((t, k)), b_spec] + ([block(n_rows)] if own else []),
+        specs + ([block(n_rows)] if own else []),
         [block(n_rows // 2)] * 2 if own else block(n_rows),
         [shape(n_rows // 2, bf16), shape(n_rows // 2, f32)] if own else shape(n_rows, other_type),
         t * k * n,
         2 * t * (k + n) + 3 * k * n,
-        [pltpu.VMEM((k // 2, t), bf16)],
+        [pltpu.VMEM((t, k // 2), bf16) for _ in operands],
         table=table,
         wait=wait,
-    )(table, a, b, *([other] if own else []))
-
-
-WIN = -(-(DMOST + 15) // 32) * 32
+    )(table, *arrays, *([other] if own else []))
+
+
+WINDOWS = (256, -(-(DMOST + 15) // 32) * 32)
 NEG = -1e30
 
 
@@ -875,15 +940,28 @@
     return lax.dot_general(a, b, (((ca,), (cb,)), ((), ())), preferred_element_type=f32)
 
 
-def spans(len_ref, row_len):
-    found = []
-    start = jnp.int32(QPR * QLEN)
-    for d in range(DPR):
-        size = len_ref[d]
-        base = pl.multiple_of(jnp.minimum((start // 16) * 16, row_len - WIN), 16)
-        found.append((base, start - base, start - base + size))
-        start = start + size
-    return found
+def document_table(lengths):
+    at = jnp.arange(DPR)
+    starts = QPR * QLEN + jnp.sum(jnp.where(at[:, None] < at[None, :], lengths[:, None], 0), axis=0)
+    need = starts % 16 + lengths
+    ahead = (need[:, None] > need[None, :]) | ((need[:, None] == need[None, :]) & (at[:, None] < at[None, :]))
+    rank = jnp.sum(ahead.astype(jnp.int32), axis=0)
+    order = rank[None, :] == at[:, None]
+    pick = lambda x: jnp.sum(jnp.where(order, x[None, :], 0), axis=1)
+    wide = jnp.sum((need > WINDOWS[0]).astype(jnp.int32))
+    return jnp.concatenate([pick(starts), pick(lengths), wide[None]]).astype(jnp.int32)
+
+
+def for_documents(doc_ref, row_len, step):
+    for wide in range(1, DPR):
+
+        @pl.when(doc_ref[2 * DPR] == wide)
+        def _():
+            for d in range(DPR):
+                window = WINDOWS[1] if d < wide else WINDOWS[0]
+                start, size = doc_ref[d], doc_ref[DPR + d]
+                base = pl.multiple_of(jnp.minimum((start // 16) * 16, row_len - window), 16)
+                step(window, base, start - base, start - base + size)
 
 
 def head_pair(x):
@@ -915,12 +993,13 @@
 
 
 def attention_kernel(len_ref, q_ref, k_ref, v_ref, o_ref):
-    row_len = q_ref.shape[0]
-    for base, low, high in spans(len_ref, row_len):
-        w = pl.ds(base, WIN)
+    def step(window, base, low, high):
+        w = pl.ds(base, window)
         o = attend(q_ref[w, :], k_ref[w, :], v_ref[w, :], low, high)
-        keep = inside(WIN, low, high, 0)
+        keep = inside(window, low, high, 0)
         o_ref[w, :] = jnp.where(keep, o, o_ref[w, :].astype(f32)).astype(bf16)
+
+    for_documents(len_ref, q_ref.shape[0], step)
     o_ref[:QLEN, :] = attend(q_ref[:QLEN, :], k_ref[:128, :], v_ref[:128, :], 0, QLEN).astype(bf16)
 
 
@@ -974,11 +1053,14 @@
     )
     for ref, x in zip(sums, parts):
         ref[: x.shape[0], :] = x
-    for base, low, high in spans(len_ref, row_len):
-        w = pl.ds(base, WIN)
+
+    def step(window, base, low, high):
+        w = pl.ds(base, window)
         parts = attend_back(q_ref[w, :], k_ref[w, :], v_ref[w, :], g_ref[w, :], low, high)
         for ref, x in zip(sums, parts):
             ref[w, :] += x
+
+    for_documents(len_ref, row_len, step)
     cosine, sine = cos_ref[...], sin_ref[...]
     for part in range(3):
         x = sums[part][...]
@@ -1040,10 +1122,10 @@
     docs = doc_ref[...]
     n_queries = score_ref.shape[2]
     live = lax.broadcasted_iota(jnp.int32, (8, n_queries), 0) < DPR
-    for head, mask in enumerate(head_masks(docs.shape[1])):
+    for head, (lanes, mask) in enumerate(head_lanes()):
         scores = jnp.zeros((8, n_queries), f32)
         for at in range(0, query_ref.shape[0], SCORE_TILE):
-            _, e = score_exps(docs, query_ref[at : at + SCORE_TILE, :], mask)
+            _, e = score_exps(docs[:, lanes], query_ref[at : at + SCORE_TILE, lanes], mask)
             total = split_dot(hot_ref[...], e)
             sum_ref[head, :, at : at + SCORE_TILE] = total
             smooth = jnp.log(total) - count_ref[:, :1]
@@ -1071,24 +1153,24 @@
     dd_ref[...] = jnp.zeros_like(dd_ref)
     dq_ref[...] = jnp.zeros_like(dq_ref)
     index = index_ref[...]
-    for head, mask in enumerate(head_masks(docs.shape[1])):
+    for head, (lanes, mask) in enumerate(head_lanes()):
         stats = stat_ref[head]
         grad = jnp.exp(score_ref[head] - stats[0:1]) / stats[1:2] - pos_ref[...]
         for at in range(0, query_ref.shape[0], SCORE_TILE):
-            queries = query_ref[at : at + SCORE_TILE, :]
-            picked, e = score_exps(docs, queries, mask)
+            queries = query_ref[at : at + SCORE_TILE, lanes]
+            picked, e = score_exps(docs[:, lanes], queries, mask)
             query = lax.broadcasted_iota(jnp.int32, (n_queries, SCORE_TILE), 0)
             hot = (id_ref[:, at : at + SCORE_TILE] == query).astype(f32)
             spread = lax.dot_general(
                 grad, hot, (((1,), (0,)), ((), ())), precision=highest, preferred_element_type=f32
             )
             coef = score_scale * spread / sum_ref[head, :, at : at + SCORE_TILE]
-            wide = coef[0:1]
-            for d in range(1, DPR):
+            wide = jnp.zeros_like(e)
+            for d in range(DPR):
                 wide = jnp.where(index == d, coef[d : d + 1], wide)
             back = (e * wide).astype(bf16)
-            dd_ref[...] += jnp.where(mask, contract(back, queries, 1, 0), 0.0)
-            dq_ref[at : at + SCORE_TILE, :] += contract(back, picked, 0, 0)
+            dd_ref[:, lanes] += jnp.where(mask, contract(back, queries, 1, 0), 0.0)
+            dq_ref[at : at + SCORE_TILE, lanes] += contract(back, picked, 0, 0)
 
 
 def score_stats(docs, queries, ids, hot, counts, positive, wait=()):
@@ -1120,7 +1202,7 @@
         12 * n * n_tokens * e,
         10**6,
         wait=wait,
-    )(docs, queries, ids[:, None], hot, counts, positive)
+    )(docs, queries, ids, hot, counts, positive)
 
 
 def score_grads(docs, queries, ids, index, sums, scores, stats, positive, wait=()):
@@ -1146,7 +1228,7 @@
         24 * n * n_tokens * e,
         10**6,
         wait=wait,
-    )(docs, queries, ids[None], index, sums, scores, stats, positive)
+    )(docs, queries, ids, index, sums, scores, stats, positive)
 
 
 def layout(lengths, row_len, q_tokens):
@@ -1208,26 +1290,29 @@
     row_len = tokens.shape[0]
     q_tokens = QPR * QLEN
 
-    g_qkv, g_out, g_up, g_down = (Gather(w) for w in (w_qkv, w_out, w_up, w_down))
+    proj_width = -(-w_proj.shape[1] // LANES) * LANES
+    w_out_proj = jnp.concatenate(
+        [w_out, jnp.pad(w_proj, ((0, 0), (0, proj_width - w_proj.shape[1])))], axis=1
+    )
+    g_qkv, g_out, g_up, g_down = (Gather(w) for w in (w_qkv, w_out_proj, w_up, w_down))
     g_qkv.all_z(())
-    g_out.all_z([[g_qkv.held]])
     g_qkv.all_rows((), ())
-    first, last = g_qkv.pieces[1:-1], g_qkv.pieces[-1]
+    first, last = g_qkv.own, g_qkv.pieces[-1]
     vectors = (b_qkv, b_out, norm1_gain, norm1_bias, b_up, b_down, norm2_gain, norm2_bias)
     widths = [v.shape[0] for v in vectors]
-    packed = jnp.concatenate([after(v, g_qkv.held) for v in vectors])
+    packed = jnp.concatenate(vectors)
     packed = jnp.pad(packed, (0, -packed.shape[0] % LANES)).reshape(-1, LANES)
-    packed = gather_small(packed).reshape(n_devices, -1)
+    packed = gather_small(packed, g_qkv.received + [first[0], last]).reshape(n_devices, -1)
     full_bqkv, full_bout, gain_one, bias_one, full_bup, full_bdown, gain_two, bias_two = unpack(
         packed, widths
     )
-    full_proj = gather_small(after(w_proj, *first)).reshape(-1, w_proj.shape[1])
-    g_up.all_z([[g_out.held, *first]], [[last]])
-    g_out.all_rows([first], [[last]])
+    g_up.all_z([[g_qkv.held], first], [first, [last]])
+    g_out.all_z([first])
     w_qkv_all = g_qkv.whole(table)
 
     own_lengths = lax.dynamic_index_in_dim(lengths, device, 0, keepdims=False)
     position, doc_index = layout(own_lengths, row_len, q_tokens)
+    documents = document_table(own_lengths)
     half = HEAD_DIM // 2
     frequency = 10000.0 ** (-jnp.arange(half, dtype=f32) / half)
     angles = position.astype(f32)[:, None] * frequency[None, :]
@@ -1235,112 +1320,145 @@
     cosine = jnp.concatenate([cosine] * 4, axis=1)
     sine = jnp.concatenate([-sine, sine] * 2, axis=1)
     qkv, full_qkv = project_qkv(
-        tokens, w_qkv_all, full_bqkv, cosine, sine, wait=[g_up.held, full_proj]
-    )
-    g_up.all_rows([[g_out.pieces[1], last], [qkv]], [[qkv]])
-    w_out_all = g_out.whole(table, [[qkv]], [[qkv]])
-    g_up_first = g_up.pieces[1:-1]
-    attended = attention(own_lengths, qkv, wait=g_up_first)
-    g_down.all_z([[g_up.held], [qkv]], [[qkv], [attended]])
-    hat1, rstd1, hidden_low, full_out = out_norm(
-        attended, w_out_all, full_bout, tokens, gain_one, bias_one, wait=[g_down.held]
-    )
-
-    w_up_all = g_up.whole(table, [[qkv], [attended]], [[attended]])
-    part = up_gelu(hidden_low, w_up_all, full_bup)
-    g_down.all_rows([[attended], [part[0]]], [[part[0]]])
-    act, slope, full_up = up_gelu(hidden_low, w_up_all, full_bup, part, wait=g_down.pieces[1:-1])
-    w_down_all = g_down.whole(table, [[part[0]], [act]], [[act]])
-    hat2, rstd2, result_low, raw, vecs, full_down = down_norm(
-        act, w_down_all, full_bdown, hat1, gain_one, bias_one, gain_two, bias_two, full_proj
-    )
-    full_qkv, full_out, full_up, full_down = (
-        w.reshape(-1, w.shape[-1]) for w in (full_qkv, full_out, full_up, full_down)
-    )
-
-    query_all = gather_relative(vecs[:q_tokens]).reshape(n_devices * q_tokens, -1)
-    query_ids = relative_order()[:, None] * QPR + jnp.arange(q_tokens, dtype=jnp.int32)[None, :] // QLEN
-    query_ids = query_ids.reshape(-1)
-    docs = vecs[q_tokens:]
-    doc_index = doc_index[q_tokens:]
+        tokens, w_qkv_all, full_bqkv, cosine, sine, wait=[g_up.held]
+    )
+    g_out.own_rows([last], [qkv])
+    g_up.own_rows([last], [qkv])
+    doc_index = jnp.where(jnp.arange(row_len) < q_tokens, -1, doc_index)
     slots = jnp.arange(8, dtype=jnp.int32)
     hot = (slots[:, None] == doc_index[None, :]).astype(bf16)
     counts = jnp.broadcast_to(
         jnp.log(jnp.pad(own_lengths, (0, 8 - DPR), constant_values=1).astype(f32))[:, None],
         (8, LANES),
     )
-    positive = ((positives[None, :] == device * DPR + slots[:, None]) & (slots < DPR)[:, None]).astype(f32)
-    sums, doc_scores, stats = score_stats(docs, query_all, query_ids, hot, counts, positive)
+    positive = (
+        (positives[None, :] == device * DPR + slots[:, None]) & (slots < DPR)[:, None]
+    ).astype(f32)
+    query_ids = relative_order()[:, None] * QPR + jnp.arange(q_tokens, dtype=jnp.int32)[None, :] // QLEN
+    query_ids = query_ids.reshape(-1, 1)
+    query_row = query_ids.reshape(1, -1)
+    doc_column = doc_index[:, None]
+    early = [hot, counts, positive, query_ids, query_row, doc_column]
+    attended = attention(documents, qkv, wait=[*g_up.pieces[1:], *early])
+    g_out.other_rows([qkv], [attended])
+    g_up.other_rows([qkv], [attended])
+    w_out_all = g_out.whole(table, [[qkv], [attended]], [[attended]])
+    g_down.all_z([[g_up.held], [qkv]], [[qkv], [attended]])
+    hat1, rstd1, hidden_low, full_out = out_norm(
+        attended, w_out_all.columns(0, D), full_bout, tokens, gain_one, bias_one, wait=[g_down.held]
+    )
+
+    w_up_all = g_up.whole(table, [[qkv], [attended]], [[attended]])
+    part = up_gelu(hidden_low, w_up_all, full_bup)
+    g_down.own_rows([attended], [part[0]])
+    g_down.other_rows([part[0]])
+    act, slope, full_up = up_gelu(hidden_low, w_up_all, full_bup, part, wait=g_down.own)
+    w_down_all = g_down.whole(table, [[part[0]], [act]], [[act]])
+    hat2, rstd2, result_low, raw, vecs, full_down, full_proj = down_norm(
+        act,
+        w_down_all,
+        full_bdown,
+        hat1,
+        gain_one,
+        bias_one,
+        gain_two,
+        bias_two,
+        w_out_all.columns(D, proj_width),
+    )
+    full_qkv, full_out, full_up, full_down, full_proj = (
+        w.reshape(-1, w.shape[-1]) for w in (full_qkv, full_out, full_up, full_down, full_proj)
+    )
+
+    query_all = gather_relative(vecs[:q_tokens]).reshape(n_devices * q_tokens, -1)
+    sums, doc_scores, stats = score_stats(
+        vecs, query_all, query_ids, hot, counts, positive
+    )
     stats = reduce_stats(stats)
     query_count = n_z * 2 * QPR
     losses = lax.dynamic_slice_in_dim(
         stats[:, 0] + jnp.log(stats[:, 1]) - stats[:, 2], row * query_count, query_count, 1
     )
     query_grads, doc_grads = score_grads(
-        docs, query_all, query_ids, doc_index[:, None], sums, doc_scores, stats, positive
-    )
-    query_grad = scatter_relative(query_grads.reshape(2, n_rows, n_z, q_tokens, -1), bf16)
-    vector_grad = jnp.concatenate([query_grad, doc_grads], axis=0)
-
-    resid_two_grad, branch_grad, grad_proj, sums2 = head_back(
-        vector_grad, raw, result_low, full_proj, hat2, rstd2, gain_two
-    )
-    def sib_half(name, a, b, tile, dtype=bf16, wait=()):
-        return weight_half(
-            name + "_sib", table, a, b, n_rows, n_z, tile, other_type=dtype, wait=wait
-        )
-
-    def own_half(name, a, b, tile, sib, wide=False, wait=()):
+        vecs, query_all, query_row, doc_column, sums, doc_scores, stats, positive
+    )
+    doc_part = head_back(doc_grads, raw, full_proj, hat2, rstd2, gain_two)
+    query_grad = scatter_relative(
+        query_grads.reshape(2, n_rows, n_z, q_tokens, -1), bf16, [doc_part[2]]
+    )
+    resid_two_grad, branch_grad, raw_grad, sums2 = head_back(
+        doc_grads, raw, full_proj, hat2, rstd2, gain_two, query_grad, doc_part[:3]
+    )
+    sums2 = sums2 + doc_part[3]
+
+    def sib_half(name, operands, tile, dtype=bf16, wait=()):
+        return weight_half(name + "_sib", table, operands, n_rows, n_z, tile, other_type=dtype, wait=wait)
+
+    def own_half(name, operands, tile, sib, wide=False, wait=()):
         other = exchange(sib, swap_core=True)
-        return Scatter(*weight_half(name, table, a, b, n_rows, n_z, tile, other, wait=wait), wide)
+        return Scatter(*weight_half(name, table, operands, n_rows, n_z, tile, other, wait=wait), wide)
 
     def attention_part(i, wait):
-        return attention_back(own_lengths, qkv, attended_grad, cosine, sine, i, 2, wait=wait)
-
-    down_sib = sib_half("grad_down", act, branch_grad, 512)
+        return attention_back(documents, qkv, attended_grad, cosine, sine, i, 2, wait=wait)
+
+    down_sib = sib_half("grad_down", [(act, branch_grad)], 512)
     inner_grad, grad_bup = act_back(branch_grad, full_down, slope, wait=[down_sib])
-    down = own_half("grad_down", act, branch_grad, 512, down_sib, True, wait=[grad_bup])
-    up_sib = sib_half("grad_up", hidden_low, inner_grad, 1024, f32, wait=[down.send])
+    down = own_half("grad_down", [(act, branch_grad)], 512, down_sib, True, wait=[grad_bup])
+    up_sib = sib_half("grad_up", [(hidden_low, inner_grad)], 1024, f32, wait=[down.send])
     resid_one_grad, out_grad, attended_grad, sums1 = hidden_back(
         inner_grad, full_up, resid_two_grad, hat1, rstd1, gain_one, full_out, wait=[up_sib]
     )
     d2 = down.step(sums1)
-    up = own_half("grad_up", hidden_low, inner_grad, 1024, up_sib, wait=[sums1, d2])
+    up = own_half("grad_up", [(hidden_low, inner_grad)], 1024, up_sib, wait=[sums1, d2])
     d3 = down.step(up.send)
     grad_a, sums_a = attention_part(0, [up.send, d3])
-    sib_a = sib_half("grad_qkv", tokens, grad_a, 512)
+    sib_a = sib_half("grad_qkv", [(tokens, grad_a)], 512)
     d4 = down.step(sums_a)
     u2 = up.step(sums_a)
-    out_sib = sib_half("grad_out", attended, out_grad, 1024, wait=[sib_a])
+    out_sib = sib_half(
+        "grad_out", [(attended, out_grad), (result_low, raw_grad)], None, wait=[sib_a]
+    )
     grad_b, sums_b = attention_part(1, [out_sib, d4, u2])
-    qkv_a = own_half("grad_qkv", tokens, grad_a, 512, sib_a, wait=[sums_b])
+    sib_b = sib_half("grad_qkv", [(tokens, grad_b)], 512)
+    out = own_half(
+        "grad_out",
+        [(attended, out_grad), (result_low, raw_grad)],
+        None,
+        out_sib,
+        True,
+        wait=[sib_b],
+    )
+    u3 = up.step(sums_b)
     sum_down = down.finish(sums_b)
-    u3 = up.step(sums_b)
-    out = own_half("grad_out", attended, out_grad, 1024, out_sib, True, wait=[qkv_a.send, u3])
-    sib_b = sib_half("grad_qkv", tokens, grad_b, 512, wait=[out.send])
-    u4 = up.step(sib_b)
-    a2 = qkv_a.step(sib_b)
-    qkv_b = own_half("grad_qkv", tokens, grad_b, 512, sib_b, wait=[u4, a2])
-    a3 = qkv_a.step(qkv_b.send)
-    o2 = out.step(qkv_b.send)
-    input_grad = input_back([grad_a, grad_b], full_qkv, resid_one_grad, wait=[qkv_b.send, a3, o2])
-    sum_up = up.finish(input_grad)
+    qkv_a = own_half("grad_qkv", [(tokens, grad_a)], 512, sib_a, wait=[out.send, u3])
+    u4 = up.step(qkv_a.send)
+    o2 = out.step(qkv_a.send)
+    qkv_b = own_half("grad_qkv", [(tokens, grad_b)], 512, sib_b, wait=[qkv_a.send, u4, o2])
+    a2 = qkv_a.step(qkv_b.send)
+    o3 = out.step(qkv_b.send)
+    input_grad = input_back([grad_a, grad_b], full_qkv, resid_one_grad, wait=[qkv_b.send, a2, o3])
+    b2 = qkv_b.step(input_grad)
+    qkv_a.step(input_grad)
+    o4 = out.step(b2)
+    sum_up = up.finish(b2)
     grads = [sums_a[i] if j == 0 else sums_b[i] for i in range(3) for j in range(2)]
     grad_bqkv = jnp.concatenate(grads, axis=1)
     small = pack(
         [grad_bqkv, sums1[2:3], sums1[0:1], sums1[1:2], grad_bup, sums2[2:3], sums2[0:1], sums2[1:2]],
         n_devices,
-        wait=[input_grad],
-    )
+        wait=[b2],
+    )
+    while qkv_b.stages[0][0] == "row":
+        qkv_b.step(small)
+    while qkv_a.stages[0][0] == "row":
+        qkv_a.step()
+    q3 = qkv_a.merge(qkv_b).send
     small = scatter_small(small.reshape(n_devices, -1, LANES), f32).reshape(-1)
-    sum_proj = scatter_small(
-        after(grad_proj, input_grad).reshape(n_devices, -1, grad_proj.shape[1]), bf16
-    )
-    sum_out = out.finish()
-    sum_a, sum_b = qkv_a.finish(), qkv_b.finish()
-    width = sum_a.shape[1] // 3
+    sum_out = out.finish(q3)
+    sum_out, sum_proj = sum_out[:, :D], sum_out[:, D : D + w_proj.shape[1]]
+    sum_qkv = qkv_a.finish()
+    width = D // 2
     sum_qkv = jnp.concatenate(
-        [x[:, i * width : (i + 1) * width] for i in range(3) for x in (sum_a, sum_b)], axis=1
+        [sum_qkv[:, at * width : (at + 1) * width] for at in (0, 3, 1, 4, 2, 5)], axis=1
     )
     pieces = []
     at = 0

time: 649 us -> 595 us (0.917)
  Pallas kernels: 345 us -> 323 us
  starting transfers between devices: 105 us -> 84 us
  waiting for transfers between devices: 134 us -> 113 us
    pallas_call x26 -> x27, Pallas kernels: 345 us -> 323 us  [call(): return lambda *operands: run(*operands, *wait)]
    ppermute x102 -> x90, waiting for transfers between devices: 134 us -> 113 us  [exchange(): return lax.ppermute(value, AXES, pairs)]
    ppermute x102 -> x90, starting transfers between devices: 105 us -> 84 us  [exchange(): return lax.ppermute(value, AXES, pairs)]
    add x11 -> x9, other arithmetic: 11.3 us -> 13.3 us  [step(): pick(parts[0], other) + pick(parts[1], other).astype(f32)]
  transfers between devices with their start and end apart: 102 -> 90, of which waited for: 42 -> 38; matrix products, arithmetic and copies ran while one was open for 6% -> 9% of each run, Pallas kernels for 38% -> 41%
where the time goes in v3:
time: 595 us; the launch traced here: 587 us
  Pallas kernels  323 us (54%)
  waiting for transfers between devices  113 us (19%)
  starting transfers between devices  84 us (14%)
  other arithmetic  37.3 us (6%)
  local copies, waits for them, and re-layouts  28.5 us (5%)
    pallas_call x27, Pallas kernels, call(): return lambda *operands: run(*operands, *wait)  323 us
    ppermute x90, waiting for transfers between devices, exchange(): return lax.ppermute(value, AXES, pairs)  113 us
    ppermute x90, starting transfers between devices, exchange(): return lax.ppermute(value, AXES, pairs)  84 us
    add x9, other arithmetic, step(): pick(parts[0], other) + pick(parts[1], other).astype(f32)  13.3 us
  transfers between devices with their start and end apart: 90, of which 38 were waited for; matrix products, arithmetic and copies ran while one was open for 9% of the time, Pallas kernels for 41%

profile of v3, /device:TPU:0, one launch (start us, length us, event | category | flops | bytes accessed | tf_op | source)
XLA Modules:
  0.0 587.0 jit_solution(14923375083935051583)
XLA Ops:
  0.7 4.1 collective-permute-start.1
  4.8 5.4 concatenate.32
  17.3 1.9 collective-permute-start.3
  22.2 5.7 collective-permute-done.3
  38.8 2.6 collective-permute-start.14
  41.4 5.0 collective-permute-done.4
  46.5 2.3 collective-permute-done.5.refs_6_
  50.3 3.8 collective-permute-done.14
  54.7 6.7 %collective-permute-done.18 = bf16[32,1408]{1,0:T(8,128)(2,1)S(1)} collective-permute-done((bf16[32,1408]{1,0:T(8,128)(2,1)S(1)}, bf16[32,1408]{1,0:T(8,128)(2,1)S(1)}, u32[]{:S(2)}, u32[]{:S(2)}) %collective-permute-start.18) | collective-permute-done | bytes 90144 | tf_op jit(solution)/shard_map/ppermute | solution.py:56
  61.6 2.1 collective-permute-start.15
  63.7 5.3 collective-permute-done.19
  69.9 6.7 %collective-permute-done.15 = bf16[2,32,4096]{2,1,0:T(8,128)(2,1)S(1)} collective-permute-done((bf16[2,32,4096]{2,1,0:T(8,128)(2,1)S(1)}, bf16[2,32,4096]{2,1,0:T(8,128)(2,1)S(1)}, u32[]{:S(2)}, u32[]{:S(2)}) %collective-permute-start.15) | collective-permute-done | bytes 524320 | tf_op jit(solution)/shard_map/ppermute | solution.py:56
  78.8 2.3 unpack.1
  84.2 2.4 collective-permute-start.27
  86.6 15.0 %project_qkv.1 = (bf16[1024,3072]{1,0:T(8,128)(2,1)}, bf16[4,4,2,32,3072]{4,3,2,1,0:T(8,128)(2,1)}) custom-call(s32[17]{0:T(128)} %concatenate.30.refs_0_, bf16[1024,1024]{1,0:T(8,128)(2,1)} %refs_1_.9, f32[1,3072]{1,0:T(1,128)} %get-tuple-element.143.refs_2_, f32[1024,128]{1,0:T(8,128)} %get-tuple-element.370.refs_3_.refs_5_, ...), custom_call_target="tpu_custom_call" | custom-call | flops 6442450944 | bytes 20971520 | tf_op jit(solution)/shard_map/project_qkv/pallas_call | solution.py:366
  101.6 9.0 %collective-permute-done.20.refs_7_.refs_17_ = bf16[4,32,1408]{2,1,0:T(8,128)(2,1)S(1)} collective-permute-done((bf16[4,32,1408]{2,1,0:T(8,128)(2,1)S(1)}, bf16[4,32,1408]{2,1,0:T(8,128)(2,1)S(1)}, u32[]{:S(2)}, u32[]{:S(2)}) %collective-permute-start.20) | collective-permute-done | bytes 360480 | tf_op jit(solution)/shard_map/ppermute | solution.py:56
  113.2 4.8 collective-permute-done.22.refs_9_.refs_19_
  118.8 18.3 %attention.1.refs_1_ = bf16[1024,1024]{1,0:T(8,128)(2,1)} custom-call(s32[9]{0:T(128)} %pad_add_fusion.refs_0_, bf16[1024,3072]{1,0:T(8,128)(2,1)} %get-tuple-element.148.refs_1_.refs_2_.refs_3_, bf16[1024,3072]{1,0:T(8,128)(2,1)} %get-tuple-element.148.refs_1_.refs_2_.refs_3_, bf16[1024,3072]{1,0:T(8,128)(2,1)} %get-tuple-element.148.refs_1_.refs_2_.refs_3_, ...), custom_call_target="tpu_custom_call" | custom-call | flops 20000000000 | bytes 8388608 | tf_op jit(solution)/shard_map/attention/pallas_call | solution.py:366
  138.5 3.9 collective-permute-done.26.refs_13_.refs_23_
  143.2 9.7 %out_norm.1 = (f32[1024,1024]{1,0:T(8,128)}, f32[1024,128]{1,0:T(8,128)}, bf16[1024,1024]{1,0:T(8,128)(2,1)}, bf16[4,4,2,32,1024]{4,3,2,1,0:T(8,128)(2,1)}) custom-call(s32[17]{0:T(128)} %concatenate.30.refs_0_, bf16[1024,1024]{1,0:T(8,128)(2,1)} %attention.1.refs_1_, f32[1,1024]{1,0:T(1,128)} %get-tuple-element.152.refs_2_, bf16[1024,1024]{1,0:T(8,128)(2,1)} %refs_1_.9, ...), custom_call_target="tpu_custom_call" | custom-call | flops 2147483648 | bytes 12582912 | tf_op jit(solution)/shard_map/out_norm/pallas_call | solution.py:366
  152.9 2.0 collective-permute-start.35
  155.9 16.5 %up_gelu.2 = (bf16[1024,4096]{1,0:T(8,128)(2,1)}, bf16[1024,4096]{1,0:T(8,128)(2,1)}, bf16[4,4,2,32,4096]{4,3,2,1,0:T(8,128)(2,1)}) custom-call(s32[17]{0:T(128)} %concatenate.30.refs_0_, bf16[1024,1024]{1,0:T(8,128)(2,1)} %get-tuple-element.172.refs_1_, f32[1,4096]{1,0:T(1,128)} %get-tuple-element.173.refs_2_, bf16[4,32,4096]{2,1,0:T(8,128)(2,1)} %bitcast.510, ...), custom_call_target="tpu_custom_call" | custom-call | flops 4294967296 | bytes 12582912 | tf_op jit(solution)/shard_map/up_gelu/pallas_call | solution.py:366
  174.0 15.8 %up_gelu.3 = (bf16[1024,4096]{1,0:T(8,128)(2,1)}, bf16[1024,4096]{1,0:T(8,128)(2,1)}, bf16[4,4,2,32,4096]{4,3,2,1,0:T(8,128)(2,1)}) custom-call(s32[17]{0:T(128)} %concatenate.30.refs_0_, bf16[1024,1024]{1,0:T(8,128)(2,1)} %get-tuple-element.172.refs_1_, ...), custom_call_target="tpu_custom_call", output_to_operand_aliasing={{0}: (11, {}), {1}: (12, {}), {2}: (13, {})} | custom-call | flops 4294967296 | bytes 12582912 | tf_op jit(solution)/shard_map/up_gelu/pallas_call | solution.py:366
  190.1 2.4 collective-permute-done.40.refs_15_
  193.5 21.6 %down_norm.1 = (f32[1024,1024]{1,0:T(8,128)}, f32[1024,128]{1,0:T(8,128)}, bf16[1024,1024]{1,0:T(8,128)(2,1)}, f32[1024,384]{1,0:T(8,128)}, bf16[1024,384]{1,0:T...) custom-call(s32[17]{0:T(128)} %concatenate.30.refs_0_, ...), custom_call_target="tpu_custom_call" | custom-call | flops 8589934592 | bytes 20971520 | tf_op jit(solution)/shard_map/down_norm/pallas_call | solution.py:366
  217.6 2.3 collective-permute-start.42
  220.3 2.1 collective-permute-done.42
  222.4 3.1 collective-permute-done.43
  236.9 10.1 %scores.1 = (f32[3,8,1024]{2,1,0:T(8,128)}, f32[3,8,32]{2,1,0:T(8,128)}, f32[3,3,32]{2,1,0:T(4,128)}) custom-call(bf16[1024,384]{1,0:T(8,128)(2,1)} %get-tuple-element.200.refs_0_, bf16[1024,384]{1,0:T(8,128)(2,1)} %bitcast.539, s32[1024,1]{1,0:T(8,128)} %add.653.refs_9_.refs_2_, bf16[8,1024]{1,0:T(8,128)(2,1)} %fusion.41.refs_6_.refs_3_, ...), custom_call_target="tpu_custom_call" | custom-call | flops 4831838208 | bytes 1000000 | tf_op jit(solution)/shard_map/scores/pallas_call | solution.py:366
  250.4 2.3 collective-permute-start.51
  256.0 3.4 collective-permute-start.54
  262.1 11.6 %score_grads.1 = (f32[1024,384]{1,0:T(8,128)}, f32[1024,384]{1,0:T(8,128)}) custom-call(bf16[1024,384]{1,0:T(8,128)(2,1)} %get-tuple-element.200.refs_0_, bf16[1024,384]{1,0:T(8,128)(2,1)} %bitcast.540, s32[1,1024]{1,0:T(1,128)} %add.565.refs_10_.refs_2_, s32[1024,1]{1,0:T(8,128)} %fusion.14.refs_11_.refs_3_, f32[3,8,1024]{2,1,0:T(8,128)} %get-tuple-element.203.refs_4_, ...), custom_call_target="tpu_custom_call" | custom-call | flops 9663676416 | bytes 1000000 | tf_op jit(solution)/shard_map/score_grads/pallas_call | solution.py:366
  276.1 7.6 %head_back.2 = (f32[1024,1024]{1,0:T(8,128)}, bf16[1024,1024]{1,0:T(8,128)(2,1)}, bf16[1024,384]{1,0:T(8,128)(2,1)}, f32[3,1024]{1,0:T(4,128)}) custom-call(f32[1024,384]{1,0:T(8,128)} %get-tuple-element.205.refs_0_, f32[1024,384]{1,0:T(8,128)} %get-tuple-element.206.refs_1_, bf16[1024,384]{1,0:T(8,128)(2,1)} %bitcast.517, ...), custom_call_target="tpu_custom_call" | custom-call | flops 603979776 | bytes 12582912 | tf_op jit(solution)/shard_map/head_back/pallas_call | solution.py:366
  289.2 2.2 collective-permute-done.57
  292.8 3.8 collective-permute-start.60
  298.4 3.8 collective-permute-done.61
  302.8 4.0 head_back.3
  306.8 11.8 %grad_down_sib.1.refs_3_ = bf16[4,4,128,1024]{3,2,1,0:T(8,128)(2,1)} custom-call(s32[17]{0:T(128)} %concatenate.30.refs_0_, bf16[1024,4096]{1,0:T(8,128)(2,1)} %get-tuple-element.188.refs_1_, bf16[1024,1024]{1,0:T(8,128)(2,1)} %get-tuple-element.215.refs_2_.refs_0_), custom_call_target="tpu_custom_call" | custom-call | flops 4294967296 | bytes 23068672 | tf_op jit(solution)/shard_map/grad_down_sib/pallas_call | solution.py:366
  318.6 15.4 %act_back.1 = (bf16[1024,4096]{1,0:T(8,128)(2,1)}, f32[1,4096]{1,0:T(1,128)}) custom-call(bf16[1024,1024]{1,0:T(8,128)(2,1)} %get-tuple-element.215.refs_2_.refs_0_, bf16[4096,1024]{1,0:T(8,128)(2,1)} %bitcast.565, bf16[1024,4096]{1,0:T(8,128)(2,1)} %get-tuple-element.217.refs_2_, bf16[4,4,128,1024]{3,2,1,0:T(8,128)(2,1)} %grad_down_sib.1.refs_3_), custom_call_target="tpu_custom_call" | custom-call | flops 8589934592 | bytes 25165824 | tf_op jit(solution)/shard_map/act_back/pallas_call | solution.py:366
  334.0 2.0 copy-done.51
  336.1 12.5 %grad_down.1 = (bf16[2,4,128,1024]{3,2,1,0:T(8,128)(2,1)}, f32[2,4,128,1024]{3,2,1,0:T(8,128)}) custom-call(s32[17]{0:T(128)} %concatenate.30.refs_0_, bf16[1024,4096]{1,0:T(8,128)(2,1)} %get-tuple-element.188.refs_1_, bf16[1024,1024]{1,0:T(8,128)(2,1)} %get-tuple-element.215.refs_2_.refs_0_, bf16[4,4,128,1024]{3,2,1,0:T(8,128)(2,1)} %copy-done.51, ...), custom_call_target="tpu_custom_call" | custom-call | flops 4294967296 | bytes 23068672 | tf_op jit(solution)/shard_map/grad_down/pallas_call | solution.py:366
  348.6 11.4 %grad_up_sib.1.refs_7_ = f32[4,4,32,4096]{3,2,1,0:T(8,128)} custom-call(s32[17]{0:T(128)} %concatenate.30.refs_0_, bf16[1024,1024]{1,0:T(8,128)(2,1)} %get-tuple-element.172.refs_1_, bf16[1024,4096]{1,0:T(8,128)(2,1)} %get-tuple-element.218.refs_2_.refs_0_, bf16[8,128,1024]{2,1,0:T(8,128)(2,1)} %bitcast.69.refs_3_), custom_call_target="tpu_custom_call" | custom-call | flops 4294967296 | bytes 23068672 | tf_op jit(solution)/shard_map/grad_up_sib/pallas_call | solution.py:366
  362.0 20.6 %hidden_back.1 = (f32[1024,1024]{1,0:T(8,128)}, bf16[1024,1024]{1,0:T(8,128)(2,1)}, bf16[1024,1024]{1,0:T(8,128)(2,1)}, f32[3,1024]{1,0:T(4,128)}) custom-call(bf16[1024,4096]{1,0:T(8,128)(2,1)} %get-tuple-element.218.refs_2_.refs_0_, bf16[1024,4096]{1,0:T(8,128)(2,1)} %bitcast.507, f32[1024,1024]{1,0:T(8,128)} %get-tuple-element.220.refs_2_, ...), custom_call_target="tpu_custom_call" | custom-call | flops 10737418240 | bytes 33554432 | tf_op jit(solution)/shard_map/hidden_back/pallas_call | solution.py:366
  382.5 4.3 collective-permute-done.64
  386.9 2.5 bitcast_add_fusion.2
  392.3 13.3 %grad_up.1 = (bf16[2,4,32,4096]{3,2,1,0:T(8,128)(2,1)}, f32[2,4,32,4096]{3,2,1,0:T(8,128)}) custom-call(s32[17]{0:T(128)} %concatenate.30.refs_0_, bf16[1024,1024]{1,0:T(8,128)(2,1)} %get-tuple-element.172.refs_1_, bf16[1024,4096]{1,0:T(8,128)(2,1)} %get-tuple-element.218.refs_2_.refs_0_, f32[4,4,32,4096]{3,2,1,0:T(8,128)} %collective-permute-done.63.refs_3_, ...), custom_call_target="tpu_custom_call" | custom-call | flops 4294967296 | bytes 23068672 | tf_op jit(solution)/shard_map/grad_up/pallas_call | solution.py:366
  407.9 21.8 %attention_back.2 = (bf16[3,1024,512]{2,1,0:T(8,128)(2,1)}, f32[3,1,512]{2,1,0:T(1,128)}) custom-call(s32[9]{0:T(128)} %pad_add_fusion.refs_0_, bf16[1024,3072]{1,0:T(8,128)(2,1)} %get-tuple-element.148.refs_1_.refs_2_.refs_3_, bf16[1024,3072]{1,0:T(8,128)(2,1)} %get-tuple-element.148.refs_1_.refs_2_.refs_3_, ...), custom_call_target="tpu_custom_call" | custom-call | flops 24999999488 | bytes 7340032 | tf_op jit(solution)/shard_map/attention_back/pallas_call | solution.py:366
  429.7 7.2 %grad_qkv_sib.2.refs_5_ = bf16[4,4,32,1536]{3,2,1,0:T(8,128)(2,1)} custom-call(s32[17]{0:T(128)} %concatenate.30.refs_0_, bf16[1024,1024]{1,0:T(8,128)(2,1)} %refs_1_.9, bf16[3,1024,512]{2,1,0:T(8,128)(2,1)} %get-tuple-element.231.refs_2_.refs_0_), custom_call_target="tpu_custom_call" | custom-call | flops 1610612736 | bytes 9961472 | tf_op jit(solution)/shard_map/grad_qkv_sib/pallas_call | solution.py:366
  437.0 8.4 %grad_out_sib.1.refs_7_ = bf16[4,4,32,1408]{3,2,1,0:T(8,128)(2,1)} custom-call(s32[17]{0:T(128)} %concatenate.30.refs_0_, bf16[1024,1024]{1,0:T(8,128)(2,1)} %attention.1.refs_1_, bf16[1024,1024]{1,0:T(8,128)(2,1)} %get-tuple-element.232.refs_2_, bf16[1024,1024]{1,0:T(8,128)(2,1)} %get-tuple-element.124.refs_3_, ...), custom_call_target="tpu_custom_call" | custom-call | flops 1476395008 | bytes 9306112 | tf_op jit(solution)/shard_map/grad_out_sib/pallas_call | solution.py:366
  448.3 3.1 bitcast_add_fusion
  451.5 21.4 %attention_back.3 = (bf16[3,1024,512]{2,1,0:T(8,128)(2,1)}, f32[3,1,512]{2,1,0:T(1,128)}) custom-call(s32[9]{0:T(128)} %pad_add_fusion.refs_0_, bf16[1024,3072]{1,0:T(8,128)(2,1)} %get-tuple-element.148.refs_1_.refs_2_.refs_3_, bf16[1024,3072]{1,0:T(8,128)(2,1)} %get-tuple-element.148.refs_1_.refs_2_.refs_3_, ...), custom_call_target="tpu_custom_call" | custom-call | flops 24999999488 | bytes 7340032 | tf_op jit(solution)/shard_map/attention_back/pallas_call | solution.py:366
  474.5 7.2 %grad_qkv_sib.3.refs_6_ = bf16[4,4,32,1536]{3,2,1,0:T(8,128)(2,1)} custom-call(s32[17]{0:T(128)} %concatenate.30.refs_0_, bf16[1024,1024]{1,0:T(8,128)(2,1)} %refs_1_.9, bf16[3,1024,512]{2,1,0:T(8,128)(2,1)} %get-tuple-element.238.refs_2_.refs_1_), custom_call_target="tpu_custom_call" | custom-call | flops 1610612736 | bytes 9961472 | tf_op jit(solution)/shard_map/grad_qkv_sib/pallas_call | solution.py:366
  483.5 8.4 %grad_out.1 = (bf16[2,4,32,1408]{3,2,1,0:T(8,128)(2,1)}, f32[2,4,32,1408]{3,2,1,0:T(8,128)}) custom-call(s32[17]{0:T(128)} %concatenate.30.refs_0_, bf16[1024,1024]{1,0:T(8,128)(2,1)} %attention.1.refs_1_, bf16[1024,1024]{1,0:T(8,128)(2,1)} %get-tuple-element.232.refs_2_, bf16[1024,1024]{1,0:T(8,128)(2,1)} %get-tuple-element.124.refs_3_, ...), custom_call_target="tpu_custom_call" | custom-call | flops 1476395008 | bytes 9306112 | tf_op jit(solution)/shard_map/grad_out/pallas_call | solution.py:366
  492.3 2.0 fusion.10
  497.0 7.4 %grad_qkv.2 = (bf16[2,4,32,1536]{3,2,1,0:T(8,128)(2,1)}, f32[2,4,32,1536]{3,2,1,0:T(8,128)}) custom-call(s32[17]{0:T(128)} %concatenate.30.refs_0_, bf16[1024,1024]{1,0:T(8,128)(2,1)} %refs_1_.9, bf16[3,1024,512]{2,1,0:T(8,128)(2,1)} %get-tuple-element.231.refs_2_.refs_0_, bf16[4,4,32,1536]{3,2,1,0:T(8,128)(2,1)} %collective-permute-done.69.refs_3_, ...), custom_call_target="tpu_custom_call" | custom-call | flops 1610612736 | bytes 9961472 | tf_op jit(solution)/shard_map/grad_qkv/pallas_call | solution.py:366
  509.9 2.5 collective-permute-start.88
  513.5 7.5 %grad_qkv.3 = (bf16[2,4,32,1536]{3,2,1,0:T(8,128)(2,1)}, f32[2,4,32,1536]{3,2,1,0:T(8,128)}) custom-call(s32[17]{0:T(128)} %concatenate.30.refs_0_, bf16[1024,1024]{1,0:T(8,128)(2,1)} %refs_1_.9, bf16[3,1024,512]{2,1,0:T(8,128)(2,1)} %get-tuple-element.238.refs_2_.refs_1_, bf16[4,4,32,1536]{3,2,1,0:T(8,128)(2,1)} %copy-done.10, ...), custom_call_target="tpu_custom_call" | custom-call | flops 1610612736 | bytes 9961472 | tf_op jit(solution)/shard_map/grad_qkv/pallas_call | solution.py:366
  523.8 2.1 bitcast_add_fusion.8
  526.4 12.3 %input_back.1 = f32[1024,1024]{1,0:T(8,128)} custom-call(bf16[3,1024,512]{2,1,0:T(8,128)(2,1)} %get-tuple-element.231.refs_2_.refs_0_, bf16[3,1024,512]{2,1,0:T(8,128)(2,1)} %get-tuple-element.238.refs_2_.refs_1_, bf16[1024,3072]{1,0:T(8,128)(2,1)} %bitcast.566, f32[1024,1024]{1,0:T(8,128)} %get-tuple-element.240.refs_3_, bf16[8,32,1536]{2,1,0:T(8,128)(2,1)} %bitcast.564, ...), custom_call_target="tpu_custom_call" | custom-call | flops 6442450944 | bytes 20971520 | tf_op jit(solution)/shard_map/input_back/pallas_call | solution.py:366
  539.7 3.4 pack.1
  556.6 2.1 collective-permute-start.85
  559.2 8.6 %collective-permute-done.85 = f32[4,128]{1,0:T(4,128)S(1)} collective-permute-done((f32[4,128]{1,0:T(4,128)S(1)}, f32[4,128]{1,0:T(4,128)S(1)}, u32[]{:S(2)}, u32[]{:S(2)}) %collective-permute-start.85) | collective-permute-done | bytes 2080 | tf_op jit(solution)/shard_map/ppermute | solution.py:56
  569.4 4.9 collective-permute-done.79
  576.7 9.1 %collective-permute-done.80 = bf16[1,32,3072]{2,1,0:T(8,128)(2,1)S(1)} collective-permute-done((bf16[1,32,3072]{2,1,0:T(8,128)(2,1)S(1)}, bf16[1,32,3072]{2,1,0:T(8,128)(2,1)S(1)}, u32[]{:S(2)}, u32[]{:S(2)}) %collective-permute-start.80) | collective-permute-done | bytes 196640 | tf_op jit(solution)/shard_map/ppermute | solution.py:56
  (398 shorter events, 120.1 us)
Async XLA Ops:
  0.7 16.5 %collective-permute-start.1 = (bf16[32,3072]{1,0:T(8,128)(2,1)}, bf16[32,3072]{1,0:T(8,128)(2,1)S(1)}, u32[]{:S(2)}, u32[]{:S(2)}) collective-permute-start(bf16[32,3072]{1,0:T(8,128)(2,1)} %param.21), channel_id=1, source_target_pairs={{0,4},{1,5},{2,6},{3,7},{4,0},{5,1},{6,2},{7,3},{8,12},{9,13},{10,... | collective-permute-start | bytes 589832 | tf_op jit(solution)/shard_map/ppermute | solution.py:56
  10.2 12.0 %collective-permute-start = (bf16[4,128]{1,0:T(4,128)(2,1)S(1)}, bf16[4,128]{1,0:T(4,128)(2,1)S(1)}, u32[]{:S(2)}, u32[]{:S(2)}) collective-permute-start(bf16[4,128]{1,0:T(4,128)(2,1)S(1)} %pad_bitcast_fusion), channel_id=1, source_target_pairs={{0,4},{1,5},{2,6},{3,7},{4,0},{5,1},{6,2},{7,3},{8,12},{9,13},{10,... | collective-permute-start | bytes 3080 | tf_op jit(solution)/shard_map/ppermute | solution.py:56
  17.3 10.6 %collective-permute-start.3 = (bf16[2,32,3072]{2,1,0:T(8,128)(2,1)S(1)}, bf16[2,32,3072]{2,1,0:T(8,128)(2,1)S(1)}, u32[]{:S(2)}, u32[]{:S(2)}) collective-permute-start(bf16[2,32,3072]{2,1,0:T(8,128)(2,1)S(1)} %pad_maximum_fusion.8), channel_id=1, source_target_pairs={{0,2},{1,3},{2,0},{3,1},{4,6},{5,7},{6,4},{7,5},{8,10},{9,11},{10,... | collective-permute-start | bytes 1179656 | tf_op jit(solution)/shard_map/ppermute | solution.py:56
  28.1 20.6 %collective-permute-start.5 = (bf16[4,32,3072]{2,1,0:T(8,128)(2,1)S(1)}, bf16[4,32,3072]{2,1,0:T(8,128)(2,1)}, u32[]{:S(2)}, u32[]{:S(2)}) collective-permute-start(bf16[4,32,3072]{2,1,0:T(8,128)(2,1)S(1)} %bitcast.535), channel_id=1, source_target_pairs={{0,8},{1,17},{2,10},{3,19},{4,12},{5,21},{6,14},{7,23},{8,0},{9,25... | collective-permute-start | bytes 2359304 | tf_op jit(solution)/shard_map/ppermute | solution.py:56
  31.4 22.7 %collective-permute-start.9 = (bf16[4,32,3072]{2,1,0:T(8,128)(2,1)S(1)}, bf16[4,32,3072]{2,1,0:T(8,128)(2,1)}, u32[]{:S(2)}, u32[]{:S(2)}) collective-permute-start(bf16[4,32,3072]{2,1,0:T(8,128)(2,1)S(1)} %bitcast.536), channel_id=1, source_target_pairs={{0,16},{1,9},{2,18},{3,11},{4,20},{5,13},{6,22},{7,15},{8,24},{9,1... | collective-permute-start | bytes 2359304 | tf_op jit(solution)/shard_map/ppermute | solution.py:56
  33.4 13.1 %collective-permute-start.4 = (bf16[2,2,4,128]{3,2,1,0:T(4,128)(2,1)S(1)}, bf16[2,2,4,128]{3,2,1,0:T(4,128)(2,1)S(1)}, u32[]{:S(2)}, u32[]{:S(2)}) collective-permute-start(bf16[2,2,4,128]{3,2,1,0:T(4,128)(2,1)S(1)} %pad_maximum_fusion.20), channel_id=1, source_target_pairs={{0,16},{1,17},{2,18},{3,19},{4,20},{5,21},{6,22},{7,23},{8,24},{9,... | collective-permute-start | bytes 12296 | tf_op jit(solution)/shard_map/ppermute | solution.py:56
  38.8 38.7 %collective-permute-start.10 = (bf16[4,32,3072]{2,1,0:T(8,128)(2,1)S(1)}, bf16[4,32,3072]{2,1,0:T(8,128)(2,1)}, u32[]{:S(2)}, u32[]{:S(2)}) collective-permute-start(bf16[4,32,3072]{2,1,0:T(8,128)(2,1)S(1)} %bitcast.537), channel_id=1, source_target_pairs={{0,1},{1,0},{2,3},{3,2},{4,5},{5,4},{6,7},{7,6},{8,9},{9,8},{10,11... | collective-permute-start | bytes 2359304 | tf_op jit(solution)/shard_map/ppermute | solution.py:56
  38.8 15.2 %collective-permute-start.14 = (bf16[32,4096]{1,0:T(8,128)(2,1)S(1)}, bf16[32,4096]{1,0:T(8,128)(2,1)S(1)}, u32[]{:S(2)}, u32[]{:S(2)}) collective-permute-start(bf16[32,4096]{1,0:T(8,128)(2,1)S(1)} %copy-done.39), channel_id=1, source_target_pairs={{0,4},{1,5},{2,6},{3,7},{4,0},{5,1},{6,2},{7,3},{8,12},{9,13},{10,... | collective-permute-start | bytes 786440 | tf_op jit(solution)/shard_map/ppermute | solution.py:56
  48.8 20.4 %collective-permute-start.6 = (bf16[2,2,2,4,128]{4,3,2,1,0:T(4,128)(2,1)S(1)}, bf16[2,2,2,4,128]{4,3,2,1,0:T(4,128)(2,1)S(1)}, u32[]{:S(2)}, u32[]{:S(2)}) collective-permute-start(bf16[2,2,2,4,128]{4,3,2,1,0:T(4,128)(2,1)S(1)} %pad_maximum_fusion.16), channel_id=1, source_target_pairs={{0,8},{1,9},{2,10},{3,11},{4,12},{5,13},{6,14},{7,15},{8,0},{9,1},... | collective-permute-start | bytes 24584 | tf_op jit(solution)/shard_map/ppermute | solution.py:56
  54.1 7.3 %collective-permute-start.18 = (bf16[32,1408]{1,0:T(8,128)(2,1)S(1)}, bf16[32,1408]{1,0:T(8,128)(2,1)S(1)}, u32[]{:S(2)}, u32[]{:S(2)}) collective-permute-start(bf16[32,1408]{1,0:T(8,128)(2,1)S(1)} %fusion.37), channel_id=1, source_target_pairs={{0,4},{1,5},{2,6},{3,7},{4,0},{5,1},{6,2},{7,3},{8,12},{9,13},{10,... | collective-permute-start | bytes 270344 | tf_op jit(solution)/shard_map/ppermute | solution.py:56
  54.2 15.6 %collective-permute-start.7 = (bf16[4,32,3072]{2,1,0:T(8,128)(2,1)}, bf16[4,32,3072]{2,1,0:T(8,128)(2,1)S(1)}, u32[]{:S(2)}, u32[]{:S(2)}) collective-permute-start(bf16[4,32,3072]{2,1,0:T(8,128)(2,1)} %collective-permute-done.5.refs_6_), channel_id=1, source_target_pairs={{0,16},{1,9},{2,18},{3,11},{4,20},{5,13},{6,22},{7,15},{8,24},{9,1... | collective-permute-start | bytes 2359304 | tf_op jit(solution)/shard_map/ppermute | solution.py:56
  61.5 7.6 %collective-permute-start.19 = (bf16[2,32,1408]{2,1,0:T(8,128)(2,1)S(1)}, bf16[2,32,1408]{2,1,0:T(8,128)(2,1)S(1)}, u32[]{:S(2)}, u32[]{:S(2)}) collective-permute-start(bf16[2,32,1408]{2,1,0:T(8,128)(2,1)S(1)} %pad_maximum_fusion.12), channel_id=1, source_target_pairs={{0,2},{1,3},{2,0},{3,1},{4,6},{5,7},{6,4},{7,5},{8,10},{9,11},{10,... | collective-permute-start | bytes 540680 | tf_op jit(solution)/shard_map/ppermute | solution.py:56
  61.6 15.0 %collective-permute-start.15 = (bf16[2,32,4096]{2,1,0:T(8,128)(2,1)S(1)}, bf16[2,32,4096]{2,1,0:T(8,128)(2,1)S(1)}, u32[]{:S(2)}, u32[]{:S(2)}) collective-permute-start(bf16[2,32,4096]{2,1,0:T(8,128)(2,1)S(1)} %pad_maximum_fusion.6), channel_id=1, source_target_pairs={{0,2},{1,3},{2,0},{3,1},{4,6},{5,7},{6,4},{7,5},{8,10},{9,11},{10,... | collective-permute-start | bytes 1572872 | tf_op jit(solution)/shard_map/ppermute | solution.py:56
  69.0 12.1 %collective-permute-start.11 = (bf16[4,32,3072]{2,1,0:T(8,128)(2,1)}, bf16[4,32,3072]{2,1,0:T(8,128)(2,1)}, u32[]{:S(2)}, u32[]{:S(2)}) collective-permute-start(bf16[4,32,3072]{2,1,0:T(8,128)(2,1)} %collective-permute-done.5.refs_6_), channel_id=1, source_target_pairs={{0,1},{1,0},{2,3},{3,2},{4,5},{5,4},{6,7},{7,6},{8,9},{9,8},{10,11... | collective-permute-start | bytes 2359304 | tf_op jit(solution)/shard_map/ppermute | solution.py:56
  69.2 13.5 %collective-permute-start.12 = (bf16[4,32,3072]{2,1,0:T(8,128)(2,1)}, bf16[4,32,3072]{2,1,0:T(8,128)(2,1)}, u32[]{:S(2)}, u32[]{:S(2)}) collective-permute-start(bf16[4,32,3072]{2,1,0:T(8,128)(2,1)} %collective-permute-done.9.refs_7_), channel_id=1, source_target_pairs={{0,1},{1,0},{2,3},{3,2},{4,5},{5,4},{6,7},{7,6},{8,9},{9,8},{10,11... | collective-permute-start | bytes 2359304 | tf_op jit(solution)/shard_map/ppermute | solution.py:56
  69.8 7.1 %collective-permute-start.8 = (bf16[2,2,2,2,4,128]{5,4,3,2,1,0:T(4,128)(2,1)S(1)}, bf16[2,2,2,2,4,128]{5,4,3,2,1,0:T(4,128)(2,1)S(1)}, u32[]{:S(2)}, u32[]{:S(2)}) collective-permute-start(bf16[2,2,2,2,4,128]{5,4,3,2,1,0:T(4,128)(2,1)S(1)} %pad_maximum_fusion.15), channel_id=1, source_target_pairs={{0,1},{1,0},{2,3},{3,2},{4,5},{5,4},{6,7},{7,6},{8,9},{9,8},{10,11... | collective-permute-start | bytes 49160 | tf_op jit(solution)/shard_map/ppermute | solution.py:56
  76.7 7.5 %collective-permute-start.13 = (bf16[4,32,3072]{2,1,0:T(8,128)(2,1)S(1)}, bf16[4,32,3072]{2,1,0:T(8,128)(2,1)S(1)}, u32[]{:S(2)}, u32[]{:S(2)}) collective-permute-start(bf16[4,32,3072]{2,1,0:T(8,128)(2,1)S(1)} %collective-permute-done.7.refs_8_), channel_id=1, source_target_pairs={{0,1},{1,0},{2,3},{3,2},{4,5},{5,4},{6,7},{7,6},{8,9},{9,8},{10,11... | collective-permute-start | bytes 2359304 | tf_op jit(solution)/shard_map/ppermute | solution.py:56
  76.9 34.4 %collective-permute-start.16 = (bf16[4,32,4096]{2,1,0:T(8,128)(2,1)S(1)}, bf16[4,32,4096]{2,1,0:T(8,128)(2,1)S(1)}, u32[]{:S(2)}, u32[]{:S(2)}) collective-permute-start(bf16[4,32,4096]{2,1,0:T(8,128)(2,1)S(1)} %bitcast.508), channel_id=1, source_target_pairs={{0,8},{1,17},{2,10},{3,19},{4,12},{5,21},{6,14},{7,23},{8,0},{9,25... | collective-permute-start | bytes 3145736 | tf_op jit(solution)/shard_map/ppermute | solution.py:56
  77.6 33.9 %collective-permute-start.17 = (bf16[4,32,4096]{2,1,0:T(8,128)(2,1)S(1)}, bf16[4,32,4096]{2,1,0:T(8,128)(2,1)S(1)}, u32[]{:S(2)}, u32[]{:S(2)}) collective-permute-start(bf16[4,32,4096]{2,1,0:T(8,128)(2,1)S(1)} %bitcast.509), channel_id=1, source_target_pairs={{0,16},{1,9},{2,18},{3,11},{4,20},{5,13},{6,22},{7,15},{8,24},{9,1... | collective-permute-start | bytes 3145736 | tf_op jit(solution)/shard_map/ppermute | solution.py:56
  81.1 29.5 %collective-permute-start.20 = (bf16[4,32,1408]{2,1,0:T(8,128)(2,1)S(1)}, bf16[4,32,1408]{2,1,0:T(8,128)(2,1)S(1)}, u32[]{:S(2)}, u32[]{:S(2)}) collective-permute-start(bf16[4,32,1408]{2,1,0:T(8,128)(2,1)S(1)} %bitcast.524), channel_id=1, source_target_pairs={{0,8},{1,17},{2,10},{3,19},{4,12},{5,21},{6,14},{7,23},{8,0},{9,25... | collective-permute-start | bytes 1081352 | tf_op jit(solution)/shard_map/ppermute | solution.py:56
  82.6 28.0 %collective-permute-start.21 = (bf16[4,32,1408]{2,1,0:T(8,128)(2,1)S(1)}, bf16[4,32,1408]{2,1,0:T(8,128)(2,1)S(1)}, u32[]{:S(2)}, u32[]{:S(2)}) collective-permute-start(bf16[4,32,1408]{2,1,0:T(8,128)(2,1)S(1)} %bitcast.525), channel_id=1, source_target_pairs={{0,16},{1,9},{2,18},{3,11},{4,20},{5,13},{6,22},{7,15},{8,24},{9,1... | collective-permute-start | bytes 1081352 | tf_op jit(solution)/shard_map/ppermute | solution.py:56
  84.2 26.5 %collective-permute-start.27 = (bf16[128,1024]{1,0:T(8,128)(2,1)S(1)}, bf16[128,1024]{1,0:T(8,128)(2,1)S(1)}, u32[]{:S(2)}, u32[]{:S(2)}) collective-permute-start(bf16[128,1024]{1,0:T(8,128)(2,1)S(1)} %copy-done.40), channel_id=1, source_target_pairs={{0,4},{1,5},{2,6},{3,7},{4,0},{5,1},{6,2},{7,3},{8,12},{9,13},{10,... | collective-permute-start | bytes 786440 | tf_op jit(solution)/shard_map/ppermute | solution.py:56
  110.6 7.4 %collective-permute-start.22 = (bf16[4,32,1408]{2,1,0:T(8,128)(2,1)S(1)}, bf16[4,32,1408]{2,1,0:T(8,128)(2,1)S(1)}, u32[]{:S(2)}, u32[]{:S(2)}) collective-permute-start(bf16[4,32,1408]{2,1,0:T(8,128)(2,1)S(1)} %collective-permute-done.20.refs_7_.refs_17_), channel_id=1, source_target_pairs={{0,16},{1,9},{2,18},{3,11},{4,20},{5,13},{6,22},{7,15},{8,24},{9,1... | collective-permute-start | bytes 1081352 | tf_op jit(solution)/shard_map/ppermute | solution.py:56
  110.6 27.2 %collective-permute-start.24 = (bf16[4,32,1408]{2,1,0:T(8,128)(2,1)S(1)}, bf16[4,32,1408]{2,1,0:T(8,128)(2,1)}, u32[]{:S(2)}, u32[]{:S(2)}) collective-permute-start(bf16[4,32,1408]{2,1,0:T(8,128)(2,1)S(1)} %collective-permute-done.20.refs_7_.refs_17_), channel_id=1, source_target_pairs={{0,1},{1,0},{2,3},{3,2},{4,5},{5,4},{6,7},{7,6},{8,9},{9,8},{10,11... | collective-permute-start | bytes 1081352 | tf_op jit(solution)/shard_map/ppermute | solution.py:56
  110.7 27.0 %collective-permute-start.25 = (bf16[4,32,1408]{2,1,0:T(8,128)(2,1)S(1)}, bf16[4,32,1408]{2,1,0:T(8,128)(2,1)}, u32[]{:S(2)}, u32[]{:S(2)}) collective-permute-start(bf16[4,32,1408]{2,1,0:T(8,128)(2,1)S(1)} %collective-permute-done.21.refs_8_.refs_18_), channel_id=1, source_target_pairs={{0,1},{1,0},{2,3},{3,2},{4,5},{5,4},{6,7},{7,6},{8,9},{9,8},{10,11... | collective-permute-start | bytes 1081352 | tf_op jit(solution)/shard_map/ppermute | solution.py:56
  111.3 26.9 %collective-permute-start.23 = (bf16[4,32,1408]{2,1,0:T(8,128)(2,1)S(1)}, bf16[4,32,1408]{2,1,0:T(8,128)(2,1)}, u32[]{:S(2)}, u32[]{:S(2)}) collective-permute-start(bf16[4,32,1408]{2,1,0:T(8,128)(2,1)S(1)} %bitcast.526), channel_id=1, source_target_pairs={{0,1},{1,0},{2,3},{3,2},{4,5},{5,4},{6,7},{7,6},{8,9},{9,8},{10,11... | collective-permute-start | bytes 1081352 | tf_op jit(solution)/shard_map/ppermute | solution.py:56
  111.5 25.6 %collective-permute-start.28 = (bf16[2,128,1024]{2,1,0:T(8,128)(2,1)S(1)}, bf16[2,128,1024]{2,1,0:T(8,128)(2,1)S(1)}, u32[]{:S(2)}, u32[]{:S(2)}) collective-permute-start(bf16[2,128,1024]{2,1,0:T(8,128)(2,1)S(1)} %pad_maximum_fusion.7), channel_id=1, source_target_pairs={{0,2},{1,3},{2,0},{3,1},{4,6},{5,7},{6,4},{7,5},{8,10},{9,11},{10,... | collective-permute-start | bytes 1572872 | tf_op jit(solution)/shard_map/ppermute | solution.py:56
  118.0 19.2 %collective-permute-start.29 = (bf16[4,32,4096]{2,1,0:T(8,128)(2,1)S(1)}, bf16[4,32,4096]{2,1,0:T(8,128)(2,1)S(1)}, u32[]{:S(2)}, u32[]{:S(2)}) collective-permute-start(bf16[4,32,4096]{2,1,0:T(8,128)(2,1)S(1)} %collective-permute-done.16.refs_4_), channel_id=1, source_target_pairs={{0,16},{1,9},{2,18},{3,11},{4,20},{5,13},{6,22},{7,15},{8,24},{9,1... | collective-permute-start | bytes 3145736 | tf_op jit(solution)/shard_map/ppermute | solution.py:56
  137.1 15.8 %collective-permute-start.30 = (bf16[4,32,4096]{2,1,0:T(8,128)(2,1)S(1)}, bf16[4,32,4096]{2,1,0:T(8,128)(2,1)S(1)}, u32[]{:S(2)}, u32[]{:S(2)}) collective-permute-start(bf16[4,32,4096]{2,1,0:T(8,128)(2,1)S(1)} %bitcast.512), channel_id=1, source_target_pairs={{0,1},{1,0},{2,3},{3,2},{4,5},{5,4},{6,7},{7,6},{8,9},{9,8},{10,11... | collective-permute-start | bytes 3145736 | tf_op jit(solution)/shard_map/ppermute | solution.py:56
  137.2 17.7 %collective-permute-start.31 = (bf16[4,32,4096]{2,1,0:T(8,128)(2,1)}, bf16[4,32,4096]{2,1,0:T(8,128)(2,1)S(1)}, u32[]{:S(2)}, u32[]{:S(2)}) collective-permute-start(bf16[4,32,4096]{2,1,0:T(8,128)(2,1)} %copy-done.17), channel_id=1, source_target_pairs={{0,1},{1,0},{2,3},{3,2},{4,5},{5,4},{6,7},{7,6},{8,9},{9,8},{10,11... | collective-permute-start | bytes 3145736 | tf_op jit(solution)/shard_map/ppermute | solution.py:56
  137.7 17.2 %collective-permute-start.32 = (bf16[4,32,4096]{2,1,0:T(8,128)(2,1)}, bf16[4,32,4096]{2,1,0:T(8,128)(2,1)}, u32[]{:S(2)}, u32[]{:S(2)}) collective-permute-start(bf16[4,32,4096]{2,1,0:T(8,128)(2,1)} %copy-done.18), channel_id=1, source_target_pairs={{0,1},{1,0},{2,3},{3,2},{4,5},{5,4},{6,7},{7,6},{8,9},{9,8},{10,11... | collective-permute-start | bytes 3145736 | tf_op jit(solution)/shard_map/ppermute | solution.py:56
  138.2 16.7 %collective-permute-start.33 = (bf16[4,32,4096]{2,1,0:T(8,128)(2,1)S(1)}, bf16[4,32,4096]{2,1,0:T(8,128)(2,1)}, u32[]{:S(2)}, u32[]{:S(2)}) collective-permute-start(bf16[4,32,4096]{2,1,0:T(8,128)(2,1)S(1)} %collective-permute-done.29.refs_6_), channel_id=1, source_target_pairs={{0,1},{1,0},{2,3},{3,2},{4,5},{5,4},{6,7},{7,6},{8,9},{9,8},{10,11... | collective-permute-start | bytes 3145736 | tf_op jit(solution)/shard_map/ppermute | solution.py:56
  142.4 29.9 %collective-permute-start.34 = (bf16[4,128,1024]{2,1,0:T(8,128)(2,1)S(1)}, bf16[4,128,1024]{2,1,0:T(8,128)(2,1)S(1)}, u32[]{:S(2)}, u32[]{:S(2)}) collective-permute-start(bf16[4,128,1024]{2,1,0:T(8,128)(2,1)S(1)} %bitcast.513), channel_id=1, source_target_pairs={{0,8},{1,17},{2,10},{3,19},{4,12},{5,21},{6,14},{7,23},{8,0},{9,25... | collective-permute-start | bytes 3145736 | tf_op jit(solution)/shard_map/ppermute | solution.py:56
  152.9 20.1 %collective-permute-start.35 = (bf16[4,128,1024]{2,1,0:T(8,128)(2,1)}, bf16[4,128,1024]{2,1,0:T(8,128)(2,1)S(1)}, u32[]{:S(2)}, u32[]{:S(2)}) collective-permute-start(bf16[4,128,1024]{2,1,0:T(8,128)(2,1)} %bitcast.514), channel_id=1, source_target_pairs={{0,16},{1,9},{2,18},{3,11},{4,20},{5,13},{6,22},{7,15},{8,24},{9,1... | collective-permute-start | bytes 3145736 | tf_op jit(solution)/shard_map/ppermute | solution.py:56
  172.4 17.4 %collective-permute-start.36 = (bf16[4,128,1024]{2,1,0:T(8,128)(2,1)S(1)}, bf16[4,128,1024]{2,1,0:T(8,128)(2,1)S(1)}, u32[]{:S(2)}, u32[]{:S(2)}) collective-permute-start(bf16[4,128,1024]{2,1,0:T(8,128)(2,1)S(1)} %collective-permute-done.34.refs_14_.refs_9_), channel_id=1, source_target_pairs={{0,16},{1,9},{2,18},{3,11},{4,20},{5,13},{6,22},{7,15},{8,24},{9,1... | collective-permute-start | bytes 3145736 | tf_op jit(solution)/shard_map/ppermute | solution.py:56
  172.7 17.4 %collective-permute-start.38 = (bf16[4,128,1024]{2,1,0:T(8,128)(2,1)S(1)}, bf16[4,128,1024]{2,1,0:T(8,128)(2,1)S(1)}, u32[]{:S(2)}, u32[]{:S(2)}) collective-permute-start(bf16[4,128,1024]{2,1,0:T(8,128)(2,1)S(1)} %collective-permute-done.34.refs_14_.refs_9_), channel_id=1, source_target_pairs={{0,1},{1,0},{2,3},{3,2},{4,5},{5,4},{6,7},{7,6},{8,9},{9,8},{10,11... | collective-permute-start | bytes 3145736 | tf_op jit(solution)/shard_map/ppermute | solution.py:56
  173.0 17.1 %collective-permute-start.39 = (bf16[4,128,1024]{2,1,0:T(8,128)(2,1)S(1)}, bf16[4,128,1024]{2,1,0:T(8,128)(2,1)S(1)}, u32[]{:S(2)}, u32[]{:S(2)}) collective-permute-start(bf16[4,128,1024]{2,1,0:T(8,128)(2,1)S(1)} %collective-permute-done.35.refs_15_.refs_10_), channel_id=1, source_target_pairs={{0,1},{1,0},{2,3},{3,2},{4,5},{5,4},{6,7},{7,6},{8,9},{9,8},{10,11... | collective-permute-start | bytes 3145736 | tf_op jit(solution)/shard_map/ppermute | solution.py:56
  173.2 16.9 %collective-permute-start.37 = (bf16[4,128,1024]{2,1,0:T(8,128)(2,1)S(1)}, bf16[4,128,1024]{2,1,0:T(8,128)(2,1)S(1)}, u32[]{:S(2)}, u32[]{:S(2)}) collective-permute-start(bf16[4,128,1024]{2,1,0:T(8,128)(2,1)S(1)} %bitcast.516), channel_id=1, source_target_pairs={{0,1},{1,0},{2,3},{3,2},{4,5},{5,4},{6,7},{7,6},{8,9},{9,8},{10,11... | collective-permute-start | bytes 3145736 | tf_op jit(solution)/shard_map/ppermute | solution.py:56
  274.9 8.9 %collective-permute-start.55 = (bf16[4,4,32,384]{3,2,1,0:T(8,128)(2,1)S(1)}, bf16[4,4,32,384]{3,2,1,0:T(8,128)(2,1)S(1)}, u32[]{:S(2)}, u32[]{:S(2)}) collective-permute-start(bf16[4,4,32,384]{3,2,1,0:T(8,128)(2,1)S(1)} %bitcast.543), channel_id=1, source_target_pairs={{0,1},{1,0},{2,3},{3,2},{4,5},{5,4},{6,7},{7,6},{8,9},{9,8},{10,11... | collective-permute-start | bytes 1179656 | tf_op jit(solution)/shard_map/ppermute | solution.py:56
  285.3 6.2 %collective-permute-start.57 = (bf16[4,32,384]{2,1,0:T(8,128)(2,1)S(1)}, bf16[4,32,384]{2,1,0:T(8,128)(2,1)S(1)}, u32[]{:S(2)}, u32[]{:S(2)}) collective-permute-start(bf16[4,32,384]{2,1,0:T(8,128)(2,1)S(1)} %get-tuple-element.303), channel_id=1, source_target_pairs={{0,16},{1,17},{2,18},{3,19},{4,20},{5,21},{6,22},{7,23},{8,24},{9,... | collective-permute-start | bytes 294920 | tf_op jit(solution)/shard_map/ppermute | solution.py:56
  318.6 15.4 %collective-permute-start.62 = (bf16[4,4,128,1024]{3,2,1,0:T(8,128)(2,1)}, bf16[4,4,128,1024]{3,2,1,0:T(8,128)(2,1)S(1)}, u32[]{:S(2)}, u32[]{:S(2)}) collective-permute-start(bf16[4,4,128,1024]{3,2,1,0:T(8,128)(2,1)} %grad_down_sib.1.refs_3_), channel_id=1, source_target_pairs={{0,1},{1,0},{2,3},{3,2},{4,5},{5,4},{6,7},{7,6},{8,9},{9,8},{10,11... | collective-permute-start | bytes 12582920 | tf_op jit(solution)/shard_map/ppermute | solution.py:56
  359.9 32.4 %collective-permute-start.63 = (f32[4,4,32,4096]{3,2,1,0:T(8,128)}, f32[4,4,32,4096]{3,2,1,0:T(8,128)}, u32[]{:S(2)}, u32[]{:S(2)}) collective-permute-start(f32[4,4,32,4096]{3,2,1,0:T(8,128)} %grad_up_sib.1.refs_7_), channel_id=1, source_target_pairs={{0,1},{1,0},{2,3},{3,2},{4,5},{5,4},{6,7},{7,6},{8,9},{9,8},{10,11... | collective-permute-start | bytes 25165832 | tf_op jit(solution)/shard_map/ppermute | solution.py:56
  360.5 26.4 %collective-permute-start.64 = (bf16[8,128,1024]{2,1,0:T(8,128)(2,1)}, bf16[8,128,1024]{2,1,0:T(8,128)(2,1)}, u32[]{:S(2)}, u32[]{:S(2)}) collective-permute-start(bf16[8,128,1024]{2,1,0:T(8,128)(2,1)} %bitcast.69.refs_3_), channel_id=1, source_target_pairs={{0,16},{1,9},{2,18},{3,11},{4,20},{5,13},{6,22},{7,15},{8,24},{9,1... | collective-permute-start | bytes 6291464 | tf_op jit(solution)/shard_map/ppermute | solution.py:56
  389.4 17.3 %collective-permute-start.65 = (bf16[4,128,1024]{2,1,0:T(8,128)(2,1)S(1)}, bf16[4,128,1024]{2,1,0:T(8,128)(2,1)S(1)}, u32[]{:S(2)}, u32[]{:S(2)}) collective-permute-start(bf16[4,128,1024]{2,1,0:T(8,128)(2,1)S(1)} %get-tuple-element.278.refs_5_), channel_id=1, source_target_pairs={{0,8},{1,17},{2,10},{3,19},{4,12},{5,21},{6,14},{7,23},{8,0},{9,25... | collective-permute-start | bytes 3145736 | tf_op jit(solution)/shard_map/ppermute | solution.py:56
  405.7 42.7 %collective-permute-start.67 = (bf16[8,32,4096]{2,1,0:T(8,128)(2,1)}, bf16[8,32,4096]{2,1,0:T(8,128)(2,1)}, u32[]{:S(2)}, u32[]{:S(2)}) collective-permute-start(bf16[8,32,4096]{2,1,0:T(8,128)(2,1)} %bitcast.561), channel_id=1, source_target_pairs={{0,16},{1,9},{2,18},{3,11},{4,20},{5,13},{6,22},{7,15},{8,24},{9,1... | collective-permute-start | bytes 6291464 | tf_op jit(solution)/shard_map/ppermute | solution.py:56
  406.9 40.2 %collective-permute-start.66 = (bf16[2,128,1024]{2,1,0:T(8,128)(2,1)S(1)}, bf16[2,128,1024]{2,1,0:T(8,128)(2,1)}, u32[]{:S(2)}, u32[]{:S(2)}) collective-permute-start(bf16[2,128,1024]{2,1,0:T(8,128)(2,1)S(1)} %fusion.7.refs_8_), channel_id=1, source_target_pairs={{0,2},{1,3},{2,0},{3,1},{4,6},{5,7},{6,4},{7,5},{8,10},{9,11},{10,... | collective-permute-start | bytes 1572872 | tf_op jit(solution)/shard_map/ppermute | solution.py:56
  436.9 60.1 %collective-permute-start.69 = (bf16[4,4,32,1536]{3,2,1,0:T(8,128)(2,1)}, bf16[4,4,32,1536]{3,2,1,0:T(8,128)(2,1)}, u32[]{:S(2)}, u32[]{:S(2)}) collective-permute-start(bf16[4,4,32,1536]{3,2,1,0:T(8,128)(2,1)} %grad_qkv_sib.2.refs_5_), channel_id=1, source_target_pairs={{0,1},{1,0},{2,3},{3,2},{4,5},{5,4},{6,7},{7,6},{8,9},{9,8},{10,11... | collective-permute-start | bytes 4718600 | tf_op jit(solution)/shard_map/ppermute | solution.py:56
  445.4 38.2 %collective-permute-start.70 = (bf16[4,4,32,1408]{3,2,1,0:T(8,128)(2,1)}, bf16[4,4,32,1408]{3,2,1,0:T(8,128)(2,1)}, u32[]{:S(2)}, u32[]{:S(2)}) collective-permute-start(bf16[4,4,32,1408]{3,2,1,0:T(8,128)(2,1)} %grad_out_sib.1.refs_7_), channel_id=1, source_target_pairs={{0,1},{1,0},{2,3},{3,2},{4,5},{5,4},{6,7},{7,6},{8,9},{9,8},{10,11... | collective-permute-start | bytes 4325384 | tf_op jit(solution)/shard_map/ppermute | solution.py:56
  448.1 26.4 %collective-permute-start.89 = (f32[1,128,1024]{2,1,0:T(8,128)S(1)}, f32[1,128,1024]{2,1,0:T(8,128)}, u32[]{:S(2)}, u32[]{:S(2)}) collective-permute-start(f32[1,128,1024]{2,1,0:T(8,128)S(1)} %bitcast_add_fusion.15.refs_8_), channel_id=1, source_target_pairs={{0,4},{1,5},{2,6},{3,7},{4,0},{5,1},{6,2},{7,3},{8,12},{9,13},{10,... | collective-permute-start | bytes 1572872 | tf_op jit(solution)/shard_map/ppermute | solution.py:56
  472.9 21.4 %collective-permute-start.71 = (bf16[4,32,4096]{2,1,0:T(8,128)(2,1)S(1)}, bf16[4,32,4096]{2,1,0:T(8,128)(2,1)S(1)}, u32[]{:S(2)}, u32[]{:S(2)}) collective-permute-start(bf16[4,32,4096]{2,1,0:T(8,128)(2,1)S(1)} %copy-done.24), channel_id=1, source_target_pairs={{0,8},{1,17},{2,10},{3,19},{4,12},{5,21},{6,14},{7,23},{8,0},{9,25... | collective-permute-start | bytes 3145736 | tf_op jit(solution)/shard_map/ppermute | solution.py:56
  481.7 30.6 %collective-permute-start.68 = (bf16[4,4,32,1536]{3,2,1,0:T(8,128)(2,1)}, bf16[4,4,32,1536]{3,2,1,0:T(8,128)(2,1)S(1)}, u32[]{:S(2)}, u32[]{:S(2)}) collective-permute-start(bf16[4,4,32,1536]{3,2,1,0:T(8,128)(2,1)} %grad_qkv_sib.3.refs_6_), channel_id=1, source_target_pairs={{0,1},{1,0},{2,3},{3,2},{4,5},{5,4},{6,7},{7,6},{8,9},{9,8},{10,11... | collective-permute-start | bytes 4718600 | tf_op jit(solution)/shard_map/ppermute | solution.py:56
  491.9 13.4 %collective-permute-start.73 = (bf16[8,32,1408]{2,1,0:T(8,128)(2,1)}, bf16[8,32,1408]{2,1,0:T(8,128)(2,1)S(1)}, u32[]{:S(2)}, u32[]{:S(2)}) collective-permute-start(bf16[8,32,1408]{2,1,0:T(8,128)(2,1)} %bitcast.541), channel_id=1, source_target_pairs={{0,16},{1,9},{2,18},{3,11},{4,20},{5,13},{6,22},{7,15},{8,24},{9,1... | collective-permute-start | bytes 2162696 | tf_op jit(solution)/shard_map/ppermute | solution.py:56
  495.4 13.7 %collective-permute-start.72 = (bf16[2,32,4096]{2,1,0:T(8,128)(2,1)S(1)}, bf16[2,32,4096]{2,1,0:T(8,128)(2,1)S(1)}, u32[]{:S(2)}, u32[]{:S(2)}) collective-permute-start(bf16[2,32,4096]{2,1,0:T(8,128)(2,1)S(1)} %fusion.8.refs_5_), channel_id=1, source_target_pairs={{0,2},{1,3},{2,0},{3,1},{4,6},{5,7},{6,4},{7,5},{8,10},{9,11},{10,... | collective-permute-start | bytes 1572872 | tf_op jit(solution)/shard_map/ppermute | solution.py:56
  504.4 19.5 %collective-permute-start.74 = (bf16[8,32,1536]{2,1,0:T(8,128)(2,1)}, bf16[8,32,1536]{2,1,0:T(8,128)(2,1)}, u32[]{:S(2)}, u32[]{:S(2)}) collective-permute-start(bf16[8,32,1536]{2,1,0:T(8,128)(2,1)} %bitcast.533), channel_id=1, source_target_pairs={{0,16},{1,9},{2,18},{3,11},{4,20},{5,13},{6,22},{7,15},{8,24},{9,1... | collective-permute-start | bytes 2359304 | tf_op jit(solution)/shard_map/ppermute | solution.py:56
  507.5 15.2 %collective-permute-start.75 = (bf16[4,32,1408]{2,1,0:T(8,128)(2,1)S(1)}, bf16[4,32,1408]{2,1,0:T(8,128)(2,1)S(1)}, u32[]{:S(2)}, u32[]{:S(2)}) collective-permute-start(bf16[4,32,1408]{2,1,0:T(8,128)(2,1)S(1)} %get-tuple-element.284.refs_6_), channel_id=1, source_target_pairs={{0,8},{1,17},{2,10},{3,19},{4,12},{5,21},{6,14},{7,23},{8,0},{9,25... | collective-permute-start | bytes 1081352 | tf_op jit(solution)/shard_map/ppermute | solution.py:56
  509.9 38.7 %collective-permute-start.88 = (bf16[1,32,4096]{2,1,0:T(8,128)(2,1)}, bf16[1,32,4096]{2,1,0:T(8,128)(2,1)}, u32[]{:S(2)}, u32[]{:S(2)}) collective-permute-start(bf16[1,32,4096]{2,1,0:T(8,128)(2,1)} %fusion.13.refs_5_), channel_id=1, source_target_pairs={{0,4},{1,5},{2,6},{3,7},{4,0},{5,1},{6,2},{7,3},{8,12},{9,13},{10,... | collective-permute-start | bytes 786440 | tf_op jit(solution)/shard_map/ppermute | solution.py:56
  521.0 17.7 %collective-permute-start.77 = (bf16[8,32,1536]{2,1,0:T(8,128)(2,1)}, bf16[8,32,1536]{2,1,0:T(8,128)(2,1)S(1)}, u32[]{:S(2)}, u32[]{:S(2)}) collective-permute-start(bf16[8,32,1536]{2,1,0:T(8,128)(2,1)} %bitcast.563), channel_id=1, source_target_pairs={{0,16},{1,9},{2,18},{3,11},{4,20},{5,13},{6,22},{7,15},{8,24},{9,1... | collective-permute-start | bytes 2359304 | tf_op jit(solution)/shard_map/ppermute | solution.py:56
  523.5 29.0 %collective-permute-start.86 = (bf16[2,32,1408]{2,1,0:T(8,128)(2,1)}, bf16[2,32,1408]{2,1,0:T(8,128)(2,1)}, u32[]{:S(2)}, u32[]{:S(2)}) collective-permute-start(bf16[2,32,1408]{2,1,0:T(8,128)(2,1)} %fusion.32.refs_6_), channel_id=1, source_target_pairs={{0,2},{1,3},{2,0},{3,1},{4,6},{5,7},{6,4},{7,5},{8,10},{9,11},{10,... | collective-permute-start | bytes 540680 | tf_op jit(solution)/shard_map/ppermute | solution.py:56
  525.9 19.2 %collective-permute-start.76 = (bf16[4,32,1536]{2,1,0:T(8,128)(2,1)}, bf16[4,32,1536]{2,1,0:T(8,128)(2,1)}, u32[]{:S(2)}, u32[]{:S(2)}) collective-permute-start(bf16[4,32,1536]{2,1,0:T(8,128)(2,1)} %get-tuple-element.282.refs_5_), channel_id=1, source_target_pairs={{0,8},{1,17},{2,10},{3,19},{4,12},{5,21},{6,14},{7,23},{8,0},{9,25... | collective-permute-start | bytes 1179656 | tf_op jit(solution)/shard_map/ppermute | solution.py:56
  548.0 10.7 %collective-permute-start.78 = (bf16[4,32,1536]{2,1,0:T(8,128)(2,1)S(1)}, bf16[4,32,1536]{2,1,0:T(8,128)(2,1)S(1)}, u32[]{:S(2)}, u32[]{:S(2)}) collective-permute-start(bf16[4,32,1536]{2,1,0:T(8,128)(2,1)S(1)} %copy-done.13), channel_id=1, source_target_pairs={{0,8},{1,17},{2,10},{3,19},{4,12},{5,21},{6,14},{7,23},{8,0},{9,25... | collective-permute-start | bytes 1179656 | tf_op jit(solution)/shard_map/ppermute | solution.py:56
  555.6 13.8 %collective-permute-start.87 = (f32[1,32,1408]{2,1,0:T(8,128)S(1)}, f32[1,32,1408]{2,1,0:T(8,128)S(1)}, u32[]{:S(2)}, u32[]{:S(2)}) collective-permute-start(f32[1,32,1408]{2,1,0:T(8,128)S(1)} %bitcast_add_fusion.21), channel_id=1, source_target_pairs={{0,4},{1,5},{2,6},{3,7},{4,0},{5,1},{6,2},{7,3},{8,12},{9,13},{10,... | collective-permute-start | bytes 540680 | tf_op jit(solution)/shard_map/ppermute | solution.py:56
  556.6 11.1 %collective-permute-start.85 = (f32[4,128]{1,0:T(4,128)S(1)}, f32[4,128]{1,0:T(4,128)S(1)}, u32[]{:S(2)}, u32[]{:S(2)}) collective-permute-start(f32[4,128]{1,0:T(4,128)S(1)} %fusion.54), channel_id=1, source_target_pairs={{0,4},{1,5},{2,6},{3,7},{4,0},{5,1},{6,2},{7,3},{8,12},{9,13},{10,... | collective-permute-start | bytes 6152 | tf_op jit(solution)/shard_map/ppermute | solution.py:56
  558.8 15.5 %collective-permute-start.79 = (bf16[2,32,3072]{2,1,0:T(8,128)(2,1)S(1)}, bf16[2,32,3072]{2,1,0:T(8,128)(2,1)S(1)}, u32[]{:S(2)}, u32[]{:S(2)}) collective-permute-start(bf16[2,32,3072]{2,1,0:T(8,128)(2,1)S(1)} %pad_maximum_fusion.10), channel_id=1, source_target_pairs={{0,2},{1,3},{2,0},{3,1},{4,6},{5,7},{6,4},{7,5},{8,10},{9,11},{10,... | collective-permute-start | bytes 1179656 | tf_op jit(solution)/shard_map/ppermute | solution.py:56
  574.4 11.4 %collective-permute-start.80 = (bf16[1,32,3072]{2,1,0:T(8,128)(2,1)S(1)}, bf16[1,32,3072]{2,1,0:T(8,128)(2,1)S(1)}, u32[]{:S(2)}, u32[]{:S(2)}) collective-permute-start(bf16[1,32,3072]{2,1,0:T(8,128)(2,1)S(1)} %fusion.17), channel_id=1, source_target_pairs={{0,4},{1,5},{2,6},{3,7},{4,0},{5,1},{6,2},{7,3},{8,12},{9,13},{10,... | collective-permute-start | bytes 589832 | tf_op jit(solution)/shard_map/ppermute | solution.py:56
  (85 other events, 699.6 us)

commit v4 on v3

--- a/solution.py
+++ b/solution.py
@@ -217,15 +217,17 @@
     return held.reshape((n_rows * n_z * 2,) + shard.shape)
 
 
-def scatter_small(blocks, dtype):
+def scatter_small(blocks, dtype, starts=()):
     n_rows, n_z, row_bits, z_bits = sizes()
     row, z, core = place()
     held = blocks.reshape((2,) * (row_bits + z_bits + 1) + blocks.shape[1:])
+    starts = list(starts)
 
     def halve(held, axis, bit, **move):
-        send = lax.dynamic_index_in_dim(held, 1 - bit, axis, keepdims=False)
+        send = lax.dynamic_index_in_dim(held, 1 - bit, axis, keepdims=False).astype(dtype)
         keep = lax.dynamic_index_in_dim(held, bit, axis, keepdims=False)
-        return keep.astype(f32) + exchange(send.astype(dtype), **move).astype(f32)
+        start = starts.pop(0) if starts else ()
+        return keep.astype(f32) + transfer(send, start, **move).astype(f32)
 
     held = halve(held, row_bits + z_bits, core, swap_core=True)
     for bit in range(row_bits):
@@ -844,6 +846,35 @@
     )(*vectors)
 
 
+def halves_kernel(n_rows, n_z, table, own_in, sib_in, own_ref, sib_ref):
+    core = table[2 * n_rows]
+    for a_ref, o_ref, side in ((own_in, own_ref, core), (sib_in, sib_ref, 1 - core)):
+        t, k = a_ref.shape
+        x = a_ref[...].T.reshape(n_z, 2, k // (2 * n_z), t)
+        o_ref[...] = jnp.where(side == 0, x[:, 0], x[:, 1]).reshape(o_ref.shape)
+
+
+def halves(table, a, n_rows, n_z, wait=()):
+    t, k = a.shape
+    block = k // n_rows
+    out = pl.BlockSpec((block // 2, t), lambda i, _: (i, 0))
+    return call(
+        functools.partial(halves_kernel, n_rows, n_z),
+        "halves",
+        (n_rows,),
+        [
+            pl.BlockSpec((t, block), lambda i, tab: (0, tab[i])),
+            pl.BlockSpec((t, block), lambda i, tab: (0, tab[n_rows + i])),
+        ],
+        [out, out],
+        [like((k // 2, t), bf16)] * 2,
+        10**6,
+        8 * t * k,
+        table=table,
+        wait=wait,
+    )(table, a, a)
+
+
 def pick_columns(table, offset, n_rows, n_z, a_ref, picked):
     t, k = a_ref.shape
     block = k // n_rows
@@ -867,19 +898,29 @@
                 picked[:, at : at + r] = x
 
 
-def weight_kernel(pairs, offset, n_rows, n_z, table, *refs):
+def weight_kernel(picks, offset, n_rows, n_z, table, *refs):
+    pairs = len(picks)
     ins, refs = refs[: 2 * pairs], refs[2 * pairs :]
-    refs, picked = refs[:-pairs], refs[-pairs:]
-
-    @pl.when(pl.program_id(0) == 0)
-    def _():
-        for a_ref, p_ref in zip(ins[::2], picked):
-            pick_columns(table, offset, n_rows, n_z, a_ref, p_ref)
+    count = sum(picks)
+    refs, picked = refs[: len(refs) - count], list(refs[len(refs) - count :])
+
+    if count:
+
+        @pl.when(pl.program_id(0) == 0)
+        def _():
+            into = list(picked)
+            for pick, a_ref in zip(picks, ins[::2]):
+                if pick:
+                    pick_columns(table, offset, n_rows, n_z, a_ref, into.pop(0))
 
     totals = []
-    for p_ref, b_ref in zip(picked, ins[1::2]):
+    for pick, a_ref, b_ref in zip(picks, ins[::2], ins[1::2]):
         b = b_ref[...]
-        totals.append(contract(p_ref[...], b.reshape(b.shape[-2:]), 0, 0))
+        b = b.reshape(b.shape[-2:])
+        if pick:
+            totals.append(contract(picked.pop(0)[...], b, 0, 0))
+        else:
+            totals.append(contract(a_ref[...], b, 1, 0))
     total = totals[0] if pairs == 1 else jnp.concatenate(totals, axis=1)
     if len(refs) == 1:
         refs[0][...] = total.reshape(refs[0].shape).astype(refs[0].dtype)
@@ -892,23 +933,28 @@
 
 
 def weight_half(name, table, operands, n_rows, n_z, tile, other=None, other_type=bf16, wait=()):
-    t, k = operands[0][0].shape
+    own = other is not None
+    picks = [not isinstance(a, tuple) for a, _ in operands]
+    lefts = [a[0 if own else 1] if isinstance(a, tuple) else a for a, _ in operands]
+    rights = [b for _, b in operands]
+    t = rights[0].shape[-2]
+    k = lefts[0].shape[1] if picks[0] else 2 * lefts[0].shape[0]
     r = k // (n_rows * n_z * 2)
-    specs, arrays = [], []
     if len(operands) == 1:
-        a, b = operands[0]
+        b = rights[0]
         per_part = b.shape[-1] // tile
         n = b.shape[-1] * (b.shape[0] if b.ndim == 3 else 1)
         if b.ndim == 3:
-            b_spec = pl.BlockSpec((1, t, tile), lambda i, _: (i // per_part, 0, i % per_part))
+            b_specs = [pl.BlockSpec((1, t, tile), lambda i, _: (i // per_part, 0, i % per_part))]
         else:
-            b_spec = col_spec(t, tile)
-        specs, arrays = [whole_spec((t, k)), b_spec], [a, b]
+            b_specs = [col_spec(t, tile)]
     else:
-        n = tile = sum(b.shape[1] for _, b in operands)
-        for a, b in operands:
-            specs += [whole_spec((t, k)), whole_spec(b.shape)]
-            arrays += [a, b]
+        n = tile = sum(b.shape[1] for b in rights)
+        b_specs = [whole_spec(b.shape) for b in rights]
+    specs, arrays = [], []
+    for a, b, b_spec in zip(lefts, rights, b_specs):
+        specs += [whole_spec(a.shape), b_spec]
+        arrays += [a, b]
 
     def block(rows):
         return pl.BlockSpec((rows, n_z, r, tile), lambda i, _: (0, 0, 0, i))
@@ -916,9 +962,8 @@
     def shape(rows, dtype):
         return like((rows, n_z, r, n), dtype)
 
-    own = other is not None
     return call(
-        functools.partial(weight_kernel, len(operands), 0 if own else n_rows, n_rows, n_z),
+        functools.partial(weight_kernel, picks, 0 if own else n_rows, n_rows, n_z),
         name,
         (n // tile,),
         specs + ([block(n_rows)] if own else []),
@@ -926,7 +971,7 @@
         [shape(n_rows // 2, bf16), shape(n_rows // 2, f32)] if own else shape(n_rows, other_type),
         t * k * n,
         2 * t * (k + n) + 3 * k * n,
-        [pltpu.VMEM((t, k // 2), bf16) for _ in operands],
+        [pltpu.VMEM((t, k // 2), bf16) for pick in picks if pick],
         table=table,
         wait=wait,
     )(table, *arrays, *([other] if own else []))
@@ -1290,26 +1335,6 @@
     row_len = tokens.shape[0]
     q_tokens = QPR * QLEN
 
-    proj_width = -(-w_proj.shape[1] // LANES) * LANES
-    w_out_proj = jnp.concatenate(
-        [w_out, jnp.pad(w_proj, ((0, 0), (0, proj_width - w_proj.shape[1])))], axis=1
-    )
-    g_qkv, g_out, g_up, g_down = (Gather(w) for w in (w_qkv, w_out_proj, w_up, w_down))
-    g_qkv.all_z(())
-    g_qkv.all_rows((), ())
-    first, last = g_qkv.own, g_qkv.pieces[-1]
-    vectors = (b_qkv, b_out, norm1_gain, norm1_bias, b_up, b_down, norm2_gain, norm2_bias)
-    widths = [v.shape[0] for v in vectors]
-    packed = jnp.concatenate(vectors)
-    packed = jnp.pad(packed, (0, -packed.shape[0] % LANES)).reshape(-1, LANES)
-    packed = gather_small(packed, g_qkv.received + [first[0], last]).reshape(n_devices, -1)
-    full_bqkv, full_bout, gain_one, bias_one, full_bup, full_bdown, gain_two, bias_two = unpack(
-        packed, widths
-    )
-    g_up.all_z([[g_qkv.held], first], [first, [last]])
-    g_out.all_z([first])
-    w_qkv_all = g_qkv.whole(table)
-
     own_lengths = lax.dynamic_index_in_dim(lengths, device, 0, keepdims=False)
     position, doc_index = layout(own_lengths, row_len, q_tokens)
     documents = document_table(own_lengths)
@@ -1319,11 +1344,6 @@
     cosine, sine = jnp.cos(angles), jnp.sin(angles)
     cosine = jnp.concatenate([cosine] * 4, axis=1)
     sine = jnp.concatenate([-sine, sine] * 2, axis=1)
-    qkv, full_qkv = project_qkv(
-        tokens, w_qkv_all, full_bqkv, cosine, sine, wait=[g_up.held]
-    )
-    g_out.own_rows([last], [qkv])
-    g_up.own_rows([last], [qkv])
     doc_index = jnp.where(jnp.arange(row_len) < q_tokens, -1, doc_index)
     slots = jnp.arange(8, dtype=jnp.int32)
     hot = (slots[:, None] == doc_index[None, :]).astype(bf16)
@@ -1339,16 +1359,38 @@
     query_row = query_ids.reshape(1, -1)
     doc_column = doc_index[:, None]
     early = [hot, counts, positive, query_ids, query_row, doc_column]
-    attended = attention(documents, qkv, wait=[*g_up.pieces[1:], *early])
-    g_out.other_rows([qkv], [attended])
+    proj_width = -(-w_proj.shape[1] // LANES) * LANES
+    w_first = jnp.concatenate(
+        [w_qkv, w_out, jnp.pad(w_proj, ((0, 0), (0, proj_width - w_proj.shape[1])))], axis=1
+    )
+    g_qkv, g_up, g_down = (Gather(w) for w in (w_first, w_up, w_down))
+    g_qkv.all_z(())
+    tokens_half = tuple(halves(table, tokens, n_rows, n_z, wait=[g_qkv.held, *early]))
+    g_qkv.all_rows([(), [tokens_half[0]]], ())
+    first, last = g_qkv.own, g_qkv.pieces[-1]
+    vectors = (b_qkv, b_out, norm1_gain, norm1_bias, b_up, b_down, norm2_gain, norm2_bias)
+    widths = [v.shape[0] for v in vectors]
+    packed = jnp.concatenate(vectors)
+    packed = jnp.pad(packed, (0, -packed.shape[0] % LANES)).reshape(-1, LANES)
+    packed = gather_small(packed, g_qkv.received + [first[0], last]).reshape(n_devices, -1)
+    full_bqkv, full_bout, gain_one, bias_one, full_bup, full_bdown, gain_two, bias_two = unpack(
+        packed, widths
+    )
+    g_up.all_z([[g_qkv.held]], [[], [last]])
+    first_all = g_qkv.whole(table)
+
+    qkv, full_qkv = project_qkv(
+        tokens, first_all.columns(0, 3 * D), full_bqkv, cosine, sine, wait=[tokens_half[0]]
+    )
+    g_up.own_rows([last], [qkv])
+    attended = attention(documents, qkv, wait=g_up.own)
     g_up.other_rows([qkv], [attended])
-    w_out_all = g_out.whole(table, [[qkv], [attended]], [[attended]])
     g_down.all_z([[g_up.held], [qkv]], [[qkv], [attended]])
     hat1, rstd1, hidden_low, full_out = out_norm(
-        attended, w_out_all.columns(0, D), full_bout, tokens, gain_one, bias_one, wait=[g_down.held]
-    )
-
-    w_up_all = g_up.whole(table, [[qkv], [attended]], [[attended]])
+        attended, first_all.columns(3 * D, D), full_bout, tokens, gain_one, bias_one, wait=[*g_up.pieces, g_down.held]
+    )
+
+    w_up_all = g_up.whole(table, [[attended]], [[attended]])
     part = up_gelu(hidden_low, w_up_all, full_bup)
     g_down.own_rows([attended], [part[0]])
     g_down.other_rows([part[0]])
@@ -1363,7 +1405,7 @@
         bias_one,
         gain_two,
         bias_two,
-        w_out_all.columns(D, proj_width),
+        first_all.columns(4 * D, proj_width),
     )
     full_qkv, full_out, full_up, full_down, full_proj = (
         w.reshape(-1, w.shape[-1]) for w in (full_qkv, full_out, full_up, full_down, full_proj)
@@ -1410,36 +1452,27 @@
     d2 = down.step(sums1)
     up = own_half("grad_up", [(hidden_low, inner_grad)], 1024, up_sib, wait=[sums1, d2])
     d3 = down.step(up.send)
-    grad_a, sums_a = attention_part(0, [up.send, d3])
-    sib_a = sib_half("grad_qkv", [(tokens, grad_a)], 512)
+    out_pairs = [(attended, out_grad), (result_low, raw_grad)]
+    out_sib = sib_half("grad_out", out_pairs, None, wait=[up.send])
+    grad_a, sums_a = attention_part(0, [out_sib, d3])
     d4 = down.step(sums_a)
     u2 = up.step(sums_a)
-    out_sib = sib_half(
-        "grad_out", [(attended, out_grad), (result_low, raw_grad)], None, wait=[sib_a]
-    )
-    grad_b, sums_b = attention_part(1, [out_sib, d4, u2])
-    sib_b = sib_half("grad_qkv", [(tokens, grad_b)], 512)
-    out = own_half(
-        "grad_out",
-        [(attended, out_grad), (result_low, raw_grad)],
-        None,
-        out_sib,
-        True,
-        wait=[sib_b],
-    )
+    sib_a = sib_half("grad_qkv", [(tokens_half, grad_a)], 512)
+    out = own_half("grad_out", out_pairs, None, out_sib, True, wait=[sib_a])
+    grad_b, sums_b = attention_part(1, [out.send, d4, u2])
+    sib_b = sib_half("grad_qkv", [(tokens_half, grad_b)], 512)
+    o2 = out.step(sums_b)
     u3 = up.step(sums_b)
     sum_down = down.finish(sums_b)
-    qkv_a = own_half("grad_qkv", [(tokens, grad_a)], 512, sib_a, wait=[out.send, u3])
+    qkv_a = own_half("grad_qkv", [(tokens_half, grad_a)], 512, sib_a, wait=[sib_b, o2, u3])
+    o3 = out.step(qkv_a.send)
     u4 = up.step(qkv_a.send)
-    o2 = out.step(qkv_a.send)
-    qkv_b = own_half("grad_qkv", [(tokens, grad_b)], 512, sib_b, wait=[qkv_a.send, u4, o2])
+    qkv_b = own_half("grad_qkv", [(tokens_half, grad_b)], 512, sib_b, wait=[qkv_a.send, o3, u4])
     a2 = qkv_a.step(qkv_b.send)
-    o3 = out.step(qkv_b.send)
-    input_grad = input_back([grad_a, grad_b], full_qkv, resid_one_grad, wait=[qkv_b.send, a2, o3])
+    o4 = out.step(qkv_b.send)
+    input_grad = input_back([grad_a, grad_b], full_qkv, resid_one_grad, wait=[qkv_b.send, a2, o4])
     b2 = qkv_b.step(input_grad)
     qkv_a.step(input_grad)
-    o4 = out.step(b2)
-    sum_up = up.finish(b2)
     grads = [sums_a[i] if j == 0 else sums_b[i] for i in range(3) for j in range(2)]
     grad_bqkv = jnp.concatenate(grads, axis=1)
     small = pack(
@@ -1452,9 +1485,13 @@
     while qkv_a.stages[0][0] == "row":
         qkv_a.step()
     q3 = qkv_a.merge(qkv_b).send
-    small = scatter_small(small.reshape(n_devices, -1, LANES), f32).reshape(-1)
+    sum_up = up.finish(q3)
     sum_out = out.finish(q3)
     sum_out, sum_proj = sum_out[:, :D], sum_out[:, D : D + w_proj.shape[1]]
+    q4 = qkv_a.step()
+    small = scatter_small(
+        small.reshape(n_devices, -1, LANES), f32, [[q3], [q3], [q3], [q4], [q4]]
+    ).reshape(-1)
     sum_qkv = qkv_a.finish()
     width = D // 2
     sum_qkv = jnp.concatenate(

time: 595 us -> 582 us (0.978)
  waiting for transfers between devices: 113 us -> 85.6 us
  Pallas kernels: 323 us -> 330 us
  starting transfers between devices: 84 us -> 90.6 us
    ppermute x90 -> x81, waiting for transfers between devices: 113 us -> 85.6 us  [exchange(): return lax.ppermute(value, AXES, pairs)]
    pallas_call x27 -> x28, Pallas kernels: 323 us -> 330 us  [call(): return lambda *operands: run(*operands, *wait)]
    ppermute x90 -> x81, starting transfers between devices: 84 us -> 90.6 us  [exchange(): return lax.ppermute(value, AXES, pairs)]
  transfers between devices with their start and end apart: 90 -> 81, of which waited for: 38 -> 31; matrix products, arithmetic and copies ran while one was open for 9% -> 9% of each run, Pallas kernels for 41% -> 43%
where the time goes in v4:
time: 582 us; the launch traced here: 576 us
  Pallas kernels  330 us (57%)
  starting transfers between devices  90.6 us (16%)
  waiting for transfers between devices  85.6 us (15%)
  other arithmetic  40.4 us (7%)
  local copies, waits for them, and re-layouts  27.8 us (5%)
    pallas_call x28, Pallas kernels, call(): return lambda *operands: run(*operands, *wait)  330 us
    ppermute x81, starting transfers between devices, exchange(): return lax.ppermute(value, AXES, pairs)  90.6 us
    ppermute x81, waiting for transfers between devices, exchange(): return lax.ppermute(value, AXES, pairs)  85.6 us
  transfers between devices with their start and end apart: 81, of which 31 were waited for; matrix products, arithmetic and copies ran while one was open for 9% of the time, Pallas kernels for 43%

profile of v4, /device:TPU:0, one launch (start us, length us, event | category | flops | bytes accessed | tf_op | source)
XLA Modules:
  0.0 576.3 jit_solution(7086147634947369048)
XLA Ops:
  1.7 4.1 collective-permute-start.1
  5.8 5.4 concatenate.32
  15.0 3.8 collective-permute-done.1
  21.4 1.9 fusion.37
  23.3 10.9 %collective-permute-done.3 = bf16[2,32,4480]{2,1,0:T(8,128)(2,1)S(1)} collective-permute-done((bf16[2,32,4480]{2,1,0:T(8,128)(2,1)S(1)}, bf16[2,32,4480]{2,1,0:T(8,128)(2,1)S(1)}, u32[]{:S(2)}, u32[]{:S(2)}) %collective-permute-start.3) | collective-permute-done | bytes 573472 | tf_op jit(solution)/shard_map/ppermute | solution.py:56
  44.3 3.4 collective-permute-start.14
  48.9 5.5 halves.1
  54.5 4.3 collective-permute-done.5.refs_6_.refs_7_.refs_17_
  58.7 2.0 collective-permute-start.7
  61.7 3.1 collective-permute-start.15
  68.8 7.4 %collective-permute-start.12 = (bf16[4,32,4480]{2,1,0:T(8,128)(2,1)}, bf16[4,32,4480]{2,1,0:T(8,128)(2,1)}, u32[]{:S(2)}, u32[]{:S(2)}) collective-permute-start(bf16[4,32,4480]{2,1,0:T(8,128)(2,1)} %collective-permute-done.9.refs_7_.refs_8_.refs_18_), channel_id=1, source_target_pairs={{0,1},{1,0},{2,3},{3,2},{4,5},{5,4},{6,7},{7,6},{8,9},{9,8},{10,11... | collective-permute-start | bytes 3440648 | tf_op jit(solution)/shard_map/ppermute | solution.py:56
  82.9 2.3 unpack.1
  85.2 3.4 collective-permute-start.19
  89.6 14.8 %project_qkv.1 = (bf16[1024,3072]{1,0:T(8,128)(2,1)}, bf16[4,4,2,32,3072]{4,3,2,1,0:T(8,128)(2,1)}) custom-call(s32[17]{0:T(128)} %concatenate.30.refs_0_, bf16[1024,1024]{1,0:T(8,128)(2,1)} %refs_3_.1, f32[1,3072]{1,0:T(1,128)} %get-tuple-element.137.refs_2_, f32[1024,128]{1,0:T(8,128)} %get-tuple-element.350.refs_3_.refs_5_, ...), custom_call_target="tpu_custom_call" | custom-call | flops 6442450944 | bytes 20971520 | tf_op jit(solution)/shard_map/project_qkv/pallas_call | solution.py:368
  105.2 2.3 collective-permute-start.20
  107.6 20.8 %attention.1.refs_1_ = bf16[1024,1024]{1,0:T(8,128)(2,1)} custom-call(s32[9]{0:T(128)} %pad_add_fusion.refs_0_, bf16[1024,3072]{1,0:T(8,128)(2,1)} %get-tuple-element.139.refs_1_.refs_2_.refs_3_, bf16[1024,3072]{1,0:T(8,128)(2,1)} %get-tuple-element.139.refs_1_.refs_2_.refs_3_, bf16[1024,3072]{1,0:T(8,128)(2,1)} %get-tuple-element.139.refs_1_.refs_2_.refs_3_, ...), custom_call_target="tpu_custom_call" | custom-call | flops 20000000000 | bytes 8388608 | tf_op jit(solution)/shard_map/attention/pallas_call | solution.py:368
  131.4 9.7 %out_norm.1 = (f32[1024,1024]{1,0:T(8,128)}, f32[1024,128]{1,0:T(8,128)}, bf16[1024,1024]{1,0:T(8,128)(2,1)}, bf16[4,4,2,32,1024]{4,3,2,1,0:T(8,128)(2,1)}) custom-call(s32[17]{0:T(128)} %concatenate.30.refs_0_, bf16[1024,1024]{1,0:T(8,128)(2,1)} %attention.1.refs_1_, f32[1,1024]{1,0:T(1,128)} %get-tuple-element.145.refs_2_, bf16[1024,1024]{1,0:T(8,128)(2,1)} %refs_3_.1, ...), custom_call_target="tpu_custom_call" | custom-call | flops 2147483648 | bytes 12582912 | tf_op jit(solution)/shard_map/out_norm/pallas_call | solution.py:368
  143.2 16.1 %up_gelu.2 = (bf16[1024,4096]{1,0:T(8,128)(2,1)}, bf16[1024,4096]{1,0:T(8,128)(2,1)}, bf16[4,4,2,32,4096]{4,3,2,1,0:T(8,128)(2,1)}) custom-call(s32[17]{0:T(128)} %concatenate.30.refs_0_, bf16[1024,1024]{1,0:T(8,128)(2,1)} %get-tuple-element.154.refs_1_, f32[1,4096]{1,0:T(1,128)} %get-tuple-element.155.refs_2_, bf16[4,32,4096]{2,1,0:T(8,128)(2,1)} %bitcast.498, ...), custom_call_target="tpu_custom_call" | custom-call | flops 4294967296 | bytes 12582912 | tf_op jit(solution)/shard_map/up_gelu/pallas_call | solution.py:368
  161.5 15.8 %up_gelu.3 = (bf16[1024,4096]{1,0:T(8,128)(2,1)}, bf16[1024,4096]{1,0:T(8,128)(2,1)}, bf16[4,4,2,32,4096]{4,3,2,1,0:T(8,128)(2,1)}) custom-call(s32[17]{0:T(128)} %concatenate.30.refs_0_, bf16[1024,1024]{1,0:T(8,128)(2,1)} %get-tuple-element.154.refs_1_, ...), custom_call_target="tpu_custom_call", output_to_operand_aliasing={{0}: (11, {}), {1}: (12, {}), {2}: (13, {})} | custom-call | flops 4294967296 | bytes 12582912 | tf_op jit(solution)/shard_map/up_gelu/pallas_call | solution.py:368
  177.9 2.2 collective-permute-done.31.refs_15_
  181.2 21.8 %down_norm.1 = (f32[1024,1024]{1,0:T(8,128)}, f32[1024,128]{1,0:T(8,128)}, bf16[1024,1024]{1,0:T(8,128)(2,1)}, f32[1024,384]{1,0:T(8,128)}, bf16[1024,384]{1,0:T...) custom-call(s32[17]{0:T(128)} %concatenate.30.refs_0_, ...), custom_call_target="tpu_custom_call" | custom-call | flops 8589934592 | bytes 20971520 | tf_op jit(solution)/shard_map/down_norm/pallas_call | solution.py:368
  203.7 3.7 collective-permute-start.33
  209.3 3.7 collective-permute-done.34
  214.5 2.2 collective-permute-start.37
  222.8 10.1 %scores.1 = (f32[3,8,1024]{2,1,0:T(8,128)}, f32[3,8,32]{2,1,0:T(8,128)}, f32[3,3,32]{2,1,0:T(4,128)}) custom-call(bf16[1024,384]{1,0:T(8,128)(2,1)} %get-tuple-element.178.refs_0_, bf16[1024,384]{1,0:T(8,128)(2,1)} %bitcast.520, s32[1024,1]{1,0:T(8,128)} %add.651.refs_7_.refs_2_, bf16[8,1024]{1,0:T(8,128)(2,1)} %fusion.41.refs_4_.refs_3_, ...), custom_call_target="tpu_custom_call" | custom-call | flops 4831838208 | bytes 1000000 | tf_op jit(solution)/shard_map/scores/pallas_call | solution.py:368
  240.7 2.4 collective-permute-done.42
  245.0 3.1 collective-permute-start.45
  248.3 2.1 collective-permute-done.45
  251.7 11.6 %score_grads.1 = (f32[1024,384]{1,0:T(8,128)}, f32[1024,384]{1,0:T(8,128)}) custom-call(bf16[1024,384]{1,0:T(8,128)(2,1)} %get-tuple-element.178.refs_0_, bf16[1024,384]{1,0:T(8,128)(2,1)} %bitcast.521, s32[1,1024]{1,0:T(1,128)} %add.562.refs_8_.refs_2_, s32[1024,1]{1,0:T(8,128)} %fusion.15.refs_9_.refs_3_, f32[3,8,1024]{2,1,0:T(8,128)} %get-tuple-element.181.refs_4_, ...), custom_call_target="tpu_custom_call" | custom-call | flops 9663676416 | bytes 1000000 | tf_op jit(solution)/shard_map/score_grads/pallas_call | solution.py:368
  265.7 7.6 %head_back.2 = (f32[1024,1024]{1,0:T(8,128)}, bf16[1024,1024]{1,0:T(8,128)(2,1)}, bf16[1024,384]{1,0:T(8,128)(2,1)}, f32[3,1024]{1,0:T(4,128)}) custom-call(f32[1024,384]{1,0:T(8,128)} %get-tuple-element.183.refs_0_, f32[1024,384]{1,0:T(8,128)} %get-tuple-element.184.refs_1_, bf16[1024,384]{1,0:T(8,128)(2,1)} %bitcast.509, ...), custom_call_target="tpu_custom_call" | custom-call | flops 603979776 | bytes 12582912 | tf_op jit(solution)/shard_map/head_back/pallas_call | solution.py:368
  279.0 2.7 collective-permute-done.48
  281.8 3.7 collective-permute-start.51
  287.3 3.8 collective-permute-done.52
  291.8 4.0 head_back.3
  295.8 11.8 %grad_down_sib.1.refs_3_ = bf16[4,4,128,1024]{3,2,1,0:T(8,128)(2,1)} custom-call(s32[17]{0:T(128)} %concatenate.30.refs_0_, bf16[1024,4096]{1,0:T(8,128)(2,1)} %get-tuple-element.166.refs_1_, bf16[1024,1024]{1,0:T(8,128)(2,1)} %get-tuple-element.193.refs_2_.refs_0_), custom_call_target="tpu_custom_call" | custom-call | flops 4294967296 | bytes 23068672 | tf_op jit(solution)/shard_map/grad_down_sib/pallas_call | solution.py:368
  307.6 15.7 %act_back.1 = (bf16[1024,4096]{1,0:T(8,128)(2,1)}, f32[1,4096]{1,0:T(1,128)}) custom-call(bf16[1024,1024]{1,0:T(8,128)(2,1)} %get-tuple-element.193.refs_2_.refs_0_, bf16[4096,1024]{1,0:T(8,128)(2,1)} %bitcast.546, bf16[1024,4096]{1,0:T(8,128)(2,1)} %get-tuple-element.195.refs_2_, bf16[4,4,128,1024]{3,2,1,0:T(8,128)(2,1)} %grad_down_sib.1.refs_3_), custom_call_target="tpu_custom_call" | custom-call | flops 8589934592 | bytes 25165824 | tf_op jit(solution)/shard_map/act_back/pallas_call | solution.py:368
  323.3 1.9 copy-done.46
  325.2 12.5 %grad_down.1 = (bf16[2,4,128,1024]{3,2,1,0:T(8,128)(2,1)}, f32[2,4,128,1024]{3,2,1,0:T(8,128)}) custom-call(s32[17]{0:T(128)} %concatenate.30.refs_0_, bf16[1024,4096]{1,0:T(8,128)(2,1)} %get-tuple-element.166.refs_1_, bf16[1024,1024]{1,0:T(8,128)(2,1)} %get-tuple-element.193.refs_2_.refs_0_, bf16[4,4,128,1024]{3,2,1,0:T(8,128)(2,1)} %copy-done.46, ...), custom_call_target="tpu_custom_call" | custom-call | flops 4294967296 | bytes 23068672 | tf_op jit(solution)/shard_map/grad_down/pallas_call | solution.py:368
  337.7 11.4 %grad_up_sib.1.refs_7_ = f32[4,4,32,4096]{3,2,1,0:T(8,128)} custom-call(s32[17]{0:T(128)} %concatenate.30.refs_0_, bf16[1024,1024]{1,0:T(8,128)(2,1)} %get-tuple-element.154.refs_1_, bf16[1024,4096]{1,0:T(8,128)(2,1)} %get-tuple-element.196.refs_2_.refs_0_, bf16[8,128,1024]{2,1,0:T(8,128)(2,1)} %bitcast.64.refs_3_), custom_call_target="tpu_custom_call" | custom-call | flops 4294967296 | bytes 23068672 | tf_op jit(solution)/shard_map/grad_up_sib/pallas_call | solution.py:368
  350.2 20.6 %hidden_back.1 = (f32[1024,1024]{1,0:T(8,128)}, bf16[1024,1024]{1,0:T(8,128)(2,1)}, bf16[1024,1024]{1,0:T(8,128)(2,1)}, f32[3,1024]{1,0:T(4,128)}) custom-call(bf16[1024,4096]{1,0:T(8,128)(2,1)} %get-tuple-element.196.refs_2_.refs_0_, bf16[1024,4096]{1,0:T(8,128)(2,1)} %bitcast.504, f32[1024,1024]{1,0:T(8,128)} %get-tuple-element.198.refs_2_, ...), custom_call_target="tpu_custom_call" | custom-call | flops 10737418240 | bytes 33554432 | tf_op jit(solution)/shard_map/hidden_back/pallas_call | solution.py:368
  370.8 5.1 collective-permute-done.55
  375.9 2.5 bitcast_add_fusion.2
  381.0 13.5 %grad_up.1 = (bf16[2,4,32,4096]{3,2,1,0:T(8,128)(2,1)}, f32[2,4,32,4096]{3,2,1,0:T(8,128)}) custom-call(s32[17]{0:T(128)} %concatenate.30.refs_0_, bf16[1024,1024]{1,0:T(8,128)(2,1)} %get-tuple-element.154.refs_1_, bf16[1024,4096]{1,0:T(8,128)(2,1)} %get-tuple-element.196.refs_2_.refs_0_, f32[4,4,32,4096]{3,2,1,0:T(8,128)} %collective-permute-done.54.refs_3_, ...), custom_call_target="tpu_custom_call" | custom-call | flops 4294967296 | bytes 23068672 | tf_op jit(solution)/shard_map/grad_up/pallas_call | solution.py:368
  395.5 7.8 %grad_out_sib.1.refs_7_ = bf16[4,4,32,1408]{3,2,1,0:T(8,128)(2,1)} custom-call(s32[17]{0:T(128)} %concatenate.30.refs_0_, bf16[1024,1024]{1,0:T(8,128)(2,1)} %attention.1.refs_1_, bf16[1024,1024]{1,0:T(8,128)(2,1)} %get-tuple-element.204.refs_2_, bf16[1024,1024]{1,0:T(8,128)(2,1)} %get-tuple-element.116.refs_3_, ...), custom_call_target="tpu_custom_call" | custom-call | flops 1476395008 | bytes 9306112 | tf_op jit(solution)/shard_map/grad_out_sib/pallas_call | solution.py:368
  403.4 23.2 %attention_back.2 = (bf16[3,1024,512]{2,1,0:T(8,128)(2,1)}, f32[3,1,512]{2,1,0:T(1,128)}) custom-call(s32[9]{0:T(128)} %pad_add_fusion.refs_0_, bf16[1024,3072]{1,0:T(8,128)(2,1)} %get-tuple-element.139.refs_1_.refs_2_.refs_3_, bf16[1024,3072]{1,0:T(8,128)(2,1)} %get-tuple-element.139.refs_1_.refs_2_.refs_3_, ...), custom_call_target="tpu_custom_call" | custom-call | flops 24999999488 | bytes 7340032 | tf_op jit(solution)/shard_map/attention_back/pallas_call | solution.py:368
  426.6 6.3 %grad_qkv_sib.2.refs_6_ = bf16[4,4,32,1536]{3,2,1,0:T(8,128)(2,1)} custom-call(s32[17]{0:T(128)} %concatenate.30.refs_0_, bf16[512,1024]{1,0:T(8,128)(2,1)} %get-tuple-element.212.refs_1_, bf16[3,1024,512]{2,1,0:T(8,128)(2,1)} %get-tuple-element.211.refs_2_.refs_0_), custom_call_target="tpu_custom_call" | custom-call | flops 1610612736 | bytes 9961472 | tf_op jit(solution)/shard_map/grad_qkv_sib/pallas_call | solution.py:368
  434.6 9.0 %grad_out.1 = (bf16[2,4,32,1408]{3,2,1,0:T(8,128)(2,1)}, f32[2,4,32,1408]{3,2,1,0:T(8,128)}) custom-call(s32[17]{0:T(128)} %concatenate.30.refs_0_, bf16[1024,1024]{1,0:T(8,128)(2,1)} %attention.1.refs_1_, bf16[1024,1024]{1,0:T(8,128)(2,1)} %get-tuple-element.204.refs_2_, bf16[1024,1024]{1,0:T(8,128)(2,1)} %get-tuple-element.116.refs_3_, ...), custom_call_target="tpu_custom_call" | custom-call | flops 1476395008 | bytes 9306112 | tf_op jit(solution)/shard_map/grad_out/pallas_call | solution.py:368
  443.6 2.6 collective-permute-start.62
  446.3 3.1 bitcast_add_fusion
  449.4 23.3 %attention_back.3 = (bf16[3,1024,512]{2,1,0:T(8,128)(2,1)}, f32[3,1,512]{2,1,0:T(1,128)}) custom-call(s32[9]{0:T(128)} %pad_add_fusion.refs_0_, bf16[1024,3072]{1,0:T(8,128)(2,1)} %get-tuple-element.139.refs_1_.refs_2_.refs_3_, bf16[1024,3072]{1,0:T(8,128)(2,1)} %get-tuple-element.139.refs_1_.refs_2_.refs_3_, ...), custom_call_target="tpu_custom_call" | custom-call | flops 24999999488 | bytes 7340032 | tf_op jit(solution)/shard_map/attention_back/pallas_call | solution.py:368
  473.5 6.0 %grad_qkv_sib.3.refs_4_ = bf16[4,4,32,1536]{3,2,1,0:T(8,128)(2,1)} custom-call(s32[17]{0:T(128)} %concatenate.30.refs_0_, bf16[512,1024]{1,0:T(8,128)(2,1)} %get-tuple-element.212.refs_1_, bf16[3,1024,512]{2,1,0:T(8,128)(2,1)} %get-tuple-element.218.refs_2_.refs_1_), custom_call_target="tpu_custom_call" | custom-call | flops 1610612736 | bytes 9961472 | tf_op jit(solution)/shard_map/grad_qkv_sib/pallas_call | solution.py:368
  479.7 2.1 collective-permute-start.64
  481.8 5.9 %collective-permute-done.63 = bf16[4,32,4096]{2,1,0:T(8,128)(2,1)} collective-permute-done((bf16[4,32,4096]{2,1,0:T(8,128)(2,1)S(1)}, bf16[4,32,4096]{2,1,0:T(8,128)(2,1)}, u32[]{:S(2)}, u32[]{:S(2)}) %collective-permute-start.63) | collective-permute-done | bytes 1048608 | tf_op jit(solution)/shard_map/ppermute | solution.py:56
  489.7 6.5 %grad_qkv.2 = (bf16[2,4,32,1536]{3,2,1,0:T(8,128)(2,1)}, f32[2,4,32,1536]{3,2,1,0:T(8,128)}) custom-call(s32[17]{0:T(128)} %concatenate.30.refs_0_, bf16[512,1024]{1,0:T(8,128)(2,1)} %get-tuple-element.133.refs_13_.refs_1_, bf16[3,1024,512]{2,1,0:T(8,128)(2,1)} %get-tuple-element.211.refs_2_.refs_0_, ...), custom_call_target="tpu_custom_call" | custom-call | flops 1610612736 | bytes 9961472 | tf_op jit(solution)/shard_map/grad_qkv/pallas_call | solution.py:368
  498.9 2.8 collective-permute-done.65
  502.5 6.5 %grad_qkv.3 = (bf16[2,4,32,1536]{3,2,1,0:T(8,128)(2,1)}, f32[2,4,32,1536]{3,2,1,0:T(8,128)}) custom-call(s32[17]{0:T(128)} %concatenate.30.refs_0_, bf16[512,1024]{1,0:T(8,128)(2,1)} %get-tuple-element.133.refs_13_.refs_1_, bf16[3,1024,512]{2,1,0:T(8,128)(2,1)} %get-tuple-element.218.refs_2_.refs_1_, ...), custom_call_target="tpu_custom_call" | custom-call | flops 1610612736 | bytes 9961472 | tf_op jit(solution)/shard_map/grad_qkv/pallas_call | solution.py:368
  512.3 12.3 %input_back.1 = f32[1024,1024]{1,0:T(8,128)} custom-call(bf16[3,1024,512]{2,1,0:T(8,128)(2,1)} %get-tuple-element.211.refs_2_.refs_0_, bf16[3,1024,512]{2,1,0:T(8,128)(2,1)} %get-tuple-element.218.refs_2_.refs_1_, bf16[1024,3072]{1,0:T(8,128)(2,1)} %bitcast.547, f32[1024,1024]{1,0:T(8,128)} %get-tuple-element.220.refs_3_, bf16[8,32,1536]{2,1,0:T(8,128)(2,1)} %bitcast.543, ...), custom_call_target="tpu_custom_call" | custom-call | flops 6442450944 | bytes 20971520 | tf_op jit(solution)/shard_map/input_back/pallas_call | solution.py:368
  527.7 3.4 pack.1
  542.1 2.1 collective-permute-start.75
  544.2 2.0 fusion.11
  546.5 7.6 %collective-permute-done.79 = bf16[1,32,4096]{2,1,0:T(8,128)(2,1)S(1)} collective-permute-done((bf16[1,32,4096]{2,1,0:T(8,128)(2,1)}, bf16[1,32,4096]{2,1,0:T(8,128)(2,1)S(1)}, u32[]{:S(2)}, u32[]{:S(2)}) %collective-permute-start.79) | collective-permute-done | bytes 262176 | tf_op jit(solution)/shard_map/ppermute | solution.py:56
  554.2 5.7 collective-permute-done.71
  565.0 2.9 collective-permute-start.72
  569.9 5.2 collective-permute-done.72
  (362 shorter events, 111.2 us)
Async XLA Ops:
  1.7 17.1 %collective-permute-start.1 = (bf16[32,4480]{1,0:T(8,128)(2,1)S(1)}, bf16[32,4480]{1,0:T(8,128)(2,1)S(1)}, u32[]{:S(2)}, u32[]{:S(2)}) collective-permute-start(bf16[32,4480]{1,0:T(8,128)(2,1)S(1)} %fusion.28), channel_id=1, source_target_pairs={{0,4},{1,5},{2,6},{3,7},{4,0},{5,1},{6,2},{7,3},{8,12},{9,13},{10,... | collective-permute-start | bytes 860168 | tf_op jit(solution)/shard_map/ppermute | solution.py:56
  11.2 26.5 %collective-permute-start = (bf16[4,128]{1,0:T(4,128)(2,1)S(1)}, bf16[4,128]{1,0:T(4,128)(2,1)}, u32[]{:S(2)}, u32[]{:S(2)}) collective-permute-start(bf16[4,128]{1,0:T(4,128)(2,1)S(1)} %pad_bitcast_fusion), channel_id=1, source_target_pairs={{0,4},{1,5},{2,6},{3,7},{4,0},{5,1},{6,2},{7,3},{8,12},{9,13},{10,... | collective-permute-start | bytes 3080 | tf_op jit(solution)/shard_map/ppermute | solution.py:56
  19.9 14.2 %collective-permute-start.3 = (bf16[2,32,4480]{2,1,0:T(8,128)(2,1)S(1)}, bf16[2,32,4480]{2,1,0:T(8,128)(2,1)S(1)}, u32[]{:S(2)}, u32[]{:S(2)}) collective-permute-start(bf16[2,32,4480]{2,1,0:T(8,128)(2,1)S(1)} %pad_maximum_fusion.4), channel_id=1, source_target_pairs={{0,2},{1,3},{2,0},{3,1},{4,6},{5,7},{6,4},{7,5},{8,10},{9,11},{10,... | collective-permute-start | bytes 1720328 | tf_op jit(solution)/shard_map/ppermute | solution.py:56
  35.5 23.3 %collective-permute-start.5 = (bf16[4,32,4480]{2,1,0:T(8,128)(2,1)}, bf16[4,32,4480]{2,1,0:T(8,128)(2,1)S(1)}, u32[]{:S(2)}, u32[]{:S(2)}) collective-permute-start(bf16[4,32,4480]{2,1,0:T(8,128)(2,1)} %bitcast.16.refs_5_.refs_6_.refs_16_), channel_id=1, source_target_pairs={{0,8},{1,17},{2,10},{3,19},{4,12},{5,21},{6,14},{7,23},{8,0},{9,25... | collective-permute-start | bytes 3440648 | tf_op jit(solution)/shard_map/ppermute | solution.py:56
  38.4 5.9 %collective-permute-start.2 = (bf16[2,4,128]{2,1,0:T(4,128)(2,1)S(1)}, bf16[2,4,128]{2,1,0:T(4,128)(2,1)S(1)}, u32[]{:S(2)}, u32[]{:S(2)}) collective-permute-start(bf16[2,4,128]{2,1,0:T(4,128)(2,1)S(1)} %pad_maximum_fusion.19), channel_id=1, source_target_pairs={{0,2},{1,3},{2,0},{3,1},{4,6},{5,7},{6,4},{7,5},{8,10},{9,11},{10,... | collective-permute-start | bytes 6152 | tf_op jit(solution)/shard_map/ppermute | solution.py:56
  42.8 25.5 %collective-permute-start.9 = (bf16[4,32,4480]{2,1,0:T(8,128)(2,1)}, bf16[4,32,4480]{2,1,0:T(8,128)(2,1)}, u32[]{:S(2)}, u32[]{:S(2)}) collective-permute-start(bf16[4,32,4480]{2,1,0:T(8,128)(2,1)} %bitcast.16.refs_5_.refs_6_.refs_16_), channel_id=1, source_target_pairs={{0,16},{1,9},{2,18},{3,11},{4,20},{5,13},{6,22},{7,15},{8,24},{9,1... | collective-permute-start | bytes 3440648 | tf_op jit(solution)/shard_map/ppermute | solution.py:56
  44.3 16.5 %collective-permute-start.14 = (bf16[32,4096]{1,0:T(8,128)(2,1)S(1)}, bf16[32,4096]{1,0:T(8,128)(2,1)S(1)}, u32[]{:S(2)}, u32[]{:S(2)}) collective-permute-start(bf16[32,4096]{1,0:T(8,128)(2,1)S(1)} %copy-done.33), channel_id=1, source_target_pairs={{0,4},{1,5},{2,6},{3,7},{4,0},{5,1},{6,2},{7,3},{8,12},{9,13},{10,... | collective-permute-start | bytes 786440 | tf_op jit(solution)/shard_map/ppermute | solution.py:56
  47.7 17.1 %collective-permute-start.4 = (bf16[2,2,4,128]{3,2,1,0:T(4,128)(2,1)S(1)}, bf16[2,2,4,128]{3,2,1,0:T(4,128)(2,1)S(1)}, u32[]{:S(2)}, u32[]{:S(2)}) collective-permute-start(bf16[2,2,4,128]{3,2,1,0:T(4,128)(2,1)S(1)} %pad_maximum_fusion.18), channel_id=1, source_target_pairs={{0,16},{1,17},{2,18},{3,19},{4,20},{5,21},{6,22},{7,23},{8,24},{9,... | collective-permute-start | bytes 12296 | tf_op jit(solution)/shard_map/ppermute | solution.py:56
  58.7 17.4 %collective-permute-start.7 = (bf16[4,32,4480]{2,1,0:T(8,128)(2,1)S(1)}, bf16[4,32,4480]{2,1,0:T(8,128)(2,1)}, u32[]{:S(2)}, u32[]{:S(2)}) collective-permute-start(bf16[4,32,4480]{2,1,0:T(8,128)(2,1)S(1)} %collective-permute-done.5.refs_6_.refs_7_.refs_17_), channel_id=1, source_target_pairs={{0,16},{1,9},{2,18},{3,11},{4,20},{5,13},{6,22},{7,15},{8,24},{9,1... | collective-permute-start | bytes 3440648 | tf_op jit(solution)/shard_map/ppermute | solution.py:56
  61.7 14.6 %collective-permute-start.15 = (bf16[2,32,4096]{2,1,0:T(8,128)(2,1)}, bf16[2,32,4096]{2,1,0:T(8,128)(2,1)}, u32[]{:S(2)}, u32[]{:S(2)}) collective-permute-start(bf16[2,32,4096]{2,1,0:T(8,128)(2,1)} %pad_maximum_fusion.7), channel_id=1, source_target_pairs={{0,2},{1,3},{2,0},{3,1},{4,6},{5,7},{6,4},{7,5},{8,10},{9,11},{10,... | collective-permute-start | bytes 1572872 | tf_op jit(solution)/shard_map/ppermute | solution.py:56
  68.2 9.9 %collective-permute-start.10 = (bf16[4,32,4480]{2,1,0:T(8,128)(2,1)}, bf16[4,32,4480]{2,1,0:T(8,128)(2,1)S(1)}, u32[]{:S(2)}, u32[]{:S(2)}) collective-permute-start(bf16[4,32,4480]{2,1,0:T(8,128)(2,1)} %bitcast.16.refs_5_.refs_6_.refs_16_), channel_id=1, source_target_pairs={{0,1},{1,0},{2,3},{3,2},{4,5},{5,4},{6,7},{7,6},{8,9},{9,8},{10,11... | collective-permute-start | bytes 3440648 | tf_op jit(solution)/shard_map/ppermute | solution.py:56
  68.2 20.4 %collective-permute-start.11 = (bf16[4,32,4480]{2,1,0:T(8,128)(2,1)S(1)}, bf16[4,32,4480]{2,1,0:T(8,128)(2,1)S(1)}, u32[]{:S(2)}, u32[]{:S(2)}) collective-permute-start(bf16[4,32,4480]{2,1,0:T(8,128)(2,1)S(1)} %collective-permute-done.5.refs_6_.refs_7_.refs_17_), channel_id=1, source_target_pairs={{0,1},{1,0},{2,3},{3,2},{4,5},{5,4},{6,7},{7,6},{8,9},{9,8},{10,11... | collective-permute-start | bytes 3440648 | tf_op jit(solution)/shard_map/ppermute | solution.py:56
  68.8 16.5 %collective-permute-start.12 = (bf16[4,32,4480]{2,1,0:T(8,128)(2,1)}, bf16[4,32,4480]{2,1,0:T(8,128)(2,1)}, u32[]{:S(2)}, u32[]{:S(2)}) collective-permute-start(bf16[4,32,4480]{2,1,0:T(8,128)(2,1)} %collective-permute-done.9.refs_7_.refs_8_.refs_18_), channel_id=1, source_target_pairs={{0,1},{1,0},{2,3},{3,2},{4,5},{5,4},{6,7},{7,6},{8,9},{9,8},{10,11... | collective-permute-start | bytes 3440648 | tf_op jit(solution)/shard_map/ppermute | solution.py:56
  76.2 12.4 %collective-permute-start.13 = (bf16[4,32,4480]{2,1,0:T(8,128)(2,1)}, bf16[4,32,4480]{2,1,0:T(8,128)(2,1)}, u32[]{:S(2)}, u32[]{:S(2)}) collective-permute-start(bf16[4,32,4480]{2,1,0:T(8,128)(2,1)} %collective-permute-done.7.refs_8_.refs_9_.refs_19_), channel_id=1, source_target_pairs={{0,1},{1,0},{2,3},{3,2},{4,5},{5,4},{6,7},{7,6},{8,9},{9,8},{10,11... | collective-permute-start | bytes 3440648 | tf_op jit(solution)/shard_map/ppermute | solution.py:56
  78.1 26.3 %collective-permute-start.16 = (bf16[4,32,4096]{2,1,0:T(8,128)(2,1)S(1)}, bf16[4,32,4096]{2,1,0:T(8,128)(2,1)S(1)}, u32[]{:S(2)}, u32[]{:S(2)}) collective-permute-start(bf16[4,32,4096]{2,1,0:T(8,128)(2,1)S(1)} %bitcast.494), channel_id=1, source_target_pairs={{0,8},{1,17},{2,10},{3,19},{4,12},{5,21},{6,14},{7,23},{8,0},{9,25... | collective-permute-start | bytes 3145736 | tf_op jit(solution)/shard_map/ppermute | solution.py:56
  79.4 25.7 %collective-permute-start.17 = (bf16[4,32,4096]{2,1,0:T(8,128)(2,1)S(1)}, bf16[4,32,4096]{2,1,0:T(8,128)(2,1)S(1)}, u32[]{:S(2)}, u32[]{:S(2)}) collective-permute-start(bf16[4,32,4096]{2,1,0:T(8,128)(2,1)S(1)} %bitcast.495), channel_id=1, source_target_pairs={{0,16},{1,9},{2,18},{3,11},{4,20},{5,13},{6,22},{7,15},{8,24},{9,1... | collective-permute-start | bytes 3145736 | tf_op jit(solution)/shard_map/ppermute | solution.py:56
  85.2 19.9 %collective-permute-start.19 = (bf16[128,1024]{1,0:T(8,128)(2,1)S(1)}, bf16[128,1024]{1,0:T(8,128)(2,1)S(1)}, u32[]{:S(2)}, u32[]{:S(2)}) collective-permute-start(bf16[128,1024]{1,0:T(8,128)(2,1)S(1)} %copy-done.34), channel_id=1, source_target_pairs={{0,4},{1,5},{2,6},{3,7},{4,0},{5,1},{6,2},{7,3},{8,12},{9,13},{10,... | collective-permute-start | bytes 786440 | tf_op jit(solution)/shard_map/ppermute | solution.py:56
  104.5 24.5 %collective-permute-start.18 = (bf16[4,32,4096]{2,1,0:T(8,128)(2,1)S(1)}, bf16[4,32,4096]{2,1,0:T(8,128)(2,1)S(1)}, u32[]{:S(2)}, u32[]{:S(2)}) collective-permute-start(bf16[4,32,4096]{2,1,0:T(8,128)(2,1)S(1)} %collective-permute-done.16.refs_4_.refs_15_), channel_id=1, source_target_pairs={{0,16},{1,9},{2,18},{3,11},{4,20},{5,13},{6,22},{7,15},{8,24},{9,1... | collective-permute-start | bytes 3145736 | tf_op jit(solution)/shard_map/ppermute | solution.py:56
  105.2 23.7 %collective-permute-start.20 = (bf16[2,128,1024]{2,1,0:T(8,128)(2,1)S(1)}, bf16[2,128,1024]{2,1,0:T(8,128)(2,1)S(1)}, u32[]{:S(2)}, u32[]{:S(2)}) collective-permute-start(bf16[2,128,1024]{2,1,0:T(8,128)(2,1)S(1)} %pad_maximum_fusion.8), channel_id=1, source_target_pairs={{0,2},{1,3},{2,0},{3,1},{4,6},{5,7},{6,4},{7,5},{8,10},{9,11},{10,... | collective-permute-start | bytes 1572872 | tf_op jit(solution)/shard_map/ppermute | solution.py:56
  128.4 12.8 %collective-permute-start.23 = (bf16[4,32,4096]{2,1,0:T(8,128)(2,1)}, bf16[4,32,4096]{2,1,0:T(8,128)(2,1)S(1)}, u32[]{:S(2)}, u32[]{:S(2)}) collective-permute-start(bf16[4,32,4096]{2,1,0:T(8,128)(2,1)} %copy-done.4), channel_id=1, source_target_pairs={{0,1},{1,0},{2,3},{3,2},{4,5},{5,4},{6,7},{7,6},{8,9},{9,8},{10,11... | collective-permute-start | bytes 3145736 | tf_op jit(solution)/shard_map/ppermute | solution.py:56
  128.4 13.8 %collective-permute-start.22 = (bf16[4,32,4096]{2,1,0:T(8,128)(2,1)}, bf16[4,32,4096]{2,1,0:T(8,128)(2,1)S(1)}, u32[]{:S(2)}, u32[]{:S(2)}) collective-permute-start(bf16[4,32,4096]{2,1,0:T(8,128)(2,1)} %copy-done.3), channel_id=1, source_target_pairs={{0,1},{1,0},{2,3},{3,2},{4,5},{5,4},{6,7},{7,6},{8,9},{9,8},{10,11... | collective-permute-start | bytes 3145736 | tf_op jit(solution)/shard_map/ppermute | solution.py:56
  128.9 13.3 %collective-permute-start.21 = (bf16[4,32,4096]{2,1,0:T(8,128)(2,1)S(1)}, bf16[4,32,4096]{2,1,0:T(8,128)(2,1)}, u32[]{:S(2)}, u32[]{:S(2)}) collective-permute-start(bf16[4,32,4096]{2,1,0:T(8,128)(2,1)S(1)} %bitcast.496), channel_id=1, source_target_pairs={{0,1},{1,0},{2,3},{3,2},{4,5},{5,4},{6,7},{7,6},{8,9},{9,8},{10,11... | collective-permute-start | bytes 3145736 | tf_op jit(solution)/shard_map/ppermute | solution.py:56
  129.0 13.2 %collective-permute-start.24 = (bf16[4,32,4096]{2,1,0:T(8,128)(2,1)S(1)}, bf16[4,32,4096]{2,1,0:T(8,128)(2,1)}, u32[]{:S(2)}, u32[]{:S(2)}) collective-permute-start(bf16[4,32,4096]{2,1,0:T(8,128)(2,1)S(1)} %collective-permute-done.18.refs_17_.refs_6_), channel_id=1, source_target_pairs={{0,1},{1,0},{2,3},{3,2},{4,5},{5,4},{6,7},{7,6},{8,9},{9,8},{10,11... | collective-permute-start | bytes 3145736 | tf_op jit(solution)/shard_map/ppermute | solution.py:56
  129.9 29.4 %collective-permute-start.25 = (bf16[4,128,1024]{2,1,0:T(8,128)(2,1)S(1)}, bf16[4,128,1024]{2,1,0:T(8,128)(2,1)S(1)}, u32[]{:S(2)}, u32[]{:S(2)}) collective-permute-start(bf16[4,128,1024]{2,1,0:T(8,128)(2,1)S(1)} %bitcast.505), channel_id=1, source_target_pairs={{0,8},{1,17},{2,10},{3,19},{4,12},{5,21},{6,14},{7,23},{8,0},{9,25... | collective-permute-start | bytes 3145736 | tf_op jit(solution)/shard_map/ppermute | solution.py:56
  141.2 19.3 %collective-permute-start.26 = (bf16[4,128,1024]{2,1,0:T(8,128)(2,1)}, bf16[4,128,1024]{2,1,0:T(8,128)(2,1)S(1)}, u32[]{:S(2)}, u32[]{:S(2)}) collective-permute-start(bf16[4,128,1024]{2,1,0:T(8,128)(2,1)} %bitcast.506), channel_id=1, source_target_pairs={{0,16},{1,9},{2,18},{3,11},{4,20},{5,13},{6,22},{7,15},{8,24},{9,1... | collective-permute-start | bytes 3145736 | tf_op jit(solution)/shard_map/ppermute | solution.py:56
  159.3 18.0 %collective-permute-start.27 = (bf16[4,128,1024]{2,1,0:T(8,128)(2,1)S(1)}, bf16[4,128,1024]{2,1,0:T(8,128)(2,1)S(1)}, u32[]{:S(2)}, u32[]{:S(2)}) collective-permute-start(bf16[4,128,1024]{2,1,0:T(8,128)(2,1)S(1)} %collective-permute-done.25.refs_14_.refs_9_), channel_id=1, source_target_pairs={{0,16},{1,9},{2,18},{3,11},{4,20},{5,13},{6,22},{7,15},{8,24},{9,1... | collective-permute-start | bytes 3145736 | tf_op jit(solution)/shard_map/ppermute | solution.py:56
  160.5 17.4 %collective-permute-start.29 = (bf16[4,128,1024]{2,1,0:T(8,128)(2,1)S(1)}, bf16[4,128,1024]{2,1,0:T(8,128)(2,1)S(1)}, u32[]{:S(2)}, u32[]{:S(2)}) collective-permute-start(bf16[4,128,1024]{2,1,0:T(8,128)(2,1)S(1)} %collective-permute-done.25.refs_14_.refs_9_), channel_id=1, source_target_pairs={{0,1},{1,0},{2,3},{3,2},{4,5},{5,4},{6,7},{7,6},{8,9},{9,8},{10,11... | collective-permute-start | bytes 3145736 | tf_op jit(solution)/shard_map/ppermute | solution.py:56
  160.5 17.4 %collective-permute-start.30 = (bf16[4,128,1024]{2,1,0:T(8,128)(2,1)S(1)}, bf16[4,128,1024]{2,1,0:T(8,128)(2,1)S(1)}, u32[]{:S(2)}, u32[]{:S(2)}) collective-permute-start(bf16[4,128,1024]{2,1,0:T(8,128)(2,1)S(1)} %collective-permute-done.26.refs_15_.refs_10_), channel_id=1, source_target_pairs={{0,1},{1,0},{2,3},{3,2},{4,5},{5,4},{6,7},{7,6},{8,9},{9,8},{10,11... | collective-permute-start | bytes 3145736 | tf_op jit(solution)/shard_map/ppermute | solution.py:56
  161.0 16.9 %collective-permute-start.28 = (bf16[4,128,1024]{2,1,0:T(8,128)(2,1)S(1)}, bf16[4,128,1024]{2,1,0:T(8,128)(2,1)S(1)}, u32[]{:S(2)}, u32[]{:S(2)}) collective-permute-start(bf16[4,128,1024]{2,1,0:T(8,128)(2,1)S(1)} %bitcast.508), channel_id=1, source_target_pairs={{0,1},{1,0},{2,3},{3,2},{4,5},{5,4},{6,7},{7,6},{8,9},{9,8},{10,11... | collective-permute-start | bytes 3145736 | tf_op jit(solution)/shard_map/ppermute | solution.py:56
  203.7 5.6 collective-permute-start.33
  207.4 5.6 collective-permute-start.34
  213.1 5.4 collective-permute-start.35
  214.5 5.5 collective-permute-start.37
  245.0 5.4 collective-permute-start.45
  264.4 8.9 %collective-permute-start.46 = (bf16[4,4,32,384]{3,2,1,0:T(8,128)(2,1)S(1)}, bf16[4,4,32,384]{3,2,1,0:T(8,128)(2,1)S(1)}, u32[]{:S(2)}, u32[]{:S(2)}) collective-permute-start(bf16[4,4,32,384]{3,2,1,0:T(8,128)(2,1)S(1)} %bitcast.524), channel_id=1, source_target_pairs={{0,1},{1,0},{2,3},{3,2},{4,5},{5,4},{6,7},{7,6},{8,9},{9,8},{10,11... | collective-permute-start | bytes 1179656 | tf_op jit(solution)/shard_map/ppermute | solution.py:56
  273.5 5.4 collective-permute-start.47
  274.6 7.0 %collective-permute-start.48 = (bf16[4,32,384]{2,1,0:T(8,128)(2,1)S(1)}, bf16[4,32,384]{2,1,0:T(8,128)(2,1)S(1)}, u32[]{:S(2)}, u32[]{:S(2)}) collective-permute-start(bf16[4,32,384]{2,1,0:T(8,128)(2,1)S(1)} %get-tuple-element.289), channel_id=1, source_target_pairs={{0,16},{1,17},{2,18},{3,19},{4,20},{5,21},{6,22},{7,23},{8,24},{9,... | collective-permute-start | bytes 294920 | tf_op jit(solution)/shard_map/ppermute | solution.py:56
  275.6 6.0 %collective-permute-start.49 = (bf16[4,32,384]{2,1,0:T(8,128)(2,1)S(1)}, bf16[4,32,384]{2,1,0:T(8,128)(2,1)S(1)}, u32[]{:S(2)}, u32[]{:S(2)}) collective-permute-start(bf16[4,32,384]{2,1,0:T(8,128)(2,1)S(1)} %get-tuple-element.288), channel_id=1, source_target_pairs={{0,24},{1,25},{2,26},{3,27},{4,28},{5,29},{6,30},{7,31},{8,16},{9,... | collective-permute-start | bytes 294920 | tf_op jit(solution)/shard_map/ppermute | solution.py:56
  281.8 5.5 collective-permute-start.51
  285.5 5.6 collective-permute-start.52
  307.6 15.7 %collective-permute-start.53 = (bf16[4,4,128,1024]{3,2,1,0:T(8,128)(2,1)}, bf16[4,4,128,1024]{3,2,1,0:T(8,128)(2,1)S(1)}, u32[]{:S(2)}, u32[]{:S(2)}) collective-permute-start(bf16[4,4,128,1024]{3,2,1,0:T(8,128)(2,1)} %grad_down_sib.1.refs_3_), channel_id=1, source_target_pairs={{0,1},{1,0},{2,3},{3,2},{4,5},{5,4},{6,7},{7,6},{8,9},{9,8},{10,11... | collective-permute-start | bytes 12582920 | tf_op jit(solution)/shard_map/ppermute | solution.py:56
  349.0 32.0 %collective-permute-start.54 = (f32[4,4,32,4096]{3,2,1,0:T(8,128)}, f32[4,4,32,4096]{3,2,1,0:T(8,128)}, u32[]{:S(2)}, u32[]{:S(2)}) collective-permute-start(f32[4,4,32,4096]{3,2,1,0:T(8,128)} %grad_up_sib.1.refs_7_), channel_id=1, source_target_pairs={{0,1},{1,0},{2,3},{3,2},{4,5},{5,4},{6,7},{7,6},{8,9},{9,8},{10,11... | collective-permute-start | bytes 25165832 | tf_op jit(solution)/shard_map/ppermute | solution.py:56
  349.6 26.4 %collective-permute-start.55 = (bf16[8,128,1024]{2,1,0:T(8,128)(2,1)}, bf16[8,128,1024]{2,1,0:T(8,128)(2,1)}, u32[]{:S(2)}, u32[]{:S(2)}) collective-permute-start(bf16[8,128,1024]{2,1,0:T(8,128)(2,1)} %bitcast.64.refs_3_), channel_id=1, source_target_pairs={{0,16},{1,9},{2,18},{3,11},{4,20},{5,13},{6,22},{7,15},{8,24},{9,1... | collective-permute-start | bytes 6291464 | tf_op jit(solution)/shard_map/ppermute | solution.py:56
  378.5 16.8 %collective-permute-start.56 = (bf16[4,128,1024]{2,1,0:T(8,128)(2,1)S(1)}, bf16[4,128,1024]{2,1,0:T(8,128)(2,1)S(1)}, u32[]{:S(2)}, u32[]{:S(2)}) collective-permute-start(bf16[4,128,1024]{2,1,0:T(8,128)(2,1)S(1)} %get-tuple-element.262.refs_5_), channel_id=1, source_target_pairs={{0,8},{1,17},{2,10},{3,19},{4,12},{5,21},{6,14},{7,23},{8,0},{9,25... | collective-permute-start | bytes 3145736 | tf_op jit(solution)/shard_map/ppermute | solution.py:56
  394.5 51.8 %collective-permute-start.59 = (bf16[8,32,4096]{2,1,0:T(8,128)(2,1)}, bf16[8,32,4096]{2,1,0:T(8,128)(2,1)}, u32[]{:S(2)}, u32[]{:S(2)}) collective-permute-start(bf16[8,32,4096]{2,1,0:T(8,128)(2,1)} %bitcast.516), channel_id=1, source_target_pairs={{0,16},{1,9},{2,18},{3,11},{4,20},{5,13},{6,22},{7,15},{8,24},{9,1... | collective-permute-start | bytes 6291464 | tf_op jit(solution)/shard_map/ppermute | solution.py:56
  395.5 38.1 %collective-permute-start.58 = (bf16[2,128,1024]{2,1,0:T(8,128)(2,1)S(1)}, bf16[2,128,1024]{2,1,0:T(8,128)(2,1)S(1)}, u32[]{:S(2)}, u32[]{:S(2)}) collective-permute-start(bf16[2,128,1024]{2,1,0:T(8,128)(2,1)S(1)} %fusion.8.refs_8_), channel_id=1, source_target_pairs={{0,2},{1,3},{2,0},{3,1},{4,6},{5,7},{6,4},{7,5},{8,10},{9,11},{10,... | collective-permute-start | bytes 1572872 | tf_op jit(solution)/shard_map/ppermute | solution.py:56
  403.4 31.2 %collective-permute-start.57 = (bf16[4,4,32,1408]{3,2,1,0:T(8,128)(2,1)}, bf16[4,4,32,1408]{3,2,1,0:T(8,128)(2,1)}, u32[]{:S(2)}, u32[]{:S(2)}) collective-permute-start(bf16[4,4,32,1408]{3,2,1,0:T(8,128)(2,1)} %grad_out_sib.1.refs_7_), channel_id=1, source_target_pairs={{0,1},{1,0},{2,3},{3,2},{4,5},{5,4},{6,7},{7,6},{8,9},{9,8},{10,11... | collective-permute-start | bytes 4325384 | tf_op jit(solution)/shard_map/ppermute | solution.py:56
  432.9 56.1 %collective-permute-start.61 = (bf16[4,4,32,1536]{3,2,1,0:T(8,128)(2,1)}, bf16[4,4,32,1536]{3,2,1,0:T(8,128)(2,1)}, u32[]{:S(2)}, u32[]{:S(2)}) collective-permute-start(bf16[4,4,32,1536]{3,2,1,0:T(8,128)(2,1)} %grad_qkv_sib.2.refs_6_), channel_id=1, source_target_pairs={{0,1},{1,0},{2,3},{3,2},{4,5},{5,4},{6,7},{7,6},{8,9},{9,8},{10,11... | collective-permute-start | bytes 4718600 | tf_op jit(solution)/shard_map/ppermute | solution.py:56
  434.5 104.7 %collective-permute-start.80 = (f32[1,128,1024]{2,1,0:T(8,128)}, f32[1,128,1024]{2,1,0:T(8,128)}, u32[]{:S(2)}, u32[]{:S(2)}) collective-permute-start(f32[1,128,1024]{2,1,0:T(8,128)} %bitcast_add_fusion.15.refs_8_), channel_id=1, source_target_pairs={{0,4},{1,5},{2,6},{3,7},{4,0},{5,1},{6,2},{7,3},{8,12},{9,13},{10,... | collective-permute-start | bytes 1572872 | tf_op jit(solution)/shard_map/ppermute | solution.py:56
  443.6 35.9 %collective-permute-start.62 = (bf16[8,32,1408]{2,1,0:T(8,128)(2,1)}, bf16[8,32,1408]{2,1,0:T(8,128)(2,1)S(1)}, u32[]{:S(2)}, u32[]{:S(2)}) collective-permute-start(bf16[8,32,1408]{2,1,0:T(8,128)(2,1)} %bitcast.544), channel_id=1, source_target_pairs={{0,16},{1,9},{2,18},{3,11},{4,20},{5,13},{6,22},{7,15},{8,24},{9,1... | collective-permute-start | bytes 2162696 | tf_op jit(solution)/shard_map/ppermute | solution.py:56
  472.8 15.0 %collective-permute-start.63 = (bf16[4,32,4096]{2,1,0:T(8,128)(2,1)S(1)}, bf16[4,32,4096]{2,1,0:T(8,128)(2,1)}, u32[]{:S(2)}, u32[]{:S(2)}) collective-permute-start(bf16[4,32,4096]{2,1,0:T(8,128)(2,1)S(1)} %copy-done.25), channel_id=1, source_target_pairs={{0,8},{1,17},{2,10},{3,19},{4,12},{5,21},{6,14},{7,23},{8,0},{9,25... | collective-permute-start | bytes 3145736 | tf_op jit(solution)/shard_map/ppermute | solution.py:56
  479.5 23.0 %collective-permute-start.60 = (bf16[4,4,32,1536]{3,2,1,0:T(8,128)(2,1)}, bf16[4,4,32,1536]{3,2,1,0:T(8,128)(2,1)}, u32[]{:S(2)}, u32[]{:S(2)}) collective-permute-start(bf16[4,4,32,1536]{3,2,1,0:T(8,128)(2,1)} %grad_qkv_sib.3.refs_4_), channel_id=1, source_target_pairs={{0,1},{1,0},{2,3},{3,2},{4,5},{5,4},{6,7},{7,6},{8,9},{9,8},{10,11... | collective-permute-start | bytes 4718600 | tf_op jit(solution)/shard_map/ppermute | solution.py:56
  479.7 16.4 %collective-permute-start.64 = (bf16[4,32,1408]{2,1,0:T(8,128)(2,1)S(1)}, bf16[4,32,1408]{2,1,0:T(8,128)(2,1)S(1)}, u32[]{:S(2)}, u32[]{:S(2)}) collective-permute-start(bf16[4,32,1408]{2,1,0:T(8,128)(2,1)S(1)} %get-tuple-element.268.refs_5_), channel_id=1, source_target_pairs={{0,8},{1,17},{2,10},{3,19},{4,12},{5,21},{6,14},{7,23},{8,0},{9,25... | collective-permute-start | bytes 1081352 | tf_op jit(solution)/shard_map/ppermute | solution.py:56
  488.9 12.8 %collective-permute-start.65 = (bf16[2,32,4096]{2,1,0:T(8,128)(2,1)S(1)}, bf16[2,32,4096]{2,1,0:T(8,128)(2,1)S(1)}, u32[]{:S(2)}, u32[]{:S(2)}) collective-permute-start(bf16[2,32,4096]{2,1,0:T(8,128)(2,1)S(1)} %fusion.9.refs_6_), channel_id=1, source_target_pairs={{0,2},{1,3},{2,0},{3,1},{4,6},{5,7},{6,4},{7,5},{8,10},{9,11},{10,... | collective-permute-start | bytes 1572872 | tf_op jit(solution)/shard_map/ppermute | solution.py:56
  496.3 15.1 %collective-permute-start.66 = (bf16[8,32,1536]{2,1,0:T(8,128)(2,1)}, bf16[8,32,1536]{2,1,0:T(8,128)(2,1)S(1)}, u32[]{:S(2)}, u32[]{:S(2)}) collective-permute-start(bf16[8,32,1536]{2,1,0:T(8,128)(2,1)} %bitcast.522), channel_id=1, source_target_pairs={{0,16},{1,9},{2,18},{3,11},{4,20},{5,13},{6,22},{7,15},{8,24},{9,1... | collective-permute-start | bytes 2359304 | tf_op jit(solution)/shard_map/ppermute | solution.py:56
  496.4 14.2 %collective-permute-start.67 = (bf16[2,32,1408]{2,1,0:T(8,128)(2,1)S(1)}, bf16[2,32,1408]{2,1,0:T(8,128)(2,1)S(1)}, u32[]{:S(2)}, u32[]{:S(2)}) collective-permute-start(bf16[2,32,1408]{2,1,0:T(8,128)(2,1)S(1)} %fusion.34.refs_5_), channel_id=1, source_target_pairs={{0,2},{1,3},{2,0},{3,1},{4,6},{5,7},{6,4},{7,5},{8,10},{9,11},{10,... | collective-permute-start | bytes 540680 | tf_op jit(solution)/shard_map/ppermute | solution.py:56
  508.9 15.7 %collective-permute-start.69 = (bf16[8,32,1536]{2,1,0:T(8,128)(2,1)}, bf16[8,32,1536]{2,1,0:T(8,128)(2,1)S(1)}, u32[]{:S(2)}, u32[]{:S(2)}) collective-permute-start(bf16[8,32,1536]{2,1,0:T(8,128)(2,1)} %bitcast.542), channel_id=1, source_target_pairs={{0,16},{1,9},{2,18},{3,11},{4,20},{5,13},{6,22},{7,15},{8,24},{9,1... | collective-permute-start | bytes 2359304 | tf_op jit(solution)/shard_map/ppermute | solution.py:56
  511.5 15.4 %collective-permute-start.68 = (bf16[4,32,1536]{2,1,0:T(8,128)(2,1)S(1)}, bf16[4,32,1536]{2,1,0:T(8,128)(2,1)S(1)}, u32[]{:S(2)}, u32[]{:S(2)}) collective-permute-start(bf16[4,32,1536]{2,1,0:T(8,128)(2,1)S(1)} %get-tuple-element.266.refs_5_), channel_id=1, source_target_pairs={{0,8},{1,17},{2,10},{3,19},{4,12},{5,21},{6,14},{7,23},{8,0},{9,25... | collective-permute-start | bytes 1179656 | tf_op jit(solution)/shard_map/ppermute | solution.py:56
  525.5 8.1 %collective-permute-start.70 = (bf16[4,32,1536]{2,1,0:T(8,128)(2,1)}, bf16[4,32,1536]{2,1,0:T(8,128)(2,1)}, u32[]{:S(2)}, u32[]{:S(2)}) collective-permute-start(bf16[4,32,1536]{2,1,0:T(8,128)(2,1)} %get-tuple-element.263.refs_8_), channel_id=1, source_target_pairs={{0,8},{1,17},{2,10},{3,19},{4,12},{5,21},{6,14},{7,23},{8,0},{9,25... | collective-permute-start | bytes 1179656 | tf_op jit(solution)/shard_map/ppermute | solution.py:56
  539.2 15.0 %collective-permute-start.79 = (bf16[1,32,4096]{2,1,0:T(8,128)(2,1)}, bf16[1,32,4096]{2,1,0:T(8,128)(2,1)S(1)}, u32[]{:S(2)}, u32[]{:S(2)}) collective-permute-start(bf16[1,32,4096]{2,1,0:T(8,128)(2,1)} %fusion.14.refs_6_), channel_id=1, source_target_pairs={{0,4},{1,5},{2,6},{3,7},{4,0},{5,1},{6,2},{7,3},{8,12},{9,13},{10,... | collective-permute-start | bytes 786440 | tf_op jit(solution)/shard_map/ppermute | solution.py:56
  540.8 19.1 %collective-permute-start.71 = (bf16[2,32,3072]{2,1,0:T(8,128)(2,1)S(1)}, bf16[2,32,3072]{2,1,0:T(8,128)(2,1)S(1)}, u32[]{:S(2)}, u32[]{:S(2)}) collective-permute-start(bf16[2,32,3072]{2,1,0:T(8,128)(2,1)S(1)} %pad_maximum_fusion.10), channel_id=1, source_target_pairs={{0,2},{1,3},{2,0},{3,1},{4,6},{5,7},{6,4},{7,5},{8,10},{9,11},{10,... | collective-permute-start | bytes 1179656 | tf_op jit(solution)/shard_map/ppermute | solution.py:56
  542.1 12.1 %collective-permute-start.75 = (f32[2,2,4,128]{3,2,1,0:T(4,128)S(1)}, f32[2,2,4,128]{3,2,1,0:T(4,128)S(1)}, u32[]{:S(2)}, u32[]{:S(2)}) collective-permute-start(f32[2,2,4,128]{3,2,1,0:T(4,128)S(1)} %fusion.44), channel_id=1, source_target_pairs={{0,16},{1,17},{2,18},{3,19},{4,20},{5,21},{6,22},{7,23},{8,24},{9,... | collective-permute-start | bytes 24584 | tf_op jit(solution)/shard_map/ppermute | solution.py:56
  546.1 15.6 %collective-permute-start.78 = (f32[1,32,1408]{2,1,0:T(8,128)S(1)}, f32[1,32,1408]{2,1,0:T(8,128)S(1)}, u32[]{:S(2)}, u32[]{:S(2)}) collective-permute-start(f32[1,32,1408]{2,1,0:T(8,128)S(1)} %copy-done.35), channel_id=1, source_target_pairs={{0,4},{1,5},{2,6},{3,7},{4,0},{5,1},{6,2},{7,3},{8,12},{9,13},{10,... | collective-permute-start | bytes 540680 | tf_op jit(solution)/shard_map/ppermute | solution.py:56
  565.0 10.1 %collective-permute-start.72 = (bf16[1,32,3072]{2,1,0:T(8,128)(2,1)S(1)}, bf16[1,32,3072]{2,1,0:T(8,128)(2,1)S(1)}, u32[]{:S(2)}, u32[]{:S(2)}) collective-permute-start(bf16[1,32,3072]{2,1,0:T(8,128)(2,1)S(1)} %fusion.18), channel_id=1, source_target_pairs={{0,4},{1,5},{2,6},{3,7},{4,0},{5,1},{6,2},{7,3},{8,12},{9,13},{10,... | collective-permute-start | bytes 589832 | tf_op jit(solution)/shard_map/ppermute | solution.py:56
  (69 other events, 480.4 us)

commit v5 on v4

--- a/solution.py
+++ b/solution.py
@@ -683,14 +683,9 @@
 
 
 def act_back_kernel(g_ref, w_ref, slope_ref, o_ref, sum_ref):
-    total = jnp.zeros(sum_ref.shape, f32)
-    for row in range(0, g_ref.shape[0], TILE):
-        rows = slice(row, row + TILE)
-        back = contract(g_ref[rows, :], w_ref[...], 1, 1) * slope_ref[rows, :].astype(f32)
-        back = back.astype(bf16)
-        o_ref[rows, :] = back
-        total = total + column_sum(back.astype(f32))
-    sum_ref[...] = total
+    back = (contract(g_ref[...], w_ref[...], 1, 1) * slope_ref[...].astype(f32)).astype(bf16)
+    o_ref[...] = back
+    sum_ref[...] = column_sum(back.astype(f32))
 
 
 def act_back(branch, w, slope, wait=()):
@@ -975,6 +970,60 @@
         table=table,
         wait=wait,
     )(table, *arrays, *([other] if own else []))
+
+
+def piece_kernel(offset, n_rows, n_z, table, a_ref, b_ref, *refs):
+    r = a_ref.shape[1] // (2 * n_z)
+    core = table[2 * n_rows]
+    side = core if offset == 0 else 1 - core
+    blocks = [a_ref[:, pl.ds(pl.multiple_of((2 * z + side) * r, LANES), r)] for z in range(n_z)]
+    total = contract(jnp.concatenate(blocks, axis=1), b_ref[...], 0, 0)
+    if len(refs) == 1:
+        refs[0][...] = total.reshape(refs[0].shape).astype(refs[0].dtype)
+        return
+    other, send_ref, keep_ref = refs
+    total = total.reshape(other.shape) + other[...].astype(f32)
+    kept = pl.program_id(0) < n_rows // 2
+
+    @pl.when(kept)
+    def _():
+        keep_ref[...] = total
+
+    @pl.when(jnp.logical_not(kept))
+    def _():
+        send_ref[...] = total.astype(send_ref.dtype)
+
+
+def weight_pieces(name, table, a, b, n_rows, n_z, other=None, wait=()):
+    (t, k), n = a.shape, b.shape[1]
+    r = k // (n_rows * n_z * 2)
+    half = n_rows // 2
+    own = other is not None
+    offset = 0 if own else n_rows
+    block = (1, n_z, r, n)
+    each = pl.BlockSpec(block, lambda i, _: (i, 0, 0, 0))
+    outs = [
+        pl.BlockSpec(block, lambda i, _: (jnp.maximum(i - half, 0), 0, 0, 0)),
+        pl.BlockSpec(block, lambda i, _: (jnp.minimum(i, half - 1), 0, 0, 0)),
+    ]
+    return call(
+        functools.partial(piece_kernel, offset, n_rows, n_z),
+        name,
+        (n_rows,),
+        [
+            pl.BlockSpec((t, k // n_rows), lambda i, tab: (0, tab[offset + i])),
+            whole_spec(b.shape),
+        ]
+        + ([each] if own else []),
+        outs if own else each,
+        [like((half, n_z, r, n), bf16), like((half, n_z, r, n), f32)]
+        if own
+        else like((n_rows, n_z, r, n), bf16),
+        t * k * n,
+        2 * t * (k + n) + 3 * k * n,
+        table=table,
+        wait=wait,
+    )(table, a, b, *([other] if own else []))
 
 
 WINDOWS = (256, -(-(DMOST + 15) // 32) * 32)
@@ -1364,8 +1413,8 @@
         [w_qkv, w_out, jnp.pad(w_proj, ((0, 0), (0, proj_width - w_proj.shape[1])))], axis=1
     )
     g_qkv, g_up, g_down = (Gather(w) for w in (w_first, w_up, w_down))
-    g_qkv.all_z(())
-    tokens_half = tuple(halves(table, tokens, n_rows, n_z, wait=[g_qkv.held, *early]))
+    g_qkv.all_z((), ((), early))
+    tokens_half = tuple(halves(table, tokens, n_rows, n_z, wait=[g_qkv.held]))
     g_qkv.all_rows([(), [tokens_half[0]]], ())
     first, last = g_qkv.own, g_qkv.pieces[-1]
     vectors = (b_qkv, b_out, norm1_gain, norm1_bias, b_up, b_down, norm2_gain, norm2_bias)
@@ -1442,9 +1491,20 @@
     def attention_part(i, wait):
         return attention_back(documents, qkv, attended_grad, cosine, sine, i, 2, wait=wait)
 
-    down_sib = sib_half("grad_down", [(act, branch_grad)], 512)
+    whole_lanes = act.shape[1] // n_devices % LANES == 0
+    if whole_lanes:
+        down_sib = weight_pieces("grad_down_sib", table, act, branch_grad, n_rows, n_z)
+    else:
+        down_sib = sib_half("grad_down", [(act, branch_grad)], 512)
     inner_grad, grad_bup = act_back(branch_grad, full_down, slope, wait=[down_sib])
-    down = own_half("grad_down", [(act, branch_grad)], 512, down_sib, True, wait=[grad_bup])
+    if whole_lanes:
+        other = exchange(down_sib, swap_core=True)
+        parts = weight_pieces(
+            "grad_down", table, act, branch_grad, n_rows, n_z, other, wait=[grad_bup]
+        )
+        down = Scatter(*parts, True)
+    else:
+        down = own_half("grad_down", [(act, branch_grad)], 512, down_sib, True, wait=[grad_bup])
     up_sib = sib_half("grad_up", [(hidden_low, inner_grad)], 1024, f32, wait=[down.send])
     resid_one_grad, out_grad, attended_grad, sums1 = hidden_back(
         inner_grad, full_up, resid_two_grad, hat1, rstd1, gain_one, full_out, wait=[up_sib]
@@ -1457,13 +1517,13 @@
     grad_a, sums_a = attention_part(0, [out_sib, d3])
     d4 = down.step(sums_a)
     u2 = up.step(sums_a)
-    sib_a = sib_half("grad_qkv", [(tokens_half, grad_a)], 512)
+    sib_a = sib_half("grad_qkv", [(tokens_half, grad_a)], 512, wait=[d4, u2])
     out = own_half("grad_out", out_pairs, None, out_sib, True, wait=[sib_a])
     grad_b, sums_b = attention_part(1, [out.send, d4, u2])
-    sib_b = sib_half("grad_qkv", [(tokens_half, grad_b)], 512)
     o2 = out.step(sums_b)
     u3 = up.step(sums_b)
     sum_down = down.finish(sums_b)
+    sib_b = sib_half("grad_qkv", [(tokens_half, grad_b)], 512, wait=[sum_down])
     qkv_a = own_half("grad_qkv", [(tokens_half, grad_a)], 512, sib_a, wait=[sib_b, o2, u3])
     o3 = out.step(qkv_a.send)
     u4 = up.step(qkv_a.send)
@@ -1471,6 +1531,8 @@
     a2 = qkv_a.step(qkv_b.send)
     o4 = out.step(qkv_b.send)
     input_grad = input_back([grad_a, grad_b], full_qkv, resid_one_grad, wait=[qkv_b.send, a2, o4])
+    sum_up = up.finish(input_grad)
+    sum_out = out.finish(input_grad)
     b2 = qkv_b.step(input_grad)
     qkv_a.step(input_grad)
     grads = [sums_a[i] if j == 0 else sums_b[i] for i in range(3) for j in range(2)]
@@ -1478,19 +1540,17 @@
     small = pack(
         [grad_bqkv, sums1[2:3], sums1[0:1], sums1[1:2], grad_bup, sums2[2:3], sums2[0:1], sums2[1:2]],
         n_devices,
-        wait=[b2],
+        wait=[b2, sum_up, sum_out],
     )
     while qkv_b.stages[0][0] == "row":
         qkv_b.step(small)
     while qkv_a.stages[0][0] == "row":
         qkv_a.step()
     q3 = qkv_a.merge(qkv_b).send
-    sum_up = up.finish(q3)
-    sum_out = out.finish(q3)
     sum_out, sum_proj = sum_out[:, :D], sum_out[:, D : D + w_proj.shape[1]]
     q4 = qkv_a.step()
     small = scatter_small(
-        small.reshape(n_devices, -1, LANES), f32, [[q3], [q3], [q3], [q4], [q4]]
+        small.reshape(n_devices, -1, LANES), f32, [[], [q3], [q3], [q4], [q4]]
     ).reshape(-1)
     sum_qkv = qkv_a.finish()
     width = D // 2

time: 582 us -> 574 us (0.986)
  Pallas kernels: 330 us -> 321 us
  waiting for transfers between devices: 85.6 us -> 78.7 us
  starting transfers between devices: 90.6 us -> 97.2 us
    pallas_call x28, Pallas kernels: 330 us -> 321 us  [call(): return lambda *operands: run(*operands, *wait)]
    ppermute x81, waiting for transfers between devices: 85.6 us -> 78.7 us  [exchange(): return lax.ppermute(value, AXES, pairs)]
    ppermute x81, starting transfers between devices: 90.6 us -> 97.2 us  [exchange(): return lax.ppermute(value, AXES, pairs)]
    unnamed x116 -> x118, local copies, waits for them, and re-layouts: 9.21 us -> 12.7 us
  transfers between devices with their start and end apart: 81 -> 81, of which waited for: 31 -> 30; matrix products, arithmetic and copies ran while one was open for 9% -> 9% of each run, Pallas kernels for 43% -> 42%
where the time goes in v5:
time: 574 us; the launch traced here: 568 us
  Pallas kernels  321 us (56%)
  starting transfers between devices  97.2 us (17%)
  waiting for transfers between devices  78.7 us (14%)
  other arithmetic  38.9 us (7%)
  local copies, waits for them, and re-layouts  30.5 us (5%)
    pallas_call x28, Pallas kernels, call(): return lambda *operands: run(*operands, *wait)  321 us
    ppermute x81, starting transfers between devices, exchange(): return lax.ppermute(value, AXES, pairs)  97.2 us
    ppermute x81, waiting for transfers between devices, exchange(): return lax.ppermute(value, AXES, pairs)  78.7 us
    unnamed x118, local copies, waits for them, and re-layouts  12.7 us
    add x9, other arithmetic, step(): pick(parts[0], other) + pick(parts[1], other).astype(f32)  11.8 us
  transfers between devices with their start and end apart: 81, of which 30 were waited for; matrix products, arithmetic and copies ran while one was open for 9% of the time, Pallas kernels for 42%

profile of v5, /device:TPU:0, one launch (start us, length us, event | category | flops | bytes accessed | tf_op | source)
XLA Modules:
  0.0 568.2 jit_solution(4246277130871945652)
XLA Ops:
  1.7 4.1 collective-permute-start.1
  5.8 5.4 concatenate.32
  15.1 3.7 collective-permute-done.1
  22.2 12.0 %collective-permute-done.3 = bf16[2,32,4480]{2,1,0:T(8,128)(2,1)S(1)} collective-permute-done((bf16[2,32,4480]{2,1,0:T(8,128)(2,1)S(1)}, bf16[2,32,4480]{2,1,0:T(8,128)(2,1)S(1)}, u32[]{:S(2)}, u32[]{:S(2)}) %collective-permute-start.3) | collective-permute-done | bytes 573472 | tf_op jit(solution)/shard_map/ppermute | solution.py:56
  43.4 3.4 collective-permute-start.14
  47.9 5.4 halves.1
  53.4 7.6 %collective-permute-done.5.refs_6_.refs_7_.refs_17_ = bf16[4,32,4480]{2,1,0:T(8,128)(2,1)S(1)} collective-permute-done((bf16[4,32,4480]{2,1,0:T(8,128)(2,1)}, bf16[4,32,4480]{2,1,0:T(8,128)(2,1)S(1)}, u32[]{:S(2)}, u32[]{:S(2)}) %collective-permute-start.5) | collective-permute-done | bytes 1146912 | tf_op jit(solution)/shard_map/ppermute | solution.py:56
  61.0 2.0 collective-permute-start.7
  63.9 3.1 collective-permute-start.15
  71.0 6.1 %collective-permute-start.12 = (bf16[4,32,4480]{2,1,0:T(8,128)(2,1)}, bf16[4,32,4480]{2,1,0:T(8,128)(2,1)}, u32[]{:S(2)}, u32[]{:S(2)}) collective-permute-start(bf16[4,32,4480]{2,1,0:T(8,128)(2,1)} %collective-permute-done.9.refs_7_.refs_8_.refs_18_), channel_id=1, source_target_pairs={{0,1},{1,0},{2,3},{3,2},{4,5},{5,4},{6,7},{7,6},{8,9},{9,8},{10,11... | collective-permute-start | bytes 3440648 | tf_op jit(solution)/shard_map/ppermute | solution.py:56
  80.6 2.0 collective-permute-start.17
  84.5 2.3 unpack.1
  86.8 3.4 collective-permute-start.19
  91.3 14.9 %project_qkv.1 = (bf16[1024,3072]{1,0:T(8,128)(2,1)}, bf16[4,4,2,32,3072]{4,3,2,1,0:T(8,128)(2,1)}) custom-call(s32[17]{0:T(128)} %concatenate.30.refs_0_, bf16[1024,1024]{1,0:T(8,128)(2,1)} %refs_3_.1, f32[1,3072]{1,0:T(1,128)} %get-tuple-element.138.refs_2_, f32[1024,128]{1,0:T(8,128)} %get-tuple-element.350.refs_3_.refs_5_, ...), custom_call_target="tpu_custom_call" | custom-call | flops 6442450944 | bytes 20971520 | tf_op jit(solution)/shard_map/project_qkv/pallas_call | solution.py:368
  106.5 3.2 collective-permute-start.20
  109.7 18.5 %attention.1.refs_1_ = bf16[1024,1024]{1,0:T(8,128)(2,1)} custom-call(s32[9]{0:T(128)} %pad_add_fusion.refs_0_, bf16[1024,3072]{1,0:T(8,128)(2,1)} %get-tuple-element.140.refs_1_.refs_2_.refs_3_, bf16[1024,3072]{1,0:T(8,128)(2,1)} %get-tuple-element.140.refs_1_.refs_2_.refs_3_, bf16[1024,3072]{1,0:T(8,128)(2,1)} %get-tuple-element.140.refs_1_.refs_2_.refs_3_, ...), custom_call_target="tpu_custom_call" | custom-call | flops 20000000000 | bytes 8388608 | tf_op jit(solution)/shard_map/attention/pallas_call | solution.py:368
  129.7 3.8 collective-permute-start.25
  133.5 9.7 %out_norm.1 = (f32[1024,1024]{1,0:T(8,128)}, f32[1024,128]{1,0:T(8,128)}, bf16[1024,1024]{1,0:T(8,128)(2,1)}, bf16[4,4,2,32,1024]{4,3,2,1,0:T(8,128)(2,1)}) custom-call(s32[17]{0:T(128)} %concatenate.30.refs_0_, bf16[1024,1024]{1,0:T(8,128)(2,1)} %attention.1.refs_1_, f32[1,1024]{1,0:T(1,128)} %get-tuple-element.146.refs_2_, bf16[1024,1024]{1,0:T(8,128)(2,1)} %refs_3_.1, ...), custom_call_target="tpu_custom_call" | custom-call | flops 2147483648 | bytes 12582912 | tf_op jit(solution)/shard_map/out_norm/pallas_call | solution.py:368
  144.6 16.0 %up_gelu.2 = (bf16[1024,4096]{1,0:T(8,128)(2,1)}, bf16[1024,4096]{1,0:T(8,128)(2,1)}, bf16[4,4,2,32,4096]{4,3,2,1,0:T(8,128)(2,1)}) custom-call(s32[17]{0:T(128)} %concatenate.30.refs_0_, bf16[1024,1024]{1,0:T(8,128)(2,1)} %get-tuple-element.155.refs_1_, f32[1,4096]{1,0:T(1,128)} %get-tuple-element.156.refs_2_, bf16[4,32,4096]{2,1,0:T(8,128)(2,1)} %bitcast.498, ...), custom_call_target="tpu_custom_call" | custom-call | flops 4294967296 | bytes 12582912 | tf_op jit(solution)/shard_map/up_gelu/pallas_call | solution.py:368
  163.4 15.9 %up_gelu.3 = (bf16[1024,4096]{1,0:T(8,128)(2,1)}, bf16[1024,4096]{1,0:T(8,128)(2,1)}, bf16[4,4,2,32,4096]{4,3,2,1,0:T(8,128)(2,1)}) custom-call(s32[17]{0:T(128)} %concatenate.30.refs_0_, bf16[1024,1024]{1,0:T(8,128)(2,1)} %get-tuple-element.155.refs_1_, ...), custom_call_target="tpu_custom_call", output_to_operand_aliasing={{0}: (11, {}), {1}: (12, {}), {2}: (13, {})} | custom-call | flops 4294967296 | bytes 12582912 | tf_op jit(solution)/shard_map/up_gelu/pallas_call | solution.py:368
  180.0 2.2 collective-permute-done.31.refs_15_
  183.2 21.8 %down_norm.1 = (f32[1024,1024]{1,0:T(8,128)}, f32[1024,128]{1,0:T(8,128)}, bf16[1024,1024]{1,0:T(8,128)(2,1)}, f32[1024,384]{1,0:T(8,128)}, bf16[1024,384]{1,0:T...) custom-call(s32[17]{0:T(128)} %concatenate.30.refs_0_, ...), custom_call_target="tpu_custom_call" | custom-call | flops 8589934592 | bytes 20971520 | tf_op jit(solution)/shard_map/down_norm/pallas_call | solution.py:368
  208.2 2.0 collective-permute-start.34
  211.3 2.5 collective-permute-done.34
  225.0 10.1 %scores.1 = (f32[3,8,1024]{2,1,0:T(8,128)}, f32[3,8,32]{2,1,0:T(8,128)}, f32[3,3,32]{2,1,0:T(4,128)}) custom-call(bf16[1024,384]{1,0:T(8,128)(2,1)} %get-tuple-element.179.refs_0_, bf16[1024,384]{1,0:T(8,128)(2,1)} %bitcast.520, s32[1024,1]{1,0:T(8,128)} %copy.110.refs_2_, bf16[8,1024]{1,0:T(8,128)(2,1)} %fusion.41.refs_3_, ...), custom_call_target="tpu_custom_call" | custom-call | flops 4831838208 | bytes 1000000 | tf_op jit(solution)/shard_map/scores/pallas_call | solution.py:368
  238.7 2.2 collective-permute-start.42
  243.3 2.5 collective-permute-start.44
  247.9 3.4 collective-permute-done.45
  251.9 11.6 %score_grads.1 = (f32[1024,384]{1,0:T(8,128)}, f32[1024,384]{1,0:T(8,128)}) custom-call(bf16[1024,384]{1,0:T(8,128)(2,1)} %get-tuple-element.179.refs_0_, bf16[1024,384]{1,0:T(8,128)(2,1)} %bitcast.521, s32[1,1024]{1,0:T(1,128)} %add.562.refs_2_, s32[1024,1]{1,0:T(8,128)} %fusion.15.refs_3_, f32[3,8,1024]{2,1,0:T(8,128)} %get-tuple-element.182.refs_4_, ...), custom_call_target="tpu_custom_call" | custom-call | flops 9663676416 | bytes 1000000 | tf_op jit(solution)/shard_map/score_grads/pallas_call | solution.py:368
  266.0 7.7 %head_back.2 = (f32[1024,1024]{1,0:T(8,128)}, bf16[1024,1024]{1,0:T(8,128)(2,1)}, bf16[1024,384]{1,0:T(8,128)(2,1)}, f32[3,1024]{1,0:T(4,128)}) custom-call(f32[1024,384]{1,0:T(8,128)} %get-tuple-element.184.refs_0_, f32[1024,384]{1,0:T(8,128)} %get-tuple-element.185.refs_1_, bf16[1024,384]{1,0:T(8,128)(2,1)} %bitcast.509, ...), custom_call_target="tpu_custom_call" | custom-call | flops 603979776 | bytes 12582912 | tf_op jit(solution)/shard_map/head_back/pallas_call | solution.py:368
  279.3 2.7 collective-permute-done.48
  282.2 2.8 collective-permute-start.51
  287.0 3.7 collective-permute-done.52
  291.3 4.0 head_back.3
  295.3 10.1 %grad_down_sib.1.refs_3_ = bf16[4,4,128,1024]{3,2,1,0:T(8,128)(2,1)} custom-call(s32[17]{0:T(128)} %concatenate.30.refs_0_, bf16[1024,4096]{1,0:T(8,128)(2,1)} %get-tuple-element.167.refs_1_, bf16[1024,1024]{1,0:T(8,128)(2,1)} %get-tuple-element.194.refs_2_.refs_0_), custom_call_target="tpu_custom_call" | custom-call | flops 4294967296 | bytes 23068672 | tf_op jit(solution)/shard_map/grad_down_sib/pallas_call | solution.py:368
  305.3 14.9 %act_back.1 = (bf16[1024,4096]{1,0:T(8,128)(2,1)}, f32[1,4096]{1,0:T(1,128)}) custom-call(bf16[1024,1024]{1,0:T(8,128)(2,1)} %get-tuple-element.194.refs_2_.refs_0_, bf16[4096,1024]{1,0:T(8,128)(2,1)} %bitcast.543, bf16[1024,4096]{1,0:T(8,128)(2,1)} %get-tuple-element.196.refs_2_, bf16[4,4,128,1024]{3,2,1,0:T(8,128)(2,1)} %grad_down_sib.1.refs_3_), custom_call_target="tpu_custom_call" | custom-call | flops 8589934592 | bytes 25165824 | tf_op jit(solution)/shard_map/act_back/pallas_call | solution.py:368
  320.2 2.0 copy-done.47
  322.2 11.9 %grad_down.1 = (bf16[2,4,128,1024]{3,2,1,0:T(8,128)(2,1)}, f32[2,4,128,1024]{3,2,1,0:T(8,128)}) custom-call(s32[17]{0:T(128)} %concatenate.30.refs_0_, bf16[1024,4096]{1,0:T(8,128)(2,1)} %get-tuple-element.167.refs_1_, bf16[1024,1024]{1,0:T(8,128)(2,1)} %get-tuple-element.194.refs_2_.refs_0_, bf16[4,4,128,1024]{3,2,1,0:T(8,128)(2,1)} %copy-done.47, ...), custom_call_target="tpu_custom_call" | custom-call | flops 4294967296 | bytes 23068672 | tf_op jit(solution)/shard_map/grad_down/pallas_call | solution.py:368
  334.1 12.0 %grad_up_sib.1.refs_7_ = f32[4,4,32,4096]{3,2,1,0:T(8,128)} custom-call(s32[17]{0:T(128)} %concatenate.30.refs_0_, bf16[1024,1024]{1,0:T(8,128)(2,1)} %get-tuple-element.155.refs_1_, bf16[1024,4096]{1,0:T(8,128)(2,1)} %get-tuple-element.197.refs_2_.refs_0_, bf16[8,128,1024]{2,1,0:T(8,128)(2,1)} %bitcast.516), custom_call_target="tpu_custom_call" | custom-call | flops 4294967296 | bytes 23068672 | tf_op jit(solution)/shard_map/grad_up_sib/pallas_call | solution.py:368
  347.8 20.5 %hidden_back.1 = (f32[1024,1024]{1,0:T(8,128)}, bf16[1024,1024]{1,0:T(8,128)(2,1)}, bf16[1024,1024]{1,0:T(8,128)(2,1)}, f32[3,1024]{1,0:T(4,128)}) custom-call(bf16[1024,4096]{1,0:T(8,128)(2,1)} %get-tuple-element.197.refs_2_.refs_0_, bf16[1024,4096]{1,0:T(8,128)(2,1)} %bitcast.504, f32[1024,1024]{1,0:T(8,128)} %get-tuple-element.199.refs_2_, ...), custom_call_target="tpu_custom_call" | custom-call | flops 10737418240 | bytes 33554432 | tf_op jit(solution)/shard_map/hidden_back/pallas_call | solution.py:368
  368.4 4.3 collective-permute-done.55
  372.7 2.4 bitcast_add_fusion.2
  377.4 13.3 %grad_up.1 = (bf16[2,4,32,4096]{3,2,1,0:T(8,128)(2,1)}, f32[2,4,32,4096]{3,2,1,0:T(8,128)}) custom-call(s32[17]{0:T(128)} %concatenate.30.refs_0_, bf16[1024,1024]{1,0:T(8,128)(2,1)} %get-tuple-element.155.refs_1_, bf16[1024,4096]{1,0:T(8,128)(2,1)} %get-tuple-element.197.refs_2_.refs_0_, f32[4,4,32,4096]{3,2,1,0:T(8,128)} %collective-permute-done.54.refs_3_, ...), custom_call_target="tpu_custom_call" | custom-call | flops 4294967296 | bytes 23068672 | tf_op jit(solution)/shard_map/grad_up/pallas_call | solution.py:368
  393.3 7.9 %grad_out_sib.1.refs_7_ = bf16[4,4,32,1408]{3,2,1,0:T(8,128)(2,1)} custom-call(s32[17]{0:T(128)} %concatenate.30.refs_0_, bf16[1024,1024]{1,0:T(8,128)(2,1)} %attention.1.refs_1_, bf16[1024,1024]{1,0:T(8,128)(2,1)} %get-tuple-element.205.refs_2_, bf16[1024,1024]{1,0:T(8,128)(2,1)} %get-tuple-element.116.refs_3_, ...), custom_call_target="tpu_custom_call" | custom-call | flops 1476395008 | bytes 9306112 | tf_op jit(solution)/shard_map/grad_out_sib/pallas_call | solution.py:368
  401.2 21.6 %attention_back.2 = (bf16[3,1024,512]{2,1,0:T(8,128)(2,1)}, f32[3,1,512]{2,1,0:T(1,128)}) custom-call(s32[9]{0:T(128)} %pad_add_fusion.refs_0_, bf16[1024,3072]{1,0:T(8,128)(2,1)} %get-tuple-element.140.refs_1_.refs_2_.refs_3_, bf16[1024,3072]{1,0:T(8,128)(2,1)} %get-tuple-element.140.refs_1_.refs_2_.refs_3_, ...), custom_call_target="tpu_custom_call" | custom-call | flops 24999999488 | bytes 7340032 | tf_op jit(solution)/shard_map/attention_back/pallas_call | solution.py:368
  427.6 3.3 bitcast_add_fusion
  432.6 5.9 %grad_qkv_sib.2.refs_6_ = bf16[4,4,32,1536]{3,2,1,0:T(8,128)(2,1)} custom-call(s32[17]{0:T(128)} %concatenate.30.refs_0_, bf16[512,1024]{1,0:T(8,128)(2,1)} %get-tuple-element.213.refs_1_, bf16[3,1024,512]{2,1,0:T(8,128)(2,1)} %get-tuple-element.212.refs_2_.refs_0_, f32[1,128,1024]{2,1,0:T(8,128)} %copy-done.15, bf16[4,32,4096]{2,1,0:T(8,128)(2,1)} %copy-done.11), custom_call_target="tpu_custom_call" | custom-call | flops 1610612736 | bytes 9961472 | tf_op jit(solution)/shard_map/grad_qkv_sib/pallas_call | solution.py:368
  439.6 8.4 %grad_out.1 = (bf16[2,4,32,1408]{3,2,1,0:T(8,128)(2,1)}, f32[2,4,32,1408]{3,2,1,0:T(8,128)}) custom-call(s32[17]{0:T(128)} %concatenate.30.refs_0_, bf16[1024,1024]{1,0:T(8,128)(2,1)} %attention.1.refs_1_, bf16[1024,1024]{1,0:T(8,128)(2,1)} %get-tuple-element.205.refs_2_, bf16[1024,1024]{1,0:T(8,128)(2,1)} %get-tuple-element.116.refs_3_, ...), custom_call_target="tpu_custom_call" | custom-call | flops 1476395008 | bytes 9306112 | tf_op jit(solution)/shard_map/grad_out/pallas_call | solution.py:368
  448.0 21.7 %attention_back.3 = (bf16[3,1024,512]{2,1,0:T(8,128)(2,1)}, f32[3,1,512]{2,1,0:T(1,128)}) custom-call(s32[9]{0:T(128)} %pad_add_fusion.refs_0_, bf16[1024,3072]{1,0:T(8,128)(2,1)} %get-tuple-element.140.refs_1_.refs_2_.refs_3_, bf16[1024,3072]{1,0:T(8,128)(2,1)} %get-tuple-element.140.refs_1_.refs_2_.refs_3_, ...), custom_call_target="tpu_custom_call" | custom-call | flops 24999999488 | bytes 7340032 | tf_op jit(solution)/shard_map/attention_back/pallas_call | solution.py:368
  472.0 2.0 fusion.14.refs_3_
  474.0 6.0 %grad_qkv_sib.3.refs_4_ = bf16[4,4,32,1536]{3,2,1,0:T(8,128)(2,1)} custom-call(s32[17]{0:T(128)} %concatenate.30.refs_0_, bf16[512,1024]{1,0:T(8,128)(2,1)} %get-tuple-element.213.refs_1_, bf16[3,1024,512]{2,1,0:T(8,128)(2,1)} %get-tuple-element.219.refs_2_.refs_1_, f32[128,1024]{1,0:T(8,128)} %fusion.14.refs_3_), custom_call_target="tpu_custom_call" | custom-call | flops 1610612736 | bytes 9961472 | tf_op jit(solution)/shard_map/grad_qkv_sib/pallas_call | solution.py:368
  481.3 2.4 bitcast_add_fusion.10
  483.7 2.8 collective-permute-start.65
  490.2 6.5 %grad_qkv.2 = (bf16[2,4,32,1536]{3,2,1,0:T(8,128)(2,1)}, f32[2,4,32,1536]{3,2,1,0:T(8,128)}) custom-call(s32[17]{0:T(128)} %concatenate.30.refs_0_, bf16[512,1024]{1,0:T(8,128)(2,1)} %get-tuple-element.134.refs_13_.refs_1_, bf16[3,1024,512]{2,1,0:T(8,128)(2,1)} %get-tuple-element.212.refs_2_.refs_0_, bf16[4,4,32,1536]{3,2,1,0:T(8,128)(2,1)} %copy-done.18, ...), custom_call_target="tpu_custom_call" | custom-call | flops 1610612736 | bytes 9961472 | tf_op jit(solution)/shard_map/grad_qkv/pallas_call | solution.py:368
  503.4 3.1 collective-permute-start.72
  506.4 6.4 %grad_qkv.3 = (bf16[2,4,32,1536]{3,2,1,0:T(8,128)(2,1)}, f32[2,4,32,1536]{3,2,1,0:T(8,128)}) custom-call(s32[17]{0:T(128)} %concatenate.30.refs_0_, bf16[512,1024]{1,0:T(8,128)(2,1)} %get-tuple-element.134.refs_13_.refs_1_, bf16[3,1024,512]{2,1,0:T(8,128)(2,1)} %get-tuple-element.219.refs_2_.refs_1_, ...), custom_call_target="tpu_custom_call" | custom-call | flops 1610612736 | bytes 9961472 | tf_op jit(solution)/shard_map/grad_qkv/pallas_call | solution.py:368
  517.3 12.3 %input_back.1 = f32[1024,1024]{1,0:T(8,128)} custom-call(bf16[3,1024,512]{2,1,0:T(8,128)(2,1)} %get-tuple-element.212.refs_2_.refs_0_, bf16[3,1024,512]{2,1,0:T(8,128)(2,1)} %get-tuple-element.219.refs_2_.refs_1_, bf16[1024,3072]{1,0:T(8,128)(2,1)} %bitcast.544, f32[1024,1024]{1,0:T(8,128)} %get-tuple-element.221.refs_3_, bf16[8,32,1536]{2,1,0:T(8,128)(2,1)} %bitcast.542, ...), custom_call_target="tpu_custom_call" | custom-call | flops 6442450944 | bytes 20971520 | tf_op jit(solution)/shard_map/input_back/pallas_call | solution.py:368
  532.2 3.4 pack.1
  540.9 2.4 collective-permute-done.77
  543.7 3.4 collective-permute-done.78
  547.0 3.3 collective-permute-done.74
  551.1 2.9 collective-permute-done.79
  554.1 2.3 collective-permute-start.80
  560.7 6.2 %collective-permute-done.75 = bf16[1,32,3072]{2,1,0:T(8,128)(2,1)S(1)} collective-permute-done((bf16[1,32,3072]{2,1,0:T(8,128)(2,1)S(1)}, bf16[1,32,3072]{2,1,0:T(8,128)(2,1)S(1)}, u32[]{:S(2)}, u32[]{:S(2)}) %collective-permute-start.75) | collective-permute-done | bytes 196640 | tf_op jit(solution)/shard_map/ppermute | solution.py:56
  (365 shorter events, 118.5 us)
Async XLA Ops:
  1.7 17.1 %collective-permute-start.1 = (bf16[32,4480]{1,0:T(8,128)(2,1)S(1)}, bf16[32,4480]{1,0:T(8,128)(2,1)S(1)}, u32[]{:S(2)}, u32[]{:S(2)}) collective-permute-start(bf16[32,4480]{1,0:T(8,128)(2,1)S(1)} %fusion.28), channel_id=1, source_target_pairs={{0,4},{1,5},{2,6},{3,7},{4,0},{5,1},{6,2},{7,3},{8,12},{9,13},{10,... | collective-permute-start | bytes 860168 | tf_op jit(solution)/shard_map/ppermute | solution.py:56
  11.2 28.1 %collective-permute-start = (bf16[4,128]{1,0:T(4,128)(2,1)S(1)}, bf16[4,128]{1,0:T(4,128)(2,1)S(1)}, u32[]{:S(2)}, u32[]{:S(2)}) collective-permute-start(bf16[4,128]{1,0:T(4,128)(2,1)S(1)} %pad_bitcast_fusion), channel_id=1, source_target_pairs={{0,4},{1,5},{2,6},{3,7},{4,0},{5,1},{6,2},{7,3},{8,12},{9,13},{10,... | collective-permute-start | bytes 3080 | tf_op jit(solution)/shard_map/ppermute | solution.py:56
  19.9 14.2 %collective-permute-start.3 = (bf16[2,32,4480]{2,1,0:T(8,128)(2,1)S(1)}, bf16[2,32,4480]{2,1,0:T(8,128)(2,1)S(1)}, u32[]{:S(2)}, u32[]{:S(2)}) collective-permute-start(bf16[2,32,4480]{2,1,0:T(8,128)(2,1)S(1)} %pad_maximum_fusion.4), channel_id=1, source_target_pairs={{0,2},{1,3},{2,0},{3,1},{4,6},{5,7},{6,4},{7,5},{8,10},{9,11},{10,... | collective-permute-start | bytes 1720328 | tf_op jit(solution)/shard_map/ppermute | solution.py:56
  36.1 24.9 %collective-permute-start.5 = (bf16[4,32,4480]{2,1,0:T(8,128)(2,1)}, bf16[4,32,4480]{2,1,0:T(8,128)(2,1)S(1)}, u32[]{:S(2)}, u32[]{:S(2)}) collective-permute-start(bf16[4,32,4480]{2,1,0:T(8,128)(2,1)} %bitcast.17.refs_5_.refs_6_.refs_16_), channel_id=1, source_target_pairs={{0,8},{1,17},{2,10},{3,19},{4,12},{5,21},{6,14},{7,23},{8,0},{9,25... | collective-permute-start | bytes 3440648 | tf_op jit(solution)/shard_map/ppermute | solution.py:56
  41.8 28.7 %collective-permute-start.9 = (bf16[4,32,4480]{2,1,0:T(8,128)(2,1)}, bf16[4,32,4480]{2,1,0:T(8,128)(2,1)}, u32[]{:S(2)}, u32[]{:S(2)}) collective-permute-start(bf16[4,32,4480]{2,1,0:T(8,128)(2,1)} %bitcast.17.refs_5_.refs_6_.refs_16_), channel_id=1, source_target_pairs={{0,16},{1,9},{2,18},{3,11},{4,20},{5,13},{6,22},{7,15},{8,24},{9,1... | collective-permute-start | bytes 3440648 | tf_op jit(solution)/shard_map/ppermute | solution.py:56
  43.4 19.7 %collective-permute-start.14 = (bf16[32,4096]{1,0:T(8,128)(2,1)S(1)}, bf16[32,4096]{1,0:T(8,128)(2,1)S(1)}, u32[]{:S(2)}, u32[]{:S(2)}) collective-permute-start(bf16[32,4096]{1,0:T(8,128)(2,1)S(1)} %copy-done.36), channel_id=1, source_target_pairs={{0,4},{1,5},{2,6},{3,7},{4,0},{5,1},{6,2},{7,3},{8,12},{9,13},{10,... | collective-permute-start | bytes 786440 | tf_op jit(solution)/shard_map/ppermute | solution.py:56
  46.8 20.3 %collective-permute-start.4 = (bf16[2,2,4,128]{3,2,1,0:T(4,128)(2,1)S(1)}, bf16[2,2,4,128]{3,2,1,0:T(4,128)(2,1)S(1)}, u32[]{:S(2)}, u32[]{:S(2)}) collective-permute-start(bf16[2,2,4,128]{3,2,1,0:T(4,128)(2,1)S(1)} %pad_maximum_fusion.18), channel_id=1, source_target_pairs={{0,16},{1,17},{2,18},{3,19},{4,20},{5,21},{6,22},{7,23},{8,24},{9,... | collective-permute-start | bytes 12296 | tf_op jit(solution)/shard_map/ppermute | solution.py:56
  61.0 16.1 %collective-permute-start.7 = (bf16[4,32,4480]{2,1,0:T(8,128)(2,1)S(1)}, bf16[4,32,4480]{2,1,0:T(8,128)(2,1)}, u32[]{:S(2)}, u32[]{:S(2)}) collective-permute-start(bf16[4,32,4480]{2,1,0:T(8,128)(2,1)S(1)} %collective-permute-done.5.refs_6_.refs_7_.refs_17_), channel_id=1, source_target_pairs={{0,16},{1,9},{2,18},{3,11},{4,20},{5,13},{6,22},{7,15},{8,24},{9,1... | collective-permute-start | bytes 3440648 | tf_op jit(solution)/shard_map/ppermute | solution.py:56
  63.9 13.3 %collective-permute-start.15 = (bf16[2,32,4096]{2,1,0:T(8,128)(2,1)}, bf16[2,32,4096]{2,1,0:T(8,128)(2,1)}, u32[]{:S(2)}, u32[]{:S(2)}) collective-permute-start(bf16[2,32,4096]{2,1,0:T(8,128)(2,1)} %pad_maximum_fusion.7), channel_id=1, source_target_pairs={{0,2},{1,3},{2,0},{3,1},{4,6},{5,7},{6,4},{7,5},{8,10},{9,11},{10,... | collective-permute-start | bytes 1572872 | tf_op jit(solution)/shard_map/ppermute | solution.py:56
  70.5 8.6 %collective-permute-start.10 = (bf16[4,32,4480]{2,1,0:T(8,128)(2,1)}, bf16[4,32,4480]{2,1,0:T(8,128)(2,1)S(1)}, u32[]{:S(2)}, u32[]{:S(2)}) collective-permute-start(bf16[4,32,4480]{2,1,0:T(8,128)(2,1)} %bitcast.17.refs_5_.refs_6_.refs_16_), channel_id=1, source_target_pairs={{0,1},{1,0},{2,3},{3,2},{4,5},{5,4},{6,7},{7,6},{8,9},{9,8},{10,11... | collective-permute-start | bytes 3440648 | tf_op jit(solution)/shard_map/ppermute | solution.py:56
  70.5 19.7 %collective-permute-start.11 = (bf16[4,32,4480]{2,1,0:T(8,128)(2,1)S(1)}, bf16[4,32,4480]{2,1,0:T(8,128)(2,1)S(1)}, u32[]{:S(2)}, u32[]{:S(2)}) collective-permute-start(bf16[4,32,4480]{2,1,0:T(8,128)(2,1)S(1)} %collective-permute-done.5.refs_6_.refs_7_.refs_17_), channel_id=1, source_target_pairs={{0,1},{1,0},{2,3},{3,2},{4,5},{5,4},{6,7},{7,6},{8,9},{9,8},{10,11... | collective-permute-start | bytes 3440648 | tf_op jit(solution)/shard_map/ppermute | solution.py:56
  71.0 15.8 %collective-permute-start.12 = (bf16[4,32,4480]{2,1,0:T(8,128)(2,1)}, bf16[4,32,4480]{2,1,0:T(8,128)(2,1)}, u32[]{:S(2)}, u32[]{:S(2)}) collective-permute-start(bf16[4,32,4480]{2,1,0:T(8,128)(2,1)} %collective-permute-done.9.refs_7_.refs_8_.refs_18_), channel_id=1, source_target_pairs={{0,1},{1,0},{2,3},{3,2},{4,5},{5,4},{6,7},{7,6},{8,9},{9,8},{10,11... | collective-permute-start | bytes 3440648 | tf_op jit(solution)/shard_map/ppermute | solution.py:56
  77.2 13.0 %collective-permute-start.13 = (bf16[4,32,4480]{2,1,0:T(8,128)(2,1)}, bf16[4,32,4480]{2,1,0:T(8,128)(2,1)}, u32[]{:S(2)}, u32[]{:S(2)}) collective-permute-start(bf16[4,32,4480]{2,1,0:T(8,128)(2,1)} %collective-permute-done.7.refs_8_.refs_9_.refs_19_), channel_id=1, source_target_pairs={{0,1},{1,0},{2,3},{3,2},{4,5},{5,4},{6,7},{7,6},{8,9},{9,8},{10,11... | collective-permute-start | bytes 3440648 | tf_op jit(solution)/shard_map/ppermute | solution.py:56
  79.1 27.1 %collective-permute-start.16 = (bf16[4,32,4096]{2,1,0:T(8,128)(2,1)S(1)}, bf16[4,32,4096]{2,1,0:T(8,128)(2,1)S(1)}, u32[]{:S(2)}, u32[]{:S(2)}) collective-permute-start(bf16[4,32,4096]{2,1,0:T(8,128)(2,1)S(1)} %bitcast.494), channel_id=1, source_target_pairs={{0,8},{1,17},{2,10},{3,19},{4,12},{5,21},{6,14},{7,23},{8,0},{9,25... | collective-permute-start | bytes 3145736 | tf_op jit(solution)/shard_map/ppermute | solution.py:56
  80.6 25.8 %collective-permute-start.17 = (bf16[4,32,4096]{2,1,0:T(8,128)(2,1)S(1)}, bf16[4,32,4096]{2,1,0:T(8,128)(2,1)S(1)}, u32[]{:S(2)}, u32[]{:S(2)}) collective-permute-start(bf16[4,32,4096]{2,1,0:T(8,128)(2,1)S(1)} %bitcast.495), channel_id=1, source_target_pairs={{0,16},{1,9},{2,18},{3,11},{4,20},{5,13},{6,22},{7,15},{8,24},{9,1... | collective-permute-start | bytes 3145736 | tf_op jit(solution)/shard_map/ppermute | solution.py:56
  86.8 19.5 %collective-permute-start.19 = (bf16[128,1024]{1,0:T(8,128)(2,1)S(1)}, bf16[128,1024]{1,0:T(8,128)(2,1)S(1)}, u32[]{:S(2)}, u32[]{:S(2)}) collective-permute-start(bf16[128,1024]{1,0:T(8,128)(2,1)S(1)} %copy-done.37), channel_id=1, source_target_pairs={{0,4},{1,5},{2,6},{3,7},{4,0},{5,1},{6,2},{7,3},{8,12},{9,13},{10,... | collective-permute-start | bytes 786440 | tf_op jit(solution)/shard_map/ppermute | solution.py:56
  106.2 22.5 %collective-permute-start.18 = (bf16[4,32,4096]{2,1,0:T(8,128)(2,1)S(1)}, bf16[4,32,4096]{2,1,0:T(8,128)(2,1)S(1)}, u32[]{:S(2)}, u32[]{:S(2)}) collective-permute-start(bf16[4,32,4096]{2,1,0:T(8,128)(2,1)S(1)} %collective-permute-done.16.refs_4_.refs_15_), channel_id=1, source_target_pairs={{0,16},{1,9},{2,18},{3,11},{4,20},{5,13},{6,22},{7,15},{8,24},{9,1... | collective-permute-start | bytes 3145736 | tf_op jit(solution)/shard_map/ppermute | solution.py:56
  106.5 22.3 %collective-permute-start.20 = (bf16[2,128,1024]{2,1,0:T(8,128)(2,1)S(1)}, bf16[2,128,1024]{2,1,0:T(8,128)(2,1)S(1)}, u32[]{:S(2)}, u32[]{:S(2)}) collective-permute-start(bf16[2,128,1024]{2,1,0:T(8,128)(2,1)S(1)} %pad_maximum_fusion.8), channel_id=1, source_target_pairs={{0,2},{1,3},{2,0},{3,1},{4,6},{5,7},{6,4},{7,5},{8,10},{9,11},{10,... | collective-permute-start | bytes 1572872 | tf_op jit(solution)/shard_map/ppermute | solution.py:56
  128.2 15.0 %collective-permute-start.23 = (bf16[4,32,4096]{2,1,0:T(8,128)(2,1)}, bf16[4,32,4096]{2,1,0:T(8,128)(2,1)S(1)}, u32[]{:S(2)}, u32[]{:S(2)}) collective-permute-start(bf16[4,32,4096]{2,1,0:T(8,128)(2,1)} %copy-done.5), channel_id=1, source_target_pairs={{0,1},{1,0},{2,3},{3,2},{4,5},{5,4},{6,7},{7,6},{8,9},{9,8},{10,11... | collective-permute-start | bytes 3145736 | tf_op jit(solution)/shard_map/ppermute | solution.py:56
  128.2 15.1 %collective-permute-start.22 = (bf16[4,32,4096]{2,1,0:T(8,128)(2,1)}, bf16[4,32,4096]{2,1,0:T(8,128)(2,1)S(1)}, u32[]{:S(2)}, u32[]{:S(2)}) collective-permute-start(bf16[4,32,4096]{2,1,0:T(8,128)(2,1)} %copy-done.4), channel_id=1, source_target_pairs={{0,1},{1,0},{2,3},{3,2},{4,5},{5,4},{6,7},{7,6},{8,9},{9,8},{10,11... | collective-permute-start | bytes 3145736 | tf_op jit(solution)/shard_map/ppermute | solution.py:56
  128.7 14.6 %collective-permute-start.21 = (bf16[4,32,4096]{2,1,0:T(8,128)(2,1)S(1)}, bf16[4,32,4096]{2,1,0:T(8,128)(2,1)}, u32[]{:S(2)}, u32[]{:S(2)}) collective-permute-start(bf16[4,32,4096]{2,1,0:T(8,128)(2,1)S(1)} %bitcast.496), channel_id=1, source_target_pairs={{0,1},{1,0},{2,3},{3,2},{4,5},{5,4},{6,7},{7,6},{8,9},{9,8},{10,11... | collective-permute-start | bytes 3145736 | tf_op jit(solution)/shard_map/ppermute | solution.py:56
  128.8 14.6 %collective-permute-start.24 = (bf16[4,32,4096]{2,1,0:T(8,128)(2,1)S(1)}, bf16[4,32,4096]{2,1,0:T(8,128)(2,1)}, u32[]{:S(2)}, u32[]{:S(2)}) collective-permute-start(bf16[4,32,4096]{2,1,0:T(8,128)(2,1)S(1)} %collective-permute-done.18.refs_17_.refs_6_), channel_id=1, source_target_pairs={{0,1},{1,0},{2,3},{3,2},{4,5},{5,4},{6,7},{7,6},{8,9},{9,8},{10,11... | collective-permute-start | bytes 3145736 | tf_op jit(solution)/shard_map/ppermute | solution.py:56
  129.7 30.8 %collective-permute-start.25 = (bf16[4,128,1024]{2,1,0:T(8,128)(2,1)S(1)}, bf16[4,128,1024]{2,1,0:T(8,128)(2,1)S(1)}, u32[]{:S(2)}, u32[]{:S(2)}) collective-permute-start(bf16[4,128,1024]{2,1,0:T(8,128)(2,1)S(1)} %bitcast.505), channel_id=1, source_target_pairs={{0,8},{1,17},{2,10},{3,19},{4,12},{5,21},{6,14},{7,23},{8,0},{9,25... | collective-permute-start | bytes 3145736 | tf_op jit(solution)/shard_map/ppermute | solution.py:56
  143.3 19.2 %collective-permute-start.26 = (bf16[4,128,1024]{2,1,0:T(8,128)(2,1)}, bf16[4,128,1024]{2,1,0:T(8,128)(2,1)S(1)}, u32[]{:S(2)}, u32[]{:S(2)}) collective-permute-start(bf16[4,128,1024]{2,1,0:T(8,128)(2,1)} %bitcast.506), channel_id=1, source_target_pairs={{0,16},{1,9},{2,18},{3,11},{4,20},{5,13},{6,22},{7,15},{8,24},{9,1... | collective-permute-start | bytes 3145736 | tf_op jit(solution)/shard_map/ppermute | solution.py:56
  160.6 18.7 %collective-permute-start.27 = (bf16[4,128,1024]{2,1,0:T(8,128)(2,1)S(1)}, bf16[4,128,1024]{2,1,0:T(8,128)(2,1)S(1)}, u32[]{:S(2)}, u32[]{:S(2)}) collective-permute-start(bf16[4,128,1024]{2,1,0:T(8,128)(2,1)S(1)} %collective-permute-done.25.refs_14_.refs_9_), channel_id=1, source_target_pairs={{0,16},{1,9},{2,18},{3,11},{4,20},{5,13},{6,22},{7,15},{8,24},{9,1... | collective-permute-start | bytes 3145736 | tf_op jit(solution)/shard_map/ppermute | solution.py:56
  162.4 17.5 %collective-permute-start.29 = (bf16[4,128,1024]{2,1,0:T(8,128)(2,1)S(1)}, bf16[4,128,1024]{2,1,0:T(8,128)(2,1)S(1)}, u32[]{:S(2)}, u32[]{:S(2)}) collective-permute-start(bf16[4,128,1024]{2,1,0:T(8,128)(2,1)S(1)} %collective-permute-done.25.refs_14_.refs_9_), channel_id=1, source_target_pairs={{0,1},{1,0},{2,3},{3,2},{4,5},{5,4},{6,7},{7,6},{8,9},{9,8},{10,11... | collective-permute-start | bytes 3145736 | tf_op jit(solution)/shard_map/ppermute | solution.py:56
  162.4 17.5 %collective-permute-start.30 = (bf16[4,128,1024]{2,1,0:T(8,128)(2,1)S(1)}, bf16[4,128,1024]{2,1,0:T(8,128)(2,1)S(1)}, u32[]{:S(2)}, u32[]{:S(2)}) collective-permute-start(bf16[4,128,1024]{2,1,0:T(8,128)(2,1)S(1)} %collective-permute-done.26.refs_15_.refs_10_), channel_id=1, source_target_pairs={{0,1},{1,0},{2,3},{3,2},{4,5},{5,4},{6,7},{7,6},{8,9},{9,8},{10,11... | collective-permute-start | bytes 3145736 | tf_op jit(solution)/shard_map/ppermute | solution.py:56
  163.0 17.0 %collective-permute-start.28 = (bf16[4,128,1024]{2,1,0:T(8,128)(2,1)S(1)}, bf16[4,128,1024]{2,1,0:T(8,128)(2,1)S(1)}, u32[]{:S(2)}, u32[]{:S(2)}) collective-permute-start(bf16[4,128,1024]{2,1,0:T(8,128)(2,1)S(1)} %bitcast.508), channel_id=1, source_target_pairs={{0,1},{1,0},{2,3},{3,2},{4,5},{5,4},{6,7},{7,6},{8,9},{9,8},{10,11... | collective-permute-start | bytes 3145736 | tf_op jit(solution)/shard_map/ppermute | solution.py:56
  206.3 5.0 collective-permute-start.33
  208.2 5.6 collective-permute-start.34
  213.8 5.4 collective-permute-start.35
  215.2 5.2 collective-permute-start.36
  216.6 5.5 collective-permute-start.37
  245.9 5.4 collective-permute-start.45
  264.8 9.0 %collective-permute-start.46 = (bf16[4,4,32,384]{3,2,1,0:T(8,128)(2,1)S(1)}, bf16[4,4,32,384]{3,2,1,0:T(8,128)(2,1)S(1)}, u32[]{:S(2)}, u32[]{:S(2)}) collective-permute-start(bf16[4,4,32,384]{3,2,1,0:T(8,128)(2,1)S(1)} %bitcast.524), channel_id=1, source_target_pairs={{0,1},{1,0},{2,3},{3,2},{4,5},{5,4},{6,7},{7,6},{8,9},{9,8},{10,11... | collective-permute-start | bytes 1179656 | tf_op jit(solution)/shard_map/ppermute | solution.py:56
  273.9 5.4 collective-permute-start.47
  275.0 7.0 %collective-permute-start.48 = (bf16[4,32,384]{2,1,0:T(8,128)(2,1)S(1)}, bf16[4,32,384]{2,1,0:T(8,128)(2,1)S(1)}, u32[]{:S(2)}, u32[]{:S(2)}) collective-permute-start(bf16[4,32,384]{2,1,0:T(8,128)(2,1)S(1)} %get-tuple-element.289), channel_id=1, source_target_pairs={{0,16},{1,17},{2,18},{3,19},{4,20},{5,21},{6,22},{7,23},{8,24},{9,... | collective-permute-start | bytes 294920 | tf_op jit(solution)/shard_map/ppermute | solution.py:56
  275.5 6.5 %collective-permute-start.49 = (bf16[4,32,384]{2,1,0:T(8,128)(2,1)S(1)}, bf16[4,32,384]{2,1,0:T(8,128)(2,1)S(1)}, u32[]{:S(2)}, u32[]{:S(2)}) collective-permute-start(bf16[4,32,384]{2,1,0:T(8,128)(2,1)S(1)} %get-tuple-element.288), channel_id=1, source_target_pairs={{0,24},{1,25},{2,26},{3,27},{4,28},{5,29},{6,30},{7,31},{8,16},{9,... | collective-permute-start | bytes 294920 | tf_op jit(solution)/shard_map/ppermute | solution.py:56
  282.2 4.8 collective-permute-start.51
  285.0 5.6 collective-permute-start.52
  305.3 14.9 %collective-permute-start.53 = (bf16[4,4,128,1024]{3,2,1,0:T(8,128)(2,1)}, bf16[4,4,128,1024]{3,2,1,0:T(8,128)(2,1)S(1)}, u32[]{:S(2)}, u32[]{:S(2)}) collective-permute-start(bf16[4,4,128,1024]{3,2,1,0:T(8,128)(2,1)} %grad_down_sib.1.refs_3_), channel_id=1, source_target_pairs={{0,1},{1,0},{2,3},{3,2},{4,5},{5,4},{6,7},{7,6},{8,9},{9,8},{10,11... | collective-permute-start | bytes 12582920 | tf_op jit(solution)/shard_map/ppermute | solution.py:56
  346.1 31.3 %collective-permute-start.54 = (f32[4,4,32,4096]{3,2,1,0:T(8,128)}, f32[4,4,32,4096]{3,2,1,0:T(8,128)}, u32[]{:S(2)}, u32[]{:S(2)}) collective-permute-start(f32[4,4,32,4096]{3,2,1,0:T(8,128)} %grad_up_sib.1.refs_7_), channel_id=1, source_target_pairs={{0,1},{1,0},{2,3},{3,2},{4,5},{5,4},{6,7},{7,6},{8,9},{9,8},{10,11... | collective-permute-start | bytes 25165832 | tf_op jit(solution)/shard_map/ppermute | solution.py:56
  346.6 26.1 %collective-permute-start.55 = (bf16[8,128,1024]{2,1,0:T(8,128)(2,1)S(1)}, bf16[8,128,1024]{2,1,0:T(8,128)(2,1)}, u32[]{:S(2)}, u32[]{:S(2)}) collective-permute-start(bf16[8,128,1024]{2,1,0:T(8,128)(2,1)S(1)} %bitcast.517), channel_id=1, source_target_pairs={{0,16},{1,9},{2,18},{3,11},{4,20},{5,13},{6,22},{7,15},{8,24},{9,1... | collective-permute-start | bytes 6291464 | tf_op jit(solution)/shard_map/ppermute | solution.py:56
  375.1 16.9 %collective-permute-start.56 = (bf16[4,128,1024]{2,1,0:T(8,128)(2,1)S(1)}, bf16[4,128,1024]{2,1,0:T(8,128)(2,1)}, u32[]{:S(2)}, u32[]{:S(2)}) collective-permute-start(bf16[4,128,1024]{2,1,0:T(8,128)(2,1)S(1)} %get-tuple-element.262.refs_5_), channel_id=1, source_target_pairs={{0,8},{1,17},{2,10},{3,19},{4,12},{5,21},{6,14},{7,23},{8,0},{9,25... | collective-permute-start | bytes 3145736 | tf_op jit(solution)/shard_map/ppermute | solution.py:56
  390.7 35.5 %collective-permute-start.59 = (bf16[8,32,4096]{2,1,0:T(8,128)(2,1)}, bf16[8,32,4096]{2,1,0:T(8,128)(2,1)S(1)}, u32[]{:S(2)}, u32[]{:S(2)}) collective-permute-start(bf16[8,32,4096]{2,1,0:T(8,128)(2,1)} %bitcast.518), channel_id=1, source_target_pairs={{0,16},{1,9},{2,18},{3,11},{4,20},{5,13},{6,22},{7,15},{8,24},{9,1... | collective-permute-start | bytes 6291464 | tf_op jit(solution)/shard_map/ppermute | solution.py:56
  393.2 31.4 %collective-permute-start.58 = (bf16[2,128,1024]{2,1,0:T(8,128)(2,1)S(1)}, bf16[2,128,1024]{2,1,0:T(8,128)(2,1)S(1)}, u32[]{:S(2)}, u32[]{:S(2)}) collective-permute-start(bf16[2,128,1024]{2,1,0:T(8,128)(2,1)S(1)} %fusion.8.refs_8_), channel_id=1, source_target_pairs={{0,2},{1,3},{2,0},{3,1},{4,6},{5,7},{6,4},{7,5},{8,10},{9,11},{10,... | collective-permute-start | bytes 1572872 | tf_op jit(solution)/shard_map/ppermute | solution.py:56
  401.2 37.2 %collective-permute-start.57 = (bf16[4,4,32,1408]{3,2,1,0:T(8,128)(2,1)}, bf16[4,4,32,1408]{3,2,1,0:T(8,128)(2,1)S(1)}, u32[]{:S(2)}, u32[]{:S(2)}) collective-permute-start(bf16[4,4,32,1408]{3,2,1,0:T(8,128)(2,1)} %grad_out_sib.1.refs_7_), channel_id=1, source_target_pairs={{0,1},{1,0},{2,3},{3,2},{4,5},{5,4},{6,7},{7,6},{8,9},{9,8},{10,11... | collective-permute-start | bytes 4325384 | tf_op jit(solution)/shard_map/ppermute | solution.py:56
  424.7 47.3 %collective-permute-start.60 = (f32[1,128,1024]{2,1,0:T(8,128)S(1)}, f32[1,128,1024]{2,1,0:T(8,128)}, u32[]{:S(2)}, u32[]{:S(2)}) collective-permute-start(f32[1,128,1024]{2,1,0:T(8,128)S(1)} %bitcast_add_fusion.15.refs_3_.refs_8_), channel_id=1, source_target_pairs={{0,4},{1,5},{2,6},{3,7},{4,0},{5,1},{6,2},{7,3},{8,12},{9,13},{10,... | collective-permute-start | bytes 1572872 | tf_op jit(solution)/shard_map/ppermute | solution.py:56
  430.9 55.5 %collective-permute-start.64 = (bf16[4,32,4096]{2,1,0:T(8,128)(2,1)S(1)}, bf16[4,32,4096]{2,1,0:T(8,128)(2,1)}, u32[]{:S(2)}, u32[]{:S(2)}) collective-permute-start(bf16[4,32,4096]{2,1,0:T(8,128)(2,1)S(1)} %get-tuple-element.260.refs_4_.refs_9_), channel_id=1, source_target_pairs={{0,8},{1,17},{2,10},{3,19},{4,12},{5,21},{6,14},{7,23},{8,0},{9,25... | collective-permute-start | bytes 3145736 | tf_op jit(solution)/shard_map/ppermute | solution.py:56
  469.7 11.6 %collective-permute-start.63 = (bf16[8,32,1408]{2,1,0:T(8,128)(2,1)}, bf16[8,32,1408]{2,1,0:T(8,128)(2,1)}, u32[]{:S(2)}, u32[]{:S(2)}) collective-permute-start(bf16[8,32,1408]{2,1,0:T(8,128)(2,1)} %bitcast.73.refs_7_), channel_id=1, source_target_pairs={{0,16},{1,9},{2,18},{3,11},{4,20},{5,13},{6,22},{7,15},{8,24},{9,1... | collective-permute-start | bytes 2162696 | tf_op jit(solution)/shard_map/ppermute | solution.py:56
  470.5 18.5 %collective-permute-start.62 = (bf16[4,4,32,1536]{3,2,1,0:T(8,128)(2,1)S(1)}, bf16[4,4,32,1536]{3,2,1,0:T(8,128)(2,1)S(1)}, u32[]{:S(2)}, u32[]{:S(2)}) collective-permute-start(bf16[4,4,32,1536]{3,2,1,0:T(8,128)(2,1)S(1)} %copy-done.3), channel_id=1, source_target_pairs={{0,1},{1,0},{2,3},{3,2},{4,5},{5,4},{6,7},{7,6},{8,9},{9,8},{10,11... | collective-permute-start | bytes 4718600 | tf_op jit(solution)/shard_map/ppermute | solution.py:56
  480.0 26.4 %collective-permute-start.61 = (bf16[4,4,32,1536]{3,2,1,0:T(8,128)(2,1)}, bf16[4,4,32,1536]{3,2,1,0:T(8,128)(2,1)}, u32[]{:S(2)}, u32[]{:S(2)}) collective-permute-start(bf16[4,4,32,1536]{3,2,1,0:T(8,128)(2,1)} %grad_qkv_sib.3.refs_4_), channel_id=1, source_target_pairs={{0,1},{1,0},{2,3},{3,2},{4,5},{5,4},{6,7},{7,6},{8,9},{9,8},{10,11... | collective-permute-start | bytes 4718600 | tf_op jit(solution)/shard_map/ppermute | solution.py:56
  483.7 16.4 %collective-permute-start.65 = (bf16[4,32,1408]{2,1,0:T(8,128)(2,1)}, bf16[4,32,1408]{2,1,0:T(8,128)(2,1)}, u32[]{:S(2)}, u32[]{:S(2)}) collective-permute-start(bf16[4,32,1408]{2,1,0:T(8,128)(2,1)} %get-tuple-element.268.refs_5_), channel_id=1, source_target_pairs={{0,8},{1,17},{2,10},{3,19},{4,12},{5,21},{6,14},{7,23},{8,0},{9,25... | collective-permute-start | bytes 1081352 | tf_op jit(solution)/shard_map/ppermute | solution.py:56
  487.7 12.5 %collective-permute-start.66 = (bf16[2,32,4096]{2,1,0:T(8,128)(2,1)S(1)}, bf16[2,32,4096]{2,1,0:T(8,128)(2,1)S(1)}, u32[]{:S(2)}, u32[]{:S(2)}) collective-permute-start(bf16[2,32,4096]{2,1,0:T(8,128)(2,1)S(1)} %fusion.9.refs_6_), channel_id=1, source_target_pairs={{0,2},{1,3},{2,0},{3,1},{4,6},{5,7},{6,4},{7,5},{8,10},{9,11},{10,... | collective-permute-start | bytes 1572872 | tf_op jit(solution)/shard_map/ppermute | solution.py:56
  496.7 18.8 %collective-permute-start.67 = (bf16[8,32,1536]{2,1,0:T(8,128)(2,1)}, bf16[8,32,1536]{2,1,0:T(8,128)(2,1)S(1)}, u32[]{:S(2)}, u32[]{:S(2)}) collective-permute-start(bf16[8,32,1536]{2,1,0:T(8,128)(2,1)} %bitcast.522), channel_id=1, source_target_pairs={{0,16},{1,9},{2,18},{3,11},{4,20},{5,13},{6,22},{7,15},{8,24},{9,1... | collective-permute-start | bytes 2359304 | tf_op jit(solution)/shard_map/ppermute | solution.py:56
  501.9 12.3 %collective-permute-start.68 = (bf16[2,32,1408]{2,1,0:T(8,128)(2,1)S(1)}, bf16[2,32,1408]{2,1,0:T(8,128)(2,1)S(1)}, u32[]{:S(2)}, u32[]{:S(2)}) collective-permute-start(bf16[2,32,1408]{2,1,0:T(8,128)(2,1)S(1)} %fusion.34.refs_5_), channel_id=1, source_target_pairs={{0,2},{1,3},{2,0},{3,1},{4,6},{5,7},{6,4},{7,5},{8,10},{9,11},{10,... | collective-permute-start | bytes 540680 | tf_op jit(solution)/shard_map/ppermute | solution.py:56
  503.4 27.0 %collective-permute-start.72 = (bf16[1,32,4096]{2,1,0:T(8,128)(2,1)S(1)}, bf16[1,32,4096]{2,1,0:T(8,128)(2,1)S(1)}, u32[]{:S(2)}, u32[]{:S(2)}) collective-permute-start(bf16[1,32,4096]{2,1,0:T(8,128)(2,1)S(1)} %fusion.12.refs_6_), channel_id=1, source_target_pairs={{0,4},{1,5},{2,6},{3,7},{4,0},{5,1},{6,2},{7,3},{8,12},{9,13},{10,... | collective-permute-start | bytes 786440 | tf_op jit(solution)/shard_map/ppermute | solution.py:56
  512.9 18.3 %collective-permute-start.70 = (bf16[8,32,1536]{2,1,0:T(8,128)(2,1)}, bf16[8,32,1536]{2,1,0:T(8,128)(2,1)S(1)}, u32[]{:S(2)}, u32[]{:S(2)}) collective-permute-start(bf16[8,32,1536]{2,1,0:T(8,128)(2,1)} %bitcast.541), channel_id=1, source_target_pairs={{0,16},{1,9},{2,18},{3,11},{4,20},{5,13},{6,22},{7,15},{8,24},{9,1... | collective-permute-start | bytes 2359304 | tf_op jit(solution)/shard_map/ppermute | solution.py:56
  514.2 15.4 %collective-permute-start.73 = (f32[1,32,1408]{2,1,0:T(8,128)S(1)}, f32[1,32,1408]{2,1,0:T(8,128)S(1)}, u32[]{:S(2)}, u32[]{:S(2)}) collective-permute-start(f32[1,32,1408]{2,1,0:T(8,128)S(1)} %bitcast_add_fusion.22.refs_6_), channel_id=1, source_target_pairs={{0,4},{1,5},{2,6},{3,7},{4,0},{5,1},{6,2},{7,3},{8,12},{9,13},{10,... | collective-permute-start | bytes 540680 | tf_op jit(solution)/shard_map/ppermute | solution.py:56
  515.7 23.6 %collective-permute-start.69 = (bf16[4,32,1536]{2,1,0:T(8,128)(2,1)S(1)}, bf16[4,32,1536]{2,1,0:T(8,128)(2,1)S(1)}, u32[]{:S(2)}, u32[]{:S(2)}) collective-permute-start(bf16[4,32,1536]{2,1,0:T(8,128)(2,1)S(1)} %get-tuple-element.266.refs_5_), channel_id=1, source_target_pairs={{0,8},{1,17},{2,10},{3,19},{4,12},{5,21},{6,14},{7,23},{8,0},{9,25... | collective-permute-start | bytes 1179656 | tf_op jit(solution)/shard_map/ppermute | solution.py:56
  531.4 7.8 %collective-permute-start.71 = (bf16[4,32,1536]{2,1,0:T(8,128)(2,1)S(1)}, bf16[4,32,1536]{2,1,0:T(8,128)(2,1)S(1)}, u32[]{:S(2)}, u32[]{:S(2)}) collective-permute-start(bf16[4,32,1536]{2,1,0:T(8,128)(2,1)S(1)} %get-tuple-element.263.refs_8_), channel_id=1, source_target_pairs={{0,8},{1,17},{2,10},{3,19},{4,12},{5,21},{6,14},{7,23},{8,0},{9,25... | collective-permute-start | bytes 1179656 | tf_op jit(solution)/shard_map/ppermute | solution.py:56
  540.2 10.2 %collective-permute-start.74 = (bf16[2,32,3072]{2,1,0:T(8,128)(2,1)S(1)}, bf16[2,32,3072]{2,1,0:T(8,128)(2,1)S(1)}, u32[]{:S(2)}, u32[]{:S(2)}) collective-permute-start(bf16[2,32,3072]{2,1,0:T(8,128)(2,1)S(1)} %pad_maximum_fusion.10), channel_id=1, source_target_pairs={{0,2},{1,3},{2,0},{3,1},{4,6},{5,7},{6,4},{7,5},{8,10},{9,11},{10,... | collective-permute-start | bytes 1179656 | tf_op jit(solution)/shard_map/ppermute | solution.py:56
  554.1 4.9 collective-permute-start.80
  558.4 8.5 %collective-permute-start.75 = (bf16[1,32,3072]{2,1,0:T(8,128)(2,1)S(1)}, bf16[1,32,3072]{2,1,0:T(8,128)(2,1)S(1)}, u32[]{:S(2)}, u32[]{:S(2)}) collective-permute-start(bf16[1,32,3072]{2,1,0:T(8,128)(2,1)S(1)} %fusion.18), channel_id=1, source_target_pairs={{0,4},{1,5},{2,6},{3,7},{4,0},{5,1},{6,2},{7,3},{8,12},{9,13},{10,... | collective-permute-start | bytes 589832 | tf_op jit(solution)/shard_map/ppermute | solution.py:56
  (70 other events, 420.3 us)

commit v6 on v5

--- a/solution.py
+++ b/solution.py
@@ -244,17 +244,17 @@
     return jnp.stack([held, exchange(held, swap_core=True)])
 
 
-def scatter_relative(blocks, dtype, use=()):
+def scatter_relative(keep, send, use=()):
     n_rows, n_z, _, _ = sizes()
-
-    def step(held, count, move, use=()):
-        parts = [after(exchange(held[m].astype(dtype), **move(m)), *use) for m in range(1, count)]
+    held = keep + after(exchange(send, swap_core=True), *use).astype(f32)
+
+    def step(held, count, move):
+        parts = [exchange(held[m].astype(send.dtype), **move(m)) for m in range(1, count)]
         total = held[0]
         for part in parts:
             total = total + part.astype(f32)
         return total
 
-    held = step(blocks, 2, lambda m: dict(swap_core=True), use)
     held = step(held, n_rows, lambda m: dict(row_masks=(m, m)))
     return step(held, n_z, lambda m: dict(z_mask=m))
 
@@ -1240,7 +1240,8 @@
 
 
 def score_grad_kernel(
-    doc_ref, query_ref, id_ref, index_ref, sum_ref, score_ref, stat_ref, pos_ref, dq_ref, dd_ref
+    doc_ref, query_ref, id_ref, index_ref, sum_ref, score_ref, stat_ref, pos_ref,
+    keep_ref, send_ref, dd_ref, dq_ref,
 ):
     docs = doc_ref[...]
     n_queries = score_ref.shape[2]
@@ -1265,6 +1266,9 @@
             back = (e * wide).astype(bf16)
             dd_ref[:, lanes] += jnp.where(mask, contract(back, queries, 1, 0), 0.0)
             dq_ref[at : at + SCORE_TILE, lanes] += contract(back, picked, 0, 0)
+    half = keep_ref.shape[0]
+    keep_ref[...] = dq_ref[:half, :]
+    send_ref[...] = dq_ref[half:, :].astype(send_ref.dtype)
 
 
 def score_stats(docs, queries, ids, hot, counts, positive, wait=()):
@@ -1317,10 +1321,11 @@
             whole_spec((3, 3, n_queries)),
             whole_spec((8, n_queries)),
         ],
-        [whole_spec((n_tokens, e)), whole_spec((n, e))],
-        [like((n_tokens, e), f32), like((n, e), f32)],
+        [whole_spec((n_tokens // 2, e)), whole_spec((n_tokens // 2, e)), whole_spec((n, e))],
+        [like((n_tokens // 2, e), f32), like((n_tokens // 2, e), bf16), like((n, e), f32)],
         24 * n * n_tokens * e,
         10**6,
+        [pltpu.VMEM((n_tokens, e), f32)],
         wait=wait,
     )(docs, queries, ids, index, sums, scores, stats, positive)
 
@@ -1469,13 +1474,12 @@
     losses = lax.dynamic_slice_in_dim(
         stats[:, 0] + jnp.log(stats[:, 1]) - stats[:, 2], row * query_count, query_count, 1
     )
-    query_grads, doc_grads = score_grads(
+    query_keep, query_send, doc_grads = score_grads(
         vecs, query_all, query_row, doc_column, sums, doc_scores, stats, positive
     )
     doc_part = head_back(doc_grads, raw, full_proj, hat2, rstd2, gain_two)
-    query_grad = scatter_relative(
-        query_grads.reshape(2, n_rows, n_z, q_tokens, -1), bf16, [doc_part[2]]
-    )
+    blocks = lambda x: x.reshape(n_rows, n_z, q_tokens, -1)
+    query_grad = scatter_relative(blocks(query_keep), blocks(query_send), [doc_part[2]])
     resid_two_grad, branch_grad, raw_grad, sums2 = head_back(
         doc_grads, raw, full_proj, hat2, rstd2, gain_two, query_grad, doc_part[:3]
     )
@@ -1550,7 +1554,7 @@
     sum_out, sum_proj = sum_out[:, :D], sum_out[:, D : D + w_proj.shape[1]]
     q4 = qkv_a.step()
     small = scatter_small(
-        small.reshape(n_devices, -1, LANES), f32, [[], [q3], [q3], [q4], [q4]]
+        small.reshape(n_devices, -1, LANES), f32, [[], [q3], [q3], [q3], [q4]]
     ).reshape(-1)
     sum_qkv = qkv_a.finish()
     width = D // 2

time: 574 us -> 569 us (level)
    unnamed x118 -> x120, local copies, waits for them, and re-layouts: 12.7 us -> 12.4 us
  transfers between devices with their start and end apart: 81 -> 81, of which waited for: 30 -> 28; matrix products, arithmetic and copies ran while one was open for 9% -> 9% of each run, Pallas kernels for 42% -> 42%
where the time goes in v6:
time: 569 us; the launch traced here: 564 us
  Pallas kernels  320 us (56%)
  starting transfers between devices  96.6 us (17%)
  waiting for transfers between devices  78.3 us (14%)
  other arithmetic  38.8 us (7%)
  local copies, waits for them, and re-layouts  27.8 us (5%)
    pallas_call x28, Pallas kernels, call(): return lambda *operands: run(*operands, *wait)  320 us
    ppermute x81, starting transfers between devices, exchange(): return lax.ppermute(value, AXES, pairs)  96.6 us
    ppermute x81, waiting for transfers between devices, exchange(): return lax.ppermute(value, AXES, pairs)  78.3 us
    unnamed x120, local copies, waits for them, and re-layouts  12.4 us
    add x9, other arithmetic, step(): pick(parts[0], other) + pick(parts[1], other).astype(f32)  11.7 us
  transfers between devices with their start and end apart: 81, of which 28 were waited for; matrix products, arithmetic and copies ran while one was open for 9% of the time, Pallas kernels for 42%

profile of v6, /device:TPU:0, one launch (start us, length us, event | category | flops | bytes accessed | tf_op | source)
XLA Modules:
  0.0 564.0 jit_solution(10833027486863998832)
XLA Ops:
  1.7 4.1 collective-permute-start.1
  5.8 5.4 concatenate.32
  15.1 3.7 collective-permute-done.1
  22.2 12.0 %collective-permute-done.3 = bf16[2,32,4480]{2,1,0:T(8,128)(2,1)S(1)} collective-permute-done((bf16[2,32,4480]{2,1,0:T(8,128)(2,1)S(1)}, bf16[2,32,4480]{2,1,0:T(8,128)(2,1)S(1)}, u32[]{:S(2)}, u32[]{:S(2)}) %collective-permute-start.3) | collective-permute-done | bytes 573472 | tf_op jit(solution)/shard_map/ppermute | solution.py:56
  43.4 3.4 collective-permute-start.14
  47.9 5.4 halves.1
  53.4 7.6 %collective-permute-done.5.refs_6_.refs_7_.refs_17_ = bf16[4,32,4480]{2,1,0:T(8,128)(2,1)S(1)} collective-permute-done((bf16[4,32,4480]{2,1,0:T(8,128)(2,1)}, bf16[4,32,4480]{2,1,0:T(8,128)(2,1)S(1)}, u32[]{:S(2)}, u32[]{:S(2)}) %collective-permute-start.5) | collective-permute-done | bytes 1146912 | tf_op jit(solution)/shard_map/ppermute | solution.py:56
  61.0 2.0 collective-permute-start.7
  64.0 3.1 collective-permute-start.15
  71.1 6.1 %collective-permute-start.12 = (bf16[4,32,4480]{2,1,0:T(8,128)(2,1)}, bf16[4,32,4480]{2,1,0:T(8,128)(2,1)}, u32[]{:S(2)}, u32[]{:S(2)}) collective-permute-start(bf16[4,32,4480]{2,1,0:T(8,128)(2,1)} %collective-permute-done.9.refs_7_.refs_8_.refs_18_), channel_id=1, source_target_pairs={{0,1},{1,0},{2,3},{3,2},{4,5},{5,4},{6,7},{7,6},{8,9},{9,8},{10,11... | collective-permute-start | bytes 3440648 | tf_op jit(solution)/shard_map/ppermute | solution.py:56
  80.6 2.0 collective-permute-start.17
  84.5 2.3 unpack.1
  86.9 3.4 collective-permute-start.19
  91.2 14.9 %project_qkv.1 = (bf16[1024,3072]{1,0:T(8,128)(2,1)}, bf16[4,4,2,32,3072]{4,3,2,1,0:T(8,128)(2,1)}) custom-call(s32[17]{0:T(128)} %concatenate.30.refs_0_, bf16[1024,1024]{1,0:T(8,128)(2,1)} %refs_3_.1, f32[1,3072]{1,0:T(1,128)} %get-tuple-element.139.refs_2_, f32[1024,128]{1,0:T(8,128)} %get-tuple-element.352.refs_3_.refs_5_, ...), custom_call_target="tpu_custom_call" | custom-call | flops 6442450944 | bytes 20971520 | tf_op jit(solution)/shard_map/project_qkv/pallas_call | solution.py:368
  106.5 3.2 collective-permute-start.20
  109.7 18.5 %attention.1.refs_1_ = bf16[1024,1024]{1,0:T(8,128)(2,1)} custom-call(s32[9]{0:T(128)} %pad_add_fusion.refs_0_, bf16[1024,3072]{1,0:T(8,128)(2,1)} %get-tuple-element.141.refs_1_.refs_2_.refs_3_, bf16[1024,3072]{1,0:T(8,128)(2,1)} %get-tuple-element.141.refs_1_.refs_2_.refs_3_, bf16[1024,3072]{1,0:T(8,128)(2,1)} %get-tuple-element.141.refs_1_.refs_2_.refs_3_, ...), custom_call_target="tpu_custom_call" | custom-call | flops 20000000000 | bytes 8388608 | tf_op jit(solution)/shard_map/attention/pallas_call | solution.py:368
  131.3 9.8 %out_norm.1 = (f32[1024,1024]{1,0:T(8,128)}, f32[1024,128]{1,0:T(8,128)}, bf16[1024,1024]{1,0:T(8,128)(2,1)}, bf16[4,4,2,32,1024]{4,3,2,1,0:T(8,128)(2,1)}) custom-call(s32[17]{0:T(128)} %concatenate.30.refs_0_, bf16[1024,1024]{1,0:T(8,128)(2,1)} %attention.1.refs_1_, f32[1,1024]{1,0:T(1,128)} %get-tuple-element.147.refs_2_, bf16[1024,1024]{1,0:T(8,128)(2,1)} %refs_3_.1, ...), custom_call_target="tpu_custom_call" | custom-call | flops 2147483648 | bytes 12582912 | tf_op jit(solution)/shard_map/out_norm/pallas_call | solution.py:368
  143.3 15.9 %up_gelu.2 = (bf16[1024,4096]{1,0:T(8,128)(2,1)}, bf16[1024,4096]{1,0:T(8,128)(2,1)}, bf16[4,4,2,32,4096]{4,3,2,1,0:T(8,128)(2,1)}) custom-call(s32[17]{0:T(128)} %concatenate.30.refs_0_, bf16[1024,1024]{1,0:T(8,128)(2,1)} %get-tuple-element.156.refs_1_, f32[1,4096]{1,0:T(1,128)} %get-tuple-element.157.refs_2_, bf16[4,32,4096]{2,1,0:T(8,128)(2,1)} %bitcast.498, ...), custom_call_target="tpu_custom_call" | custom-call | flops 4294967296 | bytes 12582912 | tf_op jit(solution)/shard_map/up_gelu/pallas_call | solution.py:368
  161.2 15.9 %up_gelu.3 = (bf16[1024,4096]{1,0:T(8,128)(2,1)}, bf16[1024,4096]{1,0:T(8,128)(2,1)}, bf16[4,4,2,32,4096]{4,3,2,1,0:T(8,128)(2,1)}) custom-call(s32[17]{0:T(128)} %concatenate.30.refs_0_, bf16[1024,1024]{1,0:T(8,128)(2,1)} %get-tuple-element.156.refs_1_, ...), custom_call_target="tpu_custom_call", output_to_operand_aliasing={{0}: (11, {}), {1}: (12, {}), {2}: (13, {})} | custom-call | flops 4294967296 | bytes 12582912 | tf_op jit(solution)/shard_map/up_gelu/pallas_call | solution.py:368
  177.8 2.2 collective-permute-done.31.refs_15_
  181.0 21.8 %down_norm.1 = (f32[1024,1024]{1,0:T(8,128)}, f32[1024,128]{1,0:T(8,128)}, bf16[1024,1024]{1,0:T(8,128)(2,1)}, f32[1024,384]{1,0:T(8,128)}, bf16[1024,384]{1,0:T...) custom-call(s32[17]{0:T(128)} %concatenate.30.refs_0_, ...), custom_call_target="tpu_custom_call" | custom-call | flops 8589934592 | bytes 20971520 | tf_op jit(solution)/shard_map/down_norm/pallas_call | solution.py:368
  203.6 2.0 collective-permute-start.32
  205.6 3.6 collective-permute-start.33
  211.1 3.7 collective-permute-done.34
  216.3 2.1 collective-permute-start.37
  224.6 10.1 %scores.1 = (f32[3,8,1024]{2,1,0:T(8,128)}, f32[3,8,32]{2,1,0:T(8,128)}, f32[3,3,32]{2,1,0:T(4,128)}) custom-call(bf16[1024,384]{1,0:T(8,128)(2,1)} %get-tuple-element.180.refs_0_, bf16[1024,384]{1,0:T(8,128)(2,1)} %bitcast.519, s32[1024,1]{1,0:T(8,128)} %copy.110.refs_2_, bf16[8,1024]{1,0:T(8,128)(2,1)} %fusion.41.refs_3_, ...), custom_call_target="tpu_custom_call" | custom-call | flops 4831838208 | bytes 1000000 | tf_op jit(solution)/shard_map/scores/pallas_call | solution.py:368
  241.9 2.4 collective-permute-done.42
  245.2 3.6 collective-permute-start.45
  251.2 11.3 %score_grads.1 = (f32[512,384]{1,0:T(8,128)}, bf16[512,384]{1,0:T(8,128)(2,1)}, f32[1024,384]{1,0:T(8,128)}) custom-call(bf16[1024,384]{1,0:T(8,128)(2,1)} %get-tuple-element.180.refs_0_, bf16[1024,384]{1,0:T(8,128)(2,1)} %bitcast.520, s32[1,1024]{1,0:T(1,128)} %add.562.refs_2_, s32[1024,1]{1,0:T(8,128)} %fusion.15.refs_3_, ...), custom_call_target="tpu_custom_call" | custom-call | flops 9663676416 | bytes 1000000 | tf_op jit(solution)/shard_map/score_grads/pallas_call | solution.py:368
  262.6 7.8 %head_back.2 = (f32[1024,1024]{1,0:T(8,128)}, bf16[1024,1024]{1,0:T(8,128)(2,1)}, bf16[1024,384]{1,0:T(8,128)(2,1)}, f32[3,1024]{1,0:T(4,128)}) custom-call(f32[1024,384]{1,0:T(8,128)} %get-tuple-element.185.refs_0_, f32[1024,384]{1,0:T(8,128)} %get-tuple-element.186.refs_1_, bf16[1024,384]{1,0:T(8,128)(2,1)} %bitcast.509, ...), custom_call_target="tpu_custom_call" | custom-call | flops 603979776 | bytes 12582912 | tf_op jit(solution)/shard_map/head_back/pallas_call | solution.py:368
  275.9 2.8 collective-permute-done.48
  279.1 3.8 collective-permute-start.51
  284.7 3.8 collective-permute-done.52
  289.2 4.0 head_back.3
  293.2 10.0 %grad_down_sib.1.refs_3_ = bf16[4,4,128,1024]{3,2,1,0:T(8,128)(2,1)} custom-call(s32[17]{0:T(128)} %concatenate.30.refs_0_, bf16[1024,4096]{1,0:T(8,128)(2,1)} %get-tuple-element.168.refs_1_, bf16[1024,1024]{1,0:T(8,128)(2,1)} %get-tuple-element.196.refs_2_.refs_0_), custom_call_target="tpu_custom_call" | custom-call | flops 4294967296 | bytes 23068672 | tf_op jit(solution)/shard_map/grad_down_sib/pallas_call | solution.py:368
  303.2 14.9 %act_back.1 = (bf16[1024,4096]{1,0:T(8,128)(2,1)}, f32[1,4096]{1,0:T(1,128)}) custom-call(bf16[1024,1024]{1,0:T(8,128)(2,1)} %get-tuple-element.196.refs_2_.refs_0_, bf16[4096,1024]{1,0:T(8,128)(2,1)} %bitcast.543, bf16[1024,4096]{1,0:T(8,128)(2,1)} %get-tuple-element.198.refs_2_, bf16[4,4,128,1024]{3,2,1,0:T(8,128)(2,1)} %grad_down_sib.1.refs_3_), custom_call_target="tpu_custom_call" | custom-call | flops 8589934592 | bytes 25165824 | tf_op jit(solution)/shard_map/act_back/pallas_call | solution.py:368
  320.1 11.9 %grad_down.1 = (bf16[2,4,128,1024]{3,2,1,0:T(8,128)(2,1)}, f32[2,4,128,1024]{3,2,1,0:T(8,128)}) custom-call(s32[17]{0:T(128)} %concatenate.30.refs_0_, bf16[1024,4096]{1,0:T(8,128)(2,1)} %get-tuple-element.168.refs_1_, bf16[1024,1024]{1,0:T(8,128)(2,1)} %get-tuple-element.196.refs_2_.refs_0_, bf16[4,4,128,1024]{3,2,1,0:T(8,128)(2,1)} %copy-done.48, ...), custom_call_target="tpu_custom_call" | custom-call | flops 4294967296 | bytes 23068672 | tf_op jit(solution)/shard_map/grad_down/pallas_call | solution.py:368
  331.9 12.0 %grad_up_sib.1.refs_7_ = f32[4,4,32,4096]{3,2,1,0:T(8,128)} custom-call(s32[17]{0:T(128)} %concatenate.30.refs_0_, bf16[1024,1024]{1,0:T(8,128)(2,1)} %get-tuple-element.156.refs_1_, bf16[1024,4096]{1,0:T(8,128)(2,1)} %get-tuple-element.199.refs_2_.refs_0_, bf16[8,128,1024]{2,1,0:T(8,128)(2,1)} %bitcast.515), custom_call_target="tpu_custom_call" | custom-call | flops 4294967296 | bytes 23068672 | tf_op jit(solution)/shard_map/grad_up_sib/pallas_call | solution.py:368
  345.1 20.5 %hidden_back.1 = (f32[1024,1024]{1,0:T(8,128)}, bf16[1024,1024]{1,0:T(8,128)(2,1)}, bf16[1024,1024]{1,0:T(8,128)(2,1)}, f32[3,1024]{1,0:T(4,128)}) custom-call(bf16[1024,4096]{1,0:T(8,128)(2,1)} %get-tuple-element.199.refs_2_.refs_0_, bf16[1024,4096]{1,0:T(8,128)(2,1)} %bitcast.504, f32[1024,1024]{1,0:T(8,128)} %get-tuple-element.201.refs_2_, ...), custom_call_target="tpu_custom_call" | custom-call | flops 10737418240 | bytes 33554432 | tf_op jit(solution)/shard_map/hidden_back/pallas_call | solution.py:368
  365.6 4.9 collective-permute-done.55
  370.6 2.4 bitcast_add_fusion.2
  375.2 13.3 %grad_up.1 = (bf16[2,4,32,4096]{3,2,1,0:T(8,128)(2,1)}, f32[2,4,32,4096]{3,2,1,0:T(8,128)}) custom-call(s32[17]{0:T(128)} %concatenate.30.refs_0_, bf16[1024,1024]{1,0:T(8,128)(2,1)} %get-tuple-element.156.refs_1_, bf16[1024,4096]{1,0:T(8,128)(2,1)} %get-tuple-element.199.refs_2_.refs_0_, f32[4,4,32,4096]{3,2,1,0:T(8,128)} %collective-permute-done.54.refs_3_, ...), custom_call_target="tpu_custom_call" | custom-call | flops 4294967296 | bytes 23068672 | tf_op jit(solution)/shard_map/grad_up/pallas_call | solution.py:368
  390.6 7.9 %grad_out_sib.1.refs_7_ = bf16[4,4,32,1408]{3,2,1,0:T(8,128)(2,1)} custom-call(s32[17]{0:T(128)} %concatenate.30.refs_0_, bf16[1024,1024]{1,0:T(8,128)(2,1)} %attention.1.refs_1_, bf16[1024,1024]{1,0:T(8,128)(2,1)} %get-tuple-element.207.refs_2_, bf16[1024,1024]{1,0:T(8,128)(2,1)} %get-tuple-element.117.refs_3_, ...), custom_call_target="tpu_custom_call" | custom-call | flops 1476395008 | bytes 9306112 | tf_op jit(solution)/shard_map/grad_out_sib/pallas_call | solution.py:368
  398.4 21.5 %attention_back.2 = (bf16[3,1024,512]{2,1,0:T(8,128)(2,1)}, f32[3,1,512]{2,1,0:T(1,128)}) custom-call(s32[9]{0:T(128)} %pad_add_fusion.refs_0_, bf16[1024,3072]{1,0:T(8,128)(2,1)} %get-tuple-element.141.refs_1_.refs_2_.refs_3_, bf16[1024,3072]{1,0:T(8,128)(2,1)} %get-tuple-element.141.refs_1_.refs_2_.refs_3_, ...), custom_call_target="tpu_custom_call" | custom-call | flops 24999999488 | bytes 7340032 | tf_op jit(solution)/shard_map/attention_back/pallas_call | solution.py:368
  424.1 3.3 bitcast_add_fusion
  428.6 5.9 %grad_qkv_sib.2.refs_6_ = bf16[4,4,32,1536]{3,2,1,0:T(8,128)(2,1)} custom-call(s32[17]{0:T(128)} %concatenate.30.refs_0_, bf16[512,1024]{1,0:T(8,128)(2,1)} %get-tuple-element.215.refs_1_, bf16[3,1024,512]{2,1,0:T(8,128)(2,1)} %get-tuple-element.214.refs_2_.refs_0_, f32[1,128,1024]{2,1,0:T(8,128)} %copy-done.15, bf16[4,32,4096]{2,1,0:T(8,128)(2,1)} %copy-done.11), custom_call_target="tpu_custom_call" | custom-call | flops 1610612736 | bytes 9961472 | tf_op jit(solution)/shard_map/grad_qkv_sib/pallas_call | solution.py:368
  435.6 8.4 %grad_out.1 = (bf16[2,4,32,1408]{3,2,1,0:T(8,128)(2,1)}, f32[2,4,32,1408]{3,2,1,0:T(8,128)}) custom-call(s32[17]{0:T(128)} %concatenate.30.refs_0_, bf16[1024,1024]{1,0:T(8,128)(2,1)} %attention.1.refs_1_, bf16[1024,1024]{1,0:T(8,128)(2,1)} %get-tuple-element.207.refs_2_, bf16[1024,1024]{1,0:T(8,128)(2,1)} %get-tuple-element.117.refs_3_, ...), custom_call_target="tpu_custom_call" | custom-call | flops 1476395008 | bytes 9306112 | tf_op jit(solution)/shard_map/grad_out/pallas_call | solution.py:368
  444.0 21.7 %attention_back.3 = (bf16[3,1024,512]{2,1,0:T(8,128)(2,1)}, f32[3,1,512]{2,1,0:T(1,128)}) custom-call(s32[9]{0:T(128)} %pad_add_fusion.refs_0_, bf16[1024,3072]{1,0:T(8,128)(2,1)} %get-tuple-element.141.refs_1_.refs_2_.refs_3_, bf16[1024,3072]{1,0:T(8,128)(2,1)} %get-tuple-element.141.refs_1_.refs_2_.refs_3_, ...), custom_call_target="tpu_custom_call" | custom-call | flops 24999999488 | bytes 7340032 | tf_op jit(solution)/shard_map/attention_back/pallas_call | solution.py:368
  467.0 2.0 fusion.14.refs_3_
  469.1 6.0 %grad_qkv_sib.3.refs_4_ = bf16[4,4,32,1536]{3,2,1,0:T(8,128)(2,1)} custom-call(s32[17]{0:T(128)} %concatenate.30.refs_0_, bf16[512,1024]{1,0:T(8,128)(2,1)} %get-tuple-element.215.refs_1_, bf16[3,1024,512]{2,1,0:T(8,128)(2,1)} %get-tuple-element.221.refs_2_.refs_1_, f32[128,1024]{1,0:T(8,128)} %fusion.14.refs_3_), custom_call_target="tpu_custom_call" | custom-call | flops 1610612736 | bytes 9961472 | tf_op jit(solution)/shard_map/grad_qkv_sib/pallas_call | solution.py:368
  477.3 2.4 bitcast_add_fusion.10
  482.0 4.3 collective-permute-start.66
  488.6 6.5 %grad_qkv.2 = (bf16[2,4,32,1536]{3,2,1,0:T(8,128)(2,1)}, f32[2,4,32,1536]{3,2,1,0:T(8,128)}) custom-call(s32[17]{0:T(128)} %concatenate.30.refs_0_, bf16[512,1024]{1,0:T(8,128)(2,1)} %get-tuple-element.135.refs_13_.refs_1_, bf16[3,1024,512]{2,1,0:T(8,128)(2,1)} %get-tuple-element.214.refs_2_.refs_0_, bf16[4,4,32,1536]{3,2,1,0:T(8,128)(2,1)} %copy-done.18, ...), custom_call_target="tpu_custom_call" | custom-call | flops 1610612736 | bytes 9961472 | tf_op jit(solution)/shard_map/grad_qkv/pallas_call | solution.py:368
  495.2 2.0 collective-permute-start.67
  500.2 3.0 collective-permute-start.72
  503.2 6.4 %grad_qkv.3 = (bf16[2,4,32,1536]{3,2,1,0:T(8,128)(2,1)}, f32[2,4,32,1536]{3,2,1,0:T(8,128)}) custom-call(s32[17]{0:T(128)} %concatenate.30.refs_0_, bf16[512,1024]{1,0:T(8,128)(2,1)} %get-tuple-element.135.refs_13_.refs_1_, bf16[3,1024,512]{2,1,0:T(8,128)(2,1)} %get-tuple-element.221.refs_2_.refs_1_, ...), custom_call_target="tpu_custom_call" | custom-call | flops 1610612736 | bytes 9961472 | tf_op jit(solution)/shard_map/grad_qkv/pallas_call | solution.py:368
  512.1 2.5 collective-permute-start.69
  514.6 12.3 %input_back.1 = f32[1024,1024]{1,0:T(8,128)} custom-call(bf16[3,1024,512]{2,1,0:T(8,128)(2,1)} %get-tuple-element.214.refs_2_.refs_0_, bf16[3,1024,512]{2,1,0:T(8,128)(2,1)} %get-tuple-element.221.refs_2_.refs_1_, bf16[1024,3072]{1,0:T(8,128)(2,1)} %bitcast.544, f32[1024,1024]{1,0:T(8,128)} %get-tuple-element.223.refs_3_, bf16[8,32,1536]{2,1,0:T(8,128)(2,1)} %bitcast.541, ...), custom_call_target="tpu_custom_call" | custom-call | flops 6442450944 | bytes 20971520 | tf_op jit(solution)/shard_map/input_back/pallas_call | solution.py:368
  529.4 3.4 pack.1
  537.4 3.1 collective-permute-done.77
  541.7 2.6 collective-permute-done.78
  544.6 5.2 collective-permute-done.79
  549.9 2.4 collective-permute-start.80
  556.5 6.1 %collective-permute-done.75 = bf16[1,32,3072]{2,1,0:T(8,128)(2,1)S(1)} collective-permute-done((bf16[1,32,3072]{2,1,0:T(8,128)(2,1)S(1)}, bf16[1,32,3072]{2,1,0:T(8,128)(2,1)S(1)}, u32[]{:S(2)}, u32[]{:S(2)}) %collective-permute-start.75) | collective-permute-done | bytes 196640 | tf_op jit(solution)/shard_map/ppermute | solution.py:56
  (365 shorter events, 109.1 us)
Async XLA Ops:
  1.7 17.1 %collective-permute-start.1 = (bf16[32,4480]{1,0:T(8,128)(2,1)S(1)}, bf16[32,4480]{1,0:T(8,128)(2,1)S(1)}, u32[]{:S(2)}, u32[]{:S(2)}) collective-permute-start(bf16[32,4480]{1,0:T(8,128)(2,1)S(1)} %fusion.28), channel_id=1, source_target_pairs={{0,4},{1,5},{2,6},{3,7},{4,0},{5,1},{6,2},{7,3},{8,12},{9,13},{10,... | collective-permute-start | bytes 860168 | tf_op jit(solution)/shard_map/ppermute | solution.py:56
  11.2 28.1 %collective-permute-start = (bf16[4,128]{1,0:T(4,128)(2,1)S(1)}, bf16[4,128]{1,0:T(4,128)(2,1)S(1)}, u32[]{:S(2)}, u32[]{:S(2)}) collective-permute-start(bf16[4,128]{1,0:T(4,128)(2,1)S(1)} %pad_bitcast_fusion), channel_id=1, source_target_pairs={{0,4},{1,5},{2,6},{3,7},{4,0},{5,1},{6,2},{7,3},{8,12},{9,13},{10,... | collective-permute-start | bytes 3080 | tf_op jit(solution)/shard_map/ppermute | solution.py:56
  19.9 14.2 %collective-permute-start.3 = (bf16[2,32,4480]{2,1,0:T(8,128)(2,1)S(1)}, bf16[2,32,4480]{2,1,0:T(8,128)(2,1)S(1)}, u32[]{:S(2)}, u32[]{:S(2)}) collective-permute-start(bf16[2,32,4480]{2,1,0:T(8,128)(2,1)S(1)} %pad_maximum_fusion.4), channel_id=1, source_target_pairs={{0,2},{1,3},{2,0},{3,1},{4,6},{5,7},{6,4},{7,5},{8,10},{9,11},{10,... | collective-permute-start | bytes 1720328 | tf_op jit(solution)/shard_map/ppermute | solution.py:56
  36.1 24.9 %collective-permute-start.5 = (bf16[4,32,4480]{2,1,0:T(8,128)(2,1)}, bf16[4,32,4480]{2,1,0:T(8,128)(2,1)S(1)}, u32[]{:S(2)}, u32[]{:S(2)}) collective-permute-start(bf16[4,32,4480]{2,1,0:T(8,128)(2,1)} %bitcast.17.refs_5_.refs_6_.refs_16_), channel_id=1, source_target_pairs={{0,8},{1,17},{2,10},{3,19},{4,12},{5,21},{6,14},{7,23},{8,0},{9,25... | collective-permute-start | bytes 3440648 | tf_op jit(solution)/shard_map/ppermute | solution.py:56
  41.9 28.7 %collective-permute-start.9 = (bf16[4,32,4480]{2,1,0:T(8,128)(2,1)}, bf16[4,32,4480]{2,1,0:T(8,128)(2,1)}, u32[]{:S(2)}, u32[]{:S(2)}) collective-permute-start(bf16[4,32,4480]{2,1,0:T(8,128)(2,1)} %bitcast.17.refs_5_.refs_6_.refs_16_), channel_id=1, source_target_pairs={{0,16},{1,9},{2,18},{3,11},{4,20},{5,13},{6,22},{7,15},{8,24},{9,1... | collective-permute-start | bytes 3440648 | tf_op jit(solution)/shard_map/ppermute | solution.py:56
  43.4 19.7 %collective-permute-start.14 = (bf16[32,4096]{1,0:T(8,128)(2,1)S(1)}, bf16[32,4096]{1,0:T(8,128)(2,1)S(1)}, u32[]{:S(2)}, u32[]{:S(2)}) collective-permute-start(bf16[32,4096]{1,0:T(8,128)(2,1)S(1)} %copy-done.37), channel_id=1, source_target_pairs={{0,4},{1,5},{2,6},{3,7},{4,0},{5,1},{6,2},{7,3},{8,12},{9,13},{10,... | collective-permute-start | bytes 786440 | tf_op jit(solution)/shard_map/ppermute | solution.py:56
  46.8 20.3 %collective-permute-start.4 = (bf16[2,2,4,128]{3,2,1,0:T(4,128)(2,1)S(1)}, bf16[2,2,4,128]{3,2,1,0:T(4,128)(2,1)S(1)}, u32[]{:S(2)}, u32[]{:S(2)}) collective-permute-start(bf16[2,2,4,128]{3,2,1,0:T(4,128)(2,1)S(1)} %pad_maximum_fusion.18), channel_id=1, source_target_pairs={{0,16},{1,17},{2,18},{3,19},{4,20},{5,21},{6,22},{7,23},{8,24},{9,... | collective-permute-start | bytes 12296 | tf_op jit(solution)/shard_map/ppermute | solution.py:56
  61.0 16.1 %collective-permute-start.7 = (bf16[4,32,4480]{2,1,0:T(8,128)(2,1)S(1)}, bf16[4,32,4480]{2,1,0:T(8,128)(2,1)}, u32[]{:S(2)}, u32[]{:S(2)}) collective-permute-start(bf16[4,32,4480]{2,1,0:T(8,128)(2,1)S(1)} %collective-permute-done.5.refs_6_.refs_7_.refs_17_), channel_id=1, source_target_pairs={{0,16},{1,9},{2,18},{3,11},{4,20},{5,13},{6,22},{7,15},{8,24},{9,1... | collective-permute-start | bytes 3440648 | tf_op jit(solution)/shard_map/ppermute | solution.py:56
  64.0 13.3 %collective-permute-start.15 = (bf16[2,32,4096]{2,1,0:T(8,128)(2,1)}, bf16[2,32,4096]{2,1,0:T(8,128)(2,1)}, u32[]{:S(2)}, u32[]{:S(2)}) collective-permute-start(bf16[2,32,4096]{2,1,0:T(8,128)(2,1)} %pad_maximum_fusion.7), channel_id=1, source_target_pairs={{0,2},{1,3},{2,0},{3,1},{4,6},{5,7},{6,4},{7,5},{8,10},{9,11},{10,... | collective-permute-start | bytes 1572872 | tf_op jit(solution)/shard_map/ppermute | solution.py:56
  70.5 8.6 %collective-permute-start.10 = (bf16[4,32,4480]{2,1,0:T(8,128)(2,1)}, bf16[4,32,4480]{2,1,0:T(8,128)(2,1)S(1)}, u32[]{:S(2)}, u32[]{:S(2)}) collective-permute-start(bf16[4,32,4480]{2,1,0:T(8,128)(2,1)} %bitcast.17.refs_5_.refs_6_.refs_16_), channel_id=1, source_target_pairs={{0,1},{1,0},{2,3},{3,2},{4,5},{5,4},{6,7},{7,6},{8,9},{9,8},{10,11... | collective-permute-start | bytes 3440648 | tf_op jit(solution)/shard_map/ppermute | solution.py:56
  70.6 19.7 %collective-permute-start.11 = (bf16[4,32,4480]{2,1,0:T(8,128)(2,1)S(1)}, bf16[4,32,4480]{2,1,0:T(8,128)(2,1)S(1)}, u32[]{:S(2)}, u32[]{:S(2)}) collective-permute-start(bf16[4,32,4480]{2,1,0:T(8,128)(2,1)S(1)} %collective-permute-done.5.refs_6_.refs_7_.refs_17_), channel_id=1, source_target_pairs={{0,1},{1,0},{2,3},{3,2},{4,5},{5,4},{6,7},{7,6},{8,9},{9,8},{10,11... | collective-permute-start | bytes 3440648 | tf_op jit(solution)/shard_map/ppermute | solution.py:56
  71.1 15.8 %collective-permute-start.12 = (bf16[4,32,4480]{2,1,0:T(8,128)(2,1)}, bf16[4,32,4480]{2,1,0:T(8,128)(2,1)}, u32[]{:S(2)}, u32[]{:S(2)}) collective-permute-start(bf16[4,32,4480]{2,1,0:T(8,128)(2,1)} %collective-permute-done.9.refs_7_.refs_8_.refs_18_), channel_id=1, source_target_pairs={{0,1},{1,0},{2,3},{3,2},{4,5},{5,4},{6,7},{7,6},{8,9},{9,8},{10,11... | collective-permute-start | bytes 3440648 | tf_op jit(solution)/shard_map/ppermute | solution.py:56
  77.3 13.0 %collective-permute-start.13 = (bf16[4,32,4480]{2,1,0:T(8,128)(2,1)}, bf16[4,32,4480]{2,1,0:T(8,128)(2,1)}, u32[]{:S(2)}, u32[]{:S(2)}) collective-permute-start(bf16[4,32,4480]{2,1,0:T(8,128)(2,1)} %collective-permute-done.7.refs_8_.refs_9_.refs_19_), channel_id=1, source_target_pairs={{0,1},{1,0},{2,3},{3,2},{4,5},{5,4},{6,7},{7,6},{8,9},{9,8},{10,11... | collective-permute-start | bytes 3440648 | tf_op jit(solution)/shard_map/ppermute | solution.py:56
  79.2 27.0 %collective-permute-start.16 = (bf16[4,32,4096]{2,1,0:T(8,128)(2,1)S(1)}, bf16[4,32,4096]{2,1,0:T(8,128)(2,1)S(1)}, u32[]{:S(2)}, u32[]{:S(2)}) collective-permute-start(bf16[4,32,4096]{2,1,0:T(8,128)(2,1)S(1)} %bitcast.494), channel_id=1, source_target_pairs={{0,8},{1,17},{2,10},{3,19},{4,12},{5,21},{6,14},{7,23},{8,0},{9,25... | collective-permute-start | bytes 3145736 | tf_op jit(solution)/shard_map/ppermute | solution.py:56
  80.6 25.8 %collective-permute-start.17 = (bf16[4,32,4096]{2,1,0:T(8,128)(2,1)S(1)}, bf16[4,32,4096]{2,1,0:T(8,128)(2,1)S(1)}, u32[]{:S(2)}, u32[]{:S(2)}) collective-permute-start(bf16[4,32,4096]{2,1,0:T(8,128)(2,1)S(1)} %bitcast.495), channel_id=1, source_target_pairs={{0,16},{1,9},{2,18},{3,11},{4,20},{5,13},{6,22},{7,15},{8,24},{9,1... | collective-permute-start | bytes 3145736 | tf_op jit(solution)/shard_map/ppermute | solution.py:56
  86.9 19.5 %collective-permute-start.19 = (bf16[128,1024]{1,0:T(8,128)(2,1)S(1)}, bf16[128,1024]{1,0:T(8,128)(2,1)S(1)}, u32[]{:S(2)}, u32[]{:S(2)}) collective-permute-start(bf16[128,1024]{1,0:T(8,128)(2,1)S(1)} %copy-done.38), channel_id=1, source_target_pairs={{0,4},{1,5},{2,6},{3,7},{4,0},{5,1},{6,2},{7,3},{8,12},{9,13},{10,... | collective-permute-start | bytes 786440 | tf_op jit(solution)/shard_map/ppermute | solution.py:56
  106.2 22.5 %collective-permute-start.18 = (bf16[4,32,4096]{2,1,0:T(8,128)(2,1)S(1)}, bf16[4,32,4096]{2,1,0:T(8,128)(2,1)S(1)}, u32[]{:S(2)}, u32[]{:S(2)}) collective-permute-start(bf16[4,32,4096]{2,1,0:T(8,128)(2,1)S(1)} %collective-permute-done.16.refs_4_.refs_15_), channel_id=1, source_target_pairs={{0,16},{1,9},{2,18},{3,11},{4,20},{5,13},{6,22},{7,15},{8,24},{9,1... | collective-permute-start | bytes 3145736 | tf_op jit(solution)/shard_map/ppermute | solution.py:56
  106.5 22.2 %collective-permute-start.20 = (bf16[2,128,1024]{2,1,0:T(8,128)(2,1)S(1)}, bf16[2,128,1024]{2,1,0:T(8,128)(2,1)S(1)}, u32[]{:S(2)}, u32[]{:S(2)}) collective-permute-start(bf16[2,128,1024]{2,1,0:T(8,128)(2,1)S(1)} %pad_maximum_fusion.8), channel_id=1, source_target_pairs={{0,2},{1,3},{2,0},{3,1},{4,6},{5,7},{6,4},{7,5},{8,10},{9,11},{10,... | collective-permute-start | bytes 1572872 | tf_op jit(solution)/shard_map/ppermute | solution.py:56
  128.2 12.9 %collective-permute-start.23 = (bf16[4,32,4096]{2,1,0:T(8,128)(2,1)}, bf16[4,32,4096]{2,1,0:T(8,128)(2,1)S(1)}, u32[]{:S(2)}, u32[]{:S(2)}) collective-permute-start(bf16[4,32,4096]{2,1,0:T(8,128)(2,1)} %copy-done.5), channel_id=1, source_target_pairs={{0,1},{1,0},{2,3},{3,2},{4,5},{5,4},{6,7},{7,6},{8,9},{9,8},{10,11... | collective-permute-start | bytes 3145736 | tf_op jit(solution)/shard_map/ppermute | solution.py:56
  128.2 14.1 %collective-permute-start.22 = (bf16[4,32,4096]{2,1,0:T(8,128)(2,1)}, bf16[4,32,4096]{2,1,0:T(8,128)(2,1)S(1)}, u32[]{:S(2)}, u32[]{:S(2)}) collective-permute-start(bf16[4,32,4096]{2,1,0:T(8,128)(2,1)} %copy-done.4), channel_id=1, source_target_pairs={{0,1},{1,0},{2,3},{3,2},{4,5},{5,4},{6,7},{7,6},{8,9},{9,8},{10,11... | collective-permute-start | bytes 3145736 | tf_op jit(solution)/shard_map/ppermute | solution.py:56
  128.7 13.6 %collective-permute-start.21 = (bf16[4,32,4096]{2,1,0:T(8,128)(2,1)S(1)}, bf16[4,32,4096]{2,1,0:T(8,128)(2,1)}, u32[]{:S(2)}, u32[]{:S(2)}) collective-permute-start(bf16[4,32,4096]{2,1,0:T(8,128)(2,1)S(1)} %bitcast.496), channel_id=1, source_target_pairs={{0,1},{1,0},{2,3},{3,2},{4,5},{5,4},{6,7},{7,6},{8,9},{9,8},{10,11... | collective-permute-start | bytes 3145736 | tf_op jit(solution)/shard_map/ppermute | solution.py:56
  128.7 13.6 %collective-permute-start.24 = (bf16[4,32,4096]{2,1,0:T(8,128)(2,1)S(1)}, bf16[4,32,4096]{2,1,0:T(8,128)(2,1)}, u32[]{:S(2)}, u32[]{:S(2)}) collective-permute-start(bf16[4,32,4096]{2,1,0:T(8,128)(2,1)S(1)} %collective-permute-done.18.refs_17_.refs_6_), channel_id=1, source_target_pairs={{0,1},{1,0},{2,3},{3,2},{4,5},{5,4},{6,7},{7,6},{8,9},{9,8},{10,11... | collective-permute-start | bytes 3145736 | tf_op jit(solution)/shard_map/ppermute | solution.py:56
  129.7 29.6 %collective-permute-start.25 = (bf16[4,128,1024]{2,1,0:T(8,128)(2,1)S(1)}, bf16[4,128,1024]{2,1,0:T(8,128)(2,1)S(1)}, u32[]{:S(2)}, u32[]{:S(2)}) collective-permute-start(bf16[4,128,1024]{2,1,0:T(8,128)(2,1)S(1)} %bitcast.505), channel_id=1, source_target_pairs={{0,8},{1,17},{2,10},{3,19},{4,12},{5,21},{6,14},{7,23},{8,0},{9,25... | collective-permute-start | bytes 3145736 | tf_op jit(solution)/shard_map/ppermute | solution.py:56
  141.1 19.2 %collective-permute-start.26 = (bf16[4,128,1024]{2,1,0:T(8,128)(2,1)}, bf16[4,128,1024]{2,1,0:T(8,128)(2,1)S(1)}, u32[]{:S(2)}, u32[]{:S(2)}) collective-permute-start(bf16[4,128,1024]{2,1,0:T(8,128)(2,1)} %bitcast.506), channel_id=1, source_target_pairs={{0,16},{1,9},{2,18},{3,11},{4,20},{5,13},{6,22},{7,15},{8,24},{9,1... | collective-permute-start | bytes 3145736 | tf_op jit(solution)/shard_map/ppermute | solution.py:56
  159.3 17.8 %collective-permute-start.27 = (bf16[4,128,1024]{2,1,0:T(8,128)(2,1)S(1)}, bf16[4,128,1024]{2,1,0:T(8,128)(2,1)S(1)}, u32[]{:S(2)}, u32[]{:S(2)}) collective-permute-start(bf16[4,128,1024]{2,1,0:T(8,128)(2,1)S(1)} %collective-permute-done.25.refs_14_.refs_9_), channel_id=1, source_target_pairs={{0,16},{1,9},{2,18},{3,11},{4,20},{5,13},{6,22},{7,15},{8,24},{9,1... | collective-permute-start | bytes 3145736 | tf_op jit(solution)/shard_map/ppermute | solution.py:56
  160.2 17.5 %collective-permute-start.29 = (bf16[4,128,1024]{2,1,0:T(8,128)(2,1)S(1)}, bf16[4,128,1024]{2,1,0:T(8,128)(2,1)S(1)}, u32[]{:S(2)}, u32[]{:S(2)}) collective-permute-start(bf16[4,128,1024]{2,1,0:T(8,128)(2,1)S(1)} %collective-permute-done.25.refs_14_.refs_9_), channel_id=1, source_target_pairs={{0,1},{1,0},{2,3},{3,2},{4,5},{5,4},{6,7},{7,6},{8,9},{9,8},{10,11... | collective-permute-start | bytes 3145736 | tf_op jit(solution)/shard_map/ppermute | solution.py:56
  160.2 17.5 %collective-permute-start.30 = (bf16[4,128,1024]{2,1,0:T(8,128)(2,1)S(1)}, bf16[4,128,1024]{2,1,0:T(8,128)(2,1)S(1)}, u32[]{:S(2)}, u32[]{:S(2)}) collective-permute-start(bf16[4,128,1024]{2,1,0:T(8,128)(2,1)S(1)} %collective-permute-done.26.refs_15_.refs_10_), channel_id=1, source_target_pairs={{0,1},{1,0},{2,3},{3,2},{4,5},{5,4},{6,7},{7,6},{8,9},{9,8},{10,11... | collective-permute-start | bytes 3145736 | tf_op jit(solution)/shard_map/ppermute | solution.py:56
  160.7 17.0 %collective-permute-start.28 = (bf16[4,128,1024]{2,1,0:T(8,128)(2,1)S(1)}, bf16[4,128,1024]{2,1,0:T(8,128)(2,1)S(1)}, u32[]{:S(2)}, u32[]{:S(2)}) collective-permute-start(bf16[4,128,1024]{2,1,0:T(8,128)(2,1)S(1)} %bitcast.508), channel_id=1, source_target_pairs={{0,1},{1,0},{2,3},{3,2},{4,5},{5,4},{6,7},{7,6},{8,9},{9,8},{10,11... | collective-permute-start | bytes 3145736 | tf_op jit(solution)/shard_map/ppermute | solution.py:56
  203.6 5.6 collective-permute-start.32
  205.6 5.5 collective-permute-start.33
  209.2 5.6 collective-permute-start.34
  214.8 5.4 collective-permute-start.35
  216.3 5.5 collective-permute-start.37
  245.2 5.4 collective-permute-start.45
  262.6 7.8 %collective-permute-start.46 = (bf16[4,4,32,384]{3,2,1,0:T(8,128)(2,1)}, bf16[4,4,32,384]{3,2,1,0:T(8,128)(2,1)S(1)}, u32[]{:S(2)}, u32[]{:S(2)}) collective-permute-start(bf16[4,4,32,384]{3,2,1,0:T(8,128)(2,1)} %bitcast.542), channel_id=1, source_target_pairs={{0,1},{1,0},{2,3},{3,2},{4,5},{5,4},{6,7},{7,6},{8,9},{9,8},{10,11... | collective-permute-start | bytes 1179656 | tf_op jit(solution)/shard_map/ppermute | solution.py:56
  270.5 5.3 collective-permute-start.47
  271.6 7.0 %collective-permute-start.48 = (bf16[4,32,384]{2,1,0:T(8,128)(2,1)S(1)}, bf16[4,32,384]{2,1,0:T(8,128)(2,1)S(1)}, u32[]{:S(2)}, u32[]{:S(2)}) collective-permute-start(bf16[4,32,384]{2,1,0:T(8,128)(2,1)S(1)} %get-tuple-element.291), channel_id=1, source_target_pairs={{0,16},{1,17},{2,18},{3,19},{4,20},{5,21},{6,22},{7,23},{8,24},{9,... | collective-permute-start | bytes 294920 | tf_op jit(solution)/shard_map/ppermute | solution.py:56
  272.1 6.6 %collective-permute-start.49 = (bf16[4,32,384]{2,1,0:T(8,128)(2,1)S(1)}, bf16[4,32,384]{2,1,0:T(8,128)(2,1)S(1)}, u32[]{:S(2)}, u32[]{:S(2)}) collective-permute-start(bf16[4,32,384]{2,1,0:T(8,128)(2,1)S(1)} %get-tuple-element.290), channel_id=1, source_target_pairs={{0,24},{1,25},{2,26},{3,27},{4,28},{5,29},{6,30},{7,31},{8,16},{9,... | collective-permute-start | bytes 294920 | tf_op jit(solution)/shard_map/ppermute | solution.py:56
  279.1 5.6 collective-permute-start.51
  282.9 5.6 collective-permute-start.52
  303.2 14.9 %collective-permute-start.53 = (bf16[4,4,128,1024]{3,2,1,0:T(8,128)(2,1)}, bf16[4,4,128,1024]{3,2,1,0:T(8,128)(2,1)S(1)}, u32[]{:S(2)}, u32[]{:S(2)}) collective-permute-start(bf16[4,4,128,1024]{3,2,1,0:T(8,128)(2,1)} %grad_down_sib.1.refs_3_), channel_id=1, source_target_pairs={{0,1},{1,0},{2,3},{3,2},{4,5},{5,4},{6,7},{7,6},{8,9},{9,8},{10,11... | collective-permute-start | bytes 12582920 | tf_op jit(solution)/shard_map/ppermute | solution.py:56
  343.9 31.3 %collective-permute-start.54 = (f32[4,4,32,4096]{3,2,1,0:T(8,128)}, f32[4,4,32,4096]{3,2,1,0:T(8,128)}, u32[]{:S(2)}, u32[]{:S(2)}) collective-permute-start(f32[4,4,32,4096]{3,2,1,0:T(8,128)} %grad_up_sib.1.refs_7_), channel_id=1, source_target_pairs={{0,1},{1,0},{2,3},{3,2},{4,5},{5,4},{6,7},{7,6},{8,9},{9,8},{10,11... | collective-permute-start | bytes 25165832 | tf_op jit(solution)/shard_map/ppermute | solution.py:56
  344.4 26.1 %collective-permute-start.55 = (bf16[8,128,1024]{2,1,0:T(8,128)(2,1)S(1)}, bf16[8,128,1024]{2,1,0:T(8,128)(2,1)}, u32[]{:S(2)}, u32[]{:S(2)}) collective-permute-start(bf16[8,128,1024]{2,1,0:T(8,128)(2,1)S(1)} %bitcast.516), channel_id=1, source_target_pairs={{0,16},{1,9},{2,18},{3,11},{4,20},{5,13},{6,22},{7,15},{8,24},{9,1... | collective-permute-start | bytes 6291464 | tf_op jit(solution)/shard_map/ppermute | solution.py:56
  373.0 16.3 %collective-permute-start.56 = (bf16[4,128,1024]{2,1,0:T(8,128)(2,1)S(1)}, bf16[4,128,1024]{2,1,0:T(8,128)(2,1)}, u32[]{:S(2)}, u32[]{:S(2)}) collective-permute-start(bf16[4,128,1024]{2,1,0:T(8,128)(2,1)S(1)} %get-tuple-element.264.refs_5_), channel_id=1, source_target_pairs={{0,8},{1,17},{2,10},{3,19},{4,12},{5,21},{6,14},{7,23},{8,0},{9,25... | collective-permute-start | bytes 3145736 | tf_op jit(solution)/shard_map/ppermute | solution.py:56
  388.5 34.3 %collective-permute-start.59 = (bf16[8,32,4096]{2,1,0:T(8,128)(2,1)}, bf16[8,32,4096]{2,1,0:T(8,128)(2,1)S(1)}, u32[]{:S(2)}, u32[]{:S(2)}) collective-permute-start(bf16[8,32,4096]{2,1,0:T(8,128)(2,1)} %bitcast.517), channel_id=1, source_target_pairs={{0,16},{1,9},{2,18},{3,11},{4,20},{5,13},{6,22},{7,15},{8,24},{9,1... | collective-permute-start | bytes 6291464 | tf_op jit(solution)/shard_map/ppermute | solution.py:56
  390.5 31.3 %collective-permute-start.58 = (bf16[2,128,1024]{2,1,0:T(8,128)(2,1)S(1)}, bf16[2,128,1024]{2,1,0:T(8,128)(2,1)S(1)}, u32[]{:S(2)}, u32[]{:S(2)}) collective-permute-start(bf16[2,128,1024]{2,1,0:T(8,128)(2,1)S(1)} %fusion.8.refs_8_), channel_id=1, source_target_pairs={{0,2},{1,3},{2,0},{3,1},{4,6},{5,7},{6,4},{7,5},{8,10},{9,11},{10,... | collective-permute-start | bytes 1572872 | tf_op jit(solution)/shard_map/ppermute | solution.py:56
  398.4 36.0 %collective-permute-start.57 = (bf16[4,4,32,1408]{3,2,1,0:T(8,128)(2,1)}, bf16[4,4,32,1408]{3,2,1,0:T(8,128)(2,1)S(1)}, u32[]{:S(2)}, u32[]{:S(2)}) collective-permute-start(bf16[4,4,32,1408]{3,2,1,0:T(8,128)(2,1)} %grad_out_sib.1.refs_7_), channel_id=1, source_target_pairs={{0,1},{1,0},{2,3},{3,2},{4,5},{5,4},{6,7},{7,6},{8,9},{9,8},{10,11... | collective-permute-start | bytes 4325384 | tf_op jit(solution)/shard_map/ppermute | solution.py:56
  421.9 45.1 %collective-permute-start.60 = (f32[1,128,1024]{2,1,0:T(8,128)S(1)}, f32[1,128,1024]{2,1,0:T(8,128)}, u32[]{:S(2)}, u32[]{:S(2)}) collective-permute-start(f32[1,128,1024]{2,1,0:T(8,128)S(1)} %bitcast_add_fusion.15.refs_3_.refs_8_), channel_id=1, source_target_pairs={{0,4},{1,5},{2,6},{3,7},{4,0},{5,1},{6,2},{7,3},{8,12},{9,13},{10,... | collective-permute-start | bytes 1572872 | tf_op jit(solution)/shard_map/ppermute | solution.py:56
  427.5 53.3 %collective-permute-start.64 = (bf16[4,32,4096]{2,1,0:T(8,128)(2,1)S(1)}, bf16[4,32,4096]{2,1,0:T(8,128)(2,1)}, u32[]{:S(2)}, u32[]{:S(2)}) collective-permute-start(bf16[4,32,4096]{2,1,0:T(8,128)(2,1)S(1)} %get-tuple-element.262.refs_4_.refs_9_), channel_id=1, source_target_pairs={{0,8},{1,17},{2,10},{3,19},{4,12},{5,21},{6,14},{7,23},{8,0},{9,25... | collective-permute-start | bytes 3145736 | tf_op jit(solution)/shard_map/ppermute | solution.py:56
  465.7 11.6 %collective-permute-start.63 = (bf16[8,32,1408]{2,1,0:T(8,128)(2,1)}, bf16[8,32,1408]{2,1,0:T(8,128)(2,1)}, u32[]{:S(2)}, u32[]{:S(2)}) collective-permute-start(bf16[8,32,1408]{2,1,0:T(8,128)(2,1)} %bitcast.73.refs_7_), channel_id=1, source_target_pairs={{0,16},{1,9},{2,18},{3,11},{4,20},{5,13},{6,22},{7,15},{8,24},{9,1... | collective-permute-start | bytes 2162696 | tf_op jit(solution)/shard_map/ppermute | solution.py:56
  467.0 20.4 %collective-permute-start.62 = (bf16[4,4,32,1536]{3,2,1,0:T(8,128)(2,1)S(1)}, bf16[4,4,32,1536]{3,2,1,0:T(8,128)(2,1)S(1)}, u32[]{:S(2)}, u32[]{:S(2)}) collective-permute-start(bf16[4,4,32,1536]{3,2,1,0:T(8,128)(2,1)S(1)} %copy-done.3), channel_id=1, source_target_pairs={{0,1},{1,0},{2,3},{3,2},{4,5},{5,4},{6,7},{7,6},{8,9},{9,8},{10,11... | collective-permute-start | bytes 4718600 | tf_op jit(solution)/shard_map/ppermute | solution.py:56
  475.1 28.1 %collective-permute-start.61 = (bf16[4,4,32,1536]{3,2,1,0:T(8,128)(2,1)}, bf16[4,4,32,1536]{3,2,1,0:T(8,128)(2,1)}, u32[]{:S(2)}, u32[]{:S(2)}) collective-permute-start(bf16[4,4,32,1536]{3,2,1,0:T(8,128)(2,1)} %grad_qkv_sib.3.refs_4_), channel_id=1, source_target_pairs={{0,1},{1,0},{2,3},{3,2},{4,5},{5,4},{6,7},{7,6},{8,9},{9,8},{10,11... | collective-permute-start | bytes 4718600 | tf_op jit(solution)/shard_map/ppermute | solution.py:56
  479.7 17.5 %collective-permute-start.65 = (bf16[4,32,1408]{2,1,0:T(8,128)(2,1)}, bf16[4,32,1408]{2,1,0:T(8,128)(2,1)}, u32[]{:S(2)}, u32[]{:S(2)}) collective-permute-start(bf16[4,32,1408]{2,1,0:T(8,128)(2,1)} %get-tuple-element.270.refs_5_), channel_id=1, source_target_pairs={{0,8},{1,17},{2,10},{3,19},{4,12},{5,21},{6,14},{7,23},{8,0},{9,25... | collective-permute-start | bytes 1081352 | tf_op jit(solution)/shard_map/ppermute | solution.py:56
  482.0 15.2 %collective-permute-start.66 = (bf16[2,32,4096]{2,1,0:T(8,128)(2,1)S(1)}, bf16[2,32,4096]{2,1,0:T(8,128)(2,1)S(1)}, u32[]{:S(2)}, u32[]{:S(2)}) collective-permute-start(bf16[2,32,4096]{2,1,0:T(8,128)(2,1)S(1)} %fusion.9.refs_6_), channel_id=1, source_target_pairs={{0,2},{1,3},{2,0},{3,1},{4,6},{5,7},{6,4},{7,5},{8,10},{9,11},{10,... | collective-permute-start | bytes 1572872 | tf_op jit(solution)/shard_map/ppermute | solution.py:56
  495.2 16.7 %collective-permute-start.67 = (bf16[8,32,1536]{2,1,0:T(8,128)(2,1)}, bf16[8,32,1536]{2,1,0:T(8,128)(2,1)S(1)}, u32[]{:S(2)}, u32[]{:S(2)}) collective-permute-start(bf16[8,32,1536]{2,1,0:T(8,128)(2,1)} %bitcast.522), channel_id=1, source_target_pairs={{0,16},{1,9},{2,18},{3,11},{4,20},{5,13},{6,22},{7,15},{8,24},{9,1... | collective-permute-start | bytes 2359304 | tf_op jit(solution)/shard_map/ppermute | solution.py:56
  499.0 12.2 %collective-permute-start.68 = (bf16[2,32,1408]{2,1,0:T(8,128)(2,1)S(1)}, bf16[2,32,1408]{2,1,0:T(8,128)(2,1)S(1)}, u32[]{:S(2)}, u32[]{:S(2)}) collective-permute-start(bf16[2,32,1408]{2,1,0:T(8,128)(2,1)S(1)} %fusion.34.refs_5_), channel_id=1, source_target_pairs={{0,2},{1,3},{2,0},{3,1},{4,6},{5,7},{6,4},{7,5},{8,10},{9,11},{10,... | collective-permute-start | bytes 540680 | tf_op jit(solution)/shard_map/ppermute | solution.py:56
  500.2 27.4 %collective-permute-start.72 = (bf16[1,32,4096]{2,1,0:T(8,128)(2,1)S(1)}, bf16[1,32,4096]{2,1,0:T(8,128)(2,1)S(1)}, u32[]{:S(2)}, u32[]{:S(2)}) collective-permute-start(bf16[1,32,4096]{2,1,0:T(8,128)(2,1)S(1)} %fusion.12.refs_6_), channel_id=1, source_target_pairs={{0,4},{1,5},{2,6},{3,7},{4,0},{5,1},{6,2},{7,3},{8,12},{9,13},{10,... | collective-permute-start | bytes 786440 | tf_op jit(solution)/shard_map/ppermute | solution.py:56
  509.7 18.8 %collective-permute-start.70 = (bf16[8,32,1536]{2,1,0:T(8,128)(2,1)}, bf16[8,32,1536]{2,1,0:T(8,128)(2,1)S(1)}, u32[]{:S(2)}, u32[]{:S(2)}) collective-permute-start(bf16[8,32,1536]{2,1,0:T(8,128)(2,1)} %bitcast.540), channel_id=1, source_target_pairs={{0,16},{1,9},{2,18},{3,11},{4,20},{5,13},{6,22},{7,15},{8,24},{9,1... | collective-permute-start | bytes 2359304 | tf_op jit(solution)/shard_map/ppermute | solution.py:56
  511.2 15.7 %collective-permute-start.73 = (f32[1,32,1408]{2,1,0:T(8,128)S(1)}, f32[1,32,1408]{2,1,0:T(8,128)S(1)}, u32[]{:S(2)}, u32[]{:S(2)}) collective-permute-start(f32[1,32,1408]{2,1,0:T(8,128)S(1)} %bitcast_add_fusion.22.refs_6_), channel_id=1, source_target_pairs={{0,4},{1,5},{2,6},{3,7},{4,0},{5,1},{6,2},{7,3},{8,12},{9,13},{10,... | collective-permute-start | bytes 540680 | tf_op jit(solution)/shard_map/ppermute | solution.py:56
  512.1 24.5 %collective-permute-start.69 = (bf16[4,32,1536]{2,1,0:T(8,128)(2,1)S(1)}, bf16[4,32,1536]{2,1,0:T(8,128)(2,1)S(1)}, u32[]{:S(2)}, u32[]{:S(2)}) collective-permute-start(bf16[4,32,1536]{2,1,0:T(8,128)(2,1)S(1)} %get-tuple-element.268.refs_5_), channel_id=1, source_target_pairs={{0,8},{1,17},{2,10},{3,19},{4,12},{5,21},{6,14},{7,23},{8,0},{9,25... | collective-permute-start | bytes 1179656 | tf_op jit(solution)/shard_map/ppermute | solution.py:56
  528.7 7.8 %collective-permute-start.71 = (bf16[4,32,1536]{2,1,0:T(8,128)(2,1)S(1)}, bf16[4,32,1536]{2,1,0:T(8,128)(2,1)S(1)}, u32[]{:S(2)}, u32[]{:S(2)}) collective-permute-start(bf16[4,32,1536]{2,1,0:T(8,128)(2,1)S(1)} %get-tuple-element.265.refs_8_), channel_id=1, source_target_pairs={{0,8},{1,17},{2,10},{3,19},{4,12},{5,21},{6,14},{7,23},{8,0},{9,25... | collective-permute-start | bytes 1179656 | tf_op jit(solution)/shard_map/ppermute | solution.py:56
  541.4 8.4 %collective-permute-start.74 = (bf16[2,32,3072]{2,1,0:T(8,128)(2,1)S(1)}, bf16[2,32,3072]{2,1,0:T(8,128)(2,1)S(1)}, u32[]{:S(2)}, u32[]{:S(2)}) collective-permute-start(bf16[2,32,3072]{2,1,0:T(8,128)(2,1)S(1)} %pad_maximum_fusion.10), channel_id=1, source_target_pairs={{0,2},{1,3},{2,0},{3,1},{4,6},{5,7},{6,4},{7,5},{8,10},{9,11},{10,... | collective-permute-start | bytes 1179656 | tf_op jit(solution)/shard_map/ppermute | solution.py:56
  544.3 5.5 collective-permute-start.79
  554.3 8.4 %collective-permute-start.75 = (bf16[1,32,3072]{2,1,0:T(8,128)(2,1)S(1)}, bf16[1,32,3072]{2,1,0:T(8,128)(2,1)S(1)}, u32[]{:S(2)}, u32[]{:S(2)}) collective-permute-start(bf16[1,32,3072]{2,1,0:T(8,128)(2,1)S(1)} %fusion.18), channel_id=1, source_target_pairs={{0,4},{1,5},{2,6},{3,7},{4,0},{5,1},{6,2},{7,3},{8,12},{9,13},{10,... | collective-permute-start | bytes 589832 | tf_op jit(solution)/shard_map/ppermute | solution.py:56
  (71 other events, 425.6 us)
